TPU v7x, 32 devices: a whole 2x2x4 slice. The times are simulated.
32 devices in a mesh: dp: 4 (over x, core), expert: 2 (over y), tensor: 4 (over z).
Axes of the slice: x: 2, y: 2, z: 4, core: 2. Of those that a mesh axis runs over, the one named last changes fastest.
Arguments:
- images: bfloat16 [32, 197, 768], P(('dp', 'expert')), may hold values from -6 to 6
- images_held: int32 [8], P(('dp', 'expert')), may hold values from 2 to 4, as said below
- routes: int32 [32, 197, 2], P(('dp', 'expert')), may hold values from 0 to 31, as said below
- slot_index: int32 [32, 197, 2], P(('dp', 'expert')), may hold values from 0 to 64, as said below
- first_gain: bfloat16 [768], P('dp'), may hold values from 0.5 to 1.5
- first_shift: bfloat16 [768], P('dp'), may hold values from -1 to 1
- w_qkv: bfloat16 [3, 768, 768], P(None, 'dp', 'tensor'), may hold values from -0.21875 to 0.21875
- qv_bias: bfloat16 [2, 768], P(None, 'tensor'), may hold values from -1 to 1
- w_out: bfloat16 [768, 768], P('tensor', 'dp'), may hold values from -0.875 to 0.875
- out_bias: bfloat16 [768], P('dp'), may hold values from -1 to 1
- second_gain: bfloat16 [768], P('dp'), may hold values from 0.5 to 1.5
- second_shift: bfloat16 [768], P('dp'), may hold values from -1 to 1
- w_router: bfloat16 [768, 32], P('dp'), may hold values from -0.15625 to 0.15625
- w_in: bfloat16 [32, 768, 3072], P('expert', 'dp', 'tensor'), may hold values from -0.21875 to 0.21875
- in_bias: bfloat16 [32, 3072], P('expert', 'tensor'), may hold values from -1 to 1
- w_back: bfloat16 [32, 3072, 768], P('expert', 'tensor', 'dp'), may hold values from -1.75 to 1.75
- back_bias: bfloat16 [32, 768], P('expert', 'dp'), may hold values from -5 to 5
- cotangent: bfloat16 [32, 197, 768], P(('dp', 'expert')), may hold values from -6 to 6
Outputs:
- output: bfloat16 [32, 197, 768], P(('dp', 'expert'))
- grad_images: float32 [32, 197, 768], P(('dp', 'expert'))
- grad_first_gain: float32 [768], P('dp')
- grad_first_shift: float32 [768], P('dp')
- grad_w_qkv: float32 [3, 768, 768], P(None, 'dp', 'tensor')
- grad_qv_bias: float32 [2, 768], P(None, 'tensor')
- grad_w_out: float32 [768, 768], P('tensor', 'dp')
- grad_out_bias: float32 [768], P('dp')
- grad_second_gain: float32 [768], P('dp')
- grad_second_shift: float32 [768], P('dp')
- grad_w_router: float32 [768, 32], P('dp')
- grad_w_in: float32 [32, 768, 3072], P('expert', 'dp', 'tensor')
- grad_in_bias: float32 [32, 3072], P('expert', 'tensor')
- grad_w_back: float32 [32, 3072, 768], P('expert', 'tensor', 'dp')
- grad_back_bias: float32 [32, 768], P('expert', 'dp')
Inputs may be any that keep to these rules, and one draw needn't show every extreme that they name: `images_held`: the first images of a group are the real ones; some group is full. `routes`: a token names two different experts. `slot_index`: within one group the kept choices of one expert take the slots 0 to n - 1 once each, in the order of tokens and choices; 64 marks a dropped choice, and every choice of a token of an image past the group's count is dropped; some expert takes all 64 slots in every group.
All inputs are finite; a program needn't handle non-finite values.
Results may differ from a plain program's by a relative error of at most 0.013.
Values may be sent and summed in bfloat16 or wider, within the bound.
No kernel may reach another device: no remote copies, remote signals or barrier semaphores. Data moves between devices by JAX's collectives and lax.ppermute only.
A program may use at most 256 MiB of HBM per device.

v0:
```python
import jax
import jax.numpy as jnp
from jax import lax
from jax.sharding import PartitionSpec as P

HEAD_DIM = 64
EXPERTS = 32
TOPK = 2
CAP = 64


EPS = 1e-06


def norm_parts(values, norm_gain, norm_shift):
    average = jnp.mean(values, axis=-1, keepdims=True)
    centred = values - average
    spread = jnp.mean(centred * centred, axis=-1, keepdims=True)
    inv_std = lax.rsqrt(spread + EPS)
    scaled = centred * inv_std
    return (scaled * norm_gain + norm_shift, scaled, inv_std)


def norm_back(grad_out, scaled, inv_std, norm_gain):
    grad_scaled = grad_out * norm_gain
    inner = grad_scaled - jnp.mean(grad_scaled, axis=-1, keepdims=True)
    inner = inner - scaled * jnp.mean(grad_scaled * scaled, axis=-1, keepdims=True)
    return (inner * inv_std, jnp.sum(grad_out * scaled, axis=0), jnp.sum(grad_out, axis=0))


def attention_forward(queries, key_rows, value_rows, scale):
    scores = (
        jnp.einsum("iqhd,ikhd->ihqk", queries, key_rows, preferred_element_type=jnp.float32) * scale
    )
    row_peak = jnp.max(scores, axis=-1, keepdims=True)
    log_total = row_peak + jnp.log(jnp.sum(jnp.exp(scores - row_peak), axis=-1, keepdims=True))
    weights = jnp.exp(scores - log_total).astype(jnp.bfloat16)
    attended = jnp.einsum(
        "ihqk,ikhd->iqhd", weights, value_rows, preferred_element_type=jnp.float32
    )
    return (attended, log_total)


def attention_backward(queries, key_rows, value_rows, log_total, grad_low, scale):
    scores = (
        jnp.einsum("iqhd,ikhd->ihqk", queries, key_rows, preferred_element_type=jnp.float32) * scale
    )
    probs = jnp.exp(scores - log_total)
    weights = probs.astype(jnp.bfloat16)
    grad_values = jnp.einsum(
        "ihqk,iqhd->ikhd", weights, grad_low, preferred_element_type=jnp.float32
    )
    grad_weights = jnp.einsum(
        "iqhd,ikhd->ihqk", grad_low, value_rows, preferred_element_type=jnp.float32
    )
    grad_scores = probs * (grad_weights - jnp.sum(probs * grad_weights, axis=-1, keepdims=True))
    scores_low = grad_scores.astype(jnp.bfloat16)
    grad_queries = (
        jnp.einsum("ihqk,ikhd->iqhd", scores_low, key_rows, preferred_element_type=jnp.float32)
        * scale
    )
    grad_keys = (
        jnp.einsum("ihqk,iqhd->ikhd", scores_low, queries, preferred_element_type=jnp.float32)
        * scale
    )
    return (grad_queries, grad_keys, grad_values)


def on_device(
    images,
    images_held,
    routes,
    slot_index,
    first_gain,
    first_shift,
    w_qkv,
    qv_bias,
    w_out,
    out_bias,
    second_gain,
    second_shift,
    w_router,
    w_in,
    in_bias,
    w_back,
    back_bias,
    cotangent,
):
    image_count, seq_len, width = images.shape
    rows_total = image_count * seq_len
    experts_here = w_in.shape[0]
    (
        gain_first,
        shift_first,
        qkv_full,
        out_full,
        bias_out_full,
        gain_second,
        shift_second,
        router_full,
        in_full,
        back_full,
        back_bias_full,
    ) = (
        lax.all_gather(first_gain, "dp", axis=0, tiled=True),
        lax.all_gather(first_shift, "dp", axis=0, tiled=True),
        lax.all_gather(w_qkv, "dp", axis=1, tiled=True),
        lax.all_gather(w_out, "dp", axis=1, tiled=True),
        lax.all_gather(out_bias, "dp", axis=0, tiled=True),
        lax.all_gather(second_gain, "dp", axis=0, tiled=True),
        lax.all_gather(second_shift, "dp", axis=0, tiled=True),
        lax.all_gather(w_router, "dp", axis=0, tiled=True),
        lax.all_gather(w_in, "dp", axis=1, tiled=True),
        lax.all_gather(w_back, "dp", axis=2, tiled=True),
        lax.all_gather(back_bias, "dp", axis=1, tiled=True),
    )
    gain_first = gain_first.astype(jnp.float32)
    gain_second = gain_second.astype(jnp.float32)
    inputs = images.reshape(rows_total, width).astype(jnp.float32)
    live_image = (jnp.arange(image_count, dtype=jnp.int32) < images_held[0]).astype(jnp.float32)
    live_rows = jnp.repeat(live_image, seq_len)[:, None]
    normed, scaled_first, inv_first = norm_parts(
        inputs, gain_first, shift_first.astype(jnp.float32)
    )
    normed_low = normed.astype(jnp.bfloat16)
    projected = jnp.einsum("td,cde->cte", normed_low, qkv_full, preferred_element_type=jnp.float32)
    local_width = projected.shape[2]
    head_count = local_width // HEAD_DIM
    head_shape = (image_count, seq_len, head_count, HEAD_DIM)
    bias_pair = qv_bias.astype(jnp.float32)
    queries = (projected[0] + bias_pair[0]).astype(jnp.bfloat16).reshape(head_shape)
    key_rows = projected[1].astype(jnp.bfloat16).reshape(head_shape)
    value_rows = (projected[2] + bias_pair[1]).astype(jnp.bfloat16).reshape(head_shape)
    scale = HEAD_DIM ** (-0.5)
    attended, log_total = attention_forward(queries, key_rows, value_rows, scale)
    attended_low = attended.reshape(rows_total, local_width).astype(jnp.bfloat16)
    head_part = jnp.dot(attended_low, out_full, preferred_element_type=jnp.float32)
    mixed = inputs + lax.psum(head_part, "tensor") + bias_out_full.astype(jnp.float32)
    routed, scaled_second, inv_second = norm_parts(
        mixed, gain_second, shift_second.astype(jnp.float32)
    )
    routed_low = routed.astype(jnp.bfloat16)
    logits = jnp.dot(routed_low, router_full, preferred_element_type=jnp.float32)
    probs = jax.nn.softmax(logits, axis=-1)
    pair_routes = routes.reshape(rows_total, TOPK)
    pair_slots = slot_index.reshape(rows_total, TOPK)
    target = jnp.where(pair_slots < CAP, pair_routes * CAP + pair_slots, EXPERTS * CAP).reshape(
        rows_total * TOPK
    )
    gates = jnp.take_along_axis(probs, pair_routes, axis=1)
    pair_rows = jnp.repeat(routed_low, TOPK, axis=0)
    outgoing = (
        jnp.zeros((EXPERTS * CAP + 1, width), jnp.bfloat16)
        .at[target]
        .set(pair_rows)[: EXPERTS * CAP]
    )
    outgoing = outgoing.reshape(EXPERTS, 1, CAP, width)
    arrived = lax.all_to_all(outgoing, "expert", split_axis=0, concat_axis=1, tiled=True)
    sources = arrived.shape[1]
    expert_rows = arrived.reshape(experts_here, sources * CAP, width)
    hidden_pre = jnp.einsum(
        "erd,edf->erf", expert_rows, in_full, preferred_element_type=jnp.float32
    )
    hidden_pre = hidden_pre + in_bias.astype(jnp.float32)[:, None, :]
    hidden_value, gelu_pull = jax.vjp(jax.nn.gelu, hidden_pre)
    hidden_low = hidden_value.astype(jnp.bfloat16)
    expert_part = jnp.einsum(
        "erf,efd->erd", hidden_low, back_full, preferred_element_type=jnp.float32
    )
    bias_back = back_bias_full.astype(jnp.float32)[:, None, :]
    shares = lax.psum_scatter(
        expert_part.reshape(experts_here, sources, CAP, width),
        "tensor",
        scatter_dimension=2,
        tiled=True,
    )
    share_low = (shares + bias_back[:, None]).astype(jnp.bfloat16)
    pieces = lax.all_to_all(share_low, "expert", split_axis=1, concat_axis=0, tiled=True)
    returned = lax.all_gather(pieces, "tensor", axis=2, tiled=True)
    padded = jnp.concatenate(
        [returned.reshape(EXPERTS * CAP, width), jnp.zeros((1, width), jnp.bfloat16)], axis=0
    )
    picked = padded[target].astype(jnp.float32).reshape(rows_total, TOPK, width)
    expert_mix = jnp.sum(gates[:, :, None] * picked, axis=1)
    output = (live_rows * (mixed + expert_mix)).astype(jnp.bfloat16).reshape(images.shape)
    grad_rows = cotangent.reshape(rows_total, width).astype(jnp.float32) * live_rows
    grad_gates = jnp.sum(grad_rows[:, None, :] * picked, axis=-1)
    grad_picked = (
        (gates[:, :, None] * grad_rows[:, None, :])
        .astype(jnp.bfloat16)
        .reshape(rows_total * TOPK, width)
    )
    grad_outgoing = (
        jnp.zeros((EXPERTS * CAP + 1, width), jnp.bfloat16)
        .at[target]
        .set(grad_picked)[: EXPERTS * CAP]
    )
    grad_outgoing = grad_outgoing.reshape(EXPERTS, 1, CAP, width)
    grad_arrived = lax.all_to_all(grad_outgoing, "expert", split_axis=0, concat_axis=1, tiled=True)
    grad_arrived = grad_arrived.reshape(experts_here, sources * CAP, width)
    grad_back_bias = jnp.sum(grad_arrived.astype(jnp.float32), axis=1)
    grad_back_w = jnp.einsum(
        "erf,erd->efd", hidden_low, grad_arrived, preferred_element_type=jnp.float32
    )
    grad_hidden = jnp.einsum(
        "erd,efd->erf", grad_arrived, back_full, preferred_element_type=jnp.float32
    )
    grad_pre = gelu_pull(grad_hidden)[0]
    grad_in_bias_local = jnp.sum(grad_pre, axis=1)
    grad_pre_low = grad_pre.astype(jnp.bfloat16)
    grad_in_w = jnp.einsum(
        "erd,erf->edf", expert_rows, grad_pre_low, preferred_element_type=jnp.float32
    )
    grad_rows_part = jnp.einsum(
        "erf,edf->erd", grad_pre_low, in_full, preferred_element_type=jnp.float32
    )
    grad_shares = lax.psum_scatter(
        grad_rows_part.reshape(experts_here, sources, CAP, width),
        "tensor",
        scatter_dimension=2,
        tiled=True,
    ).astype(jnp.bfloat16)
    grad_pieces = lax.all_to_all(grad_shares, "expert", split_axis=1, concat_axis=0, tiled=True)
    grad_returned = lax.all_gather(grad_pieces, "tensor", axis=2, tiled=True)
    grad_padded = jnp.concatenate(
        [grad_returned.reshape(EXPERTS * CAP, width), jnp.zeros((1, width), jnp.bfloat16)], axis=0
    )
    grad_routed = jnp.sum(
        grad_padded[target].astype(jnp.float32).reshape(rows_total, TOPK, width), axis=1
    )
    expert_match = (
        pair_routes[:, :, None] == jnp.arange(EXPERTS, dtype=jnp.int32)[None, None, :]
    ).astype(jnp.float32)
    grad_probs = jnp.sum(expert_match * grad_gates[:, :, None], axis=1)
    grad_logits = probs * (grad_probs - jnp.sum(probs * grad_probs, axis=-1, keepdims=True))
    grad_logits_low = grad_logits.astype(jnp.bfloat16)
    grad_router = jnp.einsum(
        "td,te->de", routed_low, grad_logits_low, preferred_element_type=jnp.float32
    )
    grad_routed = grad_routed + jnp.einsum(
        "te,de->td", grad_logits_low, router_full, preferred_element_type=jnp.float32
    )
    grad_from_norm, grad_gain_second, grad_shift_second = norm_back(
        grad_routed, scaled_second, inv_second, gain_second
    )
    grad_mixed = grad_rows + grad_from_norm
    grad_bias_out = jnp.sum(grad_mixed, axis=0)
    grad_mixed_low = grad_mixed.astype(jnp.bfloat16)
    grad_out_w = jnp.einsum(
        "te,td->ed", attended_low, grad_mixed_low, preferred_element_type=jnp.float32
    )
    grad_attended = jnp.einsum(
        "td,ed->te", grad_mixed_low, out_full, preferred_element_type=jnp.float32
    )
    grad_attended = grad_attended.astype(jnp.bfloat16).reshape(head_shape)
    grad_queries, grad_keys, grad_values = attention_backward(
        queries, key_rows, value_rows, log_total, grad_attended, scale
    )
    grad_queries = grad_queries.reshape(rows_total, local_width)
    grad_keys = grad_keys.reshape(rows_total, local_width)
    grad_values = grad_values.reshape(rows_total, local_width)
    grad_pair_bias = jnp.stack([jnp.sum(grad_queries, axis=0), jnp.sum(grad_values, axis=0)])
    grad_proj_low = jnp.stack([grad_queries, grad_keys, grad_values]).astype(jnp.bfloat16)
    grad_qkv = jnp.einsum(
        "td,cte->cde", normed_low, grad_proj_low, preferred_element_type=jnp.float32
    )
    grad_normed_part = jnp.einsum(
        "cte,cde->td", grad_proj_low, qkv_full, preferred_element_type=jnp.float32
    )
    grad_normed = lax.psum(grad_normed_part, "tensor")
    grad_from_first, grad_gain_first, grad_shift_first = norm_back(
        grad_normed, scaled_first, inv_first, gain_first
    )
    grad_images = (grad_mixed + grad_from_first).reshape(images.shape)
    expert_start = lax.axis_index("expert") * experts_here
    full_in_bias = lax.dynamic_update_slice(
        jnp.zeros((EXPERTS, grad_in_bias_local.shape[1]), jnp.float32),
        grad_in_bias_local,
        (expert_start, jnp.zeros((), jnp.int32)),
    )
    summed = lax.psum(
        (
            grad_gain_first,
            grad_shift_first,
            grad_qkv,
            grad_pair_bias,
            grad_out_w,
            grad_bias_out,
            grad_gain_second,
            grad_shift_second,
            grad_router,
            full_in_bias,
        ),
        ("dp", "expert"),
    )
    shard_width = width // lax.axis_size("dp")
    shard_start = lax.axis_index("dp") * shard_width
    grad_first_gain = lax.dynamic_slice_in_dim(summed[0], shard_start, shard_width, 0)
    grad_first_shift = lax.dynamic_slice_in_dim(summed[1], shard_start, shard_width, 0)
    grad_w_qkv = lax.dynamic_slice_in_dim(summed[2], shard_start, shard_width, 1)
    grad_qv_bias = summed[3]
    grad_w_out = lax.dynamic_slice_in_dim(summed[4], shard_start, shard_width, 1)
    grad_out_bias = lax.dynamic_slice_in_dim(summed[5], shard_start, shard_width, 0)
    grad_second_gain = lax.dynamic_slice_in_dim(summed[6], shard_start, shard_width, 0)
    grad_second_shift = lax.dynamic_slice_in_dim(summed[7], shard_start, shard_width, 0)
    grad_w_router = lax.dynamic_slice_in_dim(summed[8], shard_start, shard_width, 0)
    grad_in_bias = lax.dynamic_slice_in_dim(summed[9], expert_start, experts_here, 0)
    grad_w_in, grad_w_back, grad_back_shard = (
        lax.psum_scatter(grad_in_w, "dp", scatter_dimension=1, tiled=True),
        lax.psum_scatter(grad_back_w, "dp", scatter_dimension=2, tiled=True),
        lax.psum_scatter(grad_back_bias, "dp", scatter_dimension=1, tiled=True),
    )
    return (
        output,
        grad_images,
        grad_first_gain,
        grad_first_shift,
        grad_w_qkv,
        grad_qv_bias,
        grad_w_out,
        grad_out_bias,
        grad_second_gain,
        grad_second_shift,
        grad_w_router,
        grad_w_in,
        grad_in_bias,
        grad_w_back,
        grad_back_shard,
    )


def solution(mesh):
    return jax.shard_map(
        on_device,
        mesh=mesh,
        in_specs=(
            P(("dp", "expert"), None, None),
            P(("dp", "expert")),
            P(("dp", "expert"), None, None),
            P(("dp", "expert"), None, None),
            P("dp"),
            P("dp"),
            P(None, "dp", "tensor"),
            P(None, "tensor"),
            P("tensor", "dp"),
            P("dp"),
            P("dp"),
            P("dp"),
            P("dp", None),
            P("expert", "dp", "tensor"),
            P("expert", "tensor"),
            P("expert", "tensor", "dp"),
            P("expert", "dp"),
            P(("dp", "expert"), None, None),
        ),
        out_specs=(
            P(("dp", "expert"), None, None),
            P(("dp", "expert"), None, None),
            P("dp"),
            P("dp"),
            P(None, "dp", "tensor"),
            P(None, "tensor"),
            P("tensor", "dp"),
            P("dp"),
            P("dp"),
            P("dp"),
            P("dp", None),
            P("expert", "dp", "tensor"),
            P("expert", "tensor"),
            P("expert", "tensor", "dp"),
            P("expert", "dp"),
        ),
        check_vma=False,
    )
```

profile of v0, /device:TPU:0, one launch (start us, length us, event | category | flops | bytes accessed | tf_op | source)
XLA Modules:
  0.0 1326.8 jit_solution(15935939575635181615)
XLA Ops:
  15.4 12.6 all-reduce.9
  30.6 12.3 all_gather.41
  68.5 97.9 %all-reduce.14.cloned.1.call-done = f32[788,768]{1,0:T(8,128)} async-done(((f32[788,768]{1,0:T(8,128)}), f32[788,768]{1,0:T(8,128)}) %all-reduce.14.cloned.1.call-update) | async-done | bytes 2420752 | tf_op jit(solution)/shard_map/psum | solution.py:138
  193.1 36.3 %all-to-all-done = bf16[32,1,64,768]{3,2,1,0:T(8,128)(2,1)S(1)} async-done(((bf16[32,1,64,768]{3,2,1,0:T(8,128)(2,1)}), bf16[32,1,64,768]{3,2,1,0:T(8,128)(2,1)S(1)}, u32[]{:S(2)}, u32[]{:S(2)}) %all-to-all-start) | async-done | bytes 3145760 | tf_op jit(solution)/shard_map/all_to_all | solution.py:158
  233.2 12.8 fusion.58
  246.1 65.1 %all-gather.9.cloned.1.call-done = bf16[16,768,768]{1,2,0:T(8,128)(2,1)} async-done(((bf16[16,768,192]{1,2,0:T(8,128)(2,1)}), bf16[16,768,768]{1,2,0:T(8,128)(2,1)}) %all-gather.9.cloned.1.call-update) | async-done | bytes 18874384 | tf_op jit(solution)/shard_map/all_gather | solution.py:114
  311.2 13.1 fusion.48
  331.1 13.7 %all-gather = bf16[4,192,32]{1,2,0:T(8,128)(2,1)S(1)} all-gather(bf16[1,192,32]{1,2,0:T(8,128)(2,1)S(1)} %bitcast.130), channel_id=1, replica_groups=mesh['dp'=4,'expert'=2,'tensor'=4] {'dp'}, dimensions={0}, use_global_device_ids=true | all-gather | bytes 61440 | tf_op jit(solution)/shard_map/all_gather | solution.py:112
  365.1 20.0 %gather_fusion.2 = f32[1576]{0:T(1024)S(1)} fusion(f32[788,32]{0,1:T(8,128)S(1)} %fusion.38, s32[1576]{0:T(1024)S(1)} %reshape.371), kind=kCustom, calls=%fused_computation.2 | custom fusion | bytes 25216 | tf_op jit(solution)/shard_map/jit(take_along_axis)/gather | solution.py:150
  385.2 19.5 %scatter_custom_fusion.1 = bf16[2049,768]{1,0:T(8,128)(2,1)} fusion(s32[1576]{0:T(1024)S(1)} %copy-done.70, f32[1576,768]{1,0:T(8,128)} %mul.267, f32[1576]{0:T(1024)S(1)} %and_select_fusion.1, bf16[]{:T(256)} %constant.21.clone.1), kind=kCustom, calls=%fused_computation.34 | custom fusion | flops 2420736 | bytes 7996930 | tf_op jit(solution)/shard_map/scatter | solution.py:196
  407.1 39.8 %all_to_all.66 = bf16[32,1,64,768]{3,2,1,0:T(8,128)(2,1)S(1)} all-to-all(bf16[32,1,64,768]{3,2,1,0:T(8,128)(2,1)S(1)} %bitcast.118), channel_id=1, replica_groups=mesh['dp'=4,'expert'=2,'tensor'=4] {'expert'}, dimensions={0} | all-to-all | bytes 6291456 | tf_op jit(solution)/shard_map/all_to_all | solution.py:199
  459.9 12.8 fusion.14
  486.6 14.7 %all_to_all.67 = bf16[16,2,16,768]{3,2,0,1:T(8,128)(2,1)} all-to-all(bf16[16,2,16,768]{3,2,0,1:T(8,128)(2,1)S(1)} %add_convert_fusion.2), channel_id=1, replica_groups=mesh['dp'=4,'expert'=2,'tensor'=4] {'expert'}, dimensions={1} | all-to-all | bytes 1572864 | tf_op jit(solution)/shard_map/all_to_all | solution.py:178
  501.4 87.5 %reduce-scatter.10.cloned.1.call-done = f32[16,2,16,768]{3,2,0,1:T(8,128)} async-done(((f32[16,2,64,768]{3,2,0,1:T(8,128)}), f32[16,2,16,768]{3,2,0,1:T(8,128)}) %reduce-scatter.10.cloned.1.call-update) | async-done | bytes 1572880 | tf_op jit(solution)/shard_map/reduce_scatter | solution.py:217
  590.4 14.3 %all_to_all.68 = bf16[16,2,16,768]{3,2,0,1:T(8,128)(2,1)} all-to-all(bf16[16,2,16,768]{3,2,0,1:T(8,128)(2,1)S(1)} %convert_element_type.164), channel_id=1, replica_groups=mesh['dp'=4,'expert'=2,'tensor'=4] {'expert'}, dimensions={1} | all-to-all | bytes 1572864 | tf_op jit(solution)/shard_map/all_to_all | solution.py:223
  609.9 44.4 %all-gather.11.cloned.1.call-done = bf16[32,1,64,768]{3,2,0,1:T(8,128)(2,1)} async-done(((bf16[32,1,16,768]{3,2,0,1:T(8,128)(2,1)}), bf16[32,1,64,768]{3,2,0,1:T(8,128)(2,1)}) %all-gather.11.cloned.1.call-update) | async-done | bytes 3145744 | tf_op jit(solution)/shard_map/all_gather | solution.py:179
  669.3 13.7 %multiply_reduce_fusion = (f32[788,2]{1,0:T(8,128)S(1)}, f32[788,768]{1,0:T(8,128)}) fusion(f32[788,2,768]{2,1,0:T(2,128)} %reshape.352, f32[788,768]{1,0:T(8,128)S(1)} %copy-done.18, f32[788,2]{1,0:T(8,128)S(1)} %copy-done.38), kind=kLoop, calls=%fused_computation.15 | loop fusion | flops 4234712 | bytes 9695552 | tf_op jit(solution)/shard_map/reduce_sum | solution.py:187
  683.3 34.6 %all-gather.13.cloned.1.call-done = bf16[32,1,64,768]{3,2,0,1:T(8,128)(2,1)} async-done(((bf16[32,1,16,768]{3,2,0,1:T(8,128)(2,1)}), bf16[32,1,64,768]{3,2,0,1:T(8,128)(2,1)}) %all-gather.13.cloned.1.call-update) | async-done | bytes 3145744 | tf_op jit(solution)/shard_map/all_gather | solution.py:224
  775.0 18.3 %fusion.47 = f32[16,768,768]{1,2,0:T(8,128)} fusion(bf16[16,128,768]{2,1,0:T(8,128)(2,1)S(1)} %bitcast.115, f32[16,128,768]{2,1,0:T(8,128)} %fusion.58, f32[16,768]{1,0:T(8,128)S(1)} %convert_element_type.153), kind=kOutput, calls=%fused_computation.122 | convolution fusion | flops 2431647744 | bytes 47235072 | tf_op jit(solution)/shard_map/erf,erd->efd/dot_general | solution.py:202
  795.4 28.5 %fusion.12 = f32[16,768,768]{2,1,0:T(8,128)} fusion(bf16[16,128,768]{2,1,0:T(8,128)(2,1)S(1)} %bitcast.110, bf16[16,128,768]{2,1,0:T(8,128)(2,1)} %copy-done.12), kind=kOutput, calls=%fused_computation.47 | convolution fusion | flops 2415919104 | bytes 44040192 | tf_op jit(solution)/shard_map/erd,erf->edf/dot_general | solution.py:211
  840.7 93.8 %all-reduce.16.cloned.1.call-done = f32[788,768]{1,0:T(8,128)} async-done(((f32[788,768]{1,0:T(8,128)}), f32[788,768]{1,0:T(8,128)}) %all-reduce.16.cloned.1.call-update) | async-done | bytes 2420752 | tf_op jit(solution)/shard_map/psum | solution.py:270
  937.2 24.5 %all-reduce.7 = (f32[768]{0:T(1024)S(1)}, f32[768]{0:T(1024)S(1)}, f32[2,192]{1,0:T(2,128)}, f32[768]{0:T(1024)S(1)}, f32[768]{0:T(1024)S(1)}, /*index=5*/f32[768]{0:T(1024)S(1)}) all-reduce(f32[768]{0:T(1024)S(1)} %get-tuple-element.107, ...), channel_id=1, replica_groups=mesh['dp'=4,'expert'=2,'tensor'=4] {'dp','expert'}, use_global_device_ids=true, to_apply=%region_25.26 | all-reduce | flops 4224 | bytes 33792 | tf_op jit(solution)/shard_map/psum | solution.py:281
  973.4 80.8 %reduce-scatter.14.cloned.1.call-done = f32[16,768,192]{1,2,0:T(8,128)} async-done(((f32[16,768,768]{1,2,0:T(8,128)}), f32[16,768,192]{1,2,0:T(8,128)}) %reduce-scatter.14.cloned.1.call-update) | async-done | bytes 9437200 | tf_op jit(solution)/shard_map/reduce_scatter | solution.py:310
  1054.2 264.8 %reduce-scatter.12.cloned.1.call-done = f32[16,192,768]{2,1,0:T(8,128)} async-done(((f32[16,768,768]{2,1,0:T(8,128)}), f32[16,192,768]{2,1,0:T(8,128)}) %reduce-scatter.12.cloned.1.call-update) | async-done | bytes 9437200 | tf_op jit(solution)/shard_map/reduce_scatter | solution.py:309
  (371 shorter events, 232.4 us)
Async XLA Ops:
  8.0 158.4 %all-reduce.14.cloned.1.call-start = ((), (), s32[]{:S(2)}) async-start(), calls=%async_computation.9 | async-start | bytes 4866048 | tf_op jit(solution)/shard_map/psum | solution.py:138
  66.7 166.5 %all-gather.7.cloned.1.call-start = ((), (), s32[]{:S(2)}) async-start(), calls=%async_computation.10 | async-start | bytes 23592960 | tf_op jit(solution)/shard_map/all_gather | solution.py:113
  67.3 99.1 %copy-start.7 = (f32[788,768]{1,0:T(8,128)S(1)}, f32[788,768]{1,0:T(8,128)}, u32[]{:S(2)}) copy-start(f32[788,768]{1,0:T(8,128)} %copy-done.6) | copy-start | bytes 7262212
  67.3 243.9 %all-gather.9.cloned.1.call-start = ((), (), s32[]{:S(2)}) async-start(), calls=%async_computation.11 | async-start | bytes 23592960 | tf_op jit(solution)/shard_map/all_gather | solution.py:114
  67.9 101.0 %copy-start.57 = (f32[768]{0:T(1024)}, f32[768]{0:T(1024)S(1)}, u32[]{:S(2)}) copy-start(f32[768]{0:T(1024)S(1)} %convert_element_type.150) | copy-start | bytes 9220
  68.5 106.5 %copy-start.69 = (s32[1576]{0:T(1024)}, s32[1576]{0:T(1024)S(1)}, u32[]{:S(2)}) copy-start(s32[1576]{0:T(1024)S(1)} %fusion.43) | copy-start | bytes 18916
  189.0 40.4 %all-to-all-start = ((bf16[32,1,64,768]{3,2,1,0:T(8,128)(2,1)}), bf16[32,1,64,768]{3,2,1,0:T(8,128)(2,1)S(1)}, u32[]{:S(2)}, u32[]{:S(2)}) async-start(bf16[32,1,64,768]{3,2,1,0:T(8,128)(2,1)} %bitcast.117), calls=%async_computation | async-start | bytes 6291456 | tf_op jit(solution)/shard_map/all_to_all | solution.py:158
  193.0 291.7 %reduce-scatter.8.cloned.1.call-start = ((), (), s32[]{:S(2)}) async-start(), calls=%async_computation.12 | async-start | bytes 7864320 | tf_op jit(solution)/shard_map/reduce_scatter | solution.py:171
  330.4 258.5 %reduce-scatter.10.cloned.1.call-start = ((), (), s32[]{:S(2)}) async-start(), calls=%async_computation.14 | async-start | bytes 7864320 | tf_op jit(solution)/shard_map/reduce_scatter | solution.py:217
  364.4 20.7 %copy-start.47 = (f32[788]{0:T(1024)}, f32[788]{0:T(1024)S(1)}, u32[]{:S(2)}) copy-start(f32[788]{0:T(1024)S(1)} %get-tuple-element.147) | copy-start | bytes 9460
  365.1 20.1 %copy-start.55 = (f32[788]{0:T(1024)}, f32[788]{0:T(1024)S(1)}, u32[]{:S(2)}) copy-start(f32[788]{0:T(1024)S(1)} %fusion.39) | copy-start | bytes 9460
  404.8 43.8 %slice-start = ((s8[6291456]{0:T(1024)(128)(4,1)}), s8[4194304]{0:T(1024)(128)(4,1)S(1)}, s32[]{:S(2)}) async-start(s8[6291456]{0:T(1024)(128)(4,1)} %bitcast.107), calls=%async_computation.21 | async-start | bytes 8388608
  407.0 41.5 %slice-start.1 = ((s8[6291456]{0:T(1024)(128)(4,1)}), s8[2097152]{0:T(1024)(128)(4,1)S(1)}, s32[]{:S(2)}) async-start(s8[6291456]{0:T(1024)(128)(4,1)} %bitcast.107), calls=%async_computation.22 | async-start | bytes 4194304
  478.8 175.5 %all-gather.11.cloned.1.call-start = ((), (), s32[]{:S(2)}) async-start(), calls=%async_computation.13 | async-start | bytes 3932160 | tf_op jit(solution)/shard_map/all_gather | solution.py:179
  501.4 103.4 %copy-start.54 = (s32[4,197,2]{1,0,2:T(4,128)S(1)}, s32[4,197,2]{1,0,2:T(4,128)}, u32[]{:S(2)}) copy-start(s32[4,197,2]{1,0,2:T(4,128)} %copy-done.53) | copy-start | bytes 18916
  501.4 106.8 %copy-start.14 = (bf16[32,1,64,768]{3,2,1,0:T(8,128)(2,1)S(1)}, bf16[32,1,64,768]{3,2,1,0:T(8,128)(2,1)}, u32[]{:S(2)}) copy-start(bf16[32,1,64,768]{3,2,1,0:T(8,128)(2,1)} %copy-done.13) | copy-start | bytes 9437188
  501.4 216.5 %all-gather.13.cloned.1.call-start = ((), (), s32[]{:S(2)}) async-start(), calls=%async_computation.15 | async-start | bytes 3932160 | tf_op jit(solution)/shard_map/all_gather | solution.py:224
  604.7 219.2 %reduce-scatter.16.cloned.1.call-start = ((), (), s32[]{:S(2)}) async-start(), calls=%async_computation.19 | async-start | bytes 491520
  609.6 224.5 %all-reduce.18.cloned.1.call-start = ((), (), s32[]{:S(2)}) async-start(), calls=%async_computation.20 | async-start | bytes 5111808 | tf_op jit(solution)/shard_map/psum | solution.py:281
  609.9 46.5 %copy-start.44 = (f32[32,768]{1,0:T(8,128)}, f32[32,768]{1,0:T(8,128)S(1)}, u32[]{:S(2)}) copy-start(f32[32,768]{1,0:T(8,128)S(1)} %constant_dynamic-update-slice_fusion.3) | copy-start | bytes 294916
  770.6 163.9 %all-reduce.16.cloned.1.call-start = ((), (), s32[]{:S(2)}) async-start(), calls=%async_computation.16 | async-start | bytes 4866048 | tf_op jit(solution)/shard_map/psum | solution.py:270
  774.9 279.3 %reduce-scatter.14.cloned.1.call-start = ((), (), s32[]{:S(2)}) async-start(), calls=%async_computation.18 | async-start | bytes 47185920 | tf_op jit(solution)/shard_map/reduce_scatter | solution.py:310
  793.3 525.6 %reduce-scatter.12.cloned.1.call-start = ((), (), s32[]{:S(2)}) async-start(), calls=%async_computation.17 | async-start | bytes 47185920 | tf_op jit(solution)/shard_map/reduce_scatter | solution.py:309
  827.3 107.2 %copy-start.9 = (f32[788,768]{1,0:T(8,128)S(1)}, f32[788,768]{1,0:T(8,128)}, u32[]{:S(2)}) copy-start(f32[788,768]{1,0:T(8,128)} %copy-done.6) | copy-start | bytes 7262212
  (80 other events, 463.8 us)
Sparse Core Ops, SparseCore 0:
  66.8 99.5 all-reduce.13
  330.5 110.7 reduce-scatter.7
  478.9 109.9 reduce-scatter.9
  590.3 63.9 all-gather.10
  655.7 62.1 all-gather.12
  770.7 63.3 all-reduce.17
  836.6 97.8 all-reduce.15
Sparse Core Ops, SparseCore 1:
  68.7 121.1 all-gather.6
  191.4 119.8 all-gather.8
  609.7 20.3 reduce-scatter.15
  793.4 260.7 reduce-scatter.13
  1057.4 261.5 reduce-scatter.11
where the time goes:
time: 1330 us
  waiting for transfers between devices  810 us (61%)
  local copies, waits for them, and re-layouts  163 us (12%)
  blocking collectives  144 us (11%)
  matrix products  122 us (9%)
  other arithmetic  64.2 us (5%)
  between operations  18.7 us (1%)
    reduce_scatter x1, waiting for transfers between devices, on_device(): lax.psum_scatter(grad_in_w, 'dp', scatter_dimension=1, tiled=True)  265 us
    psum x1, waiting for transfers between devices, on_device(): lax.psum(head_part, 'tensor')  97.9 us
    psum x1, waiting for transfers between devices, on_device(): grad_normed = lax.psum(grad_normed_part, 'tensor')  93.8 us
    reduce_scatter x1, waiting for transfers between devices, on_device(): lax.psum_scatter(grad_rows_part.reshape(experts_here, sources, CAP, width...  87.5 us
    reduce_scatter x1, waiting for transfers between devices, on_device(): lax.psum_scatter(grad_back_w, 'dp', scatter_dimension=2, tiled=True)  80.8 us
    all_gather x1, waiting for transfers between devices, on_device(): lax.all_gather(w_back, 'dp', axis=2, tiled=True)  65.1 us
    all_gather x1, waiting for transfers between devices, on_device(): returned = lax.all_gather(pieces, 'tensor', axis=2, tiled=True)  44.4 us
    all_to_all x1, blocking collectives, on_device(): lax.all_to_all(grad_outgoing, 'expert', split_axis=0, concat_axis=1, tile...  39.8 us
  transfers between devices with their start and end apart: 13, of which 10 were waited for; matrix products, arithmetic and copies ran while one was open for 22% of the time, Pallas kernels for 0%

commit v1 on v0

--- a/solution.py
+++ b/solution.py
@@ -1,12 +1,14 @@
 import jax
 import jax.numpy as jnp
 from jax import lax
+from jax.sharding import Mesh
 from jax.sharding import PartitionSpec as P
 
 HEAD_DIM = 64
 EXPERTS = 32
 TOPK = 2
 CAP = 64
+FF_PAIR = 2
 
 
 EPS = 1e-06
@@ -66,7 +68,7 @@
     return (grad_queries, grad_keys, grad_values)
 
 
-def on_device(
+def gathered_plan(
     images,
     images_held,
     routes,
@@ -329,10 +331,330 @@
     )
 
 
+def swap(values, axes):
+    return lax.all_to_all(values, axes, split_axis=0, concat_axis=0, tiled=True)
+
+
+def high_low(values):
+    high = lax.reduce_precision(values, 8, 7)
+    return high.astype(jnp.bfloat16), (values - high).astype(jnp.bfloat16)
+
+
+def moved_plan(
+    images,
+    images_held,
+    routes,
+    slot_index,
+    first_gain,
+    first_shift,
+    w_qkv,
+    qv_bias,
+    w_out,
+    out_bias,
+    second_gain,
+    second_shift,
+    w_router,
+    w_in,
+    in_bias,
+    w_back,
+    back_bias,
+    cotangent,
+):
+    f32, bf16 = jnp.float32, jnp.bfloat16
+    image_count, seq_len, width = images.shape
+    rows_total = image_count * seq_len
+    experts_here, shard_width, ff_here = w_in.shape
+    data, sources = lax.axis_size("dp"), lax.axis_size("expert")
+    outer, inner = lax.axis_size("outer"), lax.axis_size("inner")
+    tensor = outer * inner
+    tensor_axes = ("outer", "inner")
+    groups = data * sources
+    owners = data * inner
+    mine = experts_here // owners
+    slots = EXPERTS * CAP
+    slots_plane = slots // inner
+    dp_at = lax.axis_index("dp")
+    inner_at = lax.axis_index("inner")
+    tensor_at = lax.axis_index(tensor_axes)
+    owner_at = dp_at * inner + inner_at
+    local_width = w_out.shape[0]
+    slice_width = width // tensor
+
+    def collect(shard):
+        parts = swap(shard, ("dp", "inner"))
+        parts = parts.reshape(data, inner, mine, shard_width, ff_here)
+        return parts.transpose(2, 0, 3, 1, 4).reshape(mine, width, inner * ff_here)
+
+    in_mine = collect(w_in)
+    back_mine = collect(w_back.transpose(0, 2, 1))
+
+    packed = jnp.concatenate(
+        [
+            w_qkv.transpose(1, 0, 2).reshape(shard_width, 3 * local_width),
+            w_out.T,
+            w_router,
+            back_bias.T,
+            jnp.stack([first_gain, first_shift, out_bias, second_gain, second_shift], axis=1),
+        ],
+        axis=1,
+    )
+    packed = lax.all_gather(packed, "dp", axis=0, tiled=True)
+    cuts = [3 * local_width, local_width, EXPERTS, experts_here]
+    qkv_full, out_turned, router_full, back_bias_turned, vectors = jnp.split(
+        packed, [sum(cuts[: i + 1]) for i in range(4)], axis=1
+    )
+    gain_first, shift_first, bias_out_full, gain_second, shift_second = (
+        vectors[:, i].astype(f32) for i in range(5)
+    )
+    out_whole = lax.all_gather(out_turned, tensor_axes, axis=1, tiled=True)
+    in_bias_all = lax.all_gather(in_bias, "inner", axis=1, tiled=True)
+    in_bias_mine = lax.dynamic_slice_in_dim(in_bias_all, owner_at * mine, mine, 0)
+
+    pair_routes = routes.reshape(rows_total, TOPK)
+    pair_slots = slot_index.reshape(rows_total, TOPK)
+    home, within = pair_routes // experts_here, pair_routes % experts_here
+    owner, nth = within // mine, within % mine
+    place = ((owner % inner) * data + owner // inner) * sources + home
+    target = jnp.where(pair_slots < CAP, (place * mine + nth) * CAP + pair_slots, slots)
+    plane_slots = inner_at * slots_plane + jnp.arange(slots_plane, dtype=jnp.int32)
+    takes = [plane_slots[:, None] == target[None, :, k] for k in range(TOPK)]
+    fill = jnp.logical_or(takes[0], takes[1]).astype(bf16)
+
+    live_image = (jnp.arange(image_count, dtype=jnp.int32) < images_held[0]).astype(f32)
+    live_rows = jnp.repeat(live_image, seq_len)[:, None]
+    grad_rows = cotangent.reshape(rows_total, width).astype(f32) * live_rows
+
+    def dispatch(rows):
+        return jnp.dot(fill, rows, preferred_element_type=f32).astype(bf16)
+
+    cot_out = dispatch(grad_rows.astype(bf16)).reshape(groups, mine * CAP, width)
+    cot_rows = swap(cot_out, ("dp", "expert")).reshape(groups, mine, CAP, width)
+
+    inputs = images.reshape(rows_total, width).astype(f32)
+    normed, scaled_first, inv_first = norm_parts(inputs, gain_first, shift_first)
+    normed_low = normed.astype(bf16)
+    projected = jnp.dot(normed_low, qkv_full, preferred_element_type=f32)
+    head_count = local_width // HEAD_DIM
+    head_shape = (image_count, seq_len, head_count, HEAD_DIM)
+    bias_pair = qv_bias.astype(f32)
+    queries, key_rows, value_rows = (
+        projected[:, i * local_width : (i + 1) * local_width] for i in range(3)
+    )
+    queries = (queries + bias_pair[0]).astype(bf16).reshape(head_shape)
+    key_rows = key_rows.astype(bf16).reshape(head_shape)
+    value_rows = (value_rows + bias_pair[1]).astype(bf16).reshape(head_shape)
+    scale = HEAD_DIM ** (-0.5)
+    attended, log_total = attention_forward(queries, key_rows, value_rows, scale)
+    attended_low = attended.reshape(rows_total, local_width).astype(bf16)
+    attended_all = lax.all_gather(attended_low, tensor_axes, axis=1, tiled=True)
+    mixed = inputs + bias_out_full
+    mixed = mixed + jnp.einsum("te,de->td", attended_all, out_whole, preferred_element_type=f32)
+    routed, scaled_second, inv_second = norm_parts(mixed, gain_second, shift_second)
+    routed_low = routed.astype(bf16)
+    logits = jnp.dot(routed_low, router_full, preferred_element_type=f32)
+    probs = jax.nn.softmax(logits, axis=-1)
+    expert_ids = jnp.arange(EXPERTS, dtype=jnp.int32)
+    matches = [(pair_routes[:, k : k + 1] == expert_ids).astype(f32) for k in range(TOPK)]
+    gates = [jnp.sum(match * probs, axis=1) for match in matches]
+
+    gate_slots = sum(
+        jnp.sum(jnp.where(take, gate[None, :], 0.0), axis=1) for take, gate in zip(takes, gates)
+    )
+    gate_parts = jnp.stack(high_low(gate_slots.reshape(groups, mine * CAP)), axis=1)
+    gate_rows = jnp.pad(gate_parts, ((0, 0), (0, 14), (0, width - mine * CAP)))
+    sent = jnp.concatenate([dispatch(routed_low).reshape(groups, mine * CAP, width), gate_rows], axis=1)
+    arrived = swap(sent, ("dp", "expert"))
+    expert_rows = arrived[:, : mine * CAP].reshape(groups, mine, CAP, width)
+    gate_here = jnp.sum(arrived[:, mine * CAP : mine * CAP + 2, : mine * CAP].astype(f32), axis=1)
+    gate_here = gate_here.reshape(groups, mine, CAP, 1)
+    to_experts = lambda rows: rows.transpose(1, 0, 2, 3).reshape(mine, groups * CAP, -1)
+    expert_rows = to_experts(expert_rows)
+    grad_returned = to_experts((gate_here * cot_rows.astype(f32)).astype(bf16))
+
+    hidden_pre = jnp.einsum("erd,edf->erf", expert_rows, in_mine, preferred_element_type=f32)
+    hidden_pre = hidden_pre + in_bias_mine.astype(f32)[:, None, :]
+    hidden_value, gelu_pull = jax.vjp(jax.nn.gelu, hidden_pre)
+    hidden_low = hidden_value.astype(bf16)
+    expert_part = jnp.einsum("erf,edf->erd", hidden_low, back_mine, preferred_element_type=f32)
+    grad_hidden = jnp.einsum("erd,edf->erf", grad_returned, back_mine, preferred_element_type=f32)
+    grad_pre = gelu_pull(grad_hidden)[0]
+    grad_in_bias_mine = jnp.sum(grad_pre, axis=1)
+    grad_pre_low = grad_pre.astype(bf16)
+    grad_rows_part = jnp.einsum("erf,edf->erd", grad_pre_low, in_mine, preferred_element_type=f32)
+    grad_back_mine = jnp.einsum("erd,erf->edf", grad_returned, hidden_low, preferred_element_type=f32)
+    grad_in_mine = jnp.einsum("erd,erf->edf", expert_rows, grad_pre_low, preferred_element_type=f32)
+    grad_back_bias_mine = jnp.sum(grad_returned.astype(f32), axis=1)
+
+    bias_here = lax.dynamic_slice(
+        back_bias_turned, (lax.axis_index("outer") * (width // outer), owner_at * mine), (width // outer, mine)
+    )
+    bias_here = bias_here.T.astype(f32)[:, None, :]
+
+    def bring(part, bias):
+        share = lax.psum_scatter(part.astype(bf16), "outer", scatter_dimension=2, tiled=True)
+        if bias is not None:
+            share = (share.astype(f32) + bias).astype(bf16)
+        share = share.reshape(mine, groups, CAP, width // outer).transpose(1, 0, 2, 3)
+        rows = swap(share, ("dp", "expert")).reshape(slots_plane, width // outer)
+        if inner > 1:
+            rows = lax.all_to_all(rows, "inner", split_axis=1, concat_axis=0, tiled=True)
+        return rows
+
+    returned = bring(expert_part, bias_here)
+    grad_buffers = bring(grad_rows_part, None)
+    all_slots = jnp.arange(slots, dtype=jnp.int32)
+    finds = [(target[:, k : k + 1] == all_slots).astype(bf16) for k in range(TOPK)]
+    picked = [jnp.dot(find, returned, preferred_element_type=f32) for find in finds]
+    cut = lambda rows: lax.dynamic_slice_in_dim(rows, tensor_at * slice_width, slice_width, 1)
+    grad_rows_cut = cut(grad_rows)
+    grad_routed_cut = jnp.dot(finds[0] + finds[1], grad_buffers, preferred_element_type=f32)
+    gate_terms = jnp.stack([jnp.sum(grad_rows_cut * rows, axis=1) for rows in picked], axis=1)
+    gate_high, gate_low = high_low(gate_terms)
+    back = jnp.concatenate([grad_routed_cut.astype(bf16), gate_high, gate_low], axis=1)
+    back = lax.all_gather(back, tensor_axes, axis=0, tiled=False)
+    grad_gates = jnp.sum(back[:, :, slice_width:].astype(f32), axis=0)
+    grad_gates = grad_gates[:, :TOPK] + grad_gates[:, TOPK:]
+    grad_routed = back[:, :, :slice_width].transpose(1, 0, 2).reshape(rows_total, width).astype(f32)
+    expert_mix = gates[0][:, None] * picked[0] + gates[1][:, None] * picked[1]
+    output_cut = (live_rows * (cut(mixed) + expert_mix)).astype(bf16)
+    output = lax.all_gather(output_cut, tensor_axes, axis=1, tiled=True).reshape(images.shape)
+
+    grad_probs = sum(match * grad_gates[:, k : k + 1] for k, match in enumerate(matches))
+    grad_logits = probs * (grad_probs - jnp.sum(probs * grad_probs, axis=-1, keepdims=True))
+    grad_logits_low = grad_logits.astype(bf16)
+    grad_router = jnp.einsum("td,te->de", routed_low, grad_logits_low, preferred_element_type=f32)
+    grad_routed = grad_routed + jnp.einsum(
+        "te,de->td", grad_logits_low, router_full, preferred_element_type=f32
+    )
+    grad_from_norm, grad_gain_second, grad_shift_second = norm_back(
+        grad_routed, scaled_second, inv_second, gain_second
+    )
+    grad_mixed = grad_rows + grad_from_norm
+    grad_bias_out = jnp.sum(grad_mixed, axis=0)
+    grad_mixed_low = grad_mixed.astype(bf16)
+    grad_out_turned = jnp.einsum("td,te->de", grad_mixed_low, attended_low, preferred_element_type=f32)
+    grad_attended = jnp.dot(grad_mixed_low, out_turned, preferred_element_type=f32)
+    grad_attended = grad_attended.astype(bf16).reshape(head_shape)
+    grad_queries, grad_keys, grad_values = (
+        grads.reshape(rows_total, local_width)
+        for grads in attention_backward(
+            queries, key_rows, value_rows, log_total, grad_attended, scale
+        )
+    )
+    grad_pair_bias = jnp.stack([jnp.sum(grad_queries, axis=0), jnp.sum(grad_values, axis=0)])
+    grad_proj_low = jnp.concatenate([grad_queries, grad_keys, grad_values], axis=1).astype(bf16)
+    grad_qkv = jnp.einsum("td,te->de", normed_low, grad_proj_low, preferred_element_type=f32)
+    grad_normed_part = jnp.einsum("te,de->td", grad_proj_low, qkv_full, preferred_element_type=f32)
+    grad_normed = lax.psum(grad_normed_part.astype(bf16), tensor_axes).astype(f32)
+    grad_from_first, grad_gain_first, grad_shift_first = norm_back(
+        grad_normed, scaled_first, inv_first, gain_first
+    )
+    grad_images = (grad_mixed + grad_from_first).reshape(images.shape)
+
+    def spread(grads):
+        parts = grads.astype(bf16).reshape(mine, data, shard_width, inner, ff_here)
+        parts = parts.transpose(1, 3, 0, 2, 4).reshape(experts_here, shard_width, ff_here)
+        return swap(parts, ("dp", "inner")).astype(f32)
+
+    grad_w_back = spread(grad_back_mine).transpose(0, 2, 1)
+    grad_w_in = spread(grad_in_mine)
+    bias_grads = jnp.concatenate([grad_in_bias_mine, grad_back_bias_mine], axis=1)
+    bias_grads = lax.all_gather(bias_grads, ("dp", "inner"), axis=0, tiled=True)
+    grad_in_bias = lax.dynamic_slice_in_dim(bias_grads, inner_at * ff_here, ff_here, 1)
+    grad_back_shard = lax.dynamic_slice_in_dim(
+        bias_grads, inner * ff_here + dp_at * shard_width, shard_width, 1
+    )
+    early = jnp.concatenate(
+        [
+            grad_qkv,
+            grad_out_turned,
+            grad_router,
+            jnp.stack([grad_bias_out, grad_gain_second, grad_shift_second], axis=1),
+        ],
+        axis=1,
+    )
+    early = lax.psum(lax.psum_scatter(early, "dp", scatter_dimension=0, tiled=True), "expert")
+    grad_w_qkv = early[:, : 3 * local_width].reshape(shard_width, 3, local_width).transpose(1, 0, 2)
+    grad_w_out = early[:, 3 * local_width : 4 * local_width].T
+    grad_w_router = early[:, 4 * local_width : 4 * local_width + EXPERTS]
+    grad_out_bias, grad_second_gain, grad_second_shift = (
+        early[:, 4 * local_width + EXPERTS + i] for i in range(3)
+    )
+    grad_qv_bias, grad_first_norm = lax.psum(
+        (grad_pair_bias, jnp.stack([grad_gain_first, grad_shift_first])), ("dp", "expert")
+    )
+    grad_first_norm = lax.dynamic_slice_in_dim(grad_first_norm, dp_at * shard_width, shard_width, 1)
+    return (
+        output,
+        grad_images,
+        grad_first_norm[0],
+        grad_first_norm[1],
+        grad_w_qkv,
+        grad_qv_bias,
+        grad_w_out,
+        grad_out_bias,
+        grad_second_gain,
+        grad_second_shift,
+        grad_w_router,
+        grad_w_in,
+        grad_in_bias,
+        grad_w_back,
+        grad_back_shard,
+    )
+
+
 def solution(mesh):
+    data, expert, tensor = (mesh.shape[name] for name in ("dp", "expert", "tensor"))
+    experts_here = EXPERTS // expert
+    inner = FF_PAIR if tensor % FF_PAIR == 0 else 1
+    if experts_here % (data * inner):
+        return jax.shard_map(
+            gathered_plan,
+            mesh=mesh,
+            in_specs=(
+                P(("dp", "expert"), None, None),
+                P(("dp", "expert")),
+                P(("dp", "expert"), None, None),
+                P(("dp", "expert"), None, None),
+                P("dp"),
+                P("dp"),
+                P(None, "dp", "tensor"),
+                P(None, "tensor"),
+                P("tensor", "dp"),
+                P("dp"),
+                P("dp"),
+                P("dp"),
+                P("dp", None),
+                P("expert", "dp", "tensor"),
+                P("expert", "tensor"),
+                P("expert", "tensor", "dp"),
+                P("expert", "dp"),
+                P(("dp", "expert"), None, None),
+            ),
+            out_specs=(
+                P(("dp", "expert"), None, None),
+                P(("dp", "expert"), None, None),
+                P("dp"),
+                P("dp"),
+                P(None, "dp", "tensor"),
+                P(None, "tensor"),
+                P("tensor", "dp"),
+                P("dp"),
+                P("dp"),
+                P("dp"),
+                P("dp", None),
+                P("expert", "dp", "tensor"),
+                P("expert", "tensor"),
+                P("expert", "tensor", "dp"),
+                P("expert", "dp"),
+            ),
+            check_vma=False,
+        )
+    devices = mesh.devices.reshape(data, expert, tensor // inner, inner)
+    split_mesh = Mesh(devices, ("dp", "expert", "outer", "inner"))
     return jax.shard_map(
-        on_device,
-        mesh=mesh,
+        moved_plan,
+        mesh=split_mesh,
         in_specs=(
             P(("dp", "expert"), None, None),
             P(("dp", "expert")),
@@ -340,16 +662,16 @@
             P(("dp", "expert"), None, None),
             P("dp"),
             P("dp"),
-            P(None, "dp", "tensor"),
-            P(None, "tensor"),
-            P("tensor", "dp"),
+            P(None, "dp", ("outer", "inner")),
+            P(None, ("outer", "inner")),
+            P(("outer", "inner"), "dp"),
             P("dp"),
             P("dp"),
             P("dp"),
             P("dp", None),
-            P("expert", "dp", "tensor"),
-            P("expert", "tensor"),
-            P("expert", "tensor", "dp"),
+            P("expert", "dp", ("outer", "inner")),
+            P("expert", ("outer", "inner")),
+            P("expert", ("outer", "inner"), "dp"),
             P("expert", "dp"),
             P(("dp", "expert"), None, None),
         ),
@@ -358,16 +680,16 @@
             P(("dp", "expert"), None, None),
             P("dp"),
             P("dp"),
-            P(None, "dp", "tensor"),
-            P(None, "tensor"),
-            P("tensor", "dp"),
+            P(None, "dp", ("outer", "inner")),
+            P(None, ("outer", "inner")),
+            P(("outer", "inner"), "dp"),
             P("dp"),
             P("dp"),
             P("dp"),
             P("dp", None),
-            P("expert", "dp", "tensor"),
-            P("expert", "tensor"),
-            P("expert", "tensor", "dp"),
+            P("expert", "dp", ("outer", "inner")),
+            P("expert", ("outer", "inner")),
+            P("expert", ("outer", "inner"), "dp"),
             P("expert", "dp"),
         ),
         check_vma=False,

time: 1330 us -> 803 us (0.60)
  waiting for transfers between devices: 810 us -> 192 us
  blocking collectives: 144 us -> 216 us
  local copies, waits for them, and re-layouts: 163 us -> 210 us
  matrix products: 122 us -> 78.8 us
  starting transfers between devices: 5.09 us -> 36.4 us
  other arithmetic: 64.2 us -> 43.9 us
    reduce_scatter x4 -> x0, waiting for transfers between devices: 433 us -> none  [the longest x1 265 us: on_device(): lax.psum_scatter(grad_in_w, 'dp', scatter_dimension=1, tiled=True)]
    psum x3 -> x2, waiting for transfers between devices: 195 us -> 14.8 us  [the longest x1 10.5 us: moved_plan(): lax.psum(lax.psum_scatter(early, 'dp', scatter_dimension=0, tiled=True),...]
    all_gather x4 -> x2, blocking collectives: 37.7 us -> 118 us  [the longest x1 74.3 us: moved_plan(): bias_grads = lax.all_gather(bias_grads, ('dp', 'inner'), axis=0, tiled=True)]
    unnamed x13, waiting for transfers between devices: 0.99 us -> 64.7 us
    reshape x9 -> x22, local copies, waits for them, and re-layouts: 20.4 us -> 83.5 us  [the longest x2 22.5 us: collect(): return parts.transpose(2, 0, 3, 1, 4).reshape(mine, width, inner * ff_here)]
    all_gather x4 -> x5, waiting for transfers between devices: 144 us -> 96 us  [the longest x1 34.5 us: moved_plan(): attended_all = lax.all_gather(attended_low, tensor_axes, axis=1, tiled=True)]
    dot_general x14 -> x20, matrix products: 114 us -> 72.9 us  [the longest x1 9.72 us: moved_plan(): jnp.einsum('erd,edf->erf', grad_returned, back_mine, preferred_element_ty...]
    gather x7 -> x0, local copies, waits for them, and re-layouts: 35.2 us -> none  [the longest x5 22.7 us: on_device(): gates = jnp.take_along_axis(probs, pair_routes, axis=1)]
  transfers between devices with their start and end apart: 13 -> 18, of which waited for: 10 -> 12; matrix products, arithmetic and copies ran while one was open for 22% -> 35% of each run, Pallas kernels for 0% -> 0%
where the time goes in v1:
time: 803 us; the launch traced here: 794 us
  blocking collectives  216 us (27%)
  local copies, waits for them, and re-layouts  210 us (26%)
  waiting for transfers between devices  192 us (24%)
  matrix products  78.8 us (10%)
  other arithmetic  43.9 us (5%)
  starting transfers between devices  36.4 us (5%)
  between operations  16.2 us (2%)
    all_to_all x2, blocking collectives, swap(): return lax.all_to_all(values, axes, split_axis=0, concat_axis=0, tiled=True)  83.2 us
    all_gather x1, blocking collectives, moved_plan(): bias_grads = lax.all_gather(bias_grads, ('dp', 'inner'), axis=0, tiled=True)  74.3 us
    unnamed x13, waiting for transfers between devices  64.7 us
    unnamed x136, local copies, waits for them, and re-layouts  54.5 us
    all_gather x1, blocking collectives, moved_plan(): in_bias_all = lax.all_gather(in_bias, 'inner', axis=1, tiled=True)  44.1 us
    all_gather x1, waiting for transfers between devices, moved_plan(): attended_all = lax.all_gather(attended_low, tensor_axes, axis=1, tiled=True)  34.5 us
    all_gather x1, waiting for transfers between devices, moved_plan(): back = lax.all_gather(back, tensor_axes, axis=0, tiled=False)  28.7 us
    all_to_all x6, starting transfers between devices, swap(): return lax.all_to_all(values, axes, split_axis=0, concat_axis=0, tiled=True)  26.2 us
  transfers between devices with their start and end apart: 18, of which 12 were waited for; matrix products, arithmetic and copies ran while one was open for 35% of the time, Pallas kernels for 0%

profile of v1, /device:TPU:0, one launch (start us, length us, event | category | flops | bytes accessed | tf_op | source)
XLA Modules:
  0.0 793.7 jit_solution(14943929678400004303)
XLA Ops:
  24.9 11.6 %all-gather.9.cloned.1.call-done = bf16[768,821]{1,0:T(8,128)(2,1)} async-done(((bf16[192,821]{1,0:T(8,128)(2,1)}), bf16[768,821]{1,0:T(8,128)(2,1)}) %all-gather.9.cloned.1.call-update) | async-done | bytes 1261072 | tf_op jit(solution)/shard_map/all_gather | solution.py:401
  54.3 21.1 %all-gather.13.cloned.1.call-done = bf16[768,768]{0,1:T(8,128)(2,1)} async-done(((bf16[768,192]{0,1:T(8,128)(2,1)}), bf16[768,768]{0,1:T(8,128)(2,1)}) %all-gather.13.cloned.1.call-update) | async-done | bytes 1179664 | tf_op jit(solution)/shard_map/all_gather | solution.py:409
  75.4 34.5 %all-gather.11.cloned.1.call-done = bf16[788,768]{0,1:T(8,128)(2,1)} async-done(((bf16[788,192]{0,1:T(8,128)(2,1)}), bf16[788,768]{0,1:T(8,128)(2,1)}) %all-gather.11.cloned.1.call-update) | async-done | bytes 1210384 | tf_op jit(solution)/shard_map/all_gather | solution.py:449
  121.5 25.8 %all_to_all.78 = bf16[8,144,768]{2,1,0:T(8,128)(2,1)} all-to-all(bf16[8,144,768]{2,1,0:T(8,128)(2,1)S(1)} %fusion.35), channel_id=1, replica_groups=mesh['dp'=4,'expert'=2,'outer'=2,'inner'=2] {'dp','expert'}, dimensions={0} | all-to-all | bytes 3538944 | tf_op jit(solution)/shard_map/all_to_all | solution.py:335
  147.2 57.5 %all_to_all.79 = bf16[16,192,768]{2,1,0:T(8,128)(2,1)} all-to-all(bf16[16,192,768]{2,1,0:T(8,128)(2,1)S(1)} %bitcast.159), channel_id=1, replica_groups=mesh['dp'=4,'expert'=2,'outer'=2,'inner'=2] {'dp','inner'}, dimensions={0} | all-to-all | bytes 9437184 | tf_op jit(solution)/shard_map/all_to_all | solution.py:335
  219.5 44.1 %all_gather.27 = bf16[16,1536]{1,0:T(8,128)(2,1)S(1)} all-gather(bf16[16,768]{1,0:T(8,128)(2,1)S(1)} %copy-done.32), channel_id=1, replica_groups=mesh['dp'=4,'expert'=2,'outer'=2,'inner'=2] {'inner'}, dimensions={1}, use_global_device_ids=true | all-gather | bytes 73728 | tf_op jit(solution)/shard_map/all_gather | solution.py:410
  271.8 9.4 %copy.477 = bf16[4,2,2,192,768]{4,1,3,0,2:T(2,128)(2,1)} copy(bf16[4,2,2,192,768]{4,3,2,1,0:T(8,128)(2,1)} %bitcast.147) | data formatting | bytes 9437184 | tf_op jit(solution)/shard_map/reshape | solution.py:385
  281.1 11.2 %reshape.321 = bf16[2,768,1536]{2,1,0:T(8,128)(2,1)} reshape(bf16[2,4,192,2,768]{4,3,2,1,0:T(2,128)(2,1)} %bitcast.148) | data formatting | bytes 9437184 | tf_op jit(solution)/shard_map/reshape | solution.py:386
  296.9 9.4 %copy.478 = bf16[4,2,2,192,768]{4,1,3,0,2:T(2,128)(2,1)} copy(bf16[4,2,2,192,768]{4,3,2,1,0:T(8,128)(2,1)} %bitcast.13) | data formatting | bytes 9437184 | tf_op jit(solution)/shard_map/reshape | solution.py:385
  306.3 11.3 %reshape.319 = bf16[2,768,1536]{2,1,0:T(8,128)(2,1)} reshape(bf16[2,4,192,2,768]{4,3,2,1,0:T(2,128)(2,1)} %bitcast.149) | data formatting | bytes 9437184 | tf_op jit(solution)/shard_map/reshape | solution.py:386
  343.1 9.7 %fusion.93 = (f32[2,1536]{1,0:T(2,128)}, bf16[2,512,1536]{2,1,0:T(8,128)(2,1)S(1)}) fusion(f32[2,512,1536]{2,1,0:T(8,128)S(1)} %copy-done.49, f32[2,1536]{1,0:T(2,128)S(1)} %dynamic-slice_convert_fusion, bf16[2,512,768]{2,1,0:T(8,128)(2,1)S(1)} %bitcast.172, bf16[2,768,1536]{2,1,0:T(8,128)(2,1)} %reshape.321), kind=kOutput, calls=%fused_computation.203 | convolution fusion | flops 2450519040 | bytes 15753216 | tf_op jit(solution)/shard_map/erd,edf->erf/dot_general | solution.py:479
  367.4 14.5 %reduce-scatter.10.cloned.1.call-done = bf16[384,1024]{1,0:T(8,128)(2,1)} async-done(((bf16[768,1024]{1,0:T(8,128)(2,1)}), bf16[384,1024]{1,0:T(8,128)(2,1)}) %reduce-scatter.10.cloned.1.call-update) | async-done | bytes 786448
  392.2 35.3 %reduce-scatter.12.cloned.1.call-done = bf16[384,1024]{1,0:T(8,128)(2,1)} async-done(((bf16[768,1024]{1,0:T(8,128)(2,1)}), bf16[384,1024]{1,0:T(8,128)(2,1)}) %reduce-scatter.12.cloned.1.call-update) | async-done | bytes 786448
  472.2 7.2 convolution_convert_fusion.1
  479.4 10.6 %reshape.333 = bf16[2,4,192,2,768]{4,3,2,1,0:T(2,128)(2,1)} reshape(bf16[2,768,1536]{2,1,0:T(8,128)(2,1)} %convolution_convert_fusion.1) | data formatting | bytes 9437184 | tf_op jit(solution)/shard_map/reshape | solution.py:555
  510.0 8.6 %convolution_convert_fusion = bf16[2,768,1536]{2,1,0:T(8,128)(2,1)} fusion(bf16[2,512,768]{2,1,0:T(8,128)(2,1)} %bitcast.173, f32[2,512,1536]{2,1,0:T(8,128)} %copy-done.48, f32[2,1536]{1,0:T(2,128)S(1)} %copy-done.43), kind=kOutput, calls=%fused_computation.18 | convolution fusion | flops 2434007040 | bytes 12595200 | tf_op jit(solution)/shard_map/erd,erf->edf/dot_general | solution.py:484
  518.6 10.6 %reshape.335 = bf16[2,4,192,2,768]{4,3,2,1,0:T(2,128)(2,1)} reshape(bf16[2,768,1536]{2,1,0:T(8,128)(2,1)} %convolution_convert_fusion) | data formatting | bytes 9437184 | tf_op jit(solution)/shard_map/reshape | solution.py:555
  534.6 28.7 %all-gather.17.cloned.1.call-done = bf16[4,788,196]{1,2,0:T(8,128)(2,1)} async-done(((bf16[1,788,196]{1,2,0:T(8,128)(2,1)}), bf16[4,788,196]{1,2,0:T(8,128)(2,1)}) %all-gather.17.cloned.1.call-update) | async-done | bytes 1235600 | tf_op jit(solution)/shard_map/all_gather | solution.py:514
  605.5 8.2 %concatenate.23 = f32[768,803]{0,1:T(8,128)} concatenate(f32[768,576]{0,1:T(8,128)} %fusion.106, f32[768,192]{0,1:T(8,128)S(1)} %fusion.63, f32[768,32]{0,1:T(8,128)S(1)} %fusion.89, f32[768,1]{0,1:T(1,128)S(1)} %stack.68, f32[768,1]{0,1:T(1,128)S(1)} %stack.69, f32[768,1]{0,1:T(1,128)S(1)} %stack.70), dimensions={1} | concatenate | bytes 4933632 | tf_op jit(solution)/shard_map/concatenate | solution.py:567
  617.1 74.3 %all-gather.2 = f32[8,2,2304]{2,1,0:T(2,128)S(1)} all-gather(f32[1,2,2304]{2,1,0:T(2,128)S(1)} %maximum_bitcast_fusion.1), channel_id=1, replica_groups=mesh['dp'=4,'expert'=2,'outer'=2,'inner'=2] {'dp','inner'}, dimensions={0}, use_global_device_ids=true | all-gather | bytes 165888 | tf_op jit(solution)/shard_map/all_gather | solution.py:562
  707.7 14.7 %all-reduce.1 = (f32[2,768]{1,0:T(2,128)S(1)}, f32[2,192]{1,0:T(2,128)}) all-reduce(f32[2,768]{1,0:T(2,128)S(1)} %pad_maximum_fusion.1, f32[2,192]{1,0:T(2,128)S(1)} %pad_maximum_fusion.3), channel_id=1, replica_groups=mesh['dp'=4,'expert'=2,'outer'=2,'inner'=2] {'dp','expert'}, use_global_device_ids=true, to_apply=%region_27.28 | all-reduce | flops 1920 | bytes 15360 | tf_op jit(solution)/shard_map/psum | solution.py:583
  727.8 14.6 %reduce-scatter.14.cloned.1.call-done = f32[192,803]{1,0:T(8,128)} async-done(((f32[768,803]{1,0:T(8,128)}), f32[192,803]{1,0:T(8,128)}) %reduce-scatter.14.cloned.1.call-update) | async-done | bytes 616720
  755.4 7.1 convert_element_type.294
  769.6 10.5 %all-reduce.7.cloned.1.call-done = f32[192,803]{0,1:T(8,128)} async-done(((f32[192,803]{0,1:T(8,128)}), f32[192,803]{0,1:T(8,128)}) %all-reduce.7.cloned.1.call-update) | async-done | bytes 616720 | tf_op jit(solution)/shard_map/psum | solution.py:576
  (322 shorter events, 286.7 us)
Async XLA Ops:
  7.2 29.4 %all-gather.9.cloned.1.call-start = ((), (), s32[]{:S(2)}) async-start(), calls=%async_computation.13 | async-start | bytes 1720320 | tf_op jit(solution)/shard_map/all_gather | solution.py:401
  15.1 60.3 %all-gather.13.cloned.1.call-start = ((), (), s32[]{:S(2)}) async-start(), calls=%async_computation.15 | async-start | bytes 1474560 | tf_op jit(solution)/shard_map/all_gather | solution.py:409
  44.8 65.2 %all-gather.11.cloned.1.call-start = ((), (), s32[]{:S(2)}) async-start(), calls=%async_computation.14 | async-start | bytes 1720320 | tf_op jit(solution)/shard_map/all_gather | solution.py:449
  54.3 211.2 %copy-start.38 = (s32[788]{0:T(1024)}, s32[788]{0:T(1024)S(1)}, u32[]{:S(2)}) copy-start(s32[788]{0:T(1024)S(1)} %get-tuple-element.154) | copy-start | bytes 9460
  54.3 211.2 %copy-start.40 = (s32[788]{0:T(1024)}, s32[788]{0:T(1024)S(1)}, u32[]{:S(2)}) copy-start(s32[788]{0:T(1024)S(1)} %get-tuple-element.155) | copy-start | bytes 9460
  115.6 31.6 %slice-start.1 = ((s8[4718592]{0:T(1024)(128)(4,1)}), s8[4194304]{0:T(1024)(128)(4,1)S(1)}, s32[]{:S(2)}) async-start(s8[4718592]{0:T(1024)(128)(4,1)} %bitcast.157), calls=%async_computation.24 | async-start | bytes 8388608
  118.0 29.2 %slice-start.2 = ((s8[4718592]{0:T(1024)(128)(4,1)}), s8[524288]{0:T(1024)(128)(4,1)S(1)}, s32[]{:S(2)}) async-start(s8[4718592]{0:T(1024)(128)(4,1)} %bitcast.157), calls=%async_computation.25 | async-start | bytes 1048576
  204.7 87.7 %all-to-all-start.1 = ((bf16[16,192,768]{2,1,0:T(8,128)(2,1)}), bf16[16,192,768]{2,1,0:T(8,128)(2,1)}, u32[]{:S(2)}, u32[]{:S(2)}) async-start(bf16[16,192,768]{2,1,0:T(8,128)(2,1)} %param.31), calls=%async_computation.1 | async-start | bytes 9437184 | tf_op jit(solution)/shard_map/all_to_all | solution.py:335
  263.6 79.0 %copy-start.42 = (f32[2,1536]{1,0:T(2,128)}, f32[2,1536]{1,0:T(2,128)S(1)}, u32[]{:S(2)}) copy-start(f32[2,1536]{1,0:T(2,128)S(1)} %dynamic-slice_convert_fusion) | copy-start | bytes 36868
  292.4 47.5 %all-to-all-start.5 = ((bf16[8,128,768]{2,1,0:T(8,128)(2,1)}), bf16[8,128,768]{2,1,0:T(8,128)(2,1)}, u32[]{:S(2)}, u32[]{:S(2)}) async-start(bf16[8,128,768]{2,1,0:T(8,128)(2,1)} %bitcast.176), calls=%async_computation.5 | async-start | bytes 3145728 | tf_op jit(solution)/shard_map/all_to_all | solution.py:335
  296.7 85.3 %reduce-scatter.10.cloned.1.call-start = ((), (), s32[]{:S(2)}) async-start(), calls=%async_computation.20 | async-start | bytes 2359296
  338.6 89.0 %reduce-scatter.12.cloned.1.call-start = ((), (), s32[]{:S(2)}) async-start(), calls=%async_computation.21 | async-start | bytes 2359296
  388.6 47.5 %all-to-all-start.3 = ((bf16[8,2,64,384]{3,2,1,0:T(8,128)(2,1)}), bf16[8,2,64,384]{3,2,1,0:T(8,128)(2,1)S(1)}, u32[]{:S(2)}, u32[]{:S(2)}) async-start(bf16[8,2,64,384]{3,2,1,0:T(8,128)(2,1)} %bitcast.165), calls=%async_computation.3 | async-start | bytes 1572864 | tf_op jit(solution)/shard_map/all_to_all | solution.py:335
  436.9 16.0 %all-to-all-start.6 = ((bf16[8,2,64,384]{3,2,1,0:T(8,128)(2,1)}), bf16[8,2,64,384]{3,2,1,0:T(8,128)(2,1)}, u32[]{:S(2)}, u32[]{:S(2)}) async-start(bf16[8,2,64,384]{3,2,1,0:T(8,128)(2,1)} %bitcast.166), calls=%async_computation.6 | async-start | bytes 1572864 | tf_op jit(solution)/shard_map/all_to_all | solution.py:335
  452.9 15.8 %all-to-all-start.4 = ((bf16[1024,2,192]{0,2,1:T(8,128)(2,1)}), bf16[1024,2,192]{0,2,1:T(8,128)(2,1)}, u32[]{:S(2)}, u32[]{:S(2)}) async-start(bf16[1024,2,192]{0,2,1:T(8,128)(2,1)} %copy.389), calls=%async_computation.4 | async-start | bytes 1572864 | tf_op jit(solution)/shard_map/all_to_all | solution.py:500
  468.6 26.7 %all-to-all-start.7 = ((bf16[1024,2,192]{0,2,1:T(8,128)(2,1)}), bf16[1024,2,192]{0,2,1:T(8,128)(2,1)S(1)}, u32[]{:S(2)}, u32[]{:S(2)}) async-start(bf16[1024,2,192]{0,2,1:T(8,128)(2,1)} %copy.396), calls=%async_computation.7 | async-start | bytes 1572864 | tf_op jit(solution)/shard_map/all_to_all | solution.py:500
  495.4 82.0 %all-to-all-start.8 = ((bf16[16,192,768]{2,1,0:T(8,128)(2,1)}), bf16[16,192,768]{2,1,0:T(8,128)(2,1)}, u32[]{:S(2)}, u32[]{:S(2)}) async-start(bf16[16,192,768]{2,1,0:T(8,128)(2,1)} %bitcast.146), calls=%async_computation.8 | async-start | bytes 9437184 | tf_op jit(solution)/shard_map/all_to_all | solution.py:335
  500.1 63.2 %all-gather.17.cloned.1.call-start = ((), (), s32[]{:S(2)}) async-start(), calls=%async_computation.19 | async-start | bytes 1792000 | tf_op jit(solution)/shard_map/all_gather | solution.py:514
  509.7 183.2 %all-gather.15.cloned.1.call-start = ((), (), s32[]{:S(2)}) async-start(), calls=%async_computation.16 | async-start | bytes 1720320 | tf_op jit(solution)/shard_map/all_gather | solution.py:520
  529.2 35.2 %copy-start.18 = (f32[788,32]{0,1:T(8,128)S(1)}, f32[788,32]{0,1:T(8,128)}, u32[]{:S(2)}) copy-start(f32[788,32]{0,1:T(8,128)} %copy-done.17) | copy-start | bytes 302596
  577.4 185.1 %all-to-all-start.9 = ((bf16[16,192,768]{2,1,0:T(8,128)(2,1)}), bf16[16,192,768]{2,1,0:T(8,128)(2,1)}, u32[]{:S(2)}, u32[]{:S(2)}) async-start(bf16[16,192,768]{2,1,0:T(8,128)(2,1)} %bitcast.145), calls=%async_computation.9 | async-start | bytes 9437184 | tf_op jit(solution)/shard_map/all_to_all | solution.py:335
  582.2 122.0 %all-reduce.5.cloned.1.call-start = ((), (), s32[]{:S(2)}) async-start(), calls=%async_computation.17 | async-start | bytes 2752512 | tf_op jit(solution)/shard_map/psum | solution.py:548
  599.9 142.6 %reduce-scatter.14.cloned.1.call-start = ((), (), s32[]{:S(2)}) async-start(), calls=%async_computation.22 | async-start | bytes 3440640
  617.0 163.1 %all-reduce.7.cloned.1.call-start = ((), (), s32[]{:S(2)}) async-start(), calls=%async_computation.18 | async-start | bytes 1654784 | tf_op jit(solution)/shard_map/psum | solution.py:576
  (52 other events, 261.7 us)
Sparse Core Ops, SparseCore 0:
  15.3 21.2 all-gather.8
  44.9 30.4 all-gather.12
  77.0 32.9 all-gather.10
  338.7 43.1 reduce-scatter.9
  384.7 42.8 reduce-scatter.11
  509.8 53.5 all-gather.16
  564.9 47.2 all-gather.14
  614.6 89.4 all-reduce.4
  706.9 35.5 reduce-scatter.13
  744.9 35.2 all-reduce.6

commit v2 on v1

--- a/solution.py
+++ b/solution.py
@@ -1,6 +1,11 @@
+import functools
+import math
+
 import jax
 import jax.numpy as jnp
 from jax import lax
+from jax.experimental import pallas as pl
+from jax.experimental.pallas import tpu as pltpu
 from jax.sharding import Mesh
 from jax.sharding import PartitionSpec as P
 
@@ -9,6 +14,15 @@
 TOPK = 2
 CAP = 64
 FF_PAIR = 2
+VMEM_LIMIT = 56 * 1024 * 1024
+GELU_SCALE = (2.0 / math.pi) ** 0.5
+GELU_CUBE = 0.044715
+
+DP = "dp"
+EXPERT = "expert"
+TENSOR = "tensor"
+OUTER = "outer"
+INNER = "inner"
 
 
 EPS = 1e-06
@@ -104,17 +118,17 @@
         back_full,
         back_bias_full,
     ) = (
-        lax.all_gather(first_gain, "dp", axis=0, tiled=True),
-        lax.all_gather(first_shift, "dp", axis=0, tiled=True),
-        lax.all_gather(w_qkv, "dp", axis=1, tiled=True),
-        lax.all_gather(w_out, "dp", axis=1, tiled=True),
-        lax.all_gather(out_bias, "dp", axis=0, tiled=True),
-        lax.all_gather(second_gain, "dp", axis=0, tiled=True),
-        lax.all_gather(second_shift, "dp", axis=0, tiled=True),
-        lax.all_gather(w_router, "dp", axis=0, tiled=True),
-        lax.all_gather(w_in, "dp", axis=1, tiled=True),
-        lax.all_gather(w_back, "dp", axis=2, tiled=True),
-        lax.all_gather(back_bias, "dp", axis=1, tiled=True),
+        lax.all_gather(first_gain, DP, axis=0, tiled=True),
+        lax.all_gather(first_shift, DP, axis=0, tiled=True),
+        lax.all_gather(w_qkv, DP, axis=1, tiled=True),
+        lax.all_gather(w_out, DP, axis=1, tiled=True),
+        lax.all_gather(out_bias, DP, axis=0, tiled=True),
+        lax.all_gather(second_gain, DP, axis=0, tiled=True),
+        lax.all_gather(second_shift, DP, axis=0, tiled=True),
+        lax.all_gather(w_router, DP, axis=0, tiled=True),
+        lax.all_gather(w_in, DP, axis=1, tiled=True),
+        lax.all_gather(w_back, DP, axis=2, tiled=True),
+        lax.all_gather(back_bias, DP, axis=1, tiled=True),
     )
     gain_first = gain_first.astype(jnp.float32)
     gain_second = gain_second.astype(jnp.float32)
@@ -137,7 +151,7 @@
     attended, log_total = attention_forward(queries, key_rows, value_rows, scale)
     attended_low = attended.reshape(rows_total, local_width).astype(jnp.bfloat16)
     head_part = jnp.dot(attended_low, out_full, preferred_element_type=jnp.float32)
-    mixed = inputs + lax.psum(head_part, "tensor") + bias_out_full.astype(jnp.float32)
+    mixed = inputs + lax.psum(head_part, TENSOR) + bias_out_full.astype(jnp.float32)
     routed, scaled_second, inv_second = norm_parts(
         mixed, gain_second, shift_second.astype(jnp.float32)
     )
@@ -157,7 +171,7 @@
         .set(pair_rows)[: EXPERTS * CAP]
     )
     outgoing = outgoing.reshape(EXPERTS, 1, CAP, width)
-    arrived = lax.all_to_all(outgoing, "expert", split_axis=0, concat_axis=1, tiled=True)
+    arrived = lax.all_to_all(outgoing, EXPERT, split_axis=0, concat_axis=1, tiled=True)
     sources = arrived.shape[1]
     expert_rows = arrived.reshape(experts_here, sources * CAP, width)
     hidden_pre = jnp.einsum(
@@ -172,13 +186,13 @@
     bias_back = back_bias_full.astype(jnp.float32)[:, None, :]
     shares = lax.psum_scatter(
         expert_part.reshape(experts_here, sources, CAP, width),
-        "tensor",
+        TENSOR,
         scatter_dimension=2,
         tiled=True,
     )
     share_low = (shares + bias_back[:, None]).astype(jnp.bfloat16)
-    pieces = lax.all_to_all(share_low, "expert", split_axis=1, concat_axis=0, tiled=True)
-    returned = lax.all_gather(pieces, "tensor", axis=2, tiled=True)
+    pieces = lax.all_to_all(share_low, EXPERT, split_axis=1, concat_axis=0, tiled=True)
+    returned = lax.all_gather(pieces, TENSOR, axis=2, tiled=True)
     padded = jnp.concatenate(
         [returned.reshape(EXPERTS * CAP, width), jnp.zeros((1, width), jnp.bfloat16)], axis=0
     )
@@ -198,7 +212,7 @@
         .set(grad_picked)[: EXPERTS * CAP]
     )
     grad_outgoing = grad_outgoing.reshape(EXPERTS, 1, CAP, width)
-    grad_arrived = lax.all_to_all(grad_outgoing, "expert", split_axis=0, concat_axis=1, tiled=True)
+    grad_arrived = lax.all_to_all(grad_outgoing, EXPERT, split_axis=0, concat_axis=1, tiled=True)
     grad_arrived = grad_arrived.reshape(experts_here, sources * CAP, width)
     grad_back_bias = jnp.sum(grad_arrived.astype(jnp.float32), axis=1)
     grad_back_w = jnp.einsum(
@@ -218,12 +232,12 @@
     )
     grad_shares = lax.psum_scatter(
         grad_rows_part.reshape(experts_here, sources, CAP, width),
-        "tensor",
+        TENSOR,
         scatter_dimension=2,
         tiled=True,
     ).astype(jnp.bfloat16)
-    grad_pieces = lax.all_to_all(grad_shares, "expert", split_axis=1, concat_axis=0, tiled=True)
-    grad_returned = lax.all_gather(grad_pieces, "tensor", axis=2, tiled=True)
+    grad_pieces = lax.all_to_all(grad_shares, EXPERT, split_axis=1, concat_axis=0, tiled=True)
+    grad_returned = lax.all_gather(grad_pieces, TENSOR, axis=2, tiled=True)
     grad_padded = jnp.concatenate(
         [grad_returned.reshape(EXPERTS * CAP, width), jnp.zeros((1, width), jnp.bfloat16)], axis=0
     )
@@ -269,12 +283,12 @@
     grad_normed_part = jnp.einsum(
         "cte,cde->td", grad_proj_low, qkv_full, preferred_element_type=jnp.float32
     )
-    grad_normed = lax.psum(grad_normed_part, "tensor")
+    grad_normed = lax.psum(grad_normed_part, TENSOR)
     grad_from_first, grad_gain_first, grad_shift_first = norm_back(
         grad_normed, scaled_first, inv_first, gain_first
     )
     grad_images = (grad_mixed + grad_from_first).reshape(images.shape)
-    expert_start = lax.axis_index("expert") * experts_here
+    expert_start = lax.axis_index(EXPERT) * experts_here
     full_in_bias = lax.dynamic_update_slice(
         jnp.zeros((EXPERTS, grad_in_bias_local.shape[1]), jnp.float32),
         grad_in_bias_local,
@@ -293,10 +307,10 @@
             grad_router,
             full_in_bias,
         ),
-        ("dp", "expert"),
-    )
-    shard_width = width // lax.axis_size("dp")
-    shard_start = lax.axis_index("dp") * shard_width
+        (DP, EXPERT),
+    )
+    shard_width = width // lax.axis_size(DP)
+    shard_start = lax.axis_index(DP) * shard_width
     grad_first_gain = lax.dynamic_slice_in_dim(summed[0], shard_start, shard_width, 0)
     grad_first_shift = lax.dynamic_slice_in_dim(summed[1], shard_start, shard_width, 0)
     grad_w_qkv = lax.dynamic_slice_in_dim(summed[2], shard_start, shard_width, 1)
@@ -308,9 +322,9 @@
     grad_w_router = lax.dynamic_slice_in_dim(summed[8], shard_start, shard_width, 0)
     grad_in_bias = lax.dynamic_slice_in_dim(summed[9], expert_start, experts_here, 0)
     grad_w_in, grad_w_back, grad_back_shard = (
-        lax.psum_scatter(grad_in_w, "dp", scatter_dimension=1, tiled=True),
-        lax.psum_scatter(grad_back_w, "dp", scatter_dimension=2, tiled=True),
-        lax.psum_scatter(grad_back_bias, "dp", scatter_dimension=1, tiled=True),
+        lax.psum_scatter(grad_in_w, DP, scatter_dimension=1, tiled=True),
+        lax.psum_scatter(grad_back_w, DP, scatter_dimension=2, tiled=True),
+        lax.psum_scatter(grad_back_bias, DP, scatter_dimension=1, tiled=True),
     )
     return (
         output,
@@ -338,6 +352,173 @@
 def high_low(values):
     high = lax.reduce_precision(values, 8, 7)
     return high.astype(jnp.bfloat16), (values - high).astype(jnp.bfloat16)
+
+
+def turned_dot(left, right, left_dim, right_dim):
+    return lax.dot_general(
+        left, right, (((left_dim,), (right_dim,)), ((), ())), preferred_element_type=jnp.float32
+    )
+
+
+def expert_kernel(
+    inner,
+    rows_ref,
+    gate_ref,
+    cot_ref,
+    in_ref,
+    back_ref,
+    in_bias_ref,
+    back_bias_ref,
+    returned_ref,
+    grads_ref,
+    hidden_ref,
+    grad_pre_ref,
+    grad_turned_ref,
+    grad_in_bias_ref,
+    grad_back_bias_ref,
+):
+    f32, bf16 = jnp.float32, jnp.bfloat16
+    groups, cap, width = rows_ref.shape
+    chunks = in_ref.shape[0]
+    data = chunks // inner
+    tensor, slice_width = returned_ref.shape[1:3]
+    mine = back_bias_ref.shape[1]
+    total = groups * cap
+    at = pl.program_id(0)
+    rows = rows_ref[...].reshape(total, width)
+    cot_turned = cot_ref[...].reshape(total, width).T.astype(f32)
+    pair = gate_ref[:, 0:1, :].astype(f32) + gate_ref[:, 1:2, :].astype(f32)
+    pair = pair.reshape(groups, pair.shape[-1])
+    gate = jnp.zeros((groups, cap), f32)
+    for j in range(mine):
+        gate = jnp.where(at == j, pair[:, j * cap : (j + 1) * cap], gate)
+    gate = jnp.concatenate([gate[g : g + 1, :] for g in range(groups)], axis=1)
+    grad_turned = (cot_turned * gate).astype(bf16)
+    grad_turned_ref[0] = grad_turned
+    grad_returned = grad_turned.T
+    grad_back_bias_ref[0] = jnp.sum(grad_returned.astype(f32), axis=0, keepdims=True)
+    bias_columns = back_bias_ref[...]
+    bias = jnp.zeros((width, 1), f32)
+    for j in range(mine):
+        bias = jnp.where(at == j, bias_columns[:, j : j + 1], bias)
+    part = jnp.broadcast_to(bias, (width, total))
+    back = jnp.zeros((width, total), f32)
+    for t in range(inner):
+        w_in = jnp.concatenate([in_ref[d * inner + t, 0] for d in range(data)], axis=0)
+        w_back = jnp.concatenate([back_ref[d * inner + t, 0] for d in range(data)], axis=0)
+        pre = jnp.dot(rows, w_in, preferred_element_type=f32) + in_bias_ref[0, t : t + 1, :]
+        square = pre * pre
+        bent = jnp.tanh(GELU_SCALE * pre * (1.0 + GELU_CUBE * square))
+        half = 0.5 * (1.0 + bent)
+        hidden = (pre * half).astype(bf16)
+        slope = half + (0.5 * GELU_SCALE) * pre * (1.0 - bent * bent) * (
+            1.0 + (3.0 * GELU_CUBE) * square
+        )
+        hidden_ref[0, t] = hidden
+        grad_pre = jnp.dot(grad_returned, w_back, preferred_element_type=f32) * slope
+        grad_in_bias_ref[0, t : t + 1, :] = jnp.sum(grad_pre, axis=0, keepdims=True)
+        grad_pre = grad_pre.astype(bf16)
+        grad_pre_ref[0, t] = grad_pre
+        part = part + turned_dot(w_back, hidden, 1, 1)
+        back = back + turned_dot(w_in, grad_pre, 1, 1)
+    gate_terms = jnp.sum(part * cot_turned, axis=0, keepdims=True)
+    high = gate_terms.astype(bf16)
+    low = (gate_terms - high.astype(f32)).astype(bf16)
+    extra = grads_ref.shape[2] - slice_width
+    tail = jnp.concatenate([high, low, jnp.zeros((extra - 2, total), bf16)], axis=0)
+    part = part.astype(bf16)
+    back = back.astype(bf16)
+    for j in range(mine):
+
+        @pl.when(at == j)
+        def _():
+            lanes = slice(j * cap, (j + 1) * cap)
+            for g in range(groups):
+                mine_lanes = slice(g * cap, (g + 1) * cap)
+                for z in range(tensor):
+                    features = slice(z * slice_width, (z + 1) * slice_width)
+                    returned_ref[g, z, :, lanes] = part[features, mine_lanes]
+                    grads_ref[g, z, :slice_width, lanes] = back[features, mine_lanes]
+                    grads_ref[g, z, slice_width:, lanes] = tail[:, mine_lanes]
+
+
+def run_experts(arrived, cot_rows, in_raw, back_raw, in_bias, back_bias, mine, inner, tensor):
+    f32, bf16 = jnp.float32, jnp.bfloat16
+    groups, _, width = cot_rows.shape
+    chunks, _, depth, ff = in_raw.shape
+    total = groups * CAP
+    slice_width = width // tensor
+    gate_at = mine * CAP // 16
+    outs = [
+        ((groups, tensor, slice_width, mine * CAP), bf16, lambda j: (0, 0, 0, 0), None),
+        ((groups, tensor, slice_width + 16, mine * CAP), bf16, lambda j: (0, 0, 0, 0), None),
+        ((mine, inner, total, ff), bf16, lambda j: (j, 0, 0, 0), 1),
+        ((mine, inner, total, ff), bf16, lambda j: (j, 0, 0, 0), 1),
+        ((mine, width, total), bf16, lambda j: (j, 0, 0), 1),
+        ((mine, inner, ff), f32, lambda j: (j, 0, 0), 1),
+        ((mine, 1, width), f32, lambda j: (j, 0, 0), 1),
+    ]
+    return pl.pallas_call(
+        functools.partial(expert_kernel, inner),
+        grid=(mine,),
+        in_specs=[
+            pl.BlockSpec((groups, CAP, width), lambda j: (0, j, 0)),
+            pl.BlockSpec((groups, 16, mine * CAP), lambda j: (0, gate_at, 0)),
+            pl.BlockSpec((groups, CAP, width), lambda j: (0, j, 0)),
+            pl.BlockSpec((chunks, 1, depth, ff), lambda j: (0, j, 0, 0)),
+            pl.BlockSpec((chunks, 1, depth, ff), lambda j: (0, j, 0, 0)),
+            pl.BlockSpec((1, inner, ff), lambda j: (j, 0, 0)),
+            pl.BlockSpec((width, mine), lambda j: (0, 0)),
+        ],
+        out_specs=[
+            pl.BlockSpec(shape if lead is None else (lead, *shape[1:]), index)
+            for shape, _, index, lead in outs
+        ],
+        out_shape=[jax.ShapeDtypeStruct(shape, dtype) for shape, dtype, _, _ in outs],
+        compiler_params=pltpu.CompilerParams(vmem_limit_bytes=VMEM_LIMIT),
+        cost_estimate=pl.CostEstimate(
+            flops=8 * mine * total * width * inner * ff,
+            bytes_accessed=4 * chunks * mine * depth * ff + 12 * mine * total * inner * ff,
+            transcendentals=mine * total * inner * ff,
+        ),
+    )(arrived, arrived, cot_rows, in_raw, back_raw, in_bias, back_bias)
+
+
+def weight_kernel(rows_ref, grad_pre_ref, grad_turned_ref, hidden_ref, grad_in_ref, grad_back_ref):
+    groups, cap, width = rows_ref.shape
+    shape = grad_in_ref.shape
+    rows = rows_ref[...].reshape(groups * cap, width)
+    grad_in = turned_dot(rows, grad_pre_ref[0, 0], 0, 0)
+    grad_in_ref[...] = grad_in.astype(jnp.bfloat16).reshape(shape)
+    grad_back = jnp.dot(grad_turned_ref[0], hidden_ref[0, 0], preferred_element_type=jnp.float32)
+    grad_back_ref[...] = grad_back.astype(jnp.bfloat16).reshape(shape)
+
+
+def weight_grads(arrived, grad_pre, grad_turned, hidden, data):
+    mine, inner, total, ff = hidden.shape
+    groups, _, width = arrived.shape
+    depth = width // data
+    out = (data, inner, mine, depth, ff)
+    kept = pl.BlockSpec((1, 1, total, ff), lambda j, t: (j, t, 0, 0))
+    given = pl.BlockSpec((data, 1, 1, depth, ff), lambda j, t: (0, t, j, 0, 0))
+    return pl.pallas_call(
+        weight_kernel,
+        grid=(mine, inner),
+        in_specs=[
+            pl.BlockSpec((groups, CAP, width), lambda j, t: (0, j, 0)),
+            kept,
+            pl.BlockSpec((1, width, total), lambda j, t: (j, 0, 0)),
+            kept,
+        ],
+        out_specs=[given, given],
+        out_shape=[jax.ShapeDtypeStruct(out, jnp.bfloat16)] * 2,
+        compiler_params=pltpu.CompilerParams(vmem_limit_bytes=VMEM_LIMIT),
+        cost_estimate=pl.CostEstimate(
+            flops=4 * mine * total * width * inner * ff,
+            bytes_accessed=4 * mine * inner * (total + width) * ff,
+            transcendentals=0,
+        ),
+    )(arrived, grad_pre, grad_turned, hidden)
 
 
 def moved_plan(
@@ -364,29 +545,25 @@
     image_count, seq_len, width = images.shape
     rows_total = image_count * seq_len
     experts_here, shard_width, ff_here = w_in.shape
-    data, sources = lax.axis_size("dp"), lax.axis_size("expert")
-    outer, inner = lax.axis_size("outer"), lax.axis_size("inner")
+    data, sources = lax.axis_size(DP), lax.axis_size(EXPERT)
+    outer, inner = lax.axis_size(OUTER), lax.axis_size(INNER)
     tensor = outer * inner
-    tensor_axes = ("outer", "inner")
+    tensor_axes = (OUTER, INNER)
     groups = data * sources
     owners = data * inner
     mine = experts_here // owners
     slots = EXPERTS * CAP
     slots_plane = slots // inner
-    dp_at = lax.axis_index("dp")
-    inner_at = lax.axis_index("inner")
+    dp_at = lax.axis_index(DP)
+    inner_at = lax.axis_index(INNER)
     tensor_at = lax.axis_index(tensor_axes)
     owner_at = dp_at * inner + inner_at
     local_width = w_out.shape[0]
     slice_width = width // tensor
 
-    def collect(shard):
-        parts = swap(shard, ("dp", "inner"))
-        parts = parts.reshape(data, inner, mine, shard_width, ff_here)
-        return parts.transpose(2, 0, 3, 1, 4).reshape(mine, width, inner * ff_here)
-
-    in_mine = collect(w_in)
-    back_mine = collect(w_back.transpose(0, 2, 1))
+    chunk_shape = (owners, mine, shard_width, ff_here)
+    in_raw = swap(w_in, (DP, INNER)).reshape(chunk_shape)
+    back_raw = swap(w_back.transpose(0, 2, 1), (DP, INNER)).reshape(chunk_shape)
 
     packed = jnp.concatenate(
         [
@@ -398,7 +575,7 @@
         ],
         axis=1,
     )
-    packed = lax.all_gather(packed, "dp", axis=0, tiled=True)
+    packed = lax.all_gather(packed, DP, axis=0, tiled=True)
     cuts = [3 * local_width, local_width, EXPERTS, experts_here]
     qkv_full, out_turned, router_full, back_bias_turned, vectors = jnp.split(
         packed, [sum(cuts[: i + 1]) for i in range(4)], axis=1
@@ -407,16 +584,24 @@
         vectors[:, i].astype(f32) for i in range(5)
     )
     out_whole = lax.all_gather(out_turned, tensor_axes, axis=1, tiled=True)
-    in_bias_all = lax.all_gather(in_bias, "inner", axis=1, tiled=True)
-    in_bias_mine = lax.dynamic_slice_in_dim(in_bias_all, owner_at * mine, mine, 0)
+    in_bias_all = jnp.stack(
+        [
+            lax.ppermute(in_bias, INNER, [(i, (i + s) % inner) for i in range(inner)])
+            for s in range(inner)
+        ]
+    )
+    in_bias_all = jnp.take(in_bias_all, (inner_at - jnp.arange(inner)) % inner, axis=0)
+    in_bias_mine = lax.dynamic_slice_in_dim(in_bias_all, owner_at * mine, mine, 1)
+    in_bias_mine = in_bias_mine.transpose(1, 0, 2).astype(f32)
 
     pair_routes = routes.reshape(rows_total, TOPK)
     pair_slots = slot_index.reshape(rows_total, TOPK)
     home, within = pair_routes // experts_here, pair_routes % experts_here
     owner, nth = within // mine, within % mine
-    place = ((owner % inner) * data + owner // inner) * sources + home
+    place = ((owner // inner) * sources + home) * inner + owner % inner
     target = jnp.where(pair_slots < CAP, (place * mine + nth) * CAP + pair_slots, slots)
-    plane_slots = inner_at * slots_plane + jnp.arange(slots_plane, dtype=jnp.int32)
+    plane_slots = jnp.arange(slots, dtype=jnp.int32).reshape(groups, inner, mine * CAP)
+    plane_slots = lax.dynamic_slice_in_dim(plane_slots, inner_at, 1, 1).reshape(slots_plane)
     takes = [plane_slots[:, None] == target[None, :, k] for k in range(TOPK)]
     fill = jnp.logical_or(takes[0], takes[1]).astype(bf16)
 
@@ -428,7 +613,7 @@
         return jnp.dot(fill, rows, preferred_element_type=f32).astype(bf16)
 
     cot_out = dispatch(grad_rows.astype(bf16)).reshape(groups, mine * CAP, width)
-    cot_rows = swap(cot_out, ("dp", "expert")).reshape(groups, mine, CAP, width)
+    cot_rows = swap(cot_out, (DP, EXPERT))
 
     inputs = images.reshape(rows_total, width).astype(f32)
     normed, scaled_first, inv_first = norm_parts(inputs, gain_first, shift_first)
@@ -447,6 +632,7 @@
     attended, log_total = attention_forward(queries, key_rows, value_rows, scale)
     attended_low = attended.reshape(rows_total, local_width).astype(bf16)
     attended_all = lax.all_gather(attended_low, tensor_axes, axis=1, tiled=True)
+    attended_all, in_raw = lax.optimization_barrier((attended_all, in_raw))
     mixed = inputs + bias_out_full
     mixed = mixed + jnp.einsum("te,de->td", attended_all, out_whole, preferred_element_type=f32)
     routed, scaled_second, inv_second = norm_parts(mixed, gain_second, shift_second)
@@ -463,60 +649,53 @@
     gate_parts = jnp.stack(high_low(gate_slots.reshape(groups, mine * CAP)), axis=1)
     gate_rows = jnp.pad(gate_parts, ((0, 0), (0, 14), (0, width - mine * CAP)))
     sent = jnp.concatenate([dispatch(routed_low).reshape(groups, mine * CAP, width), gate_rows], axis=1)
-    arrived = swap(sent, ("dp", "expert"))
-    expert_rows = arrived[:, : mine * CAP].reshape(groups, mine, CAP, width)
-    gate_here = jnp.sum(arrived[:, mine * CAP : mine * CAP + 2, : mine * CAP].astype(f32), axis=1)
-    gate_here = gate_here.reshape(groups, mine, CAP, 1)
-    to_experts = lambda rows: rows.transpose(1, 0, 2, 3).reshape(mine, groups * CAP, -1)
-    expert_rows = to_experts(expert_rows)
-    grad_returned = to_experts((gate_here * cot_rows.astype(f32)).astype(bf16))
-
-    hidden_pre = jnp.einsum("erd,edf->erf", expert_rows, in_mine, preferred_element_type=f32)
-    hidden_pre = hidden_pre + in_bias_mine.astype(f32)[:, None, :]
-    hidden_value, gelu_pull = jax.vjp(jax.nn.gelu, hidden_pre)
-    hidden_low = hidden_value.astype(bf16)
-    expert_part = jnp.einsum("erf,edf->erd", hidden_low, back_mine, preferred_element_type=f32)
-    grad_hidden = jnp.einsum("erd,edf->erf", grad_returned, back_mine, preferred_element_type=f32)
-    grad_pre = gelu_pull(grad_hidden)[0]
-    grad_in_bias_mine = jnp.sum(grad_pre, axis=1)
-    grad_pre_low = grad_pre.astype(bf16)
-    grad_rows_part = jnp.einsum("erf,edf->erd", grad_pre_low, in_mine, preferred_element_type=f32)
-    grad_back_mine = jnp.einsum("erd,erf->edf", grad_returned, hidden_low, preferred_element_type=f32)
-    grad_in_mine = jnp.einsum("erd,erf->edf", expert_rows, grad_pre_low, preferred_element_type=f32)
-    grad_back_bias_mine = jnp.sum(grad_returned.astype(f32), axis=1)
-
-    bias_here = lax.dynamic_slice(
-        back_bias_turned, (lax.axis_index("outer") * (width // outer), owner_at * mine), (width // outer, mine)
-    )
-    bias_here = bias_here.T.astype(f32)[:, None, :]
-
-    def bring(part, bias):
-        share = lax.psum_scatter(part.astype(bf16), "outer", scatter_dimension=2, tiled=True)
-        if bias is not None:
-            share = (share.astype(f32) + bias).astype(bf16)
-        share = share.reshape(mine, groups, CAP, width // outer).transpose(1, 0, 2, 3)
-        rows = swap(share, ("dp", "expert")).reshape(slots_plane, width // outer)
-        if inner > 1:
-            rows = lax.all_to_all(rows, "inner", split_axis=1, concat_axis=0, tiled=True)
-        return rows
-
-    returned = bring(expert_part, bias_here)
-    grad_buffers = bring(grad_rows_part, None)
+    sent, back_raw = lax.optimization_barrier((sent, back_raw))
+    arrived = swap(sent, (DP, EXPERT))
+    back_bias_mine = lax.dynamic_slice_in_dim(back_bias_turned, owner_at * mine, mine, 1)
+    back_bias_mine = jnp.where(lax.axis_index(OUTER) == 0, back_bias_mine.astype(f32), 0.0)
+    (
+        returned_out,
+        grads_out,
+        hidden_low,
+        grad_pre_low,
+        grad_turned,
+        grad_in_bias_mine,
+        grad_back_bias_mine,
+    ) = run_experts(
+        arrived, cot_rows, in_raw, back_raw, in_bias_mine, back_bias_mine, mine, inner, tensor
+    )
+
+    everywhere = (DP, EXPERT, OUTER, INNER)
+
+    def bring(parts):
+        parts = parts.reshape(groups * tensor, *parts.shape[2:])
+        parts = swap(parts, everywhere).astype(f32)
+        parts = jnp.sum(parts.reshape(groups, outer, inner, *parts.shape[1:]), axis=1)
+        return parts.reshape(groups * inner, *parts.shape[2:])
+
+    def in_line(parts):
+        return parts.transpose(1, 0, 2).reshape(parts.shape[1], slots)
+
+    grad_parts = bring(grads_out)
+    grad_slots = in_line(grad_parts[:, :slice_width]).astype(bf16)
+    gate_slots_back = in_line(grad_parts[:, slice_width : slice_width + 2])
+    gate_slots_back = gate_slots_back[0] + gate_slots_back[1]
     all_slots = jnp.arange(slots, dtype=jnp.int32)
-    finds = [(target[:, k : k + 1] == all_slots).astype(bf16) for k in range(TOPK)]
-    picked = [jnp.dot(find, returned, preferred_element_type=f32) for find in finds]
-    cut = lambda rows: lax.dynamic_slice_in_dim(rows, tensor_at * slice_width, slice_width, 1)
-    grad_rows_cut = cut(grad_rows)
-    grad_routed_cut = jnp.dot(finds[0] + finds[1], grad_buffers, preferred_element_type=f32)
-    gate_terms = jnp.stack([jnp.sum(grad_rows_cut * rows, axis=1) for rows in picked], axis=1)
-    gate_high, gate_low = high_low(gate_terms)
-    back = jnp.concatenate([grad_routed_cut.astype(bf16), gate_high, gate_low], axis=1)
-    back = lax.all_gather(back, tensor_axes, axis=0, tiled=False)
-    grad_gates = jnp.sum(back[:, :, slice_width:].astype(f32), axis=0)
-    grad_gates = grad_gates[:, :TOPK] + grad_gates[:, TOPK:]
-    grad_routed = back[:, :, :slice_width].transpose(1, 0, 2).reshape(rows_total, width).astype(f32)
-    expert_mix = gates[0][:, None] * picked[0] + gates[1][:, None] * picked[1]
-    output_cut = (live_rows * (cut(mixed) + expert_mix)).astype(bf16)
+    found = [target[None, :, k] == all_slots[:, None] for k in range(TOPK)]
+    finds = [hit.astype(bf16) for hit in found]
+    both = jnp.logical_or(found[0], found[1]).astype(bf16)
+    grad_gates = jnp.stack(
+        [jnp.sum(jnp.where(hit, gate_slots_back[:, None], 0.0), axis=0) for hit in found], axis=1
+    )
+    grad_routed_cut = jnp.dot(grad_slots, both, preferred_element_type=f32).astype(bf16)
+    grad_routed = lax.all_gather(grad_routed_cut, tensor_axes, axis=0, tiled=True).T.astype(f32)
+
+    grad_in_out, grad_back_out = weight_grads(arrived, grad_pre_low, grad_turned, hidden_low, data)
+    returned = in_line(bring(returned_out)).astype(bf16)
+    picked = [jnp.dot(returned, find, preferred_element_type=f32) for find in finds]
+    mixed_cut = lax.dynamic_slice_in_dim(mixed, tensor_at * slice_width, slice_width, 1)
+    expert_mix = gates[0][None, :] * picked[0] + gates[1][None, :] * picked[1]
+    output_cut = (live_rows * (mixed_cut + expert_mix.T)).astype(bf16)
     output = lax.all_gather(output_cut, tensor_axes, axis=1, tiled=True).reshape(images.shape)
 
     grad_probs = sum(match * grad_gates[:, k : k + 1] for k, match in enumerate(matches))
@@ -546,20 +725,22 @@
     grad_qkv = jnp.einsum("td,te->de", normed_low, grad_proj_low, preferred_element_type=f32)
     grad_normed_part = jnp.einsum("te,de->td", grad_proj_low, qkv_full, preferred_element_type=f32)
     grad_normed = lax.psum(grad_normed_part.astype(bf16), tensor_axes).astype(f32)
-    grad_from_first, grad_gain_first, grad_shift_first = norm_back(
-        grad_normed, scaled_first, inv_first, gain_first
+    grad_from_first, _, _ = norm_back(grad_normed, scaled_first, inv_first, gain_first)
+    first_terms = jnp.stack(
+        [jnp.sum(grad_normed_part * scaled_first, axis=0), jnp.sum(grad_normed_part, axis=0)]
     )
     grad_images = (grad_mixed + grad_from_first).reshape(images.shape)
 
-    def spread(grads):
-        parts = grads.astype(bf16).reshape(mine, data, shard_width, inner, ff_here)
-        parts = parts.transpose(1, 3, 0, 2, 4).reshape(experts_here, shard_width, ff_here)
-        return swap(parts, ("dp", "inner")).astype(f32)
-
-    grad_w_back = spread(grad_back_mine).transpose(0, 2, 1)
-    grad_w_in = spread(grad_in_mine)
-    bias_grads = jnp.concatenate([grad_in_bias_mine, grad_back_bias_mine], axis=1)
-    bias_grads = lax.all_gather(bias_grads, ("dp", "inner"), axis=0, tiled=True)
+    def spread(parts):
+        parts = parts.reshape(experts_here, shard_width, ff_here)
+        return swap(parts, (DP, INNER)).astype(f32)
+
+    grad_w_back = spread(grad_back_out).transpose(0, 2, 1)
+    grad_w_in = spread(grad_in_out)
+    bias_grads = jnp.concatenate(
+        [grad_in_bias_mine.reshape(mine, inner * ff_here), grad_back_bias_mine[:, 0]], axis=1
+    )
+    bias_grads = lax.all_gather(bias_grads, (DP, INNER), axis=0, tiled=True)
     grad_in_bias = lax.dynamic_slice_in_dim(bias_grads, inner_at * ff_here, ff_here, 1)
     grad_back_shard = lax.dynamic_slice_in_dim(
         bias_grads, inner * ff_here + dp_at * shard_width, shard_width, 1
@@ -573,16 +754,15 @@
         ],
         axis=1,
     )
-    early = lax.psum(lax.psum_scatter(early, "dp", scatter_dimension=0, tiled=True), "expert")
+    early = lax.psum(lax.psum_scatter(early, DP, scatter_dimension=0, tiled=True), EXPERT)
     grad_w_qkv = early[:, : 3 * local_width].reshape(shard_width, 3, local_width).transpose(1, 0, 2)
     grad_w_out = early[:, 3 * local_width : 4 * local_width].T
     grad_w_router = early[:, 4 * local_width : 4 * local_width + EXPERTS]
     grad_out_bias, grad_second_gain, grad_second_shift = (
         early[:, 4 * local_width + EXPERTS + i] for i in range(3)
     )
-    grad_qv_bias, grad_first_norm = lax.psum(
-        (grad_pair_bias, jnp.stack([grad_gain_first, grad_shift_first])), ("dp", "expert")
-    )
+    grad_qv_bias = lax.psum(grad_pair_bias, (DP, EXPERT))
+    grad_first_norm = lax.psum(first_terms, everywhere)
     grad_first_norm = lax.dynamic_slice_in_dim(grad_first_norm, dp_at * shard_width, shard_width, 1)
     return (
         output,
@@ -603,94 +783,29 @@
     )
 
 
+def specs(tensor):
+    rows = P((DP, EXPERT), None, None)
+    vector, square = P(DP), P(tensor, DP)
+    qkv, pair, router = P(None, DP, tensor), P(None, tensor), P(DP, None)
+    inward, outward = P(EXPERT, DP, tensor), P(EXPERT, tensor, DP)
+    params = (vector, vector, qkv, pair, square, vector, vector, vector, router)
+    experts = (inward, P(EXPERT, tensor), outward, P(EXPERT, DP))
+    taken = (rows, P((DP, EXPERT)), rows, rows, *params, *experts, rows)
+    given = (rows, rows, *params, *experts)
+    return taken, given
+
+
 def solution(mesh):
-    data, expert, tensor = (mesh.shape[name] for name in ("dp", "expert", "tensor"))
-    experts_here = EXPERTS // expert
+    data, expert, tensor = (mesh.shape[name] for name in (DP, EXPERT, TENSOR))
     inner = FF_PAIR if tensor % FF_PAIR == 0 else 1
-    if experts_here % (data * inner):
+    if (EXPERTS // expert) % (data * inner):
+        taken, given = specs(TENSOR)
         return jax.shard_map(
-            gathered_plan,
-            mesh=mesh,
-            in_specs=(
-                P(("dp", "expert"), None, None),
-                P(("dp", "expert")),
-                P(("dp", "expert"), None, None),
-                P(("dp", "expert"), None, None),
-                P("dp"),
-                P("dp"),
-                P(None, "dp", "tensor"),
-                P(None, "tensor"),
-                P("tensor", "dp"),
-                P("dp"),
-                P("dp"),
-                P("dp"),
-                P("dp", None),
-                P("expert", "dp", "tensor"),
-                P("expert", "tensor"),
-                P("expert", "tensor", "dp"),
-                P("expert", "dp"),
-                P(("dp", "expert"), None, None),
-            ),
-            out_specs=(
-                P(("dp", "expert"), None, None),
-                P(("dp", "expert"), None, None),
-                P("dp"),
-                P("dp"),
-                P(None, "dp", "tensor"),
-                P(None, "tensor"),
-                P("tensor", "dp"),
-                P("dp"),
-                P("dp"),
-                P("dp"),
-                P("dp", None),
-                P("expert", "dp", "tensor"),
-                P("expert", "tensor"),
-                P("expert", "tensor", "dp"),
-                P("expert", "dp"),
-            ),
-            check_vma=False,
+            gathered_plan, mesh=mesh, in_specs=taken, out_specs=given, check_vma=False
         )
     devices = mesh.devices.reshape(data, expert, tensor // inner, inner)
-    split_mesh = Mesh(devices, ("dp", "expert", "outer", "inner"))
+    split_mesh = Mesh(devices, (DP, EXPERT, OUTER, INNER))
+    taken, given = specs((OUTER, INNER))
     return jax.shard_map(
-        moved_plan,
-        mesh=split_mesh,
-        in_specs=(
-            P(("dp", "expert"), None, None),
-            P(("dp", "expert")),
-            P(("dp", "expert"), None, None),
-            P(("dp", "expert"), None, None),
-            P("dp"),
-            P("dp"),
-            P(None, "dp", ("outer", "inner")),
-            P(None, ("outer", "inner")),
-            P(("outer", "inner"), "dp"),
-            P("dp"),
-            P("dp"),
-            P("dp"),
-            P("dp", None),
-            P("expert", "dp", ("outer", "inner")),
-            P("expert", ("outer", "inner")),
-            P("expert", ("outer", "inner"), "dp"),
-            P("expert", "dp"),
-            P(("dp", "expert"), None, None),
-        ),
-        out_specs=(
-            P(("dp", "expert"), None, None),
-            P(("dp", "expert"), None, None),
-            P("dp"),
-            P("dp"),
-            P(None, "dp", ("outer", "inner")),
-            P(None, ("outer", "inner")),
-            P(("outer", "inner"), "dp"),
-            P("dp"),
-            P("dp"),
-            P("dp"),
-            P("dp", None),
-            P("expert", "dp", ("outer", "inner")),
-            P("expert", ("outer", "inner")),
-            P("expert", ("outer", "inner"), "dp"),
-            P("expert", "dp"),
-        ),
-        check_vma=False,
-    )
+        moved_plan, mesh=split_mesh, in_specs=taken, out_specs=given, check_vma=False
+    )

time: 803 us -> 680 us (0.85)
  local copies, waits for them, and re-layouts: 210 us -> 93.1 us
  blocking collectives: 216 us -> 158 us
  waiting for transfers between devices: 192 us -> 247 us
  matrix products: 78.8 us -> 44.4 us
  Pallas kernels: 0 us -> 30 us
    all_to_all x6 -> x7, waiting for transfers between devices: 10.7 us -> 127 us  [swap(): return lax.all_to_all(values, axes, split_axis=0, concat_axis=0, tiled=True)]
    reshape x9 -> x1, local copies, waits for them, and re-layouts: 66.9 us -> 0.18 us  [moved_plan(): w_qkv.transpose(1, 0, 2).reshape(shard_width, 3 * local_width)]
    unnamed x13 -> x9, waiting for transfers between devices: 64.7 us -> 0.13 us
    all_gather x2 -> x1, blocking collectives: 118 us -> 63.6 us  [moved_plan(): bias_grads = lax.all_gather(bias_grads, (DP, INNER), axis=0, tiled=True)]
    all_to_all x2 -> x1, blocking collectives: 83.2 us -> 41.6 us  [swap(): return lax.all_to_all(values, axes, split_axis=0, concat_axis=0, tiled=True)]
    dot_general x9 -> x3, matrix products: 46.9 us -> 7.88 us  [the longest x2 5.2 us: moved_plan(): jnp.dot(returned, find, preferred_element_type=f32)]
    psum x1 -> x2, blocking collectives: 14.7 us -> 52.3 us  [the longest x1 39.9 us: moved_plan(): grad_first_norm = lax.psum(first_terms, everywhere)]
    unnamed x136 -> x87, local copies, waits for them, and re-layouts: 54.5 us -> 23.1 us
  transfers between devices with their start and end apart: 18 -> 17, of which waited for: 12 -> 10; matrix products, arithmetic and copies ran while one was open for 35% -> 26% of each run, Pallas kernels for 0% -> 2%
where the time goes in v2:
time: 680 us; the launch traced here: 669 us
  waiting for transfers between devices  247 us (36%)
  blocking collectives  158 us (23%)
  local copies, waits for them, and re-layouts  93.1 us (14%)
  other arithmetic  46.8 us (7%)
  matrix products  44.4 us (7%)
  starting transfers between devices  33.9 us (5%)
  Pallas kernels  30 us (4%)
  between operations  16.2 us (2%)
    all_to_all x7, waiting for transfers between devices, swap(): return lax.all_to_all(values, axes, split_axis=0, concat_axis=0, tiled=True)  127 us
    all_gather x1, blocking collectives, moved_plan(): bias_grads = lax.all_gather(bias_grads, (DP, INNER), axis=0, tiled=True)  63.6 us
    all_to_all x1, blocking collectives, swap(): return lax.all_to_all(values, axes, split_axis=0, concat_axis=0, tiled=True)  41.6 us
    all_gather x1, waiting for transfers between devices, moved_plan(): lax.all_gather(grad_routed_cut, tensor_axes, axis=0, tiled=True)  40.1 us
    psum x1, blocking collectives, moved_plan(): grad_first_norm = lax.psum(first_terms, everywhere)  39.9 us
    all_gather x1, waiting for transfers between devices, moved_plan(): out_whole = lax.all_gather(out_turned, tensor_axes, axis=1, tiled=True)  36 us
    all_to_all x7, starting transfers between devices, swap(): return lax.all_to_all(values, axes, split_axis=0, concat_axis=0, tiled=True)  31.9 us
    all_gather x1, waiting for transfers between devices, moved_plan(): attended_all = lax.all_gather(attended_low, tensor_axes, axis=1, tiled=True)  30.8 us
  transfers between devices with their start and end apart: 17, of which 10 were waited for; matrix products, arithmetic and copies ran while one was open for 26% of the time, Pallas kernels for 2%

profile of v2, /device:TPU:0, one launch (start us, length us, event | category | flops | bytes accessed | tf_op | source)
XLA Modules:
  0.0 669.4 jit_solution(16916587800803953179)
XLA Ops:
  7.3 5.4 all-to-all-start
  16.7 57.2 %all-to-all-done = bf16[16,192,768]{2,1,0:T(8,128)(2,1)} async-done(((bf16[16,192,768]{2,1,0:T(8,128)(2,1)}), bf16[16,192,768]{2,1,0:T(8,128)(2,1)}, u32[]{:S(2)}, u32[]{:S(2)}) %all-to-all-start) | async-done | bytes 4718624 | tf_op jit(solution)/shard_map/all_to_all | solution.py:349
  81.3 5.0 reshape.428
  110.2 5.0 reshape.423
  116.3 5.3 fusion.20
  121.5 30.8 %all-gather.9.cloned.1.call-done = bf16[788,768]{0,1:T(8,128)(2,1)} async-done(((bf16[788,192]{0,1:T(8,128)(2,1)}), bf16[788,768]{0,1:T(8,128)(2,1)}) %all-gather.9.cloned.1.call-update) | async-done | bytes 1210384 | tf_op jit(solution)/shard_map/all_gather | solution.py:634
  152.3 36.0 %all-gather.11.cloned.1.call-done = bf16[768,768]{0,1:T(8,128)(2,1)} async-done(((bf16[768,192]{0,1:T(8,128)(2,1)}), bf16[768,768]{0,1:T(8,128)(2,1)}) %all-gather.11.cloned.1.call-update) | async-done | bytes 1179664 | tf_op jit(solution)/shard_map/all_gather | solution.py:586
  206.8 14.1 %all-to-all-done.3.cot_ref = bf16[8,128,768]{2,1,0:T(8,128)(2,1)} async-done(((bf16[8,128,768]{2,1,0:T(8,128)(2,1)}), bf16[8,128,768]{2,1,0:T(8,128)(2,1)}, u32[]{:S(2)}, u32[]{:S(2)}) %all-to-all-start.3) | async-done | bytes 1572896 | tf_op jit(solution)/shard_map/all_to_all | solution.py:349
  232.7 15.2 %all-to-all-done.2.rows_ref.gate_ref = bf16[8,144,768]{2,1,0:T(8,128)(2,1)} async-done(((bf16[8,144,768]{2,1,0:T(8,128)(2,1)}), bf16[8,144,768]{2,1,0:T(8,128)(2,1)}, u32[]{:S(2)}, u32[]{:S(2)}) %all-to-all-start.2) | async-done | bytes 1769504 | tf_op jit(solution)/shard_map/all_to_all | solution.py:349
  247.9 18.9 %shard_map.289 = (bf16[8,4,192,128]{3,2,1,0:T(8,128)(2,1)}, bf16[8,4,208,128]{3,2,1,0:T(8,128)(2,1)}, bf16[2,2,512,768]{3,2,1,0:T(8,128)(2,1)}, bf16[2,2,512,768...) custom-call(bf16[8,144,768]{2,1,0:T(8,128)(2,1)} %all-to-all-done.2.rows_ref.gate_, ...), custom_call_target="tpu_custom_call" | custom-call | flops 9663676416 | bytes 28311552 | tf_op jit(solution)/shard_map/pallas_call | solution.py:461
  266.8 41.6 %all_to_all.40 = bf16[32,192,128]{2,1,0:T(8,128)(2,1)} all-to-all(bf16[32,192,128]{2,1,0:T(8,128)(2,1)} %bitcast.125), channel_id=1, replica_groups=mesh['dp'=4,'expert'=2,'outer'=2,'inner'=2] {'dp','expert','outer','inner'}, dimensions={0} | all-to-all | bytes 3145728 | tf_op jit(solution)/shard_map/all_to_all | solution.py:349
  311.9 11.1 %shard_map.290 = (bf16[4,2,2,192,768]{4,3,2,1,0:T(8,128)(2,1)}, bf16[4,2,2,192,768]{4,3,2,1,0:T(8,128)(2,1)}) custom-call(bf16[8,144,768]{2,1,0:T(8,128)(2,1)} %all-to-all-done.2.rows_ref.gate_ref, bf16[2,2,512,768]{3,2,1,0:T(8,128)(2,1)} %get-tuple-element.34.grad_pre_ref, bf16[2,768,512]{2,1,0:T(8,128)(2,1)} %get-tuple-element.35.grad_turned_ref, ...), custom_call_target="tpu_custom_call" | custom-call | flops 4831838208 | bytes 15728640 | tf_op jit(solution)/shard_map/pallas_call | solution.py:504
  323.0 29.4 %all-to-all-done.5 = bf16[32,208,128]{2,1,0:T(8,128)(2,1)} async-done(((bf16[32,208,128]{2,1,0:T(8,128)(2,1)}), bf16[32,208,128]{2,1,0:T(8,128)(2,1)}, u32[]{:S(2)}, u32[]{:S(2)}) %all-to-all-start.5) | async-done | bytes 1703968 | tf_op jit(solution)/shard_map/all_to_all | solution.py:349
  376.2 40.1 %all-gather.15.cloned.1.call-done = bf16[768,788]{1,0:T(8,128)(2,1)} async-done(((bf16[192,788]{1,0:T(8,128)(2,1)}), bf16[768,788]{1,0:T(8,128)(2,1)}) %all-gather.15.cloned.1.call-update) | async-done | bytes 1210384 | tf_op jit(solution)/shard_map/all_gather | solution.py:691
  427.7 10.8 %all-to-all-done.6 = bf16[16,192,768]{2,1,0:T(8,128)(2,1)} async-done(((bf16[16,192,768]{2,1,0:T(8,128)(2,1)}), bf16[16,192,768]{2,1,0:T(8,128)(2,1)}, u32[]{:S(2)}, u32[]{:S(2)}) %all-to-all-start.6) | async-done | bytes 4718624 | tf_op jit(solution)/shard_map/all_to_all | solution.py:349
  471.8 8.2 %concatenate.19 = f32[768,803]{0,1:T(8,128)} concatenate(f32[768,576]{0,1:T(8,128)} %fusion.102, f32[768,192]{0,1:T(8,128)S(1)} %fusion.54, f32[768,32]{0,1:T(8,128)S(1)} %fusion.88, f32[768,1]{0,1:T(1,128)S(1)} %stack.70, f32[768,1]{0,1:T(1,128)S(1)} %stack.71, f32[768,1]{0,1:T(1,128)S(1)} %stack.72), dimensions={1} | concatenate | bytes 4933632 | tf_op jit(solution)/shard_map/concatenate | solution.py:748
  484.1 63.6 %all-gather = f32[8,2,2304]{2,1,0:T(2,128)S(1)} all-gather(f32[1,2,2304]{2,1,0:T(2,128)S(1)} %maximum_bitcast_fusion), channel_id=1, replica_groups=mesh['dp'=4,'expert'=2,'outer'=2,'inner'=2] {'dp','inner'}, dimensions={0}, use_global_device_ids=true | all-gather | bytes 165888 | tf_op jit(solution)/shard_map/all_gather | solution.py:743
  556.1 12.4 %psum.31 = f32[2,192]{1,0:T(2,128)} all-reduce(f32[2,192]{1,0:T(2,128)S(1)} %pad_maximum_fusion.3), channel_id=1, replica_groups=mesh['dp'=4,'expert'=2,'outer'=2,'inner'=2] {'dp','expert'}, use_global_device_ids=true, to_apply=%region_33.34 | all-reduce | flops 384 | bytes 3072 | tf_op jit(solution)/shard_map/psum | solution.py:764
  572.6 39.9 %psum.29 = f32[2,768]{1,0:T(2,128)S(1)} all-reduce(f32[2,768]{1,0:T(2,128)S(1)} %pad_maximum_fusion.2), channel_id=1, replica_groups=mesh['dp'=4,'expert'=2,'outer'=2,'inner'=2] {'dp','expert','outer','inner'}, use_global_device_ids=true, to_apply=%region_25.26 | all-reduce | flops 1536 | bytes 12288 | tf_op jit(solution)/shard_map/psum | solution.py:765
  612.6 5.0 multiply_add_fusion
  620.5 5.5 reshape.425
  630.5 7.1 %convert_element_type.248 = f32[16,192,768]{2,1,0:T(8,128)} convert(bf16[16,192,768]{2,1,0:T(8,128)(2,1)} %all-to-all-done.6) | non-fusion elementwise | flops 2359296 | bytes 14155776 | tf_op jit(solution)/shard_map/convert_element_type | solution.py:736
  637.6 7.1 %convert_bitcast_fusion = f32[16,768,192]{1,2,0:T(8,128)} fusion(bf16[16,192,768]{2,1,0:T(8,128)(2,1)} %all-to-all-done.7), kind=kLoop, calls=%fused_computation.1 | loop fusion | flops 2359296 | bytes 14155776 | tf_op jit(solution)/shard_map/transpose | solution.py:738
  644.7 10.9 %all-reduce.6.cloned.1.call-done = f32[192,803]{0,1:T(8,128)} async-done(((f32[192,803]{0,1:T(8,128)}), f32[192,803]{0,1:T(8,128)}) %all-reduce.6.cloned.1.call-update) | async-done | bytes 616720 | tf_op jit(solution)/shard_map/psum | solution.py:757
  (243 shorter events, 167.5 us)
Async XLA Ops:
  7.2 6.4 copy-start.30
  7.3 6.5 copy-start.31
  7.3 6.6 copy-start.32
  7.3 66.6 %all-to-all-start = ((bf16[16,192,768]{2,1,0:T(8,128)(2,1)}), bf16[16,192,768]{2,1,0:T(8,128)(2,1)}, u32[]{:S(2)}, u32[]{:S(2)}) async-start(bf16[16,192,768]{2,1,0:T(8,128)(2,1)} %param.31), calls=%async_computation | async-start | bytes 9437184 | tf_op jit(solution)/shard_map/all_to_all | solution.py:349
  12.7 74.0 %all-gather.7.cloned.1.call-start = ((), (), s32[]{:S(2)}) async-start(), calls=%async_computation.9 | async-start | bytes 1720320 | tf_op jit(solution)/shard_map/all_gather | solution.py:578
  73.9 122.5 %all-to-all-start.1 = ((bf16[16,192,768]{2,1,0:T(8,128)(2,1)}), bf16[16,192,768]{2,1,0:T(8,128)(2,1)}, u32[]{:S(2)}, u32[]{:S(2)}) async-start(bf16[16,192,768]{2,1,0:T(8,128)(2,1)} %bitcast.115), calls=%async_computation.1 | async-start | bytes 9437184 | tf_op jit(solution)/shard_map/all_to_all | solution.py:349
  78.5 73.8 %all-gather.9.cloned.1.call-start = ((), (), s32[]{:S(2)}) async-start(), calls=%async_computation.10 | async-start | bytes 1720320 | tf_op jit(solution)/shard_map/all_gather | solution.py:634
  98.3 7.3 %copy-start.24 = (s32[4,197,2]{1,2,0:T(2,128)S(1)}, s32[4,197,2]{1,2,0:T(2,128)}, u32[]{:S(2)}) copy-start(s32[4,197,2]{1,2,0:T(2,128)} %param.21) | copy-start | bytes 18916
  98.3 7.4 %copy-start.25 = (s32[4,197,2]{1,2,0:T(2,128)S(1)}, s32[4,197,2]{1,2,0:T(2,128)}, u32[]{:S(2)}) copy-start(s32[4,197,2]{1,2,0:T(2,128)} %param.20) | copy-start | bytes 18916
  101.5 86.8 %all-gather.11.cloned.1.call-start = ((), (), s32[]{:S(2)}) async-start(), calls=%async_computation.11 | async-start | bytes 1474560 | tf_op jit(solution)/shard_map/all_gather | solution.py:586
  196.4 24.5 %all-to-all-start.3 = ((bf16[8,128,768]{2,1,0:T(8,128)(2,1)}), bf16[8,128,768]{2,1,0:T(8,128)(2,1)}, u32[]{:S(2)}, u32[]{:S(2)}) async-start(bf16[8,128,768]{2,1,0:T(8,128)(2,1)} %bitcast.124), calls=%async_computation.3 | async-start | bytes 3145728 | tf_op jit(solution)/shard_map/all_to_all | solution.py:349
  206.8 18.9 %copy-start.33 = (bf16[16,768]{1,0:T(8,128)(2,1)S(1)}, bf16[16,768]{1,0:T(8,128)(2,1)}, u32[]{:S(2)}) copy-start(bf16[16,768]{1,0:T(8,128)(2,1)} %param.32) | copy-start | bytes 73732
  220.9 27.0 %all-to-all-start.2 = ((bf16[8,144,768]{2,1,0:T(8,128)(2,1)}), bf16[8,144,768]{2,1,0:T(8,128)(2,1)}, u32[]{:S(2)}, u32[]{:S(2)}) async-start(bf16[8,144,768]{2,1,0:T(8,128)(2,1)} %pad_maximum_fusion), calls=%async_computation.2 | async-start | bytes 3538944 | tf_op jit(solution)/shard_map/all_to_all | solution.py:349
  225.6 3.9 collective-permute-start.1
  226.7 2.8 collective-permute-start
  308.4 44.0 %all-to-all-start.5 = ((bf16[32,208,128]{2,1,0:T(8,128)(2,1)}), bf16[32,208,128]{2,1,0:T(8,128)(2,1)}, u32[]{:S(2)}, u32[]{:S(2)}) async-start(bf16[32,208,128]{2,1,0:T(8,128)(2,1)} %bitcast.122), calls=%async_computation.5 | async-start | bytes 3407872 | tf_op jit(solution)/shard_map/all_to_all | solution.py:349
  352.4 86.1 %all-to-all-start.6 = ((bf16[16,192,768]{2,1,0:T(8,128)(2,1)}), bf16[16,192,768]{2,1,0:T(8,128)(2,1)}, u32[]{:S(2)}, u32[]{:S(2)}) async-start(bf16[16,192,768]{2,1,0:T(8,128)(2,1)} %bitcast.117), calls=%async_computation.6 | async-start | bytes 9437184 | tf_op jit(solution)/shard_map/all_to_all | solution.py:349
  357.0 59.3 %all-gather.15.cloned.1.call-start = ((), (), s32[]{:S(2)}) async-start(), calls=%async_computation.13 | async-start | bytes 1720320 | tf_op jit(solution)/shard_map/all_gather | solution.py:691
  363.6 185.5 %all-gather.13.cloned.1.call-start = ((), (), s32[]{:S(2)}) async-start(), calls=%async_computation.12 | async-start | bytes 1720320 | tf_op jit(solution)/shard_map/all_gather | solution.py:699
  438.5 199.1 %all-to-all-start.7 = ((bf16[16,192,768]{2,1,0:T(8,128)(2,1)}), bf16[16,192,768]{2,1,0:T(8,128)(2,1)}, u32[]{:S(2)}, u32[]{:S(2)}) async-start(bf16[16,192,768]{2,1,0:T(8,128)(2,1)} %bitcast.116), calls=%async_computation.7 | async-start | bytes 9437184 | tf_op jit(solution)/shard_map/all_to_all | solution.py:349
  443.3 125.2 %all-reduce.4.cloned.1.call-start = ((), (), s32[]{:S(2)}) async-start(), calls=%async_computation.14 | async-start | bytes 2752512 | tf_op jit(solution)/shard_map/psum | solution.py:727
  466.1 151.4 %reduce-scatter.4.cloned.1.call-start = ((), (), s32[]{:S(2)}) async-start(), calls=%async_computation.16 | async-start | bytes 3440640
  483.3 172.2 %all-reduce.6.cloned.1.call-start = ((), (), s32[]{:S(2)}) async-start(), calls=%async_computation.15 | async-start | bytes 1654784 | tf_op jit(solution)/shard_map/psum | solution.py:757
  568.5 44.0 %copy-start.8 = (bf16[788,768]{0,1:T(8,128)(2,1)S(1)}, bf16[788,768]{0,1:T(8,128)(2,1)}, u32[]{:S(2)}) copy-start(bf16[788,768]{0,1:T(8,128)(2,1)} %all-reduce.4.cloned.1.call-done) | copy-start | bytes 3631108
  (27 other events, 90.9 us)
Sparse Core Ops, SparseCore 0:
  15.6 53.6 all-gather.6
  101.6 50.6 all-gather.8
  154.5 33.7 all-gather.10
  363.7 52.5 all-gather.14
  417.8 43.2 all-gather.12
  466.3 88.1 all-reduce.3
  557.2 36.1 reduce-scatter.3
  620.0 35.5 all-reduce.5

commit v3 on v2

--- a/solution.py
+++ b/solution.py
@@ -14,6 +14,7 @@
 TOPK = 2
 CAP = 64
 FF_PAIR = 2
+EXTRA = 16
 VMEM_LIMIT = 56 * 1024 * 1024
 GELU_SCALE = (2.0 / math.pi) ** 0.5
 GELU_CUBE = 0.044715
@@ -347,6 +348,15 @@
 
 def swap(values, axes):
     return lax.all_to_all(values, axes, split_axis=0, concat_axis=0, tiled=True)
+
+
+def hop_gather(values, axes):
+    count, at = lax.axis_size(axes), lax.axis_index(axes)
+    hops = [values]
+    for s in range(1, count):
+        hops.append(lax.ppermute(values, axes, [(i, (i + s) % count) for i in range(count)]))
+    order = (at - jnp.arange(count, dtype=jnp.int32)) % count
+    return jnp.take(jnp.stack(hops), order, axis=0)
 
 
 def high_low(values):
@@ -484,41 +494,79 @@
     )(arrived, arrived, cot_rows, in_raw, back_raw, in_bias, back_bias)
 
 
-def weight_kernel(rows_ref, grad_pre_ref, grad_turned_ref, hidden_ref, grad_in_ref, grad_back_ref):
+def weight_kernel(
+    rows_ref,
+    grad_pre_ref,
+    grad_turned_ref,
+    hidden_ref,
+    in_bias_ref,
+    back_bias_ref,
+    grad_in_ref,
+    grad_back_ref,
+):
+    f32, bf16 = jnp.float32, jnp.bfloat16
     groups, cap, width = rows_ref.shape
-    shape = grad_in_ref.shape
+    data, ff = grad_in_ref.shape[0], grad_in_ref.shape[-1]
+    depth = width // data
+    mine = back_bias_ref.shape[0]
+    at = pl.program_id(1)
     rows = rows_ref[...].reshape(groups * cap, width)
-    grad_in = turned_dot(rows, grad_pre_ref[0, 0], 0, 0)
-    grad_in_ref[...] = grad_in.astype(jnp.bfloat16).reshape(shape)
-    grad_back = jnp.dot(grad_turned_ref[0], hidden_ref[0, 0], preferred_element_type=jnp.float32)
-    grad_back_ref[...] = grad_back.astype(jnp.bfloat16).reshape(shape)
-
-
-def weight_grads(arrived, grad_pre, grad_turned, hidden, data):
+    grad_in = turned_dot(rows, grad_pre_ref[0, 0], 0, 0).astype(bf16)
+    grad_back = jnp.dot(grad_turned_ref[0], hidden_ref[0, 0], preferred_element_type=f32)
+    grad_back = grad_back.astype(bf16)
+    for j in range(mine):
+
+        @pl.when(at == j)
+        def _():
+            for d in range(data):
+                block = slice(j * depth, (j + 1) * depth)
+                grad_in_ref[d, 0, block] = grad_in[d * depth : (d + 1) * depth]
+                grad_back_ref[d, 0, block] = grad_back[d * depth : (d + 1) * depth]
+
+    @pl.when(at == mine - 1)
+    def _():
+        pairs = []
+        for j in range(mine):
+            values = in_bias_ref[j, 0]
+            high = values.astype(bf16).astype(f32)
+            pairs += [high, values - high]
+        for d in range(data):
+            lines = list(pairs)
+            for j in range(mine):
+                values = back_bias_ref[j, :, d * depth : (d + 1) * depth]
+                high = values.astype(bf16).astype(f32)
+                gap = jnp.zeros((1, ff // 2 - depth), f32)
+                lines.append(jnp.concatenate([high, gap, values - high, gap], axis=1))
+            lines.append(jnp.zeros((EXTRA - len(lines), ff), f32))
+            grad_in_ref[d, 0, mine * depth :] = jnp.concatenate(lines, axis=0).astype(bf16)
+
+
+def weight_grads(arrived, grad_pre, grad_turned, hidden, grad_in_bias, grad_back_bias, data):
     mine, inner, total, ff = hidden.shape
     groups, _, width = arrived.shape
     depth = width // data
-    out = (data, inner, mine, depth, ff)
-    kept = pl.BlockSpec((1, 1, total, ff), lambda j, t: (j, t, 0, 0))
-    given = pl.BlockSpec((data, 1, 1, depth, ff), lambda j, t: (0, t, j, 0, 0))
+    kept = pl.BlockSpec((1, 1, total, ff), lambda t, j: (j, t, 0, 0))
+    lines = (mine * depth + EXTRA, mine * depth)
     return pl.pallas_call(
         weight_kernel,
-        grid=(mine, inner),
+        grid=(inner, mine),
         in_specs=[
-            pl.BlockSpec((groups, CAP, width), lambda j, t: (0, j, 0)),
+            pl.BlockSpec((groups, CAP, width), lambda t, j: (0, j, 0)),
             kept,
-            pl.BlockSpec((1, width, total), lambda j, t: (j, 0, 0)),
+            pl.BlockSpec((1, width, total), lambda t, j: (j, 0, 0)),
             kept,
+            pl.BlockSpec((mine, 1, 1, ff), lambda t, j: (0, t, 0, 0)),
+            pl.BlockSpec((mine, 1, width), lambda t, j: (0, 0, 0)),
         ],
-        out_specs=[given, given],
-        out_shape=[jax.ShapeDtypeStruct(out, jnp.bfloat16)] * 2,
+        out_specs=[pl.BlockSpec((data, 1, n, ff), lambda t, j: (0, t, 0, 0)) for n in lines],
+        out_shape=[jax.ShapeDtypeStruct((data, inner, n, ff), jnp.bfloat16) for n in lines],
         compiler_params=pltpu.CompilerParams(vmem_limit_bytes=VMEM_LIMIT),
         cost_estimate=pl.CostEstimate(
             flops=4 * mine * total * width * inner * ff,
             bytes_accessed=4 * mine * inner * (total + width) * ff,
             transcendentals=0,
         ),
-    )(arrived, grad_pre, grad_turned, hidden)
+    )(arrived, grad_pre, grad_turned, hidden, grad_in_bias[:, :, None], grad_back_bias)
 
 
 def moved_plan(
@@ -576,6 +624,7 @@
         axis=1,
     )
     packed = lax.all_gather(packed, DP, axis=0, tiled=True)
+    packed, in_raw = lax.optimization_barrier((packed, in_raw))
     cuts = [3 * local_width, local_width, EXPERTS, experts_here]
     qkv_full, out_turned, router_full, back_bias_turned, vectors = jnp.split(
         packed, [sum(cuts[: i + 1]) for i in range(4)], axis=1
@@ -583,14 +632,9 @@
     gain_first, shift_first, bias_out_full, gain_second, shift_second = (
         vectors[:, i].astype(f32) for i in range(5)
     )
-    out_whole = lax.all_gather(out_turned, tensor_axes, axis=1, tiled=True)
-    in_bias_all = jnp.stack(
-        [
-            lax.ppermute(in_bias, INNER, [(i, (i + s) % inner) for i in range(inner)])
-            for s in range(inner)
-        ]
-    )
-    in_bias_all = jnp.take(in_bias_all, (inner_at - jnp.arange(inner)) % inner, axis=0)
+    out_whole = hop_gather(out_turned, tensor_axes)
+    out_whole = out_whole.transpose(1, 0, 2).reshape(width, width)
+    in_bias_all = hop_gather(in_bias, INNER)
     in_bias_mine = lax.dynamic_slice_in_dim(in_bias_all, owner_at * mine, mine, 1)
     in_bias_mine = in_bias_mine.transpose(1, 0, 2).astype(f32)
 
@@ -632,7 +676,7 @@
     attended, log_total = attention_forward(queries, key_rows, value_rows, scale)
     attended_low = attended.reshape(rows_total, local_width).astype(bf16)
     attended_all = lax.all_gather(attended_low, tensor_axes, axis=1, tiled=True)
-    attended_all, in_raw = lax.optimization_barrier((attended_all, in_raw))
+    attended_all, back_raw = lax.optimization_barrier((attended_all, back_raw))
     mixed = inputs + bias_out_full
     mixed = mixed + jnp.einsum("te,de->td", attended_all, out_whole, preferred_element_type=f32)
     routed, scaled_second, inv_second = norm_parts(mixed, gain_second, shift_second)
@@ -649,7 +693,7 @@
     gate_parts = jnp.stack(high_low(gate_slots.reshape(groups, mine * CAP)), axis=1)
     gate_rows = jnp.pad(gate_parts, ((0, 0), (0, 14), (0, width - mine * CAP)))
     sent = jnp.concatenate([dispatch(routed_low).reshape(groups, mine * CAP, width), gate_rows], axis=1)
-    sent, back_raw = lax.optimization_barrier((sent, back_raw))
+    sent, cot_rows = lax.optimization_barrier((sent, cot_rows))
     arrived = swap(sent, (DP, EXPERT))
     back_bias_mine = lax.dynamic_slice_in_dim(back_bias_turned, owner_at * mine, mine, 1)
     back_bias_mine = jnp.where(lax.axis_index(OUTER) == 0, back_bias_mine.astype(f32), 0.0)
@@ -688,9 +732,13 @@
         [jnp.sum(jnp.where(hit, gate_slots_back[:, None], 0.0), axis=0) for hit in found], axis=1
     )
     grad_routed_cut = jnp.dot(grad_slots, both, preferred_element_type=f32).astype(bf16)
+    grad_in_out, grad_back_out = weight_grads(
+        arrived, grad_pre_low, grad_turned, hidden_low, grad_in_bias_mine, grad_back_bias_mine, data
+    )
+    grad_routed_cut, returned_out, grad_in_out, grad_back_out = lax.optimization_barrier(
+        (grad_routed_cut, returned_out, grad_in_out, grad_back_out)
+    )
     grad_routed = lax.all_gather(grad_routed_cut, tensor_axes, axis=0, tiled=True).T.astype(f32)
-
-    grad_in_out, grad_back_out = weight_grads(arrived, grad_pre_low, grad_turned, hidden_low, data)
     returned = in_line(bring(returned_out)).astype(bf16)
     picked = [jnp.dot(returned, find, preferred_element_type=f32) for find in finds]
     mixed_cut = lax.dynamic_slice_in_dim(mixed, tensor_at * slice_width, slice_width, 1)
@@ -732,43 +780,43 @@
     grad_images = (grad_mixed + grad_from_first).reshape(images.shape)
 
     def spread(parts):
-        parts = parts.reshape(experts_here, shard_width, ff_here)
-        return swap(parts, (DP, INNER)).astype(f32)
-
-    grad_w_back = spread(grad_back_out).transpose(0, 2, 1)
-    grad_w_in = spread(grad_in_out)
-    bias_grads = jnp.concatenate(
-        [grad_in_bias_mine.reshape(mine, inner * ff_here), grad_back_bias_mine[:, 0]], axis=1
-    )
-    bias_grads = lax.all_gather(bias_grads, (DP, INNER), axis=0, tiled=True)
-    grad_in_bias = lax.dynamic_slice_in_dim(bias_grads, inner_at * ff_here, ff_here, 1)
-    grad_back_shard = lax.dynamic_slice_in_dim(
-        bias_grads, inner * ff_here + dp_at * shard_width, shard_width, 1
-    )
+        return swap(parts.reshape(owners, *parts.shape[2:]), (DP, INNER)).astype(f32)
+
+    experts_shape = (experts_here, shard_width, ff_here)
+    grad_in_parts = spread(grad_in_out)
+    grad_w_in = grad_in_parts[:, : mine * shard_width].reshape(experts_shape)
+    lines = grad_in_parts[:, mine * shard_width :]
+    grad_in_bias = lines[:, : 2 * mine].reshape(owners, mine, 2, ff_here)
+    grad_in_bias = jnp.sum(grad_in_bias, axis=2).reshape(experts_here, ff_here)
+    lines = lines[:, 2 * mine : 3 * mine].reshape(experts_here, 2, ff_here // 2)
+    grad_back_shard = jnp.sum(lines[:, :, :shard_width], axis=1)
     early = jnp.concatenate(
-        [
-            grad_qkv,
-            grad_out_turned,
-            grad_router,
-            jnp.stack([grad_bias_out, grad_gain_second, grad_shift_second], axis=1),
-        ],
-        axis=1,
-    )
-    early = lax.psum(lax.psum_scatter(early, DP, scatter_dimension=0, tiled=True), EXPERT)
+        [grad_qkv.astype(bf16), grad_out_turned.astype(bf16), grad_router.astype(bf16)], axis=1
+    )
+    early, grad_back_out = lax.optimization_barrier((early, grad_back_out))
+    early = swap(early.reshape(groups, shard_width // sources, -1), (DP, EXPERT))
+    early, grad_back_out = lax.optimization_barrier((early, grad_back_out))
+    grad_w_back = spread(grad_back_out).reshape(experts_shape).transpose(0, 2, 1)
+    early = jnp.sum(early.astype(f32), axis=0)
+    early = hop_gather(early, EXPERT).reshape(shard_width, -1)
     grad_w_qkv = early[:, : 3 * local_width].reshape(shard_width, 3, local_width).transpose(1, 0, 2)
     grad_w_out = early[:, 3 * local_width : 4 * local_width].T
-    grad_w_router = early[:, 4 * local_width : 4 * local_width + EXPERTS]
-    grad_out_bias, grad_second_gain, grad_second_shift = (
-        early[:, 4 * local_width + EXPERTS + i] for i in range(3)
-    )
-    grad_qv_bias = lax.psum(grad_pair_bias, (DP, EXPERT))
-    grad_first_norm = lax.psum(first_terms, everywhere)
-    grad_first_norm = lax.dynamic_slice_in_dim(grad_first_norm, dp_at * shard_width, shard_width, 1)
+    grad_w_router = early[:, 4 * local_width :]
+    once = (tensor_at == 0).astype(f32)
+    pair_bias = lax.dynamic_update_slice(
+        jnp.zeros((2, width), f32), grad_pair_bias, (0, tensor_at * local_width)
+    )
+    vectors = [grad_bias_out, grad_gain_second, grad_shift_second]
+    vectors = jnp.concatenate([first_terms, pair_bias, once * jnp.stack(vectors)], axis=0)
+    vectors = lax.psum(vectors, everywhere)
+    grad_qv_bias = lax.dynamic_slice_in_dim(vectors[2:4], tensor_at * local_width, local_width, 1)
+    vectors = lax.dynamic_slice_in_dim(vectors, dp_at * shard_width, shard_width, 1)
+    grad_first_gain, grad_first_shift, _, _, grad_out_bias, grad_second_gain, grad_second_shift = vectors
     return (
         output,
         grad_images,
-        grad_first_norm[0],
-        grad_first_norm[1],
+        grad_first_gain,
+        grad_first_shift,
         grad_w_qkv,
         grad_qv_bias,
         grad_w_out,

time: 680 us -> 732 us (1.076)
  waiting for transfers between devices: 247 us -> 290 us
  starting transfers between devices: 33.9 us -> 50 us
  local copies, waits for them, and re-layouts: 93.1 us -> 79.5 us
    psum x1, waiting for transfers between devices: 0.01 us -> 84.3 us  [moved_plan(): lax.psum(grad_normed_part.astype(bf16), tensor_axes).astype(f32)]
    all_to_all x1 -> x3, blocking collectives: 41.6 us -> 122 us  [swap(): return lax.all_to_all(values, axes, split_axis=0, concat_axis=0, tiled=True)]
    all_gather x1 -> x0, blocking collectives: 63.6 us -> none  [moved_plan(): bias_grads = lax.all_gather(bias_grads, (DP, INNER), axis=0, tiled=True)]
    all_gather x1, waiting for transfers between devices: 0.02 us -> 41.6 us  [moved_plan(): packed = lax.all_gather(packed, DP, axis=0, tiled=True)]
    all_gather x1 -> x0, waiting for transfers between devices: 36 us -> none  [moved_plan(): out_whole = lax.all_gather(out_turned, tensor_axes, axis=1, tiled=True)]
    ppermute x2 -> x5, waiting for transfers between devices: 2.78 us -> 37.6 us  [hop_gather(): lax.ppermute(values, axes, [(i, (i + s) % count) for i in range(count)])]
    all_gather x1, waiting for transfers between devices: 30.8 us -> 0.02 us  [moved_plan(): attended_all = lax.all_gather(attended_low, tensor_axes, axis=1, tiled=True)]
    all_to_all x7 -> x6, waiting for transfers between devices: 127 us -> 99.5 us  [swap(): return lax.all_to_all(values, axes, split_axis=0, concat_axis=0, tiled=True)]
  transfers between devices with their start and end apart: 17 -> 16, of which waited for: 10 -> 10; matrix products, arithmetic and copies ran while one was open for 26% -> 18% of each run, Pallas kernels for 2% -> 2%
where the time goes in v3:
time: 732 us; the launch traced here: 721 us
  waiting for transfers between devices  290 us (40%)
  blocking collectives  162 us (22%)
  local copies, waits for them, and re-layouts  79.5 us (11%)
  starting transfers between devices  50 us (7%)
  other arithmetic  48.1 us (7%)
  matrix products  42.9 us (6%)
  Pallas kernels  31.9 us (4%)
  between operations  16.3 us (2%)
    all_to_all x3, blocking collectives, swap(): return lax.all_to_all(values, axes, split_axis=0, concat_axis=0, tiled=True)  122 us
    all_to_all x6, waiting for transfers between devices, swap(): return lax.all_to_all(values, axes, split_axis=0, concat_axis=0, tiled=True)  99.5 us
    psum x1, waiting for transfers between devices, moved_plan(): lax.psum(grad_normed_part.astype(bf16), tensor_axes).astype(f32)  84.3 us
    all_gather x1, waiting for transfers between devices, moved_plan(): packed = lax.all_gather(packed, DP, axis=0, tiled=True)  41.6 us
    psum x1, blocking collectives, moved_plan(): vectors = lax.psum(vectors, everywhere)  40.3 us
    ppermute x5, waiting for transfers between devices, hop_gather(): lax.ppermute(values, axes, [(i, (i + s) % count) for i in range(count)])  37.6 us
    all_to_all x6, starting transfers between devices, swap(): return lax.all_to_all(values, axes, split_axis=0, concat_axis=0, tiled=True)  34.1 us
    all_gather x1, waiting for transfers between devices, moved_plan(): lax.all_gather(grad_routed_cut, tensor_axes, axis=0, tiled=True)  26.7 us
  transfers between devices with their start and end apart: 16, of which 10 were waited for; matrix products, arithmetic and copies ran while one was open for 18% of the time, Pallas kernels for 2%

profile of v3, /device:TPU:0, one launch (start us, length us, event | category | flops | bytes accessed | tf_op | source)
XLA Modules:
  0.0 721.0 jit_solution(13114130229460606492)
XLA Ops:
  7.2 59.3 %all_to_all.45 = bf16[16,192,768]{2,1,0:T(8,128)(2,1)} all-to-all(bf16[16,192,768]{2,1,0:T(8,128)(2,1)} %param.31), channel_id=1, replica_groups=mesh['dp'=4,'expert'=2,'outer'=2,'inner'=2] {'dp','inner'}, dimensions={0} | all-to-all | bytes 9437184 | tf_op jit(solution)/shard_map/all_to_all | solution.py:350
  66.6 4.8 all-to-all-start.1
  86.5 41.6 %all-gather.5.cloned.1.call-done = bf16[768,821]{1,0:T(8,128)(2,1)} async-done(((bf16[192,821]{1,0:T(8,128)(2,1)}), bf16[768,821]{1,0:T(8,128)(2,1)}) %all-gather.5.cloned.1.call-update) | async-done | bytes 1261072 | tf_op jit(solution)/shard_map/all_gather | solution.py:626
  145.8 5.0 reshape.574
  157.8 5.3 fusion.20
  163.1 11.6 %collective-permute-done = bf16[768,192]{1,0:T(8,128)(2,1)S(1)} collective-permute-done((bf16[768,192]{1,0:T(8,128)(2,1)S(1)}, bf16[768,192]{1,0:T(8,128)(2,1)S(1)}, u32[]{:S(2)}, u32[]{:S(2)}) %collective-permute-start) | collective-permute-done | bytes 294944 | tf_op jit(solution)/shard_map/ppermute | solution.py:357
  174.7 24.3 %collective-permute-done.1 = bf16[768,192]{1,0:T(8,128)(2,1)S(1)} collective-permute-done((bf16[768,192]{1,0:T(8,128)(2,1)S(1)}, bf16[768,192]{1,0:T(8,128)(2,1)S(1)}, u32[]{:S(2)}, u32[]{:S(2)}) %collective-permute-start.1) | collective-permute-done | bytes 294944 | tf_op jit(solution)/shard_map/ppermute | solution.py:357
  225.3 8.2 %all-to-all-done.2.cot_ref = bf16[8,128,768]{2,1,0:T(8,128)(2,1)} async-done(((bf16[8,128,768]{2,1,0:T(8,128)(2,1)}), bf16[8,128,768]{2,1,0:T(8,128)(2,1)}, u32[]{:S(2)}, u32[]{:S(2)}) %all-to-all-start.2) | async-done | bytes 1572896 | tf_op jit(solution)/shard_map/all_to_all | solution.py:350
  233.4 4.7 all-to-all-start.3
  238.2 9.1 %collective-permute-start.3 = (bf16[16,768]{1,0:T(8,128)(2,1)S(1)}, bf16[16,768]{1,0:T(8,128)(2,1)S(1)}, u32[]{:S(2)}, u32[]{:S(2)}) collective-permute-start(bf16[16,768]{1,0:T(8,128)(2,1)S(1)} %copy-done.32), channel_id=1, source_target_pairs={{0,1},{1,0},{2,3},{3,2},{4,5},{5,4},{6,7},{7,6},{8,9},{9,8},{10,11... | collective-permute-start | bytes 73736 | tf_op jit(solution)/shard_map/ppermute | solution.py:357
  252.3 8.1 %all-to-all-done.3.rows_ref.gate_ref = bf16[8,144,768]{2,1,0:T(8,128)(2,1)} async-done(((bf16[8,144,768]{2,1,0:T(8,128)(2,1)}), bf16[8,144,768]{2,1,0:T(8,128)(2,1)}, u32[]{:S(2)}, u32[]{:S(2)}) %all-to-all-start.3) | async-done | bytes 1769504 | tf_op jit(solution)/shard_map/all_to_all | solution.py:350
  260.4 18.9 %shard_map.289 = (bf16[8,4,192,128]{3,2,1,0:T(8,128)(2,1)}, bf16[8,4,208,128]{3,2,1,0:T(8,128)(2,1)}, bf16[2,2,512,768]{3,2,1,0:T(8,128)(2,1)}, bf16[2,2,512,768...) custom-call(bf16[8,144,768]{2,1,0:T(8,128)(2,1)} %all-to-all-done.3.rows_ref.gate_, ...), custom_call_target="tpu_custom_call" | custom-call | flops 9663676416 | bytes 28311552 | tf_op jit(solution)/shard_map/pallas_call | solution.py:471
  279.3 10.9 %all-to-all-start.4 = ((bf16[32,208,128]{2,1,0:T(8,128)(2,1)}), bf16[32,208,128]{2,1,0:T(8,128)(2,1)}, u32[]{:S(2)}, u32[]{:S(2)}) async-start(bf16[32,208,128]{2,1,0:T(8,128)(2,1)} %bitcast.138), calls=%async_computation.4 | async-start | bytes 3407872 | tf_op jit(solution)/shard_map/all_to_all | solution.py:350
  291.0 13.0 %shard_map.290 = (bf16[4,2,400,768]{3,2,1,0:T(8,128)(2,1)}, bf16[4,2,384,768]{3,2,1,0:T(8,128)(2,1)}) custom-call(bf16[8,144,768]{2,1,0:T(8,128)(2,1)} %all-to-all-done.3.rows_ref.gate_ref, bf16[2,2,512,768]{3,2,1,0:T(8,128)(2,1)} %get-tuple-element.46.grad_pre_ref, bf16[2,768,512]{2,1,0:T(8,128)(2,1)} %get-tuple-element.47.grad_turned_ref, ...), custom_call_target="tpu_custom_call" | custom-call | flops 4831838208 | bytes 15728640 | tf_op jit(solution)/shard_map/pallas_call | solution.py:550
  303.9 26.9 %all-to-all-done.4 = bf16[32,208,128]{2,1,0:T(8,128)(2,1)} async-done(((bf16[32,208,128]{2,1,0:T(8,128)(2,1)}), bf16[32,208,128]{2,1,0:T(8,128)(2,1)}, u32[]{:S(2)}, u32[]{:S(2)}) %all-to-all-start.4) | async-done | bytes 1703968 | tf_op jit(solution)/shard_map/all_to_all | solution.py:350
  342.5 26.7 %all-gather.11.cloned.1.call-done = bf16[768,788]{1,0:T(8,128)(2,1)} async-done(((bf16[192,788]{1,0:T(8,128)(2,1)}), bf16[768,788]{1,0:T(8,128)(2,1)}) %all-gather.11.cloned.1.call-update) | async-done | bytes 1210384 | tf_op jit(solution)/shard_map/all_gather | solution.py:741
  391.9 22.3 %all_to_all.46 = bf16[8,96,800]{2,1,0:T(8,128)(2,1)} all-to-all(bf16[8,96,800]{2,1,0:T(8,128)(2,1)S(1)} %bitcast.129), channel_id=1, replica_groups=mesh['dp'=4,'expert'=2,'outer'=2,'inner'=2] {'dp','expert'}, dimensions={0} | all-to-all | bytes 2457600 | tf_op jit(solution)/shard_map/all_to_all | solution.py:350
  414.2 40.6 %all_to_all.47 = bf16[32,192,128]{2,1,0:T(8,128)(2,1)} all-to-all(bf16[32,192,128]{2,1,0:T(8,128)(2,1)S(1)} %bitcast.140), channel_id=1, replica_groups=mesh['dp'=4,'expert'=2,'outer'=2,'inner'=2] {'dp','expert','outer','inner'}, dimensions={0} | all-to-all | bytes 3145728 | tf_op jit(solution)/shard_map/all_to_all | solution.py:350
  459.5 56.4 %all-to-all-done.7 = bf16[8,400,768]{2,1,0:T(8,128)(2,1)} async-done(((bf16[8,400,768]{2,1,0:T(8,128)(2,1)}), bf16[8,400,768]{2,1,0:T(8,128)(2,1)}, u32[]{:S(2)}, u32[]{:S(2)}) %all-to-all-start.7) | async-done | bytes 4915232 | tf_op jit(solution)/shard_map/all_to_all | solution.py:350
  515.9 4.7 all-to-all-start.8
  534.6 84.3 %all-reduce.3.cloned.1.call-done = bf16[788,768]{0,1:T(8,128)(2,1)} async-done(((bf16[788,768]{0,1:T(8,128)(2,1)}), bf16[788,768]{0,1:T(8,128)(2,1)}) %all-reduce.3.cloned.1.call-update) | async-done | bytes 1210384 | tf_op jit(solution)/shard_map/psum | solution.py:775
  636.3 40.3 %psum.15 = f32[7,768]{1,0:T(8,128)S(1)} all-reduce(f32[7,768]{1,0:T(8,128)S(1)} %pad_maximum_fusion.5), channel_id=1, replica_groups=mesh['dp'=4,'expert'=2,'outer'=2,'inner'=2] {'dp','expert','outer','inner'}, use_global_device_ids=true, to_apply=%region_30.31 | all-reduce | flops 5376 | bytes 43008 | tf_op jit(solution)/shard_map/psum | solution.py:811
  699.4 6.9 slice.141
  707.0 7.1 convert_bitcast_fusion
  (317 shorter events, 163.8 us)
Async XLA Ops:
  66.6 142.4 %all-to-all-start.1 = ((bf16[16,192,768]{2,1,0:T(8,128)(2,1)}), bf16[16,192,768]{2,1,0:T(8,128)(2,1)}, u32[]{:S(2)}, u32[]{:S(2)}) async-start(bf16[16,192,768]{2,1,0:T(8,128)(2,1)} %bitcast.131), calls=%async_computation.1 | async-start | bytes 9437184 | tf_op jit(solution)/shard_map/all_to_all | solution.py:350
  71.4 56.7 %all-gather.5.cloned.1.call-start = ((), (), s32[]{:S(2)}) async-start(), calls=%async_computation.9 | async-start | bytes 1720320 | tf_op jit(solution)/shard_map/all_gather | solution.py:626
  73.6 139.6 %all-gather.7.cloned.1.call-start = ((), (), s32[]{:S(2)}) async-start(), calls=%async_computation.10 | async-start | bytes 1720320 | tf_op jit(solution)/shard_map/all_gather | solution.py:678
  141.4 232.2 %copy-start.34 = (f32[788]{0:T(1024)}, f32[788]{0:T(1024)S(1)}, u32[]{:S(2)}) copy-start(f32[788]{0:T(1024)S(1)} %mul.214) | copy-start | bytes 9460
  151.0 187.2 %copy-start.40 = (s32[788]{0:T(1024)}, s32[788]{0:T(1024)S(1)}, u32[]{:S(2)}) copy-start(s32[788]{0:T(1024)S(1)} %get-tuple-element.169) | copy-start | bytes 9460
  151.0 187.2 %copy-start.42 = (s32[788]{0:T(1024)}, s32[788]{0:T(1024)S(1)}, u32[]{:S(2)}) copy-start(s32[788]{0:T(1024)S(1)} %get-tuple-element.170) | copy-start | bytes 9460
  152.2 22.4 %collective-permute-start = (bf16[768,192]{1,0:T(8,128)(2,1)S(1)}, bf16[768,192]{1,0:T(8,128)(2,1)S(1)}, u32[]{:S(2)}, u32[]{:S(2)}) collective-permute-start(bf16[768,192]{1,0:T(8,128)(2,1)S(1)} %get-tuple-element.178), channel_id=1, source_target_pairs={{0,1},{1,2},{2,3},{3,0},{4,5},{5,6},{6,7},{7,4},{8,9},{9,10},{10,1... | collective-permute-start | bytes 884744 | tf_op jit(solution)/shard_map/ppermute | solution.py:357
  152.5 46.4 %collective-permute-start.1 = (bf16[768,192]{1,0:T(8,128)(2,1)S(1)}, bf16[768,192]{1,0:T(8,128)(2,1)S(1)}, u32[]{:S(2)}, u32[]{:S(2)}) collective-permute-start(bf16[768,192]{1,0:T(8,128)(2,1)S(1)} %get-tuple-element.178), channel_id=1, source_target_pairs={{0,2},{1,3},{2,0},{3,1},{4,6},{5,7},{6,4},{7,5},{8,10},{9,11},{10,... | collective-permute-start | bytes 884744 | tf_op jit(solution)/shard_map/ppermute | solution.py:357
  155.0 44.0 %collective-permute-start.2 = (bf16[768,192]{1,0:T(8,128)(2,1)S(1)}, bf16[768,192]{1,0:T(8,128)(2,1)S(1)}, u32[]{:S(2)}, u32[]{:S(2)}) collective-permute-start(bf16[768,192]{1,0:T(8,128)(2,1)S(1)} %get-tuple-element.178), channel_id=1, source_target_pairs={{0,3},{1,0},{2,1},{3,2},{4,7},{5,4},{6,5},{7,6},{8,11},{9,8},{10,9... | collective-permute-start | bytes 884744 | tf_op jit(solution)/shard_map/ppermute | solution.py:357
  208.9 24.5 %all-to-all-start.2 = ((bf16[8,128,768]{2,1,0:T(8,128)(2,1)}), bf16[8,128,768]{2,1,0:T(8,128)(2,1)}, u32[]{:S(2)}, u32[]{:S(2)}) async-start(bf16[8,128,768]{2,1,0:T(8,128)(2,1)} %bitcast.141), calls=%async_computation.2 | async-start | bytes 3145728 | tf_op jit(solution)/shard_map/all_to_all | solution.py:350
  233.4 27.0 %all-to-all-start.3 = ((bf16[8,144,768]{2,1,0:T(8,128)(2,1)}), bf16[8,144,768]{2,1,0:T(8,128)(2,1)}, u32[]{:S(2)}, u32[]{:S(2)}) async-start(bf16[8,144,768]{2,1,0:T(8,128)(2,1)} %pad_maximum_fusion), calls=%async_computation.3 | async-start | bytes 3538944 | tf_op jit(solution)/shard_map/all_to_all | solution.py:350
  238.2 10.9 %collective-permute-start.3 = (bf16[16,768]{1,0:T(8,128)(2,1)S(1)}, bf16[16,768]{1,0:T(8,128)(2,1)S(1)}, u32[]{:S(2)}, u32[]{:S(2)}) collective-permute-start(bf16[16,768]{1,0:T(8,128)(2,1)S(1)} %copy-done.32), channel_id=1, source_target_pairs={{0,1},{1,0},{2,3},{3,2},{4,5},{5,4},{6,7},{7,6},{8,9},{9,8},{10,11... | collective-permute-start | bytes 73736 | tf_op jit(solution)/shard_map/ppermute | solution.py:357
  279.3 51.5 %all-to-all-start.4 = ((bf16[32,208,128]{2,1,0:T(8,128)(2,1)}), bf16[32,208,128]{2,1,0:T(8,128)(2,1)}, u32[]{:S(2)}, u32[]{:S(2)}) async-start(bf16[32,208,128]{2,1,0:T(8,128)(2,1)} %bitcast.138), calls=%async_computation.4 | async-start | bytes 3407872 | tf_op jit(solution)/shard_map/all_to_all | solution.py:350
  290.3 78.9 %all-gather.11.cloned.1.call-start = ((), (), s32[]{:S(2)}) async-start(), calls=%async_computation.12 | async-start | bytes 1720320 | tf_op jit(solution)/shard_map/all_gather | solution.py:741
  454.8 61.0 %all-to-all-start.7 = ((bf16[8,400,768]{2,1,0:T(8,128)(2,1)}), bf16[8,400,768]{2,1,0:T(8,128)(2,1)}, u32[]{:S(2)}, u32[]{:S(2)}) async-start(bf16[8,400,768]{2,1,0:T(8,128)(2,1)} %bitcast.130), calls=%async_computation.7 | async-start | bytes 9830400 | tf_op jit(solution)/shard_map/all_to_all | solution.py:350
  515.9 191.1 %all-to-all-start.8 = ((bf16[8,384,768]{2,1,0:T(8,128)(2,1)}), bf16[8,384,768]{2,1,0:T(8,128)(2,1)}, u32[]{:S(2)}, u32[]{:S(2)}) async-start(bf16[8,384,768]{2,1,0:T(8,128)(2,1)} %bitcast.132), calls=%async_computation.8 | async-start | bytes 9437184 | tf_op jit(solution)/shard_map/all_to_all | solution.py:350
  520.6 98.3 %all-reduce.3.cloned.1.call-start = ((), (), s32[]{:S(2)}) async-start(), calls=%async_computation.13 | async-start | bytes 2752512 | tf_op jit(solution)/shard_map/psum | solution.py:775
  528.2 90.7 %copy-start.1 = (f32[788,768]{0,1:T(8,128)S(1)}, f32[788,768]{0,1:T(8,128)}, u32[]{:S(2)}) copy-start(f32[788,768]{0,1:T(8,128)} %copy-done) | copy-start | bytes 7262212
  528.2 90.7 %copy-start.23 = (f32[768]{0:T(1024)S(1)}, f32[768]{0:T(1024)}, u32[]{:S(2)}) copy-start(f32[768]{0:T(1024)} %copy-done.22) | copy-start | bytes 9220
  528.2 90.7 %copy-start.25 = (f32[788]{0:T(1024)S(1)}, f32[788]{0:T(1024)}, u32[]{:S(2)}) copy-start(f32[788]{0:T(1024)} %copy-done.24) | copy-start | bytes 9460
  528.2 90.7 %copy-start.27 = (f32[788]{0:T(1024)S(1)}, f32[788]{0:T(1024)}, u32[]{:S(2)}) copy-start(f32[788]{0:T(1024)} %copy-done.26) | copy-start | bytes 9460
  528.3 161.6 %all-gather.9.cloned.1.call-start = ((), (), s32[]{:S(2)}) async-start(), calls=%async_computation.11 | async-start | bytes 1720320 | tf_op jit(solution)/shard_map/all_gather | solution.py:747
  530.6 92.1 %copy-start.30 = (f32[2,768]{1,0:T(2,128)}, f32[2,768]{1,0:T(2,128)S(1)}, u32[]{:S(2)}) copy-start(f32[2,768]{1,0:T(2,128)S(1)} %dynamic_update_slice.3) | copy-start | bytes 18436
  533.6 151.3 %collective-permute-start.4 = (f32[96,800]{1,0:T(8,128)}, f32[96,800]{1,0:T(8,128)}, u32[]{:S(2)}, u32[]{:S(2)}) collective-permute-start(f32[96,800]{1,0:T(8,128)} %convert_reduce_fusion.1), channel_id=1, source_target_pairs={{0,4},{4,0},{1,5},{5,1},{2,6},{6,2},{3,7},{7,3},{8,12},{12,8},{9,1... | collective-permute-start | bytes 921608 | tf_op jit(solution)/shard_map/ppermute | solution.py:357
  (54 other events, 354.3 us)
Sparse Core Ops, SparseCore 0:
  74.3 53.7 all-gather.4
  141.1 58.4 all-gather.6
  337.4 31.6 all-gather.10
  528.4 90.4 all-reduce.2
  631.7 32.9 all-gather.8

commit v4 on v3

--- a/solution.py
+++ b/solution.py
@@ -13,7 +13,7 @@
 EXPERTS = 32
 TOPK = 2
 CAP = 64
-FF_PAIR = 2
+FF_PAIR = 1
 EXTRA = 16
 VMEM_LIMIT = 56 * 1024 * 1024
 GELU_SCALE = (2.0 / math.pi) ** 0.5
@@ -359,6 +359,11 @@
     return jnp.take(jnp.stack(hops), order, axis=0)
 
 
+def cross(values, s):
+    count = lax.axis_size((DP, INNER))
+    return lax.ppermute(values, (DP, INNER), [(i, i ^ s) for i in range(count)]) if s else values
+
+
 def high_low(values):
     high = lax.reduce_precision(values, 8, 7)
     return high.astype(jnp.bfloat16), (values - high).astype(jnp.bfloat16)
@@ -370,27 +375,18 @@
     )
 
 
-def expert_kernel(
-    inner,
-    rows_ref,
-    gate_ref,
-    cot_ref,
-    in_ref,
-    back_ref,
-    in_bias_ref,
-    back_bias_ref,
-    returned_ref,
-    grads_ref,
-    hidden_ref,
-    grad_pre_ref,
-    grad_turned_ref,
-    grad_in_bias_ref,
-    grad_back_bias_ref,
-):
+def expert_kernel(inner, owners, at_ref, rows_ref, gate_ref, cot_ref, in_bias_ref, back_bias_ref, *refs):
+    piece_refs, refs = refs[:owners], refs[owners:]
+    returned_ref, grads_ref, hidden_ref, grad_pre_ref, grad_turned_ref = refs[:5]
+    grad_in_bias_ref, grad_back_bias_ref, weight_ref = refs[5:]
     f32, bf16 = jnp.float32, jnp.bfloat16
     groups, cap, width = rows_ref.shape
-    chunks = in_ref.shape[0]
-    data = chunks // inner
+    depth = piece_refs[0].shape[2]
+    for s, piece_ref in enumerate(piece_refs):
+        source = at_ref[0] ^ s
+        place = pl.ds(pl.multiple_of((source // inner) * depth, depth), depth)
+        for k in range(2):
+            weight_ref[k, source % inner, place] = piece_ref[k, 0]
     tensor, slice_width = returned_ref.shape[1:3]
     mine = back_bias_ref.shape[1]
     total = groups * cap
@@ -414,8 +410,7 @@
     part = jnp.broadcast_to(bias, (width, total))
     back = jnp.zeros((width, total), f32)
     for t in range(inner):
-        w_in = jnp.concatenate([in_ref[d * inner + t, 0] for d in range(data)], axis=0)
-        w_back = jnp.concatenate([back_ref[d * inner + t, 0] for d in range(data)], axis=0)
+        w_in, w_back = weight_ref[0, t], weight_ref[1, t]
         pre = jnp.dot(rows, w_in, preferred_element_type=f32) + in_bias_ref[0, t : t + 1, :]
         square = pre * pre
         bent = jnp.tanh(GELU_SCALE * pre * (1.0 + GELU_CUBE * square))
@@ -452,16 +447,17 @@
                     grads_ref[g, z, slice_width:, lanes] = tail[:, mine_lanes]
 
 
-def run_experts(arrived, cot_rows, in_raw, back_raw, in_bias, back_bias, mine, inner, tensor):
+def run_experts(owner_at, arrived, cot_rows, pieces, in_bias, back_bias, inner, tensor):
     f32, bf16 = jnp.float32, jnp.bfloat16
     groups, _, width = cot_rows.shape
-    chunks, _, depth, ff = in_raw.shape
+    owners = len(pieces)
+    _, mine, depth, ff = pieces[0].shape
     total = groups * CAP
     slice_width = width // tensor
-    gate_at = mine * CAP // 16
+    gate_at = mine * CAP // EXTRA
     outs = [
         ((groups, tensor, slice_width, mine * CAP), bf16, lambda j: (0, 0, 0, 0), None),
-        ((groups, tensor, slice_width + 16, mine * CAP), bf16, lambda j: (0, 0, 0, 0), None),
+        ((groups, tensor, slice_width + EXTRA, mine * CAP), bf16, lambda j: (0, 0, 0, 0), None),
         ((mine, inner, total, ff), bf16, lambda j: (j, 0, 0, 0), 1),
         ((mine, inner, total, ff), bf16, lambda j: (j, 0, 0, 0), 1),
         ((mine, width, total), bf16, lambda j: (j, 0, 0), 1),
@@ -469,59 +465,55 @@
         ((mine, 1, width), f32, lambda j: (j, 0, 0), 1),
     ]
     return pl.pallas_call(
-        functools.partial(expert_kernel, inner),
+        functools.partial(expert_kernel, inner, owners),
         grid=(mine,),
         in_specs=[
+            pl.BlockSpec(memory_space=pltpu.SMEM),
             pl.BlockSpec((groups, CAP, width), lambda j: (0, j, 0)),
-            pl.BlockSpec((groups, 16, mine * CAP), lambda j: (0, gate_at, 0)),
+            pl.BlockSpec((groups, EXTRA, mine * CAP), lambda j: (0, gate_at, 0)),
             pl.BlockSpec((groups, CAP, width), lambda j: (0, j, 0)),
-            pl.BlockSpec((chunks, 1, depth, ff), lambda j: (0, j, 0, 0)),
-            pl.BlockSpec((chunks, 1, depth, ff), lambda j: (0, j, 0, 0)),
             pl.BlockSpec((1, inner, ff), lambda j: (j, 0, 0)),
             pl.BlockSpec((width, mine), lambda j: (0, 0)),
-        ],
+        ]
+        + [pl.BlockSpec((2, 1, depth, ff), lambda j: (0, j, 0, 0))] * owners,
         out_specs=[
             pl.BlockSpec(shape if lead is None else (lead, *shape[1:]), index)
             for shape, _, index, lead in outs
         ],
         out_shape=[jax.ShapeDtypeStruct(shape, dtype) for shape, dtype, _, _ in outs],
+        scratch_shapes=[pltpu.VMEM((2, inner, width, ff), bf16)],
         compiler_params=pltpu.CompilerParams(vmem_limit_bytes=VMEM_LIMIT),
         cost_estimate=pl.CostEstimate(
             flops=8 * mine * total * width * inner * ff,
-            bytes_accessed=4 * chunks * mine * depth * ff + 12 * mine * total * inner * ff,
+            bytes_accessed=4 * owners * mine * depth * ff + 12 * mine * total * inner * ff,
             transcendentals=mine * total * inner * ff,
         ),
-    )(arrived, arrived, cot_rows, in_raw, back_raw, in_bias, back_bias)
+    )(owner_at.reshape(1), arrived, arrived, cot_rows, in_bias, back_bias, *pieces)
 
 
 def weight_kernel(
+    inner,
+    at_ref,
     rows_ref,
     grad_pre_ref,
     grad_turned_ref,
     hidden_ref,
     in_bias_ref,
     back_bias_ref,
-    grad_in_ref,
-    grad_back_ref,
+    *refs,
 ):
     f32, bf16 = jnp.float32, jnp.bfloat16
+    out_refs, sums_ref, tail_ref = refs[:-2], refs[-2], refs[-1]
     groups, cap, width = rows_ref.shape
-    data, ff = grad_in_ref.shape[0], grad_in_ref.shape[-1]
-    depth = width // data
     mine = back_bias_ref.shape[0]
-    at = pl.program_id(1)
+    ff = sums_ref.shape[-1]
+    depth = width * inner // len(out_refs)
+    data = width // depth
+    part, at = pl.program_id(0), pl.program_id(1)
     rows = rows_ref[...].reshape(groups * cap, width)
-    grad_in = turned_dot(rows, grad_pre_ref[0, 0], 0, 0).astype(bf16)
+    sums_ref[0] = turned_dot(rows, grad_pre_ref[0, 0], 0, 0).astype(bf16)
     grad_back = jnp.dot(grad_turned_ref[0], hidden_ref[0, 0], preferred_element_type=f32)
-    grad_back = grad_back.astype(bf16)
-    for j in range(mine):
-
-        @pl.when(at == j)
-        def _():
-            for d in range(data):
-                block = slice(j * depth, (j + 1) * depth)
-                grad_in_ref[d, 0, block] = grad_in[d * depth : (d + 1) * depth]
-                grad_back_ref[d, 0, block] = grad_back[d * depth : (d + 1) * depth]
+    sums_ref[1] = grad_back.astype(bf16)
 
     @pl.when(at == mine - 1)
     def _():
@@ -538,19 +530,37 @@
                 gap = jnp.zeros((1, ff // 2 - depth), f32)
                 lines.append(jnp.concatenate([high, gap, values - high, gap], axis=1))
             lines.append(jnp.zeros((EXTRA - len(lines), ff), f32))
-            grad_in_ref[d, 0, mine * depth :] = jnp.concatenate(lines, axis=0).astype(bf16)
-
-
-def weight_grads(arrived, grad_pre, grad_turned, hidden, grad_in_bias, grad_back_bias, data):
+            tail_ref[d] = jnp.concatenate(lines, axis=0).astype(bf16)
+
+    for s, out_ref in enumerate(out_refs):
+        owner = at_ref[0] ^ s
+        d = owner // inner
+        place = pl.ds(pl.multiple_of(d * depth, depth), depth)
+
+        @pl.when(owner % inner == part)
+        def _():
+            for k in range(2):
+                line = pl.multiple_of((k * mine + at) * depth, depth)
+                out_ref[pl.ds(line, depth)] = sums_ref[k, place]
+
+            @pl.when(at == mine - 1)
+            def _():
+                out_ref[2 * mine * depth :] = tail_ref[d]
+
+
+def weight_grads(
+    owner_at, arrived, grad_pre, grad_turned, hidden, grad_in_bias, grad_back_bias, owners
+):
     mine, inner, total, ff = hidden.shape
     groups, _, width = arrived.shape
-    depth = width // data
+    depth = width * inner // owners
     kept = pl.BlockSpec((1, 1, total, ff), lambda t, j: (j, t, 0, 0))
-    lines = (mine * depth + EXTRA, mine * depth)
+    out = (2 * mine * depth + EXTRA, ff)
     return pl.pallas_call(
-        weight_kernel,
+        functools.partial(weight_kernel, inner),
         grid=(inner, mine),
         in_specs=[
+            pl.BlockSpec(memory_space=pltpu.SMEM),
             pl.BlockSpec((groups, CAP, width), lambda t, j: (0, j, 0)),
             kept,
             pl.BlockSpec((1, width, total), lambda t, j: (j, 0, 0)),
@@ -558,15 +568,27 @@
             pl.BlockSpec((mine, 1, 1, ff), lambda t, j: (0, t, 0, 0)),
             pl.BlockSpec((mine, 1, width), lambda t, j: (0, 0, 0)),
         ],
-        out_specs=[pl.BlockSpec((data, 1, n, ff), lambda t, j: (0, t, 0, 0)) for n in lines],
-        out_shape=[jax.ShapeDtypeStruct((data, inner, n, ff), jnp.bfloat16) for n in lines],
+        out_specs=[pl.BlockSpec(out, lambda t, j: (0, 0))] * owners,
+        out_shape=[jax.ShapeDtypeStruct(out, jnp.bfloat16)] * owners,
+        scratch_shapes=[
+            pltpu.VMEM((2, width, ff), jnp.bfloat16),
+            pltpu.VMEM((width // depth, EXTRA, ff), jnp.bfloat16),
+        ],
         compiler_params=pltpu.CompilerParams(vmem_limit_bytes=VMEM_LIMIT),
         cost_estimate=pl.CostEstimate(
             flops=4 * mine * total * width * inner * ff,
             bytes_accessed=4 * mine * inner * (total + width) * ff,
             transcendentals=0,
         ),
-    )(arrived, grad_pre, grad_turned, hidden, grad_in_bias[:, :, None], grad_back_bias)
+    )(
+        owner_at.reshape(1),
+        arrived,
+        grad_pre,
+        grad_turned,
+        hidden,
+        grad_in_bias[:, :, None],
+        grad_back_bias,
+    )
 
 
 def moved_plan(
@@ -609,10 +631,6 @@
     local_width = w_out.shape[0]
     slice_width = width // tensor
 
-    chunk_shape = (owners, mine, shard_width, ff_here)
-    in_raw = swap(w_in, (DP, INNER)).reshape(chunk_shape)
-    back_raw = swap(w_back.transpose(0, 2, 1), (DP, INNER)).reshape(chunk_shape)
-
     packed = jnp.concatenate(
         [
             w_qkv.transpose(1, 0, 2).reshape(shard_width, 3 * local_width),
@@ -624,7 +642,16 @@
         axis=1,
     )
     packed = lax.all_gather(packed, DP, axis=0, tiled=True)
-    packed, in_raw = lax.optimization_barrier((packed, in_raw))
+
+    back_turned = w_back.transpose(0, 2, 1)
+    pieces = []
+    for s in range(owners):
+        start = (owner_at ^ s) * mine
+        piece = [lax.dynamic_slice_in_dim(shard, start, mine, 0) for shard in (w_in, back_turned)]
+        pieces.append(jnp.stack(piece))
+    near = owners // 2
+    packed, *pieces[near:] = lax.optimization_barrier((packed, *pieces[near:]))
+    pieces = [cross(piece, s) for s, piece in enumerate(pieces)]
     cuts = [3 * local_width, local_width, EXPERTS, experts_here]
     qkv_full, out_turned, router_full, back_bias_turned, vectors = jnp.split(
         packed, [sum(cuts[: i + 1]) for i in range(4)], axis=1
@@ -676,7 +703,6 @@
     attended, log_total = attention_forward(queries, key_rows, value_rows, scale)
     attended_low = attended.reshape(rows_total, local_width).astype(bf16)
     attended_all = lax.all_gather(attended_low, tensor_axes, axis=1, tiled=True)
-    attended_all, back_raw = lax.optimization_barrier((attended_all, back_raw))
     mixed = inputs + bias_out_full
     mixed = mixed + jnp.einsum("te,de->td", attended_all, out_whole, preferred_element_type=f32)
     routed, scaled_second, inv_second = norm_parts(mixed, gain_second, shift_second)
@@ -706,7 +732,7 @@
         grad_in_bias_mine,
         grad_back_bias_mine,
     ) = run_experts(
-        arrived, cot_rows, in_raw, back_raw, in_bias_mine, back_bias_mine, mine, inner, tensor
+        owner_at, arrived, cot_rows, pieces, in_bias_mine, back_bias_mine, inner, tensor
     )
 
     everywhere = (DP, EXPERT, OUTER, INNER)
@@ -732,11 +758,18 @@
         [jnp.sum(jnp.where(hit, gate_slots_back[:, None], 0.0), axis=0) for hit in found], axis=1
     )
     grad_routed_cut = jnp.dot(grad_slots, both, preferred_element_type=f32).astype(bf16)
-    grad_in_out, grad_back_out = weight_grads(
-        arrived, grad_pre_low, grad_turned, hidden_low, grad_in_bias_mine, grad_back_bias_mine, data
-    )
-    grad_routed_cut, returned_out, grad_in_out, grad_back_out = lax.optimization_barrier(
-        (grad_routed_cut, returned_out, grad_in_out, grad_back_out)
+    weight_out = weight_grads(
+        owner_at,
+        arrived,
+        grad_pre_low,
+        grad_turned,
+        hidden_low,
+        grad_in_bias_mine,
+        grad_back_bias_mine,
+        owners,
+    )
+    grad_routed_cut, returned_out, *weight_out = lax.optimization_barrier(
+        (grad_routed_cut, returned_out, *weight_out)
     )
     grad_routed = lax.all_gather(grad_routed_cut, tensor_axes, axis=0, tiled=True).T.astype(f32)
     returned = in_line(bring(returned_out)).astype(bf16)
@@ -779,24 +812,27 @@
     )
     grad_images = (grad_mixed + grad_from_first).reshape(images.shape)
 
-    def spread(parts):
-        return swap(parts.reshape(owners, *parts.shape[2:]), (DP, INNER)).astype(f32)
-
     experts_shape = (experts_here, shard_width, ff_here)
-    grad_in_parts = spread(grad_in_out)
-    grad_w_in = grad_in_parts[:, : mine * shard_width].reshape(experts_shape)
-    lines = grad_in_parts[:, mine * shard_width :]
-    grad_in_bias = lines[:, : 2 * mine].reshape(owners, mine, 2, ff_here)
-    grad_in_bias = jnp.sum(grad_in_bias, axis=2).reshape(experts_here, ff_here)
-    lines = lines[:, 2 * mine : 3 * mine].reshape(experts_here, 2, ff_here // 2)
-    grad_back_shard = jnp.sum(lines[:, :, :shard_width], axis=1)
+    grad_w_in, grad_w_back = jnp.zeros(experts_shape, f32), jnp.zeros(experts_shape, f32)
+    grad_in_bias = jnp.zeros((experts_here, ff_here), f32)
+    grad_back_shard = jnp.zeros((experts_here, shard_width), f32)
+    for s in range(owners):
+        piece = cross(weight_out[s], s).astype(f32)
+        start = (owner_at ^ s) * mine
+        two = piece[: 2 * mine * shard_width].reshape(2, mine, shard_width, ff_here)
+        grad_w_in = lax.dynamic_update_slice_in_dim(grad_w_in, two[0], start, 0)
+        grad_w_back = lax.dynamic_update_slice_in_dim(grad_w_back, two[1], start, 0)
+        lines = piece[2 * mine * shard_width :]
+        line = jnp.sum(lines[: 2 * mine].reshape(mine, 2, ff_here), axis=1)
+        grad_in_bias = lax.dynamic_update_slice_in_dim(grad_in_bias, line, start, 0)
+        line = lines[2 * mine : 3 * mine]
+        line = line[:, :shard_width] + line[:, ff_here // 2 : ff_here // 2 + shard_width]
+        grad_back_shard = lax.dynamic_update_slice_in_dim(grad_back_shard, line, start, 0)
+    grad_w_back = grad_w_back.transpose(0, 2, 1)
     early = jnp.concatenate(
         [grad_qkv.astype(bf16), grad_out_turned.astype(bf16), grad_router.astype(bf16)], axis=1
     )
-    early, grad_back_out = lax.optimization_barrier((early, grad_back_out))
     early = swap(early.reshape(groups, shard_width // sources, -1), (DP, EXPERT))
-    early, grad_back_out = lax.optimization_barrier((early, grad_back_out))
-    grad_w_back = spread(grad_back_out).reshape(experts_shape).transpose(0, 2, 1)
     early = jnp.sum(early.astype(f32), axis=0)
     early = hop_gather(early, EXPERT).reshape(shard_width, -1)
     grad_w_qkv = early[:, : 3 * local_width].reshape(shard_width, 3, local_width).transpose(1, 0, 2)
@@ -846,7 +882,8 @@
 def solution(mesh):
     data, expert, tensor = (mesh.shape[name] for name in (DP, EXPERT, TENSOR))
     inner = FF_PAIR if tensor % FF_PAIR == 0 else 1
-    if (EXPERTS // expert) % (data * inner):
+    owners = data * inner
+    if (EXPERTS // expert) % owners or owners & (owners - 1):
         taken, given = specs(TENSOR)
         return jax.shard_map(
             gathered_plan, mesh=mesh, in_specs=taken, out_specs=given, check_vma=False

time: 732 us -> 737 us (level)
  blocking collectives: 162 us -> 65.7 us
  waiting for transfers between devices: 290 us -> 362 us
  local copies, waits for them, and re-layouts: 79.5 us -> 110 us
  starting transfers between devices: 50 us -> 35.6 us
    ppermute x0 -> x6, waiting for transfers between devices: none -> 239 us  [cross(): lax.ppermute(values, (DP, INNER), [(i, i ^ s) for i in range(count)])]
    all_to_all x3 -> x1, blocking collectives: 122 us -> 22.2 us  [swap(): return lax.all_to_all(values, axes, split_axis=0, concat_axis=0, tiled=True)]
    psum x1, waiting for transfers between devices: 84.3 us -> 0.01 us  [moved_plan(): lax.psum(grad_normed_part.astype(bf16), tensor_axes).astype(f32)]
    all_gather x1, waiting for transfers between devices: 41.6 us -> 1.42 us  [moved_plan(): packed = lax.all_gather(packed, DP, axis=0, tiled=True)]
    all_to_all x6 -> x4, waiting for transfers between devices: 99.5 us -> 63.1 us  [swap(): return lax.all_to_all(values, axes, split_axis=0, concat_axis=0, tiled=True)]
    another operation x2 -> x6, local copies, waits for them, and re-layouts: 0.62 us -> 17 us
    dynamic_update_slice x0 -> x11, local copies, waits for them, and re-layouts: none -> 11.9 us  [the longest x4 7.17 us: moved_plan(): grad_w_back = lax.dynamic_update_slice_in_dim(grad_w_back, two[1], start, 0)]
    all_to_all x6 -> x4, starting transfers between devices: 34.1 us -> 23.2 us  [swap(): return lax.all_to_all(values, axes, split_axis=0, concat_axis=0, tiled=True)]
  transfers between devices with their start and end apart: 16 -> 19, of which waited for: 10 -> 8; matrix products, arithmetic and copies ran while one was open for 18% -> 21% of each run, Pallas kernels for 2% -> 2%
where the time goes in v4:
time: 737 us; the launch traced here: 726 us
  waiting for transfers between devices  362 us (49%)
  local copies, waits for them, and re-layouts  110 us (15%)
  blocking collectives  65.7 us (9%)
  other arithmetic  54.6 us (7%)
  matrix products  45.7 us (6%)
  Pallas kernels  35.9 us (5%)
  starting transfers between devices  35.6 us (5%)
  between operations  16.1 us (2%)
    ppermute x6, waiting for transfers between devices, cross(): lax.ppermute(values, (DP, INNER), [(i, i ^ s) for i in range(count)])  239 us
    all_to_all x4, waiting for transfers between devices, swap(): return lax.all_to_all(values, axes, split_axis=0, concat_axis=0, tiled=True)  63.1 us
    psum x1, blocking collectives, moved_plan(): vectors = lax.psum(vectors, everywhere)  43.6 us
    ppermute x4, waiting for transfers between devices, hop_gather(): lax.ppermute(values, axes, [(i, (i + s) % count) for i in range(count)])  31 us
    all_gather x1, waiting for transfers between devices, moved_plan(): lax.all_gather(grad_routed_cut, tensor_axes, axis=0, tiled=True)  28 us
    all_to_all x4, starting transfers between devices, swap(): return lax.all_to_all(values, axes, split_axis=0, concat_axis=0, tiled=True)  23.2 us
    pallas_call x1, Pallas kernels, run_experts(): pl.pallas_call(functools.partial(expert_kernel, inner, owners), grid=(min...  23 us
    all_to_all x1, blocking collectives, swap(): return lax.all_to_all(values, axes, split_axis=0, concat_axis=0, tiled=True)  22.2 us
  transfers between devices with their start and end apart: 19, of which 8 were waited for; matrix products, arithmetic and copies ran while one was open for 21% of the time, Pallas kernels for 2%

profile of v4, /device:TPU:0, one launch (start us, length us, event | category | flops | bytes accessed | tf_op | source)
XLA Modules:
  0.0 725.6 jit_solution(10553957097703137172)
XLA Ops:
  25.7 5.1 dynamic-slice_bitcast_fusion.1
  50.4 4.4 copy.307
  54.8 5.1 reshape.563
  59.9 7.3 %fusion.15 = bf16[2048,768]{1,0:T(8,128)(2,1)} fusion(s32[2048]{0:T(1024)S(1)} %bitcast.174, s32[788]{0:T(1024)S(1)} %get-tuple-element.167, s32[788]{0:T(1024)S(1)} %get-tuple-element.168, f32[788,768]{0,1:T(8,128)} %reshape.563, f32[788]{0:T(1024)S(1)} %mul.220), kind=kOutput, calls=%fused_computation.20 | convolution fusion | flops 2488072192 | bytes 5584112 | tf_op jit(solution)/shard_map/dot_general | solution.py:684
  67.2 4.4 all-to-all-start
  79.6 31.0 %collective-permute-done.1 = bf16[768,192]{1,0:T(8,128)(2,1)S(1)} collective-permute-done((bf16[768,192]{1,0:T(8,128)(2,1)S(1)}, bf16[768,192]{1,0:T(8,128)(2,1)S(1)}, u32[]{:S(2)}, u32[]{:S(2)}) %collective-permute-start.1) | collective-permute-done | bytes 294944 | tf_op jit(solution)/shard_map/ppermute | solution.py:357
  135.5 4.7 all-to-all-start.1
  152.1 78.3 %collective-permute-done.4.refs_2_ = bf16[2,4,192,768]{3,2,1,0:T(8,128)(2,1)} collective-permute-done((bf16[2,4,192,768]{3,2,1,0:T(8,128)(2,1)}, bf16[2,4,192,768]{3,2,1,0:T(8,128)(2,1)}, u32[]{:S(2)}, u32[]{:S(2)}) %collective-permute-start.4) | collective-permute-done | bytes 2359328 | tf_op jit(solution)/shard_map/ppermute | solution.py:364
  230.4 49.6 %collective-permute-done.5.refs_3_ = bf16[2,4,192,768]{3,2,1,0:T(8,128)(2,1)} collective-permute-done((bf16[2,4,192,768]{3,2,1,0:T(8,128)(2,1)}, bf16[2,4,192,768]{3,2,1,0:T(8,128)(2,1)}, u32[]{:S(2)}, u32[]{:S(2)}) %collective-permute-start.5) | collective-permute-done | bytes 2359328 | tf_op jit(solution)/shard_map/ppermute | solution.py:364
  280.0 23.0 %shard_map.289 = (bf16[8,4,192,256]{3,2,1,0:T(8,128)(2,1)}, bf16[8,4,208,256]{3,2,1,0:T(8,128)(2,1)}, bf16[4,1,512,768]{3,2,1,0:T(8,128)(2,1)}, bf16[4,1,512,768...) custom-call(s32[1]{0:T(128)} %bitcast.21.at_ref, ...), custom_call_target="tpu_custom_call" | custom-call | flops 9663676416 | bytes 28311552 | tf_op jit(solution)/shard_map/pallas_call | solution.py:467
  303.0 10.3 %all-to-all-start.2 = ((bf16[32,208,256]{2,1,0:T(8,128)(2,1)}), bf16[32,208,256]{2,1,0:T(8,128)(2,1)}, u32[]{:S(2)}, u32[]{:S(2)}) async-start(bf16[32,208,256]{2,1,0:T(8,128)(2,1)} %bitcast.155), calls=%async_computation.2 | async-start | bytes 6815744 | tf_op jit(solution)/shard_map/all_to_all | solution.py:350
  313.4 12.9 %shard_map.290 = (bf16[1552,768]{1,0:T(8,128)(2,1)}, bf16[1552,768]{1,0:T(8,128)(2,1)}, bf16[1552,768]{1,0:T(8,128)(2,1)}, bf16[1552,768]{1,0:T(8,128)(2,1)}) custom-call(s32[1]{0:T(128)} %bitcast.21.at_ref, bf16[8,272,768]{2,1,0:T(8,128)(2,1)} %all-to-all-done.1.rows_ref.gate_ref, bf16[4,1,512,768]{3,2,1,0:T(8,128)(2,1)} %get-tuple-element.44.grad_pre_ref, ...), custom_call_target="tpu_custom_call" | custom-call | flops 4831838208 | bytes 15728640 | tf_op jit(solution)/shard_map/pallas_call | solution.py:559
  326.3 63.1 %all-to-all-done.2 = bf16[32,208,256]{2,1,0:T(8,128)(2,1)} async-done(((bf16[32,208,256]{2,1,0:T(8,128)(2,1)}), bf16[32,208,256]{2,1,0:T(8,128)(2,1)}, u32[]{:S(2)}, u32[]{:S(2)}) %all-to-all-start.2) | async-done | bytes 3407904 | tf_op jit(solution)/shard_map/all_to_all | solution.py:350
  401.3 28.0 %all-gather.11.cloned.1.call-done = bf16[768,788]{1,0:T(8,128)(2,1)} async-done(((bf16[192,788]{1,0:T(8,128)(2,1)}), bf16[768,788]{1,0:T(8,128)(2,1)}) %all-gather.11.cloned.1.call-update) | async-done | bytes 1210384 | tf_op jit(solution)/shard_map/all_gather | solution.py:774
  429.3 4.4 multiply_reduce_fusion
  452.0 22.2 %all_to_all.25 = bf16[8,96,800]{2,1,0:T(8,128)(2,1)} all-to-all(bf16[8,96,800]{2,1,0:T(8,128)(2,1)S(1)} %bitcast.152), channel_id=1, replica_groups=mesh['dp'=4,'expert'=2,'tensor'=4] {'dp','expert'}, dimensions={0} | all-to-all | bytes 2457600 | tf_op jit(solution)/shard_map/all_to_all | solution.py:350
  483.0 4.7 broadcast.392.clone
  489.3 4.7 broadcast.392.clone.1
  504.6 58.1 %collective-permute-done.8 = bf16[1552,768]{1,0:T(8,128)(2,1)} collective-permute-done((bf16[1552,768]{1,0:T(8,128)(2,1)}, bf16[1552,768]{1,0:T(8,128)(2,1)}, u32[]{:S(2)}, u32[]{:S(2)}) %collective-permute-start.8) | collective-permute-done | bytes 2383904 | tf_op jit(solution)/shard_map/ppermute | solution.py:364
  563.4 52.6 %collective-permute-done.9 = bf16[1552,768]{1,0:T(8,128)(2,1)} collective-permute-done((bf16[1552,768]{1,0:T(8,128)(2,1)}, bf16[1552,768]{1,0:T(8,128)(2,1)}, u32[]{:S(2)}, u32[]{:S(2)}) %collective-permute-start.9) | collective-permute-done | bytes 2383904 | tf_op jit(solution)/shard_map/ppermute | solution.py:364
  650.8 4.6 multiply_add_fusion
  655.4 43.6 %psum.15 = f32[7,768]{1,0:T(8,128)S(1)} all-reduce(f32[7,768]{1,0:T(8,128)S(1)} %pad_maximum_fusion.8), channel_id=1, replica_groups=mesh['dp'=4,'expert'=2,'tensor'=4] {'dp','expert','tensor'}, use_global_device_ids=true, to_apply=%region_30.31 | all-reduce | flops 5376 | bytes 43008 | tf_op jit(solution)/shard_map/psum | solution.py:847
  699.0 4.2 reshape.565
  712.1 4.1 reshape.564
  (326 shorter events, 179.1 us)
Async XLA Ops:
  7.2 30.2 %all-gather.5.cloned.1.call-start = ((), (), s32[]{:S(2)}) async-start(), calls=%async_computation.5 | async-start | bytes 1720320 | tf_op jit(solution)/shard_map/all_gather | solution.py:644
  16.0 104.7 %all-gather.7.cloned.1.call-start = ((), (), s32[]{:S(2)}) async-start(), calls=%async_computation.6 | async-start | bytes 1720320 | tf_op jit(solution)/shard_map/all_gather | solution.py:705
  20.4 19.1 %copy-start.23 = (f32[788]{0:T(1024)}, f32[788]{0:T(1024)S(1)}, u32[]{:S(2)}) copy-start(f32[788]{0:T(1024)S(1)} %div.59) | copy-start | bytes 9460
  21.7 17.8 %copy-start.25 = (f32[788]{0:T(1024)}, f32[788]{0:T(1024)S(1)}, u32[]{:S(2)}) copy-start(f32[788]{0:T(1024)S(1)} %rsqrt.20) | copy-start | bytes 9460
  25.7 371.3 %copy-start.37 = (s32[788]{0:T(1024)}, s32[788]{0:T(1024)S(1)}, u32[]{:S(2)}) copy-start(s32[788]{0:T(1024)S(1)} %get-tuple-element.167) | copy-start | bytes 9460
  25.7 371.3 %copy-start.39 = (s32[788]{0:T(1024)}, s32[788]{0:T(1024)S(1)}, u32[]{:S(2)}) copy-start(s32[788]{0:T(1024)S(1)} %get-tuple-element.168) | copy-start | bytes 9460
  50.4 383.3 %copy-start.30 = (f32[788]{0:T(1024)}, f32[788]{0:T(1024)S(1)}, u32[]{:S(2)}) copy-start(f32[788]{0:T(1024)S(1)} %mul.220) | copy-start | bytes 9460
  67.2 68.3 %all-to-all-start = ((bf16[8,256,768]{2,1,0:T(8,128)(2,1)}), bf16[8,256,768]{2,1,0:T(8,128)(2,1)}, u32[]{:S(2)}, u32[]{:S(2)}) async-start(bf16[8,256,768]{2,1,0:T(8,128)(2,1)} %bitcast.157), calls=%async_computation | async-start | bytes 6291456 | tf_op jit(solution)/shard_map/all_to_all | solution.py:350
  73.0 37.6 %collective-permute-start.1 = (bf16[768,192]{1,0:T(8,128)(2,1)S(1)}, bf16[768,192]{1,0:T(8,128)(2,1)S(1)}, u32[]{:S(2)}, u32[]{:S(2)}) collective-permute-start(bf16[768,192]{1,0:T(8,128)(2,1)S(1)} %get-tuple-element.192), channel_id=1, source_target_pairs={{0,2},{1,3},{2,0},{3,1},{4,6},{5,7},{6,4},{7,5},{8,10},{9,11},{10,... | collective-permute-start | bytes 884744 | tf_op jit(solution)/shard_map/ppermute | solution.py:357
  75.7 34.8 %collective-permute-start = (bf16[768,192]{1,0:T(8,128)(2,1)S(1)}, bf16[768,192]{1,0:T(8,128)(2,1)S(1)}, u32[]{:S(2)}, u32[]{:S(2)}) collective-permute-start(bf16[768,192]{1,0:T(8,128)(2,1)S(1)} %get-tuple-element.192), channel_id=1, source_target_pairs={{0,1},{1,2},{2,3},{3,0},{4,5},{5,6},{6,7},{7,4},{8,9},{9,10},{10,1... | collective-permute-start | bytes 884744 | tf_op jit(solution)/shard_map/ppermute | solution.py:357
  77.3 33.3 %collective-permute-start.2 = (bf16[768,192]{1,0:T(8,128)(2,1)S(1)}, bf16[768,192]{1,0:T(8,128)(2,1)S(1)}, u32[]{:S(2)}, u32[]{:S(2)}) collective-permute-start(bf16[768,192]{1,0:T(8,128)(2,1)S(1)} %get-tuple-element.192), channel_id=1, source_target_pairs={{0,3},{1,0},{2,1},{3,2},{4,7},{5,4},{6,5},{7,6},{8,11},{9,8},{10,9... | collective-permute-start | bytes 884744 | tf_op jit(solution)/shard_map/ppermute | solution.py:357
  135.5 144.5 %all-to-all-start.1 = ((bf16[8,272,768]{2,1,0:T(8,128)(2,1)}), bf16[8,272,768]{2,1,0:T(8,128)(2,1)}, u32[]{:S(2)}, u32[]{:S(2)}) async-start(bf16[8,272,768]{2,1,0:T(8,128)(2,1)} %pad_maximum_fusion), calls=%async_computation.1 | async-start | bytes 6684672 | tf_op jit(solution)/shard_map/all_to_all | solution.py:350
  143.5 8.6 %collective-permute-start.3 = (bf16[2,4,192,768]{3,2,1,0:T(8,128)(2,1)}, bf16[2,4,192,768]{3,2,1,0:T(8,128)(2,1)}, u32[]{:S(2)}, u32[]{:S(2)}) collective-permute-start(bf16[2,4,192,768]{3,2,1,0:T(8,128)(2,1)} %pad_maximum_fusion.4), channel_id=1, source_target_pairs={{0,8},{8,0},{16,24},{24,16},{1,9},{9,1},{17,25},{25,17},{2,10},{10... | collective-permute-start | bytes 7077896 | tf_op jit(solution)/shard_map/ppermute | solution.py:364
  143.9 86.4 %collective-permute-start.4 = (bf16[2,4,192,768]{3,2,1,0:T(8,128)(2,1)}, bf16[2,4,192,768]{3,2,1,0:T(8,128)(2,1)}, u32[]{:S(2)}, u32[]{:S(2)}) collective-permute-start(bf16[2,4,192,768]{3,2,1,0:T(8,128)(2,1)} %pad_maximum_fusion.1), channel_id=1, source_target_pairs={{0,16},{8,24},{16,0},{24,8},{1,17},{9,25},{17,1},{25,9},{2,18},{10... | collective-permute-start | bytes 7077896 | tf_op jit(solution)/shard_map/ppermute | solution.py:364
  145.6 134.4 %collective-permute-start.5 = (bf16[2,4,192,768]{3,2,1,0:T(8,128)(2,1)}, bf16[2,4,192,768]{3,2,1,0:T(8,128)(2,1)}, u32[]{:S(2)}, u32[]{:S(2)}) collective-permute-start(bf16[2,4,192,768]{3,2,1,0:T(8,128)(2,1)} %pad_maximum_fusion.2), channel_id=1, source_target_pairs={{0,24},{8,16},{16,8},{24,0},{1,25},{9,17},{17,9},{25,1},{2,26},{10... | collective-permute-start | bytes 7077896 | tf_op jit(solution)/shard_map/ppermute | solution.py:364
  303.0 86.4 %all-to-all-start.2 = ((bf16[32,208,256]{2,1,0:T(8,128)(2,1)}), bf16[32,208,256]{2,1,0:T(8,128)(2,1)}, u32[]{:S(2)}, u32[]{:S(2)}) async-start(bf16[32,208,256]{2,1,0:T(8,128)(2,1)} %bitcast.155), calls=%async_computation.2 | async-start | bytes 6815744 | tf_op jit(solution)/shard_map/all_to_all | solution.py:350
  313.4 115.9 %all-gather.11.cloned.1.call-start = ((), (), s32[]{:S(2)}) async-start(), calls=%async_computation.8 | async-start | bytes 1720320 | tf_op jit(solution)/shard_map/all_gather | solution.py:774
  474.2 169.1 %all-to-all-start.3 = ((bf16[32,192,256]{2,1,0:T(8,128)(2,1)}), bf16[32,192,256]{2,1,0:T(8,128)(2,1)}, u32[]{:S(2)}, u32[]{:S(2)}) async-start(bf16[32,192,256]{2,1,0:T(8,128)(2,1)} %bitcast.156), calls=%async_computation.3 | async-start | bytes 6291456 | tf_op jit(solution)/shard_map/all_to_all | solution.py:350
  477.8 162.1 %all-reduce.3.cloned.1.call-start = ((), (), s32[]{:S(2)}) async-start(), calls=%async_computation.9 | async-start | bytes 2752512 | tf_op jit(solution)/shard_map/psum | solution.py:808
  477.9 26.0 %collective-permute-start.7 = (bf16[1552,768]{1,0:T(8,128)(2,1)}, bf16[1552,768]{1,0:T(8,128)(2,1)}, u32[]{:S(2)}, u32[]{:S(2)}) collective-permute-start(bf16[1552,768]{1,0:T(8,128)(2,1)} %get-tuple-element.56), channel_id=1, source_target_pairs={{0,8},{8,0},{16,24},{24,16},{1,9},{9,1},{17,25},{25,17},{2,10},{10... | collective-permute-start | bytes 7151624 | tf_op jit(solution)/shard_map/ppermute | solution.py:364
  478.0 84.7 %collective-permute-start.8 = (bf16[1552,768]{1,0:T(8,128)(2,1)}, bf16[1552,768]{1,0:T(8,128)(2,1)}, u32[]{:S(2)}, u32[]{:S(2)}) collective-permute-start(bf16[1552,768]{1,0:T(8,128)(2,1)} %get-tuple-element.57), channel_id=1, source_target_pairs={{0,16},{8,24},{16,0},{24,8},{1,17},{9,25},{17,1},{25,9},{2,18},{10... | collective-permute-start | bytes 7151624 | tf_op jit(solution)/shard_map/ppermute | solution.py:364
  479.7 136.3 %collective-permute-start.9 = (bf16[1552,768]{1,0:T(8,128)(2,1)}, bf16[1552,768]{1,0:T(8,128)(2,1)}, u32[]{:S(2)}, u32[]{:S(2)}) collective-permute-start(bf16[1552,768]{1,0:T(8,128)(2,1)} %get-tuple-element.58), channel_id=1, source_target_pairs={{0,24},{8,16},{16,8},{24,0},{1,25},{9,17},{17,9},{25,1},{2,26},{10... | collective-permute-start | bytes 7151624 | tf_op jit(solution)/shard_map/ppermute | solution.py:364
  503.4 208.7 %all-gather.9.cloned.1.call-start = ((), (), s32[]{:S(2)}) async-start(), calls=%async_computation.7 | async-start | bytes 1720320 | tf_op jit(solution)/shard_map/all_gather | solution.py:780
  638.3 69.0 %collective-permute-start.6 = (f32[96,800]{1,0:T(8,128)S(1)}, f32[96,800]{1,0:T(8,128)}, u32[]{:S(2)}, u32[]{:S(2)}) collective-permute-start(f32[96,800]{1,0:T(8,128)S(1)} %convert_reduce_fusion.1), channel_id=1, source_target_pairs={{0,4},{4,0},{1,5},{5,1},{2,6},{6,2},{3,7},{7,3},{8,12},{12,8},{9,1... | collective-permute-start | bytes 921608 | tf_op jit(solution)/shard_map/ppermute | solution.py:357
  (44 other events, 136.6 us)
Sparse Core Ops, SparseCore 0:
  16.1 21.2 all-gather.4
  50.4 56.0 all-gather.6
  396.2 33.0 all-gather.10
  502.9 90.7 all-reduce.2
  650.9 36.3 all-gather.8

commit v5 on v3

--- a/solution.py
+++ b/solution.py
@@ -14,6 +14,7 @@
 TOPK = 2
 CAP = 64
 FF_PAIR = 2
+PAIR = 2
 EXTRA = 16
 VMEM_LIMIT = 56 * 1024 * 1024
 GELU_SCALE = (2.0 / math.pi) ** 0.5
@@ -352,16 +353,13 @@
 
 def hop_gather(values, axes):
     count, at = lax.axis_size(axes), lax.axis_index(axes)
-    hops = [values]
-    for s in range(1, count):
-        hops.append(lax.ppermute(values, axes, [(i, (i + s) % count) for i in range(count)]))
-    order = (at - jnp.arange(count, dtype=jnp.int32)) % count
-    return jnp.take(jnp.stack(hops), order, axis=0)
-
-
-def high_low(values):
-    high = lax.reduce_precision(values, 8, 7)
-    return high.astype(jnp.bfloat16), (values - high).astype(jnp.bfloat16)
+    gathered = jnp.zeros((count, *values.shape), values.dtype)
+    for s in range(count):
+        hop = values
+        if s:
+            hop = lax.ppermute(values, axes, [(i, (i + s) % count) for i in range(count)])
+        gathered = lax.dynamic_update_slice_in_dim(gathered, hop[None], (at - s) % count, 0)
+    return gathered
 
 
 def turned_dot(left, right, left_dim, right_dim):
@@ -569,6 +567,465 @@
     )(arrived, grad_pre, grad_turned, hidden, grad_in_bias[:, :, None], grad_back_bias)
 
 
+def norm_rows(values):
+    average = jnp.mean(values, axis=-1, keepdims=True)
+    centred = values - average
+    spread = jnp.mean(centred * centred, axis=-1, keepdims=True)
+    inv_std = lax.rsqrt(spread + EPS)
+    return centred * inv_std, inv_std
+
+
+def norm_rows_back(grad_out, scaled, inv_std, norm_gain):
+    grad_scaled = grad_out * norm_gain
+    inner = grad_scaled - jnp.mean(grad_scaled, axis=-1, keepdims=True)
+    inner = inner - scaled * jnp.mean(grad_scaled * scaled, axis=-1, keepdims=True)
+    return inner * inv_std
+
+
+def call_kernel(kernel, grid, inputs, outputs, scratch=(), flops=0):
+    smem = pl.BlockSpec(memory_space=pltpu.SMEM)
+    return pl.pallas_call(
+        kernel,
+        grid=grid,
+        in_specs=[smem if b is None else pl.BlockSpec(b, i) for _, b, i in inputs],
+        out_specs=[pl.BlockSpec(b, i) for _, _, b, i in outputs],
+        out_shape=[jax.ShapeDtypeStruct(shape, dtype) for shape, dtype, _, _ in outputs],
+        scratch_shapes=list(scratch),
+        compiler_params=pltpu.CompilerParams(vmem_limit_bytes=VMEM_LIMIT),
+        cost_estimate=pl.CostEstimate(
+            flops=flops,
+            bytes_accessed=sum(a.size * a.dtype.itemsize for a, _, _ in inputs),
+            transcendentals=0,
+        ),
+    )(*(a for a, _, _ in inputs))
+
+
+def whole(array):
+    return array, array.shape, lambda p: (0,) * array.ndim
+
+
+def by_step(array, lead):
+    return array, (lead, *array.shape[1:]), lambda p: (p,) + (0,) * (array.ndim - 1)
+
+
+def attend_kernel(images_ref, packed_ref, vector_ref, bias_ref, attended_ref, proj_ref):
+    f32, bf16 = jnp.float32, jnp.bfloat16
+    local = bias_ref.shape[1]
+    weight = packed_ref[:, : 3 * local]
+    for h in range(images_ref.shape[0]):
+        scaled, _ = norm_rows(images_ref[h].astype(f32))
+        normed = (scaled * vector_ref[0:1] + vector_ref[1:2]).astype(bf16)
+        proj = jnp.dot(normed, weight, preferred_element_type=f32)
+        queries = (proj[:, :local] + bias_ref[0:1]).astype(bf16)
+        keys = proj[:, local : 2 * local].astype(bf16)
+        values = (proj[:, 2 * local :] + bias_ref[1:2]).astype(bf16)
+        proj_ref[h] = jnp.concatenate([queries, keys, values], axis=1)
+        parts = []
+        for n in range(0, local, HEAD_DIM):
+            head = slice(n, n + HEAD_DIM)
+            scores = turned_dot(queries[:, head], keys[:, head], 1, 1) * HEAD_DIM**-0.5
+            scores = jnp.exp(scores - jnp.max(scores, axis=-1, keepdims=True))
+            weights = scores / jnp.sum(scores, axis=-1, keepdims=True)
+            parts.append(
+                jnp.dot(weights.astype(bf16), values[:, head], preferred_element_type=f32)
+            )
+        attended_ref[0, :, h * local : (h + 1) * local] = jnp.concatenate(parts, axis=1).astype(bf16)
+
+
+def run_attend(images, packed, vectors, qv_bias):
+    count, length, width = images.shape
+    local = qv_bias.shape[1]
+    return call_kernel(
+        attend_kernel,
+        (count // PAIR,),
+        [by_step(images, PAIR), whole(packed), whole(vectors), whole(qv_bias)],
+        [
+            ((count // PAIR, length, PAIR * local), jnp.bfloat16, (1, length, PAIR * local), lambda p: (p, 0, 0)),
+            ((count, length, 3 * local), jnp.bfloat16, (PAIR, length, 3 * local), lambda p: (p, 0, 0)),
+        ],
+        flops=2 * count * length * local * (3 * width + 4 * length),
+    )
+
+
+def slot_hits(target_row, count):
+    return lax.broadcasted_iota(jnp.int32, (count, target_row.shape[1]), 0) == target_row
+
+
+def send_kernel(rows_ref, target_ref, out_ref, sum_ref):
+    f32, bf16 = jnp.float32, jnp.bfloat16
+    slots = sum_ref.shape[0]
+    at = pl.program_id(0)
+
+    @pl.when(at == 0)
+    def _():
+        sum_ref[...] = jnp.zeros_like(sum_ref)
+
+    for h in range(rows_ref.shape[0]):
+        hits = [slot_hits(target_ref[h, k : k + 1], slots) for k in range(TOPK)]
+        fill = jnp.logical_or(hits[0], hits[1]).astype(f32).astype(bf16)
+        sum_ref[...] += jnp.dot(fill, rows_ref[h], preferred_element_type=f32)
+
+    @pl.when(at == pl.num_programs(0) - 1)
+    def _():
+        out_ref[...] = sum_ref[...].astype(bf16).reshape(out_ref.shape)
+
+
+def run_send(rows, plane_target, groups, slots_plane):
+    count, length, width = rows.shape
+    out = (groups, slots_plane // groups, width)
+    return call_kernel(
+        send_kernel,
+        (count // PAIR,),
+        [by_step(rows, PAIR), by_step(plane_target, PAIR)],
+        [(out, jnp.bfloat16, out, lambda p: (0, 0, 0))],
+        [pltpu.VMEM((slots_plane, width), jnp.float32)],
+        flops=2 * count * length * width * slots_plane,
+    )[0]
+
+
+def route_kernel(
+    router_at,
+    images_ref,
+    attended_ref,
+    out_ref,
+    packed_ref,
+    vector_ref,
+    routes_ref,
+    target_ref,
+    mixed_ref,
+    probs_ref,
+    sent_ref,
+    sum_ref,
+    gate_ref,
+):
+    f32, bf16 = jnp.float32, jnp.bfloat16
+    slots = sum_ref.shape[0]
+    tensor, local = attended_ref.shape[0], attended_ref.shape[3] // images_ref.shape[0]
+    at = pl.program_id(0)
+
+    @pl.when(at == 0)
+    def _():
+        sum_ref[...] = jnp.zeros_like(sum_ref)
+        gate_ref[...] = jnp.zeros_like(gate_ref)
+
+    router = packed_ref[:, router_at : router_at + EXPERTS]
+    for h in range(images_ref.shape[0]):
+        mixed = images_ref[h].astype(f32) + vector_ref[2:3]
+        for z in range(tensor):
+            part = attended_ref[z, 0, :, h * local : (h + 1) * local]
+            weight = out_ref[z * local : (z + 1) * local]
+            mixed = mixed + jnp.dot(part, weight, preferred_element_type=f32)
+        mixed_ref[h] = mixed
+        scaled, _ = norm_rows(mixed)
+        routed = (scaled * vector_ref[3:4] + vector_ref[4:5]).astype(bf16)
+        logits = jnp.dot(routed, router, preferred_element_type=f32)
+        logits = jnp.exp(logits - jnp.max(logits, axis=-1, keepdims=True))
+        probs = logits / jnp.sum(logits, axis=-1, keepdims=True)
+        probs_ref[h] = probs
+        experts = lax.broadcasted_iota(jnp.int32, probs.shape, 1)
+        fill = jnp.zeros((slots, probs.shape[0]), f32)
+        for k in range(TOPK):
+            match = experts == routes_ref[h, :, k : k + 1]
+            gate = jnp.sum(jnp.where(match, probs, 0.0), axis=1, keepdims=True)
+            high = gate.astype(bf16)
+            low = (gate - high.astype(f32)).astype(bf16)
+            pair = jnp.concatenate([high, low, jnp.zeros((gate.shape[0], 6), bf16)], axis=1)
+            hit = slot_hits(target_ref[h, k : k + 1], slots).astype(f32)
+            fill = fill + hit
+            gate_ref[...] += turned_dot(pair, hit.astype(bf16), 0, 1)
+        sum_ref[...] += jnp.dot(fill.astype(bf16), routed, preferred_element_type=f32)
+
+    @pl.when(at == pl.num_programs(0) - 1)
+    def _():
+        groups, lines, width = sent_ref.shape
+        here = slots // groups
+        for g in range(groups):
+            lanes = slice(g * here, (g + 1) * here)
+            sent_ref[g, :here] = sum_ref[lanes].astype(bf16)
+            gates = jnp.concatenate([gate_ref[:, lanes], jnp.zeros((8, width - here), f32)], axis=1)
+            gates = jnp.concatenate([gates, jnp.zeros((lines - here - 8, width), f32)], axis=0)
+            sent_ref[g, here:] = gates.astype(bf16)
+
+
+def run_route(images, attended_all, out_whole, packed, vectors, routes, plane_target, groups, slots_plane, router_at):
+    f32, bf16 = jnp.float32, jnp.bfloat16
+    count, length, width = images.shape
+    tensor = attended_all.shape[0]
+    sent = (groups, slots_plane // groups + EXTRA, width)
+    return call_kernel(
+        functools.partial(route_kernel, router_at),
+        (count // PAIR,),
+        [
+            by_step(images, PAIR),
+            (attended_all, (tensor, 1, *attended_all.shape[2:]), lambda p: (0, p, 0, 0)),
+            whole(out_whole),
+            whole(packed),
+            whole(vectors),
+            by_step(routes, PAIR),
+            by_step(plane_target, PAIR),
+        ],
+        [
+            ((count, length, width), f32, (PAIR, length, width), lambda p: (p, 0, 0)),
+            ((count, length, EXPERTS), f32, (PAIR, length, EXPERTS), lambda p: (p, 0, 0)),
+            (sent, bf16, sent, lambda p: (0, 0, 0)),
+        ],
+        [pltpu.VMEM((slots_plane, width), f32), pltpu.VMEM((8, slots_plane), f32)],
+        flops=2 * count * length * width * (width + slots_plane),
+    )
+
+
+def slot_blocks(parts_ref, slots_ref, outer, inner):
+    here = parts_ref.shape[2]
+    for b in range(slots_ref.shape[1] // here):
+        first = (b // inner) * outer * inner + b % inner
+        total = parts_ref[first].astype(jnp.float32)
+        for o in range(1, outer):
+            total = total + parts_ref[first + o * inner].astype(jnp.float32)
+        slots_ref[:, b * here : (b + 1) * here] = total
+
+
+def token_hits(target_column, count):
+    return lax.broadcasted_iota(jnp.int32, (target_column.shape[0], count), 1) == target_column
+
+
+def take_grads_kernel(outer, inner, parts_ref, target_ref, rows_ref, gates_ref, slots_ref):
+    f32, bf16 = jnp.float32, jnp.bfloat16
+    slots = slots_ref.shape[1]
+    local = rows_ref.shape[2] // target_ref.shape[0]
+
+    @pl.when(pl.program_id(0) == 0)
+    def _():
+        slot_blocks(parts_ref, slots_ref, outer, inner)
+
+    grads = slots_ref[:local].astype(bf16)
+    gate_terms = slots_ref[local : local + 1] + slots_ref[local + 1 : local + 2]
+    for h in range(target_ref.shape[0]):
+        hits = [token_hits(target_ref[h, :, k : k + 1], slots) for k in range(TOPK)]
+        find = jnp.logical_or(hits[0], hits[1]).astype(f32).astype(bf16)
+        rows_ref[0, :, h * local : (h + 1) * local] = turned_dot(find, grads, 1, 1).astype(bf16)
+        terms = [
+            jnp.sum(jnp.where(hit, gate_terms, 0.0), axis=1, keepdims=True) for hit in hits
+        ]
+        gates_ref[h] = jnp.concatenate(terms, axis=1)
+
+
+def run_take_grads(parts, target, local, outer, inner, slots):
+    count, length, _ = target.shape
+    return call_kernel(
+        functools.partial(take_grads_kernel, outer, inner),
+        (count // PAIR,),
+        [whole(parts), by_step(target, PAIR)],
+        [
+            ((count // PAIR, length, PAIR * local), jnp.bfloat16, (1, length, PAIR * local), lambda p: (p, 0, 0)),
+            ((count, length, TOPK), jnp.float32, (PAIR, length, TOPK), lambda p: (p, 0, 0)),
+        ],
+        [pltpu.VMEM((parts.shape[1], slots), jnp.float32)],
+        flops=2 * count * length * slots * local,
+    )
+
+
+def take_rows_kernel(
+    outer, inner, held_ref, parts_ref, target_ref, probs_ref, routes_ref, mixed_ref, out_ref, slots_ref
+):
+    f32, bf16 = jnp.float32, jnp.bfloat16
+    slots = slots_ref.shape[1]
+    pair = target_ref.shape[0]
+    local = out_ref.shape[2] // pair
+    at = pl.program_id(0)
+
+    @pl.when(at == 0)
+    def _():
+        slot_blocks(parts_ref, slots_ref, outer, inner)
+
+    returned = slots_ref[...].astype(bf16)
+    for h in range(pair):
+        probs = probs_ref[h]
+        experts = lax.broadcasted_iota(jnp.int32, probs.shape, 1)
+        rows = mixed_ref[h]
+        for k in range(TOPK):
+            match = experts == routes_ref[h, :, k : k + 1]
+            gate = jnp.sum(jnp.where(match, probs, 0.0), axis=1, keepdims=True)
+            find = token_hits(target_ref[h, :, k : k + 1], slots).astype(f32).astype(bf16)
+            rows = rows + gate * turned_dot(find, returned, 1, 1)
+        live = (at * pair + h < held_ref[0]).astype(f32)
+        out_ref[0, :, h * local : (h + 1) * local] = (live * rows).astype(bf16)
+
+
+def run_take_rows(held, parts, target, probs, routes, mixed_cut, outer, inner, slots):
+    count, length, local = mixed_cut.shape
+    return call_kernel(
+        functools.partial(take_rows_kernel, outer, inner),
+        (count // PAIR,),
+        [
+            (held, None, None),
+            whole(parts),
+            by_step(target, PAIR),
+            by_step(probs, PAIR),
+            by_step(routes, PAIR),
+            by_step(mixed_cut, PAIR),
+        ],
+        [((count // PAIR, length, PAIR * local), jnp.bfloat16, (1, length, PAIR * local), lambda p: (p, 0, 0))],
+        [pltpu.VMEM((parts.shape[1], slots), jnp.float32)],
+        flops=4 * count * length * slots * local,
+    )[0]
+
+
+def pull_kernel(
+    router_at,
+    held_ref,
+    images_ref,
+    cot_ref,
+    mixed_ref,
+    probs_ref,
+    routes_ref,
+    gates_ref,
+    rows_ref,
+    attended_ref,
+    proj_ref,
+    packed_ref,
+    vector_ref,
+    grad_mixed_ref,
+    normed_ref,
+    matrix_ref,
+    sums_ref,
+    matrix_sum_ref,
+):
+    f32, bf16 = jnp.float32, jnp.bfloat16
+    pair = images_ref.shape[0]
+    tensor = rows_ref.shape[0]
+    local = attended_ref.shape[2] // pair
+    width = images_ref.shape[2]
+    at = pl.program_id(0)
+
+    @pl.when(at == 0)
+    def _():
+        sums_ref[...] = jnp.zeros_like(sums_ref)
+        matrix_sum_ref[...] = jnp.zeros_like(matrix_sum_ref)
+
+    qkv = packed_ref[:, : 3 * local]
+    out_turned = packed_ref[:, 3 * local : 4 * local]
+    router = packed_ref[:, router_at : router_at + EXPERTS]
+    scale = HEAD_DIM**-0.5
+    for h in range(pair):
+        lanes = slice(h * local, (h + 1) * local)
+        live = (at * pair + h < held_ref[0]).astype(f32)
+        cot = cot_ref[h].astype(f32) * live
+        scaled, inv_std = norm_rows(mixed_ref[h])
+        routed = (scaled * vector_ref[3:4] + vector_ref[4:5]).astype(bf16)
+        probs = probs_ref[h]
+        experts = lax.broadcasted_iota(jnp.int32, probs.shape, 1)
+        grad_probs = jnp.zeros(probs.shape, f32)
+        for k in range(TOPK):
+            match = experts == routes_ref[h, :, k : k + 1]
+            grad_probs = grad_probs + jnp.where(match, gates_ref[h, :, k : k + 1], 0.0)
+        grad_logits = probs * (grad_probs - jnp.sum(probs * grad_probs, axis=-1, keepdims=True))
+        grad_logits = grad_logits.astype(bf16)
+        grad_routed = jnp.concatenate([rows_ref[z, 0, :, lanes] for z in range(tensor)], axis=1)
+        grad_routed = grad_routed.astype(f32) + turned_dot(grad_logits, router, 1, 1)
+        grad_mixed = cot + norm_rows_back(grad_routed, scaled, inv_std, vector_ref[3:4])
+        grad_mixed_ref[h] = grad_mixed
+        low = grad_mixed.astype(bf16)
+        grad_attended = jnp.dot(low, out_turned, preferred_element_type=f32).astype(bf16)
+        proj = proj_ref[h]
+        grads = [[], [], []]
+        for n in range(0, local, HEAD_DIM):
+            queries = proj[:, n : n + HEAD_DIM]
+            keys = proj[:, local + n : local + n + HEAD_DIM]
+            values = proj[:, 2 * local + n : 2 * local + n + HEAD_DIM]
+            grad_head = grad_attended[:, n : n + HEAD_DIM]
+            scores = turned_dot(queries, keys, 1, 1) * scale
+            scores = jnp.exp(scores - jnp.max(scores, axis=-1, keepdims=True))
+            weights = scores / jnp.sum(scores, axis=-1, keepdims=True)
+            grads[2].append(turned_dot(weights.astype(bf16), grad_head, 0, 0))
+            grad_weights = turned_dot(grad_head, values, 1, 1)
+            inner = jnp.sum(weights * grad_weights, axis=-1, keepdims=True)
+            grad_scores = (weights * (grad_weights - inner)).astype(bf16)
+            grads[0].append(jnp.dot(grad_scores, keys, preferred_element_type=f32) * scale)
+            grads[1].append(turned_dot(grad_scores, queries, 0, 0) * scale)
+        grad_proj = jnp.concatenate(grads[0] + grads[1] + grads[2], axis=1)
+        proj_sum = jnp.sum(grad_proj, axis=0, keepdims=True)
+        grad_proj = grad_proj.astype(bf16)
+        first, _ = norm_rows(images_ref[h].astype(f32))
+        normed = (first * vector_ref[0:1] + vector_ref[1:2]).astype(bf16)
+        grad_normed = turned_dot(grad_proj, qkv, 1, 1)
+        normed_ref[h] = grad_normed.astype(bf16)
+        attended = attended_ref[0, :, lanes]
+        matrix = jnp.concatenate(
+            [
+                turned_dot(normed, grad_proj, 0, 0),
+                turned_dot(low, attended, 0, 0),
+                turned_dot(routed, grad_logits, 0, 0),
+            ],
+            axis=1,
+        )
+        matrix_sum_ref[...] += matrix
+        column = lambda values: jnp.sum(values, axis=0, keepdims=True)
+        sums_ref[0:1] += column(grad_normed * first)
+        sums_ref[1:2] += column(grad_normed)
+        sums_ref[2:3] += column(grad_mixed)
+        sums_ref[3:4] += column(grad_routed * scaled)
+        sums_ref[4:5] += column(grad_routed)
+        sums_ref[5:6, : 3 * local] += proj_sum
+
+    @pl.when(at == pl.num_programs(0) - 1)
+    def _():
+        matrix_ref[...] = matrix_sum_ref[...].astype(bf16)
+
+
+def run_pull(held, images, cot, mixed, probs, routes, gates, rows_all, attended, proj, packed, vectors, router_at):
+    f32, bf16 = jnp.float32, jnp.bfloat16
+    count, length, width = images.shape
+    tensor = rows_all.shape[0]
+    local = proj.shape[2] // 3
+    tokens = (count, length, width)
+    block = (PAIR, length, width)
+    step = lambda p: (p, 0, 0)
+    still = lambda p: (0, 0)
+    matrix = (width, 4 * local + EXPERTS)
+    return call_kernel(
+        functools.partial(pull_kernel, router_at),
+        (count // PAIR,),
+        [
+            (held, None, None),
+            by_step(images, PAIR),
+            by_step(cot, PAIR),
+            by_step(mixed, PAIR),
+            by_step(probs, PAIR),
+            by_step(routes, PAIR),
+            by_step(gates, PAIR),
+            (rows_all, (tensor, 1, *rows_all.shape[2:]), lambda p: (0, p, 0, 0)),
+            by_step(attended, 1),
+            by_step(proj, PAIR),
+            whole(packed),
+            whole(vectors),
+        ],
+        [
+            (tokens, f32, block, step),
+            (tokens, bf16, block, step),
+            (matrix, bf16, matrix, still),
+            ((8, width), f32, (8, width), still),
+        ],
+        [pltpu.VMEM(matrix, f32)],
+        flops=2 * count * length * (width * 12 * local + 14 * length * local),
+    )
+
+
+def last_kernel(images_ref, normed_ref, mixed_ref, vector_ref, out_ref):
+    for h in range(images_ref.shape[0]):
+        scaled, inv_std = norm_rows(images_ref[h].astype(jnp.float32))
+        grad = normed_ref[h].astype(jnp.float32)
+        out_ref[h] = mixed_ref[h] + norm_rows_back(grad, scaled, inv_std, vector_ref[0:1])
+
+
+def run_last(images, grad_normed, grad_mixed, vectors):
+    return call_kernel(
+        last_kernel,
+        (images.shape[0],),
+        [by_step(images, 1), by_step(grad_normed, 1), by_step(grad_mixed, 1), whole(vectors)],
+        [(images.shape, jnp.float32, (1, *images.shape[1:]), lambda p: (p, 0, 0))],
+    )[0]
+
+
 def moved_plan(
     images,
     images_held,
@@ -591,23 +1048,23 @@
 ):
     f32, bf16 = jnp.float32, jnp.bfloat16
     image_count, seq_len, width = images.shape
-    rows_total = image_count * seq_len
     experts_here, shard_width, ff_here = w_in.shape
     data, sources = lax.axis_size(DP), lax.axis_size(EXPERT)
     outer, inner = lax.axis_size(OUTER), lax.axis_size(INNER)
     tensor = outer * inner
     tensor_axes = (OUTER, INNER)
+    everywhere = (DP, EXPERT, OUTER, INNER)
     groups = data * sources
     owners = data * inner
     mine = experts_here // owners
     slots = EXPERTS * CAP
-    slots_plane = slots // inner
     dp_at = lax.axis_index(DP)
     inner_at = lax.axis_index(INNER)
     tensor_at = lax.axis_index(tensor_axes)
     owner_at = dp_at * inner + inner_at
     local_width = w_out.shape[0]
     slice_width = width // tensor
+    router_at = 4 * local_width
 
     chunk_shape = (owners, mine, shard_width, ff_here)
     in_raw = swap(w_in, (DP, INNER)).reshape(chunk_shape)
@@ -624,78 +1081,43 @@
         axis=1,
     )
     packed = lax.all_gather(packed, DP, axis=0, tiled=True)
-    packed, in_raw = lax.optimization_barrier((packed, in_raw))
-    cuts = [3 * local_width, local_width, EXPERTS, experts_here]
-    qkv_full, out_turned, router_full, back_bias_turned, vectors = jnp.split(
-        packed, [sum(cuts[: i + 1]) for i in range(4)], axis=1
-    )
-    gain_first, shift_first, bias_out_full, gain_second, shift_second = (
-        vectors[:, i].astype(f32) for i in range(5)
-    )
-    out_whole = hop_gather(out_turned, tensor_axes)
-    out_whole = out_whole.transpose(1, 0, 2).reshape(width, width)
+    vectors = packed[:, router_at + EXPERTS + experts_here :].T.astype(f32)
+    out_whole = hop_gather(w_out, tensor_axes).reshape(width, shard_width)
+    out_whole = hop_gather(out_whole, DP).transpose(1, 0, 2).reshape(width, width)
     in_bias_all = hop_gather(in_bias, INNER)
     in_bias_mine = lax.dynamic_slice_in_dim(in_bias_all, owner_at * mine, mine, 1)
     in_bias_mine = in_bias_mine.transpose(1, 0, 2).astype(f32)
 
-    pair_routes = routes.reshape(rows_total, TOPK)
-    pair_slots = slot_index.reshape(rows_total, TOPK)
-    home, within = pair_routes // experts_here, pair_routes % experts_here
+    home, within = routes // experts_here, routes % experts_here
     owner, nth = within // mine, within % mine
-    place = ((owner // inner) * sources + home) * inner + owner % inner
-    target = jnp.where(pair_slots < CAP, (place * mine + nth) * CAP + pair_slots, slots)
-    plane_slots = jnp.arange(slots, dtype=jnp.int32).reshape(groups, inner, mine * CAP)
-    plane_slots = lax.dynamic_slice_in_dim(plane_slots, inner_at, 1, 1).reshape(slots_plane)
-    takes = [plane_slots[:, None] == target[None, :, k] for k in range(TOPK)]
-    fill = jnp.logical_or(takes[0], takes[1]).astype(bf16)
-
-    live_image = (jnp.arange(image_count, dtype=jnp.int32) < images_held[0]).astype(f32)
-    live_rows = jnp.repeat(live_image, seq_len)[:, None]
-    grad_rows = cotangent.reshape(rows_total, width).astype(f32) * live_rows
-
-    def dispatch(rows):
-        return jnp.dot(fill, rows, preferred_element_type=f32).astype(bf16)
-
-    cot_out = dispatch(grad_rows.astype(bf16)).reshape(groups, mine * CAP, width)
+    kept = slot_index < CAP
+    group_place = (owner // inner) * sources + home
+    target = ((group_place * inner + owner % inner) * mine + nth) * CAP + slot_index
+    target = jnp.where(kept, target, slots)
+    plane_target = (group_place * mine + nth) * CAP + slot_index
+    plane_target = jnp.where(jnp.logical_and(kept, owner % inner == inner_at), plane_target, -1)
+    plane_target = plane_target.transpose(0, 2, 1)
+    cot_out = run_send(cotangent, plane_target, groups, slots // inner)
     cot_rows = swap(cot_out, (DP, EXPERT))
 
-    inputs = images.reshape(rows_total, width).astype(f32)
-    normed, scaled_first, inv_first = norm_parts(inputs, gain_first, shift_first)
-    normed_low = normed.astype(bf16)
-    projected = jnp.dot(normed_low, qkv_full, preferred_element_type=f32)
-    head_count = local_width // HEAD_DIM
-    head_shape = (image_count, seq_len, head_count, HEAD_DIM)
-    bias_pair = qv_bias.astype(f32)
-    queries, key_rows, value_rows = (
-        projected[:, i * local_width : (i + 1) * local_width] for i in range(3)
-    )
-    queries = (queries + bias_pair[0]).astype(bf16).reshape(head_shape)
-    key_rows = key_rows.astype(bf16).reshape(head_shape)
-    value_rows = (value_rows + bias_pair[1]).astype(bf16).reshape(head_shape)
-    scale = HEAD_DIM ** (-0.5)
-    attended, log_total = attention_forward(queries, key_rows, value_rows, scale)
-    attended_low = attended.reshape(rows_total, local_width).astype(bf16)
-    attended_all = lax.all_gather(attended_low, tensor_axes, axis=1, tiled=True)
-    attended_all, back_raw = lax.optimization_barrier((attended_all, back_raw))
-    mixed = inputs + bias_out_full
-    mixed = mixed + jnp.einsum("te,de->td", attended_all, out_whole, preferred_element_type=f32)
-    routed, scaled_second, inv_second = norm_parts(mixed, gain_second, shift_second)
-    routed_low = routed.astype(bf16)
-    logits = jnp.dot(routed_low, router_full, preferred_element_type=f32)
-    probs = jax.nn.softmax(logits, axis=-1)
-    expert_ids = jnp.arange(EXPERTS, dtype=jnp.int32)
-    matches = [(pair_routes[:, k : k + 1] == expert_ids).astype(f32) for k in range(TOPK)]
-    gates = [jnp.sum(match * probs, axis=1) for match in matches]
-
-    gate_slots = sum(
-        jnp.sum(jnp.where(take, gate[None, :], 0.0), axis=1) for take, gate in zip(takes, gates)
-    )
-    gate_parts = jnp.stack(high_low(gate_slots.reshape(groups, mine * CAP)), axis=1)
-    gate_rows = jnp.pad(gate_parts, ((0, 0), (0, 14), (0, width - mine * CAP)))
-    sent = jnp.concatenate([dispatch(routed_low).reshape(groups, mine * CAP, width), gate_rows], axis=1)
-    sent, cot_rows = lax.optimization_barrier((sent, cot_rows))
+    attended, proj = run_attend(images, packed, vectors, qv_bias.astype(f32))
+    attended_all = lax.all_gather(attended, tensor_axes)
+    attended_all, in_raw = lax.optimization_barrier((attended_all, in_raw))
+    mixed, probs, sent = run_route(
+        images,
+        attended_all,
+        out_whole,
+        packed,
+        vectors,
+        routes,
+        plane_target,
+        groups,
+        slots // inner,
+        router_at,
+    )
+    sent, back_raw = lax.optimization_barrier((sent, back_raw))
     arrived = swap(sent, (DP, EXPERT))
-    back_bias_mine = lax.dynamic_slice_in_dim(back_bias_turned, owner_at * mine, mine, 1)
+    back_bias_mine = lax.dynamic_slice_in_dim(packed, router_at + EXPERTS + owner_at * mine, mine, 1)
     back_bias_mine = jnp.where(lax.axis_index(OUTER) == 0, back_bias_mine.astype(f32), 0.0)
     (
         returned_out,
@@ -709,120 +1131,86 @@
         arrived, cot_rows, in_raw, back_raw, in_bias_mine, back_bias_mine, mine, inner, tensor
     )
 
-    everywhere = (DP, EXPERT, OUTER, INNER)
-
     def bring(parts):
-        parts = parts.reshape(groups * tensor, *parts.shape[2:])
-        parts = swap(parts, everywhere).astype(f32)
-        parts = jnp.sum(parts.reshape(groups, outer, inner, *parts.shape[1:]), axis=1)
-        return parts.reshape(groups * inner, *parts.shape[2:])
-
-    def in_line(parts):
-        return parts.transpose(1, 0, 2).reshape(parts.shape[1], slots)
+        return swap(parts.reshape(groups * tensor, *parts.shape[2:]), everywhere)
+
+    def spread(parts):
+        return swap(parts.reshape(owners, *parts.shape[2:]), (DP, INNER))
 
     grad_parts = bring(grads_out)
-    grad_slots = in_line(grad_parts[:, :slice_width]).astype(bf16)
-    gate_slots_back = in_line(grad_parts[:, slice_width : slice_width + 2])
-    gate_slots_back = gate_slots_back[0] + gate_slots_back[1]
-    all_slots = jnp.arange(slots, dtype=jnp.int32)
-    found = [target[None, :, k] == all_slots[:, None] for k in range(TOPK)]
-    finds = [hit.astype(bf16) for hit in found]
-    both = jnp.logical_or(found[0], found[1]).astype(bf16)
-    grad_gates = jnp.stack(
-        [jnp.sum(jnp.where(hit, gate_slots_back[:, None], 0.0), axis=0) for hit in found], axis=1
-    )
-    grad_routed_cut = jnp.dot(grad_slots, both, preferred_element_type=f32).astype(bf16)
+    rows_cut, grad_gates = run_take_grads(grad_parts, target, slice_width, outer, inner, slots)
+    rows_all = lax.all_gather(rows_cut, tensor_axes)
     grad_in_out, grad_back_out = weight_grads(
         arrived, grad_pre_low, grad_turned, hidden_low, grad_in_bias_mine, grad_back_bias_mine, data
     )
-    grad_routed_cut, returned_out, grad_in_out, grad_back_out = lax.optimization_barrier(
-        (grad_routed_cut, returned_out, grad_in_out, grad_back_out)
-    )
-    grad_routed = lax.all_gather(grad_routed_cut, tensor_axes, axis=0, tiled=True).T.astype(f32)
-    returned = in_line(bring(returned_out)).astype(bf16)
-    picked = [jnp.dot(returned, find, preferred_element_type=f32) for find in finds]
-    mixed_cut = lax.dynamic_slice_in_dim(mixed, tensor_at * slice_width, slice_width, 1)
-    expert_mix = gates[0][None, :] * picked[0] + gates[1][None, :] * picked[1]
-    output_cut = (live_rows * (mixed_cut + expert_mix.T)).astype(bf16)
-    output = lax.all_gather(output_cut, tensor_axes, axis=1, tiled=True).reshape(images.shape)
-
-    grad_probs = sum(match * grad_gates[:, k : k + 1] for k, match in enumerate(matches))
-    grad_logits = probs * (grad_probs - jnp.sum(probs * grad_probs, axis=-1, keepdims=True))
-    grad_logits_low = grad_logits.astype(bf16)
-    grad_router = jnp.einsum("td,te->de", routed_low, grad_logits_low, preferred_element_type=f32)
-    grad_routed = grad_routed + jnp.einsum(
-        "te,de->td", grad_logits_low, router_full, preferred_element_type=f32
-    )
-    grad_from_norm, grad_gain_second, grad_shift_second = norm_back(
-        grad_routed, scaled_second, inv_second, gain_second
-    )
-    grad_mixed = grad_rows + grad_from_norm
-    grad_bias_out = jnp.sum(grad_mixed, axis=0)
-    grad_mixed_low = grad_mixed.astype(bf16)
-    grad_out_turned = jnp.einsum("td,te->de", grad_mixed_low, attended_low, preferred_element_type=f32)
-    grad_attended = jnp.dot(grad_mixed_low, out_turned, preferred_element_type=f32)
-    grad_attended = grad_attended.astype(bf16).reshape(head_shape)
-    grad_queries, grad_keys, grad_values = (
-        grads.reshape(rows_total, local_width)
-        for grads in attention_backward(
-            queries, key_rows, value_rows, log_total, grad_attended, scale
-        )
-    )
-    grad_pair_bias = jnp.stack([jnp.sum(grad_queries, axis=0), jnp.sum(grad_values, axis=0)])
-    grad_proj_low = jnp.concatenate([grad_queries, grad_keys, grad_values], axis=1).astype(bf16)
-    grad_qkv = jnp.einsum("td,te->de", normed_low, grad_proj_low, preferred_element_type=f32)
-    grad_normed_part = jnp.einsum("te,de->td", grad_proj_low, qkv_full, preferred_element_type=f32)
-    grad_normed = lax.psum(grad_normed_part.astype(bf16), tensor_axes).astype(f32)
-    grad_from_first, _, _ = norm_back(grad_normed, scaled_first, inv_first, gain_first)
-    first_terms = jnp.stack(
-        [jnp.sum(grad_normed_part * scaled_first, axis=0), jnp.sum(grad_normed_part, axis=0)]
-    )
-    grad_images = (grad_mixed + grad_from_first).reshape(images.shape)
-
-    def spread(parts):
-        return swap(parts.reshape(owners, *parts.shape[2:]), (DP, INNER)).astype(f32)
-
-    experts_shape = (experts_here, shard_width, ff_here)
+    rows_cut, grad_in_out = lax.optimization_barrier((rows_cut, grad_in_out))
     grad_in_parts = spread(grad_in_out)
-    grad_w_in = grad_in_parts[:, : mine * shard_width].reshape(experts_shape)
-    lines = grad_in_parts[:, mine * shard_width :]
-    grad_in_bias = lines[:, : 2 * mine].reshape(owners, mine, 2, ff_here)
-    grad_in_bias = jnp.sum(grad_in_bias, axis=2).reshape(experts_here, ff_here)
-    lines = lines[:, 2 * mine : 3 * mine].reshape(experts_here, 2, ff_here // 2)
-    grad_back_shard = jnp.sum(lines[:, :, :shard_width], axis=1)
-    early = jnp.concatenate(
-        [grad_qkv.astype(bf16), grad_out_turned.astype(bf16), grad_router.astype(bf16)], axis=1
-    )
+    rows_all, grad_in_parts = lax.optimization_barrier((rows_all, grad_in_parts))
+    grad_mixed, normed_part, matrix, sums = run_pull(
+        images_held,
+        images,
+        cotangent,
+        mixed,
+        probs,
+        routes,
+        grad_gates,
+        rows_all,
+        attended,
+        proj,
+        packed,
+        vectors,
+        router_at,
+    )
+    grad_normed = lax.psum(normed_part, tensor_axes)
+    grad_images = run_last(images, grad_normed, grad_mixed, vectors)
+
+    normed_part, returned_out = lax.optimization_barrier((normed_part, returned_out))
+    returned = bring(returned_out)
+    mixed_cut = lax.dynamic_slice_in_dim(mixed, tensor_at * slice_width, slice_width, 2)
+    output_cut = run_take_rows(
+        images_held, returned, target, probs, routes, mixed_cut, outer, inner, slots
+    )
+    output = lax.all_gather(output_cut, tensor_axes)
+    output = output.reshape(tensor, image_count // PAIR, seq_len, PAIR, slice_width)
+    output = output.transpose(1, 3, 2, 0, 4).reshape(images.shape)
+
+    matrix, returned = lax.optimization_barrier((matrix, returned))
+    early = swap(matrix.reshape(groups, shard_width // sources, -1), (DP, EXPERT))
     early, grad_back_out = lax.optimization_barrier((early, grad_back_out))
-    early = swap(early.reshape(groups, shard_width // sources, -1), (DP, EXPERT))
-    early, grad_back_out = lax.optimization_barrier((early, grad_back_out))
-    grad_w_back = spread(grad_back_out).reshape(experts_shape).transpose(0, 2, 1)
+    grad_back_parts = spread(grad_back_out)
     early = jnp.sum(early.astype(f32), axis=0)
     early = hop_gather(early, EXPERT).reshape(shard_width, -1)
     grad_w_qkv = early[:, : 3 * local_width].reshape(shard_width, 3, local_width).transpose(1, 0, 2)
     grad_w_out = early[:, 3 * local_width : 4 * local_width].T
     grad_w_router = early[:, 4 * local_width :]
+    experts_shape = (experts_here, shard_width, ff_here)
+    grad_w_in = grad_in_parts[:, : mine * shard_width].astype(f32).reshape(experts_shape)
+    grad_w_back = grad_back_parts.astype(f32).reshape(experts_shape).transpose(0, 2, 1)
+    lines = grad_in_parts[:, mine * shard_width :].astype(f32)
+    grad_in_bias = lines[:, : 2 * mine].reshape(owners, mine, 2, ff_here)
+    grad_in_bias = jnp.sum(grad_in_bias, axis=2).reshape(experts_here, ff_here)
+    lines = lines[:, 2 * mine : 3 * mine].reshape(experts_here, 2, ff_here // 2)
+    grad_back_shard = jnp.sum(lines[:, :, :shard_width], axis=1)
     once = (tensor_at == 0).astype(f32)
+    pair_bias = jnp.stack([sums[5, :local_width], sums[5, 2 * local_width : 3 * local_width]])
     pair_bias = lax.dynamic_update_slice(
-        jnp.zeros((2, width), f32), grad_pair_bias, (0, tensor_at * local_width)
-    )
-    vectors = [grad_bias_out, grad_gain_second, grad_shift_second]
-    vectors = jnp.concatenate([first_terms, pair_bias, once * jnp.stack(vectors)], axis=0)
-    vectors = lax.psum(vectors, everywhere)
-    grad_qv_bias = lax.dynamic_slice_in_dim(vectors[2:4], tensor_at * local_width, local_width, 1)
-    vectors = lax.dynamic_slice_in_dim(vectors, dp_at * shard_width, shard_width, 1)
-    grad_first_gain, grad_first_shift, _, _, grad_out_bias, grad_second_gain, grad_second_shift = vectors
+        jnp.zeros((2, width), f32), pair_bias, (0, tensor_at * local_width)
+    )
+    totals = jnp.concatenate([sums[0:2], pair_bias, once * sums[2:5]], axis=0)
+    totals = lax.psum(totals, everywhere)
+    grad_qv_bias = lax.dynamic_slice_in_dim(totals[2:4], tensor_at * local_width, local_width, 1)
+    totals = lax.dynamic_slice_in_dim(totals, dp_at * shard_width, shard_width, 1)
     return (
         output,
         grad_images,
-        grad_first_gain,
-        grad_first_shift,
+        totals[0],
+        totals[1],
         grad_w_qkv,
         grad_qv_bias,
         grad_w_out,
-        grad_out_bias,
-        grad_second_gain,
-        grad_second_shift,
+        totals[4],
+        totals[5],
+        totals[6],
         grad_w_router,
         grad_w_in,
         grad_in_bias,
@@ -846,7 +1234,8 @@
 def solution(mesh):
     data, expert, tensor = (mesh.shape[name] for name in (DP, EXPERT, TENSOR))
     inner = FF_PAIR if tensor % FF_PAIR == 0 else 1
-    if (EXPERTS // expert) % (data * inner):
+    owners = data * inner
+    if (EXPERTS // expert) % owners or owners & (owners - 1):
         taken, given = specs(TENSOR)
         return jax.shard_map(
             gathered_plan, mesh=mesh, in_specs=taken, out_specs=given, check_vma=False

time: 732 us -> 645 us (0.88)
  waiting for transfers between devices: 290 us -> 181 us
  Pallas kernels: 31.9 us -> 94.2 us
  blocking collectives: 162 us -> 220 us
  matrix products: 42.9 us -> 0 us
  local copies, waits for them, and re-layouts: 79.5 us -> 49.8 us
  other arithmetic: 48.1 us -> 22.5 us
    psum x1, waiting for transfers between devices: 84.3 us -> 0.01 us  [moved_plan(): grad_normed = lax.psum(normed_part, tensor_axes)]
    pallas_call x0 -> x7, Pallas kernels: none -> 62.5 us  [call_kernel(): pl.pallas_call(kernel, grid=grid, in_specs=[smem if b is None else pl.Blo...]
    psum x1, blocking collectives: 40.3 us -> 98.4 us  [moved_plan(): totals = lax.psum(totals, everywhere)]
    dot_general x20 -> x0, matrix products: 42.9 us -> none  [the longest x2 7.61 us: dispatch(): return jnp.dot(fill, rows, preferred_element_type=f32).astype(bf16)]
    all_to_all x6, waiting for transfers between devices: 99.5 us -> 61.7 us  [swap(): return lax.all_to_all(values, axes, split_axis=0, concat_axis=0, tiled=True)]
    all_gather x3, waiting for transfers between devices: 26.7 us -> 49.6 us  [the longest x1 49.6 us: moved_plan(): rows_all = lax.all_gather(rows_cut, tensor_axes)]
    convert_element_type x7 -> x0, local copies, waits for them, and re-layouts: 19.5 us -> none  [the longest x2 9.39 us: moved_plan(): grad_rows = cotangent.reshape(rows_total, width).astype(f32) * live_rows]
    reduce_sum x13 -> x0, other arithmetic: 18.2 us -> none  [the longest x1 3.79 us: moved_plan(): jnp.sum(grad_normed_part * scaled_first, axis=0)]
  transfers between devices with their start and end apart: 16 -> 19, of which waited for: 10 -> 11; matrix products, arithmetic and copies ran while one was open for 18% -> 10% of each run, Pallas kernels for 2% -> 7%
where the time goes in v5:
time: 645 us; the launch traced here: 636 us
  blocking collectives  220 us (34%)
  waiting for transfers between devices  181 us (28%)
  Pallas kernels  94.2 us (15%)
  starting transfers between devices  52.8 us (8%)
  local copies, waits for them, and re-layouts  49.8 us (8%)
  other arithmetic  22.5 us (3%)
  between operations  15.4 us (2%)
    all_to_all x3, blocking collectives, swap(): return lax.all_to_all(values, axes, split_axis=0, concat_axis=0, tiled=True)  122 us
    psum x1, blocking collectives, moved_plan(): totals = lax.psum(totals, everywhere)  98.4 us
    pallas_call x7, Pallas kernels, call_kernel(): pl.pallas_call(kernel, grid=grid, in_specs=[smem if b is None else pl.Blo...  62.5 us
    all_to_all x6, waiting for transfers between devices, swap(): return lax.all_to_all(values, axes, split_axis=0, concat_axis=0, tiled=True)  61.7 us
    all_gather x1, waiting for transfers between devices, moved_plan(): rows_all = lax.all_gather(rows_cut, tensor_axes)  49.6 us
    all_gather x1, waiting for transfers between devices, moved_plan(): packed = lax.all_gather(packed, DP, axis=0, tiled=True)  49.2 us
    all_to_all x6, starting transfers between devices, swap(): return lax.all_to_all(values, axes, split_axis=0, concat_axis=0, tiled=True)  33.6 us
    ppermute x8, waiting for transfers between devices, hop_gather(): lax.ppermute(values, axes, [(i, (i + s) % count) for i in range(count)])  19.5 us
  transfers between devices with their start and end apart: 19, of which 11 were waited for; matrix products, arithmetic and copies ran while one was open for 10% of the time, Pallas kernels for 7%

profile of v5, /device:TPU:0, one launch (start us, length us, event | category | flops | bytes accessed | tf_op | source)
XLA Modules:
  0.0 635.9 jit_solution(1995663495807385866)
XLA Ops:
  7.2 59.3 %all_to_all.45 = bf16[16,192,768]{2,1,0:T(8,128)(2,1)} all-to-all(bf16[16,192,768]{2,1,0:T(8,128)(2,1)} %param.31), channel_id=1, replica_groups=mesh['dp'=4,'expert'=2,'outer'=2,'inner'=2] {'dp','inner'}, dimensions={0} | all-to-all | bytes 9437184 | tf_op jit(solution)/shard_map/all_to_all | solution.py:351
  78.8 49.2 %all-gather.8.cloned.1.call-done.packed_ref = bf16[768,821]{1,0:T(8,128)(2,1)} async-done(((bf16[192,821]{1,0:T(8,128)(2,1)}), bf16[768,821]{1,0:T(8,128)(2,1)}) %all-gather.8.cloned.1.call-update) | async-done | bytes 1261072 | tf_op jit(solution)/shard_map/all_gather | solution.py:1083
  129.8 6.6 %shard_map.289 = (bf16[2,197,384]{2,1,0:T(8,128)(2,1)}, bf16[4,197,576]{2,1,0:T(8,128)(2,1)}) custom-call(bf16[4,197,768]{2,1,0:T(8,128)(2,1)} %copy.267.images_ref, bf16[768,821]{1,0:T(8,128)(2,1)} %all-gather.8.cloned.1.call-done.packed_ref, f32[5,768]{1,0:T(8,128)} %convert_bitcast_fusion.1.vector_ref, f32[2,192]{1,0:T(2,128)} %convert_element_type.29.bias_ref), custom_call_target="tpu_custom_call" | custom-call | flops 935614464 | bytes 2488320 | tf_op jit(solution)/shard_map/pallas_call | solution.py:587
  156.6 6.1 collective-permute-done.1
  188.6 13.3 %shard_map.290 = (f32[4,197,768]{2,1,0:T(8,128)}, f32[4,197,32]{2,1,0:T(8,128)}, bf16[8,144,768]{2,1,0:T(8,128)(2,1)}) custom-call(bf16[4,197,768]{2,1,0:T(8,128)(2,1)} %copy.267.images_ref, bf16[4,2,197,384]{3,2,1,0:T(8,128)(2,1)} %bitcast.104, bf16[768,768]{1,0:T(8,128)(2,1)} %copy.257.out_ref, bf16[768,821]{1,0:T(8,128)(2,1)} %all-gather.8.cloned.1.call-done.packed_ref, ...), custom_call_target="tpu_custom_call" | custom-call | flops 2168979456 | bytes 4889408 | tf_op jit(solution)/shard_map/pallas_call | solution.py:587
  207.1 7.8 %collective-permute-start.6 = (bf16[16,768]{1,0:T(8,128)(2,1)S(1)}, bf16[16,768]{1,0:T(8,128)(2,1)S(1)}, u32[]{:S(2)}, u32[]{:S(2)}) collective-permute-start(bf16[16,768]{1,0:T(8,128)(2,1)S(1)} %copy-done.12), channel_id=1, source_target_pairs={{0,1},{1,0},{2,3},{3,2},{4,5},{5,4},{6,7},{7,6},{8,9},{9,8},{10,11... | collective-permute-start | bytes 73736 | tf_op jit(solution)/shard_map/ppermute | solution.py:360
  219.9 9.4 %all-to-all-done.2.rows_ref.gate_ref = bf16[8,144,768]{2,1,0:T(8,128)(2,1)S(1)} async-done(((bf16[8,144,768]{2,1,0:T(8,128)(2,1)}), bf16[8,144,768]{2,1,0:T(8,128)(2,1)S(1)}, u32[]{:S(2)}, u32[]{:S(2)}) %all-to-all-start.2) | async-done | bytes 1769504 | tf_op jit(solution)/shard_map/all_to_all | solution.py:351
  230.6 18.9 %shard_map.292 = (bf16[8,4,192,128]{3,2,1,0:T(8,128)(2,1)}, bf16[8,4,208,128]{3,2,1,0:T(8,128)(2,1)}, bf16[2,2,512,768]{3,2,1,0:T(8,128)(2,1)}, bf16[2,2,512,768...) custom-call(bf16[8,144,768]{2,1,0:T(8,128)(2,1)} %copy-done.1, ...), custom_call_target="tpu_custom_call" | custom-call | flops 9663676416 | bytes 28311552 | tf_op jit(solution)/shard_map/pallas_call | solution.py:469
  249.5 11.9 %all-to-all-start.4 = ((bf16[32,208,128]{2,1,0:T(8,128)(2,1)}), bf16[32,208,128]{2,1,0:T(8,128)(2,1)S(1)}, u32[]{:S(2)}, u32[]{:S(2)}) async-start(bf16[32,208,128]{2,1,0:T(8,128)(2,1)} %bitcast.81), calls=%async_computation.4 | async-start | bytes 3407872 | tf_op jit(solution)/shard_map/all_to_all | solution.py:351
  262.0 12.8 %shard_map.294 = (bf16[4,2,400,768]{3,2,1,0:T(8,128)(2,1)}, bf16[4,2,384,768]{3,2,1,0:T(8,128)(2,1)}) custom-call(bf16[8,144,768]{2,1,0:T(8,128)(2,1)} %copy-done.1, bf16[2,2,512,768]{3,2,1,0:T(8,128)(2,1)} %get-tuple-element.57.grad_pre_ref, bf16[2,768,512]{2,1,0:T(8,128)(2,1)} %get-tuple-element.58.grad_turned_ref, ...), custom_call_target="tpu_custom_call" | custom-call | flops 4831838208 | bytes 15728640 | tf_op jit(solution)/shard_map/pallas_call | solution.py:548
  274.8 27.1 %all-to-all-done.4.parts_ref = bf16[32,208,128]{2,1,0:T(8,128)(2,1)S(1)} async-done(((bf16[32,208,128]{2,1,0:T(8,128)(2,1)}), bf16[32,208,128]{2,1,0:T(8,128)(2,1)S(1)}, u32[]{:S(2)}, u32[]{:S(2)}) %all-to-all-start.4) | async-done | bytes 1703968 | tf_op jit(solution)/shard_map/all_to_all | solution.py:351
  303.1 6.2 shard_map.293
  309.3 4.8 all-to-all-start.5
  315.5 49.6 %all-gather.12.cloned.1.call-done = bf16[8,197,384]{2,1,0:T(8,128)(2,1)} async-done(((bf16[2,197,384]{2,1,0:T(8,128)(2,1)}), bf16[8,197,384]{2,1,0:T(8,128)(2,1)}) %all-gather.12.cloned.1.call-update) | async-done | bytes 1210384 | tf_op jit(solution)/shard_map/all_gather | solution.py:1142
  365.1 25.1 %all-to-all-done.5 = bf16[8,400,768]{2,1,0:T(8,128)(2,1)} async-done(((bf16[8,400,768]{2,1,0:T(8,128)(2,1)}), bf16[8,400,768]{2,1,0:T(8,128)(2,1)}, u32[]{:S(2)}, u32[]{:S(2)}) %all-to-all-start.5) | async-done | bytes 4915232 | tf_op jit(solution)/shard_map/all_to_all | solution.py:351
  390.2 21.4 %shard_map.295 = (f32[4,197,768]{2,1,0:T(8,128)}, bf16[4,197,768]{2,1,0:T(8,128)(2,1)}, bf16[768,800]{1,0:T(8,128)(2,1)}, f32[8,768]{1,0:T(8,128)}) custom-call(s32[1]{0:T(128)S(6)} %copy.369.held_ref, bf16[4,197,768]{2,1,0:T(8,128)(2,1)} %copy.267.images_ref, bf16[4,197,768]{2,1,0:T(8,128)(2,1)} %copy.268.rows_ref.cot_ref, ...), custom_call_target="tpu_custom_call" | custom-call | flops 3623236608 | bytes 8652100 | tf_op jit(solution)/shard_map/pallas_call | solution.py:587
  411.6 41.1 %all_to_all.46.parts_ref = bf16[32,192,128]{2,1,0:T(8,128)(2,1)} all-to-all(bf16[32,192,128]{2,1,0:T(8,128)(2,1)S(1)} %bitcast.82), channel_id=1, replica_groups=mesh['dp'=4,'expert'=2,'outer'=2,'inner'=2] {'dp','expert','outer','inner'}, dimensions={0} | all-to-all | bytes 3145728 | tf_op jit(solution)/shard_map/all_to_all | solution.py:351
  452.7 21.2 %all_to_all.47 = bf16[8,96,800]{2,1,0:T(8,128)(2,1)S(1)} all-to-all(bf16[8,96,800]{2,1,0:T(8,128)(2,1)S(1)} %bitcast.83), channel_id=1, replica_groups=mesh['dp'=4,'expert'=2,'outer'=2,'inner'=2] {'dp','expert'}, dimensions={0} | all-to-all | bytes 2457600 | tf_op jit(solution)/shard_map/all_to_all | solution.py:351
  481.6 4.8 slice.71
  487.5 5.2 shard_map.296
  493.0 98.4 %psum.15 = f32[7,768]{1,0:T(8,128)S(1)} all-reduce(f32[7,768]{1,0:T(8,128)S(1)} %pad_maximum_fusion), channel_id=1, replica_groups=mesh['dp'=4,'expert'=2,'outer'=2,'inner'=2] {'dp','expert','outer','inner'}, use_global_device_ids=true, to_apply=%region_1.2 | all-reduce | flops 5376 | bytes 43008 | tf_op jit(solution)/shard_map/psum | solution.py:1200
  591.4 7.1 %convert.5 = f32[16,192,768]{2,1,0:T(8,128)} convert(bf16[16,192,768]{2,1,0:T(8,128)(2,1)} %bitcast.70) | non-fusion elementwise | flops 2359296 | bytes 14155776 | tf_op jit(solution)/shard_map/reshape | solution.py:1187
  604.0 5.2 shard_map.297
  622.1 7.1 %convert_bitcast_fusion = f32[16,768,192]{1,2,0:T(8,128)} fusion(bf16[16,192,768]{2,1,0:T(8,128)(2,1)} %bitcast.46), kind=kLoop, calls=%fused_computation | loop fusion | flops 2359296 | bytes 14155776 | tf_op jit(solution)/shard_map/transpose | solution.py:1188
  (168 shorter events, 100.8 us)
Async XLA Ops:
  66.6 76.7 %all-to-all-start.1 = ((bf16[16,192,768]{2,1,0:T(8,128)(2,1)}), bf16[16,192,768]{2,1,0:T(8,128)(2,1)}, u32[]{:S(2)}, u32[]{:S(2)}) async-start(bf16[16,192,768]{2,1,0:T(8,128)(2,1)} %bitcast.73), calls=%async_computation.1 | async-start | bytes 9437184 | tf_op jit(solution)/shard_map/all_to_all | solution.py:351
  71.3 56.7 %all-gather.8.cloned.1.call-start = ((), (), s32[]{:S(2)}) async-start(), calls=%async_computation.9 | async-start | bytes 1720320 | tf_op jit(solution)/shard_map/all_gather | solution.py:1083
  72.8 115.8 %all-gather.10.cloned.1.call-start = ((), (), s32[]{:S(2)}) async-start(), calls=%async_computation.11 | async-start | bytes 1536000 | tf_op jit(solution)/shard_map/all_gather | solution.py:1104
  76.3 60.9 %copy-start = (s32[4,197,2]{2,1,0:T(8,128)}, s32[4,197,2]{2,1,0:T(8,128)S(1)}, u32[]{:S(2)}) copy-start(s32[4,197,2]{2,1,0:T(8,128)S(1)} %copy.258.routes_ref) | copy-start | bytes 18916
  143.3 58.6 %all-to-all-start.3 = ((bf16[8,128,768]{2,1,0:T(8,128)(2,1)}), bf16[8,128,768]{2,1,0:T(8,128)(2,1)S(1)}, u32[]{:S(2)}, u32[]{:S(2)}) async-start(bf16[8,128,768]{2,1,0:T(8,128)(2,1)} %shard_map.291), calls=%async_computation.3 | async-start | bytes 3145728 | tf_op jit(solution)/shard_map/all_to_all | solution.py:351
  146.9 9.6 %collective-permute-start = (bf16[192,192]{1,0:T(8,128)(2,1)S(1)}, bf16[192,192]{1,0:T(8,128)(2,1)S(1)}, u32[]{:S(2)}, u32[]{:S(2)}) collective-permute-start(bf16[192,192]{1,0:T(8,128)(2,1)S(1)} %copy-done.8), channel_id=1, source_target_pairs={{0,1},{1,2},{2,3},{3,0},{4,5},{5,6},{6,7},{7,4},{8,9},{9,10},{10,1... | collective-permute-start | bytes 221192 | tf_op jit(solution)/shard_map/ppermute | solution.py:360
  146.9 15.8 %collective-permute-start.1 = (bf16[192,192]{1,0:T(8,128)(2,1)S(1)}, bf16[192,192]{1,0:T(8,128)(2,1)S(1)}, u32[]{:S(2)}, u32[]{:S(2)}) collective-permute-start(bf16[192,192]{1,0:T(8,128)(2,1)S(1)} %copy-done.8), channel_id=1, source_target_pairs={{0,2},{1,3},{2,0},{3,1},{4,6},{5,7},{6,4},{7,5},{8,10},{9,11},{10,... | collective-permute-start | bytes 221192 | tf_op jit(solution)/shard_map/ppermute | solution.py:360
  149.4 13.5 %collective-permute-start.2 = (bf16[192,192]{1,0:T(8,128)(2,1)S(1)}, bf16[192,192]{1,0:T(8,128)(2,1)S(1)}, u32[]{:S(2)}, u32[]{:S(2)}) collective-permute-start(bf16[192,192]{1,0:T(8,128)(2,1)S(1)} %copy-done.8), channel_id=1, source_target_pairs={{0,3},{1,0},{2,1},{3,2},{4,7},{5,4},{6,5},{7,6},{8,11},{9,8},{10,9... | collective-permute-start | bytes 221192 | tf_op jit(solution)/shard_map/ppermute | solution.py:360
  172.1 8.5 %collective-permute-start.3 = (bf16[768,192]{0,1:T(8,128)(2,1)}, bf16[768,192]{0,1:T(8,128)(2,1)S(1)}, u32[]{:S(2)}, u32[]{:S(2)}) collective-permute-start(bf16[768,192]{0,1:T(8,128)(2,1)} %reshape.93), channel_id=1, source_target_pairs={{0,8},{8,16},{16,24},{24,0},{1,9},{9,17},{17,25},{25,1},{2,10},{10... | collective-permute-start | bytes 884744 | tf_op jit(solution)/shard_map/ppermute | solution.py:360
  172.5 10.2 %collective-permute-start.4 = (bf16[768,192]{0,1:T(8,128)(2,1)}, bf16[768,192]{0,1:T(8,128)(2,1)S(1)}, u32[]{:S(2)}, u32[]{:S(2)}) collective-permute-start(bf16[768,192]{0,1:T(8,128)(2,1)} %reshape.93), channel_id=1, source_target_pairs={{0,16},{8,24},{16,0},{24,8},{1,17},{9,25},{17,1},{25,9},{2,18},{10... | collective-permute-start | bytes 884744 | tf_op jit(solution)/shard_map/ppermute | solution.py:360
  174.1 13.0 %collective-permute-start.5 = (bf16[768,192]{0,1:T(8,128)(2,1)}, bf16[768,192]{0,1:T(8,128)(2,1)S(1)}, u32[]{:S(2)}, u32[]{:S(2)}) collective-permute-start(bf16[768,192]{0,1:T(8,128)(2,1)} %reshape.93), channel_id=1, source_target_pairs={{0,24},{8,0},{16,8},{24,16},{1,25},{9,1},{17,9},{25,17},{2,26},{10... | collective-permute-start | bytes 884744 | tf_op jit(solution)/shard_map/ppermute | solution.py:360
  203.1 26.3 %all-to-all-start.2 = ((bf16[8,144,768]{2,1,0:T(8,128)(2,1)}), bf16[8,144,768]{2,1,0:T(8,128)(2,1)S(1)}, u32[]{:S(2)}, u32[]{:S(2)}) async-start(bf16[8,144,768]{2,1,0:T(8,128)(2,1)} %get-tuple-element.51), calls=%async_computation.2 | async-start | bytes 3538944 | tf_op jit(solution)/shard_map/all_to_all | solution.py:351
  207.1 9.7 %collective-permute-start.6 = (bf16[16,768]{1,0:T(8,128)(2,1)S(1)}, bf16[16,768]{1,0:T(8,128)(2,1)S(1)}, u32[]{:S(2)}, u32[]{:S(2)}) collective-permute-start(bf16[16,768]{1,0:T(8,128)(2,1)S(1)} %copy-done.12), channel_id=1, source_target_pairs={{0,1},{1,0},{2,3},{3,2},{4,5},{5,4},{6,7},{7,6},{8,9},{9,8},{10,11... | collective-permute-start | bytes 73736 | tf_op jit(solution)/shard_map/ppermute | solution.py:360
  249.5 11.9 %copy-start.15 = (f32[2,2,768]{2,1,0:T(2,128)S(1)}, f32[2,2,768]{2,1,0:T(2,128)}, u32[]{:S(2)}) copy-start(f32[2,2,768]{2,1,0:T(2,128)} %get-tuple-element.60) | copy-start | bytes 36868
  249.5 52.4 %all-to-all-start.4 = ((bf16[32,208,128]{2,1,0:T(8,128)(2,1)}), bf16[32,208,128]{2,1,0:T(8,128)(2,1)S(1)}, u32[]{:S(2)}, u32[]{:S(2)}) async-start(bf16[32,208,128]{2,1,0:T(8,128)(2,1)} %bitcast.81), calls=%async_computation.4 | async-start | bytes 3407872 | tf_op jit(solution)/shard_map/all_to_all | solution.py:351
  309.3 80.9 %all-to-all-start.5 = ((bf16[8,400,768]{2,1,0:T(8,128)(2,1)}), bf16[8,400,768]{2,1,0:T(8,128)(2,1)}, u32[]{:S(2)}, u32[]{:S(2)}) async-start(bf16[8,400,768]{2,1,0:T(8,128)(2,1)} %bitcast.72), calls=%async_computation.5 | async-start | bytes 9830400 | tf_op jit(solution)/shard_map/all_to_all | solution.py:351
  314.1 50.9 %all-gather.12.cloned.1.call-start = ((), (), s32[]{:S(2)}) async-start(), calls=%async_computation.12 | async-start | bytes 1536000 | tf_op jit(solution)/shard_map/all_gather | solution.py:1142
  390.2 21.4 %copy-start.4 = (bf16[8,4,192,128]{3,2,1,0:T(8,128)(2,1)S(1)}, bf16[8,4,192,128]{3,2,1,0:T(8,128)(2,1)}, u32[]{:S(2)}) copy-start(bf16[8,4,192,128]{3,2,1,0:T(8,128)(2,1)} %get-tuple-element.68) | copy-start | bytes 4718596
  411.6 41.1 %copy-start.5 = (bf16[768,800]{1,0:T(8,128)(2,1)S(1)}, bf16[768,800]{1,0:T(8,128)(2,1)}, u32[]{:S(2)}) copy-start(bf16[768,800]{1,0:T(8,128)(2,1)} %get-tuple-element.72) | copy-start | bytes 3686404
  473.9 148.2 %all-to-all-start.8 = ((bf16[8,384,768]{2,1,0:T(8,128)(2,1)}), bf16[8,384,768]{2,1,0:T(8,128)(2,1)}, u32[]{:S(2)}, u32[]{:S(2)}) async-start(bf16[8,384,768]{2,1,0:T(8,128)(2,1)} %bitcast.75), calls=%async_computation.8 | async-start | bytes 9437184 | tf_op jit(solution)/shard_map/all_to_all | solution.py:351
  478.5 125.5 %all-reduce.2.cloned.1.call-start = ((), (), s32[]{:S(2)}) async-start(), calls=%async_computation.10 | async-start | bytes 2457600 | tf_op jit(solution)/shard_map/psum | solution.py:1164
  479.1 137.3 %all-gather.14.cloned.1.call-start = ((), (), s32[]{:S(2)}) async-start(), calls=%async_computation.13 | async-start | bytes 1536000 | tf_op jit(solution)/shard_map/all_gather | solution.py:1173
  481.6 5.9 copy-start.13
  601.0 12.3 %collective-permute-start.7 = (f32[96,800]{1,0:T(8,128)S(1)}, f32[96,800]{1,0:T(8,128)S(1)}, u32[]{:S(2)}, u32[]{:S(2)}) collective-permute-start(f32[96,800]{1,0:T(8,128)S(1)} %convert_reduce_fusion), channel_id=1, source_target_pairs={{0,4},{4,0},{1,5},{5,1},{2,6},{6,2},{3,7},{7,3},{8,12},{12,8},{9,1... | collective-permute-start | bytes 921608 | tf_op jit(solution)/shard_map/ppermute | solution.py:360
  (18 other events, 63.2 us)
Sparse Core Ops, SparseCore 0:
  74.3 53.6 all-gather.7
  136.6 38.9 all-gather.9
  317.1 47.9 all-gather.11
  481.4 88.7 all-reduce.1
  571.7 31.7 all-gather.13

commit v6 on v5

--- a/solution.py
+++ b/solution.py
@@ -353,13 +353,21 @@
 
 def hop_gather(values, axes):
     count, at = lax.axis_size(axes), lax.axis_index(axes)
-    gathered = jnp.zeros((count, *values.shape), values.dtype)
-    for s in range(count):
-        hop = values
-        if s:
-            hop = lax.ppermute(values, axes, [(i, (i + s) % count) for i in range(count)])
-        gathered = lax.dynamic_update_slice_in_dim(gathered, hop[None], (at - s) % count, 0)
+    hops = [values]
+    for s in range(1, count):
+        hops.append(lax.ppermute(values, axes, [(i, i ^ s) for i in range(count)]))
+    gathered = []
+    for i in range(count):
+        found = hops[0]
+        for s in range(1, count):
+            found = jnp.where(at ^ i == s, hops[s], found)
+        gathered.append(found)
     return gathered
+
+
+def high_low(values):
+    high = lax.reduce_precision(values, 8, 7)
+    return high.astype(jnp.bfloat16), (values - high).astype(jnp.bfloat16)
 
 
 def turned_dot(left, right, left_dim, right_dim):
@@ -450,16 +458,16 @@
                     grads_ref[g, z, slice_width:, lanes] = tail[:, mine_lanes]
 
 
-def run_experts(arrived, cot_rows, in_raw, back_raw, in_bias, back_bias, mine, inner, tensor):
+def run_experts(arrived, in_raw, back_raw, in_bias, back_bias, inner, tensor):
     f32, bf16 = jnp.float32, jnp.bfloat16
-    groups, _, width = cot_rows.shape
-    chunks, _, depth, ff = in_raw.shape
+    groups, _, width = arrived.shape
+    chunks, mine, depth, ff = in_raw.shape
     total = groups * CAP
     slice_width = width // tensor
-    gate_at = mine * CAP // 16
+    gate_at = 2 * mine * CAP // EXTRA
     outs = [
         ((groups, tensor, slice_width, mine * CAP), bf16, lambda j: (0, 0, 0, 0), None),
-        ((groups, tensor, slice_width + 16, mine * CAP), bf16, lambda j: (0, 0, 0, 0), None),
+        ((groups, tensor, slice_width + EXTRA, mine * CAP), bf16, lambda j: (0, 0, 0, 0), None),
         ((mine, inner, total, ff), bf16, lambda j: (j, 0, 0, 0), 1),
         ((mine, inner, total, ff), bf16, lambda j: (j, 0, 0, 0), 1),
         ((mine, width, total), bf16, lambda j: (j, 0, 0), 1),
@@ -471,8 +479,8 @@
         grid=(mine,),
         in_specs=[
             pl.BlockSpec((groups, CAP, width), lambda j: (0, j, 0)),
-            pl.BlockSpec((groups, 16, mine * CAP), lambda j: (0, gate_at, 0)),
-            pl.BlockSpec((groups, CAP, width), lambda j: (0, j, 0)),
+            pl.BlockSpec((groups, EXTRA, mine * CAP), lambda j: (0, gate_at, 0)),
+            pl.BlockSpec((groups, CAP, width), lambda j: (0, mine + j, 0)),
             pl.BlockSpec((chunks, 1, depth, ff), lambda j: (0, j, 0, 0)),
             pl.BlockSpec((chunks, 1, depth, ff), lambda j: (0, j, 0, 0)),
             pl.BlockSpec((1, inner, ff), lambda j: (j, 0, 0)),
@@ -489,7 +497,7 @@
             bytes_accessed=4 * chunks * mine * depth * ff + 12 * mine * total * inner * ff,
             transcendentals=mine * total * inner * ff,
         ),
-    )(arrived, arrived, cot_rows, in_raw, back_raw, in_bias, back_bias)
+    )(arrived, arrived, arrived, in_raw, back_raw, in_bias, back_bias)
 
 
 def weight_kernel(
@@ -499,12 +507,11 @@
     hidden_ref,
     in_bias_ref,
     back_bias_ref,
-    grad_in_ref,
-    grad_back_ref,
+    out_ref,
 ):
     f32, bf16 = jnp.float32, jnp.bfloat16
     groups, cap, width = rows_ref.shape
-    data, ff = grad_in_ref.shape[0], grad_in_ref.shape[-1]
+    data, ff = out_ref.shape[0], out_ref.shape[-1]
     depth = width // data
     mine = back_bias_ref.shape[0]
     at = pl.program_id(1)
@@ -517,9 +524,9 @@
         @pl.when(at == j)
         def _():
             for d in range(data):
-                block = slice(j * depth, (j + 1) * depth)
-                grad_in_ref[d, 0, block] = grad_in[d * depth : (d + 1) * depth]
-                grad_back_ref[d, 0, block] = grad_back[d * depth : (d + 1) * depth]
+                lines = slice(d * depth, (d + 1) * depth)
+                out_ref[d, 0, j * depth : (j + 1) * depth] = grad_in[lines]
+                out_ref[d, 0, (mine + j) * depth : (mine + j + 1) * depth] = grad_back[lines]
 
     @pl.when(at == mine - 1)
     def _():
@@ -536,7 +543,7 @@
                 gap = jnp.zeros((1, ff // 2 - depth), f32)
                 lines.append(jnp.concatenate([high, gap, values - high, gap], axis=1))
             lines.append(jnp.zeros((EXTRA - len(lines), ff), f32))
-            grad_in_ref[d, 0, mine * depth :] = jnp.concatenate(lines, axis=0).astype(bf16)
+            out_ref[d, 0, 2 * mine * depth :] = jnp.concatenate(lines, axis=0).astype(bf16)
 
 
 def weight_grads(arrived, grad_pre, grad_turned, hidden, grad_in_bias, grad_back_bias, data):
@@ -544,7 +551,7 @@
     groups, _, width = arrived.shape
     depth = width // data
     kept = pl.BlockSpec((1, 1, total, ff), lambda t, j: (j, t, 0, 0))
-    lines = (mine * depth + EXTRA, mine * depth)
+    out = (data, inner, 2 * mine * depth + EXTRA, ff)
     return pl.pallas_call(
         weight_kernel,
         grid=(inner, mine),
@@ -556,8 +563,8 @@
             pl.BlockSpec((mine, 1, 1, ff), lambda t, j: (0, t, 0, 0)),
             pl.BlockSpec((mine, 1, width), lambda t, j: (0, 0, 0)),
         ],
-        out_specs=[pl.BlockSpec((data, 1, n, ff), lambda t, j: (0, t, 0, 0)) for n in lines],
-        out_shape=[jax.ShapeDtypeStruct((data, inner, n, ff), jnp.bfloat16) for n in lines],
+        out_specs=pl.BlockSpec((data, 1, *out[2:]), lambda t, j: (0, t, 0, 0)),
+        out_shape=jax.ShapeDtypeStruct(out, jnp.bfloat16),
         compiler_params=pltpu.CompilerParams(vmem_limit_bytes=VMEM_LIMIT),
         cost_estimate=pl.CostEstimate(
             flops=4 * mine * total * width * inner * ff,
@@ -565,6 +572,19 @@
             transcendentals=0,
         ),
     )(arrived, grad_pre, grad_turned, hidden, grad_in_bias[:, :, None], grad_back_bias)
+
+
+def widen_kernel(parts_ref, in_ref, back_ref):
+    mine, depth, ff = in_ref.shape
+    rows = mine * depth
+    in_ref[...] = parts_ref[0, :rows].astype(jnp.float32).reshape(mine, depth, ff)
+    back_ref[...] = parts_ref[0, rows : 2 * rows].astype(jnp.float32).reshape(mine, depth, ff)
+
+
+def run_widen(parts, mine, depth):
+    owners, _, ff = parts.shape
+    out = ((owners * mine, depth, ff), jnp.float32, (mine, depth, ff), lambda p: (p, 0, 0))
+    return call_kernel(widen_kernel, (owners,), [by_step(parts, 1)], [out, out])
 
 
 def norm_rows(values):
@@ -651,41 +671,10 @@
     return lax.broadcasted_iota(jnp.int32, (count, target_row.shape[1]), 0) == target_row
 
 
-def send_kernel(rows_ref, target_ref, out_ref, sum_ref):
-    f32, bf16 = jnp.float32, jnp.bfloat16
-    slots = sum_ref.shape[0]
-    at = pl.program_id(0)
-
-    @pl.when(at == 0)
-    def _():
-        sum_ref[...] = jnp.zeros_like(sum_ref)
-
-    for h in range(rows_ref.shape[0]):
-        hits = [slot_hits(target_ref[h, k : k + 1], slots) for k in range(TOPK)]
-        fill = jnp.logical_or(hits[0], hits[1]).astype(f32).astype(bf16)
-        sum_ref[...] += jnp.dot(fill, rows_ref[h], preferred_element_type=f32)
-
-    @pl.when(at == pl.num_programs(0) - 1)
-    def _():
-        out_ref[...] = sum_ref[...].astype(bf16).reshape(out_ref.shape)
-
-
-def run_send(rows, plane_target, groups, slots_plane):
-    count, length, width = rows.shape
-    out = (groups, slots_plane // groups, width)
-    return call_kernel(
-        send_kernel,
-        (count // PAIR,),
-        [by_step(rows, PAIR), by_step(plane_target, PAIR)],
-        [(out, jnp.bfloat16, out, lambda p: (0, 0, 0))],
-        [pltpu.VMEM((slots_plane, width), jnp.float32)],
-        flops=2 * count * length * width * slots_plane,
-    )[0]
-
-
 def route_kernel(
     router_at,
     images_ref,
+    cot_ref,
     attended_ref,
     out_ref,
     packed_ref,
@@ -699,7 +688,7 @@
     gate_ref,
 ):
     f32, bf16 = jnp.float32, jnp.bfloat16
-    slots = sum_ref.shape[0]
+    slots = sum_ref.shape[1]
     tensor, local = attended_ref.shape[0], attended_ref.shape[3] // images_ref.shape[0]
     at = pl.program_id(0)
 
@@ -733,7 +722,9 @@
             hit = slot_hits(target_ref[h, k : k + 1], slots).astype(f32)
             fill = fill + hit
             gate_ref[...] += turned_dot(pair, hit.astype(bf16), 0, 1)
-        sum_ref[...] += jnp.dot(fill.astype(bf16), routed, preferred_element_type=f32)
+        fill = fill.astype(bf16)
+        sum_ref[0] += jnp.dot(fill, routed, preferred_element_type=f32)
+        sum_ref[1] += jnp.dot(fill, cot_ref[h], preferred_element_type=f32)
 
     @pl.when(at == pl.num_programs(0) - 1)
     def _():
@@ -741,22 +732,26 @@
         here = slots // groups
         for g in range(groups):
             lanes = slice(g * here, (g + 1) * here)
-            sent_ref[g, :here] = sum_ref[lanes].astype(bf16)
+            sent_ref[g, :here] = sum_ref[0, lanes].astype(bf16)
+            sent_ref[g, here : 2 * here] = sum_ref[1, lanes].astype(bf16)
             gates = jnp.concatenate([gate_ref[:, lanes], jnp.zeros((8, width - here), f32)], axis=1)
-            gates = jnp.concatenate([gates, jnp.zeros((lines - here - 8, width), f32)], axis=0)
-            sent_ref[g, here:] = gates.astype(bf16)
-
-
-def run_route(images, attended_all, out_whole, packed, vectors, routes, plane_target, groups, slots_plane, router_at):
+            gates = jnp.concatenate([gates, jnp.zeros((lines - 2 * here - 8, width), f32)], axis=0)
+            sent_ref[g, 2 * here :] = gates.astype(bf16)
+
+
+def run_route(
+    images, cot, attended_all, out_whole, packed, vectors, routes, plane_target, groups, slots_plane
+):
     f32, bf16 = jnp.float32, jnp.bfloat16
     count, length, width = images.shape
     tensor = attended_all.shape[0]
-    sent = (groups, slots_plane // groups + EXTRA, width)
+    sent = (groups, 2 * slots_plane // groups + EXTRA, width)
     return call_kernel(
-        functools.partial(route_kernel, router_at),
+        functools.partial(route_kernel, tensor * attended_all.shape[3] // PAIR),
         (count // PAIR,),
         [
             by_step(images, PAIR),
+            by_step(cot, PAIR),
             (attended_all, (tensor, 1, *attended_all.shape[2:]), lambda p: (0, p, 0, 0)),
             whole(out_whole),
             whole(packed),
@@ -769,8 +764,8 @@
             ((count, length, EXPERTS), f32, (PAIR, length, EXPERTS), lambda p: (p, 0, 0)),
             (sent, bf16, sent, lambda p: (0, 0, 0)),
         ],
-        [pltpu.VMEM((slots_plane, width), f32), pltpu.VMEM((8, slots_plane), f32)],
-        flops=2 * count * length * width * (width + slots_plane),
+        [pltpu.VMEM((2, slots_plane, width), f32), pltpu.VMEM((8, slots_plane), f32)],
+        flops=2 * count * length * width * (width + 2 * slots_plane),
     )
 
 
@@ -960,8 +955,6 @@
         )
         matrix_sum_ref[...] += matrix
         column = lambda values: jnp.sum(values, axis=0, keepdims=True)
-        sums_ref[0:1] += column(grad_normed * first)
-        sums_ref[1:2] += column(grad_normed)
         sums_ref[2:3] += column(grad_mixed)
         sums_ref[3:4] += column(grad_routed * scaled)
         sums_ref[4:5] += column(grad_routed)
@@ -1010,20 +1003,30 @@
     )
 
 
-def last_kernel(images_ref, normed_ref, mixed_ref, vector_ref, out_ref):
+def last_kernel(images_ref, normed_ref, mixed_ref, vector_ref, out_ref, sums_ref):
+    @pl.when(pl.program_id(0) == 0)
+    def _():
+        sums_ref[...] = jnp.zeros_like(sums_ref)
+
     for h in range(images_ref.shape[0]):
         scaled, inv_std = norm_rows(images_ref[h].astype(jnp.float32))
         grad = normed_ref[h].astype(jnp.float32)
         out_ref[h] = mixed_ref[h] + norm_rows_back(grad, scaled, inv_std, vector_ref[0:1])
+        sums_ref[0:1] += jnp.sum(grad * scaled, axis=0, keepdims=True)
+        sums_ref[1:2] += jnp.sum(grad, axis=0, keepdims=True)
 
 
 def run_last(images, grad_normed, grad_mixed, vectors):
+    width = images.shape[2]
     return call_kernel(
         last_kernel,
         (images.shape[0],),
         [by_step(images, 1), by_step(grad_normed, 1), by_step(grad_mixed, 1), whole(vectors)],
-        [(images.shape, jnp.float32, (1, *images.shape[1:]), lambda p: (p, 0, 0))],
-    )[0]
+        [
+            (images.shape, jnp.float32, (1, *images.shape[1:]), lambda p: (p, 0, 0)),
+            ((8, width), jnp.float32, (8, width), lambda p: (0, 0)),
+        ],
+    )
 
 
 def moved_plan(
@@ -1066,10 +1069,6 @@
     slice_width = width // tensor
     router_at = 4 * local_width
 
-    chunk_shape = (owners, mine, shard_width, ff_here)
-    in_raw = swap(w_in, (DP, INNER)).reshape(chunk_shape)
-    back_raw = swap(w_back.transpose(0, 2, 1), (DP, INNER)).reshape(chunk_shape)
-
     packed = jnp.concatenate(
         [
             w_qkv.transpose(1, 0, 2).reshape(shard_width, 3 * local_width),
@@ -1080,13 +1079,21 @@
         ],
         axis=1,
     )
-    packed = lax.all_gather(packed, DP, axis=0, tiled=True)
+    packed = swap(jnp.broadcast_to(packed[None], (data, *packed.shape)), DP).reshape(width, -1)
+    out_rows = jnp.concatenate(hop_gather(w_out, tensor_axes), axis=0)
+    in_bias_all = jnp.stack(hop_gather(in_bias, INNER))
+    packed, out_rows, in_bias_all, w_in = lax.optimization_barrier(
+        (packed, out_rows, in_bias_all, w_in)
+    )
     vectors = packed[:, router_at + EXPERTS + experts_here :].T.astype(f32)
-    out_whole = hop_gather(w_out, tensor_axes).reshape(width, shard_width)
-    out_whole = hop_gather(out_whole, DP).transpose(1, 0, 2).reshape(width, width)
-    in_bias_all = hop_gather(in_bias, INNER)
+    out_whole = jnp.concatenate(hop_gather(out_rows, DP), axis=1)
     in_bias_mine = lax.dynamic_slice_in_dim(in_bias_all, owner_at * mine, mine, 1)
     in_bias_mine = in_bias_mine.transpose(1, 0, 2).astype(f32)
+
+    chunk_shape = (owners, mine, shard_width, ff_here)
+    in_raw, w_back = lax.optimization_barrier((swap(w_in, (DP, INNER)), w_back))
+    in_raw = in_raw.reshape(chunk_shape)
+    back_raw = swap(w_back.transpose(0, 2, 1), (DP, INNER)).reshape(chunk_shape)
 
     home, within = routes // experts_here, routes % experts_here
     owner, nth = within // mine, within % mine
@@ -1097,14 +1104,13 @@
     plane_target = (group_place * mine + nth) * CAP + slot_index
     plane_target = jnp.where(jnp.logical_and(kept, owner % inner == inner_at), plane_target, -1)
     plane_target = plane_target.transpose(0, 2, 1)
-    cot_out = run_send(cotangent, plane_target, groups, slots // inner)
-    cot_rows = swap(cot_out, (DP, EXPERT))
 
     attended, proj = run_attend(images, packed, vectors, qv_bias.astype(f32))
     attended_all = lax.all_gather(attended, tensor_axes)
     attended_all, in_raw = lax.optimization_barrier((attended_all, in_raw))
     mixed, probs, sent = run_route(
         images,
+        cotangent,
         attended_all,
         out_whole,
         packed,
@@ -1113,7 +1119,6 @@
         plane_target,
         groups,
         slots // inner,
-        router_at,
     )
     sent, back_raw = lax.optimization_barrier((sent, back_raw))
     arrived = swap(sent, (DP, EXPERT))
@@ -1128,24 +1133,23 @@
         grad_in_bias_mine,
         grad_back_bias_mine,
     ) = run_experts(
-        arrived, cot_rows, in_raw, back_raw, in_bias_mine, back_bias_mine, mine, inner, tensor
+        arrived, in_raw, back_raw, in_bias_mine, back_bias_mine, inner, tensor
     )
 
     def bring(parts):
         return swap(parts.reshape(groups * tensor, *parts.shape[2:]), everywhere)
 
-    def spread(parts):
-        return swap(parts.reshape(owners, *parts.shape[2:]), (DP, INNER))
-
     grad_parts = bring(grads_out)
+    weight_out = weight_grads(
+        arrived, grad_pre_low, grad_turned, hidden_low, grad_in_bias_mine, grad_back_bias_mine, data
+    )
     rows_cut, grad_gates = run_take_grads(grad_parts, target, slice_width, outer, inner, slots)
+    rows_cut, returned_out = lax.optimization_barrier((rows_cut, returned_out))
     rows_all = lax.all_gather(rows_cut, tensor_axes)
-    grad_in_out, grad_back_out = weight_grads(
-        arrived, grad_pre_low, grad_turned, hidden_low, grad_in_bias_mine, grad_back_bias_mine, data
-    )
-    rows_cut, grad_in_out = lax.optimization_barrier((rows_cut, grad_in_out))
-    grad_in_parts = spread(grad_in_out)
-    rows_all, grad_in_parts = lax.optimization_barrier((rows_all, grad_in_parts))
+    returned = bring(returned_out)
+    rows_all, returned = lax.optimization_barrier((rows_all, returned))
+    returned, weight_out = lax.optimization_barrier((returned, weight_out))
+    weight_parts = swap(weight_out.reshape(owners, *weight_out.shape[2:]), (DP, INNER))
     grad_mixed, normed_part, matrix, sums = run_pull(
         images_held,
         images,
@@ -1162,10 +1166,7 @@
         router_at,
     )
     grad_normed = lax.psum(normed_part, tensor_axes)
-    grad_images = run_last(images, grad_normed, grad_mixed, vectors)
-
-    normed_part, returned_out = lax.optimization_barrier((normed_part, returned_out))
-    returned = bring(returned_out)
+    grad_images, first_sums = run_last(images, grad_normed, grad_mixed, vectors)
     mixed_cut = lax.dynamic_slice_in_dim(mixed, tensor_at * slice_width, slice_width, 2)
     output_cut = run_take_rows(
         images_held, returned, target, probs, routes, mixed_cut, outer, inner, slots
@@ -1174,43 +1175,37 @@
     output = output.reshape(tensor, image_count // PAIR, seq_len, PAIR, slice_width)
     output = output.transpose(1, 3, 2, 0, 4).reshape(images.shape)
 
-    matrix, returned = lax.optimization_barrier((matrix, returned))
-    early = swap(matrix.reshape(groups, shard_width // sources, -1), (DP, EXPERT))
-    early, grad_back_out = lax.optimization_barrier((early, grad_back_out))
-    grad_back_parts = spread(grad_back_out)
-    early = jnp.sum(early.astype(f32), axis=0)
-    early = hop_gather(early, EXPERT).reshape(shard_width, -1)
-    grad_w_qkv = early[:, : 3 * local_width].reshape(shard_width, 3, local_width).transpose(1, 0, 2)
-    grad_w_out = early[:, 3 * local_width : 4 * local_width].T
-    grad_w_router = early[:, 4 * local_width :]
-    experts_shape = (experts_here, shard_width, ff_here)
-    grad_w_in = grad_in_parts[:, : mine * shard_width].astype(f32).reshape(experts_shape)
-    grad_w_back = grad_back_parts.astype(f32).reshape(experts_shape).transpose(0, 2, 1)
-    lines = grad_in_parts[:, mine * shard_width :].astype(f32)
+    pair_sums = [sums[5, :local_width], sums[5, 2 * local_width : 3 * local_width]]
+    pair_sums = jnp.tile(jnp.stack(pair_sums), (1, data))
+    vector_grads = jnp.concatenate([first_sums[:2], sums[2:5], pair_sums], axis=0)
+    high, low = high_low(vector_grads)
+    small = jnp.concatenate([matrix, high.T, low.T], axis=1)
+    small = swap(small.reshape(groups, shard_width // sources, -1), (DP, EXPERT))
+    small = jnp.sum(small.astype(f32), axis=0)
+    small = jnp.concatenate(hop_gather(small, EXPERT), axis=0)
+    grad_w_qkv = small[:, : 3 * local_width].reshape(shard_width, 3, local_width).transpose(1, 0, 2)
+    grad_w_out = small[:, 3 * local_width : router_at].T
+    grad_w_router = small[:, router_at : router_at + EXPERTS]
+    vector_grads = small[:, router_at + EXPERTS :].T
+    vector_grads = vector_grads[:7] + vector_grads[7:]
+    grad_w_in, grad_w_back = run_widen(weight_parts, mine, shard_width)
+    grad_w_back = grad_w_back.transpose(0, 2, 1)
+    lines = weight_parts[:, 2 * mine * shard_width :].astype(f32)
     grad_in_bias = lines[:, : 2 * mine].reshape(owners, mine, 2, ff_here)
     grad_in_bias = jnp.sum(grad_in_bias, axis=2).reshape(experts_here, ff_here)
     lines = lines[:, 2 * mine : 3 * mine].reshape(experts_here, 2, ff_here // 2)
     grad_back_shard = jnp.sum(lines[:, :, :shard_width], axis=1)
-    once = (tensor_at == 0).astype(f32)
-    pair_bias = jnp.stack([sums[5, :local_width], sums[5, 2 * local_width : 3 * local_width]])
-    pair_bias = lax.dynamic_update_slice(
-        jnp.zeros((2, width), f32), pair_bias, (0, tensor_at * local_width)
-    )
-    totals = jnp.concatenate([sums[0:2], pair_bias, once * sums[2:5]], axis=0)
-    totals = lax.psum(totals, everywhere)
-    grad_qv_bias = lax.dynamic_slice_in_dim(totals[2:4], tensor_at * local_width, local_width, 1)
-    totals = lax.dynamic_slice_in_dim(totals, dp_at * shard_width, shard_width, 1)
     return (
         output,
         grad_images,
-        totals[0],
-        totals[1],
+        vector_grads[0],
+        vector_grads[1],
         grad_w_qkv,
-        grad_qv_bias,
+        vector_grads[5:7],
         grad_w_out,
-        totals[4],
-        totals[5],
-        totals[6],
+        vector_grads[2],
+        vector_grads[3],
+        vector_grads[4],
         grad_w_router,
         grad_w_in,
         grad_in_bias,
@@ -1235,7 +1230,7 @@
     data, expert, tensor = (mesh.shape[name] for name in (DP, EXPERT, TENSOR))
     inner = FF_PAIR if tensor % FF_PAIR == 0 else 1
     owners = data * inner
-    if (EXPERTS // expert) % owners or owners & (owners - 1):
+    if (EXPERTS // expert) % owners or any(n & (n - 1) for n in (data, expert, tensor)):
         taken, given = specs(TENSOR)
         return jax.shard_map(
             gathered_plan, mesh=mesh, in_specs=taken, out_specs=given, check_vma=False

time: 645 us -> 638 us (0.989)
  waiting for transfers between devices: 181 us -> 312 us
  blocking collectives: 220 us -> 109 us
  starting transfers between devices: 52.8 us -> 35.4 us
  local copies, waits for them, and re-layouts: 49.8 us -> 36.3 us
  Pallas kernels: 94.2 us -> 103 us
  other arithmetic: 22.5 us -> 14.8 us
    psum x1 -> x0, blocking collectives: 98.4 us -> none  [moved_plan(): totals = lax.psum(totals, everywhere)]
    psum x1, waiting for transfers between devices: 0.01 us -> 54.1 us  [moved_plan(): grad_normed = lax.psum(normed_part, tensor_axes)]
    all_gather x1 -> x0, waiting for transfers between devices: 49.2 us -> none  [moved_plan(): packed = lax.all_gather(packed, DP, axis=0, tiled=True)]
    all_to_all x6, waiting for transfers between devices: 61.7 us -> 106 us  [swap(): return lax.all_to_all(values, axes, split_axis=0, concat_axis=0, tiled=True)]
    all_gather x1, waiting for transfers between devices: 0.01 us -> 42.3 us  [moved_plan(): output = lax.all_gather(output_cut, tensor_axes)]
    ppermute x8, waiting for transfers between devices: 19.5 us -> 56.5 us  [hop_gather(): hops.append(lax.ppermute(values, axes, [(i, i ^ s) for i in range(count)]))]
    all_to_all x3 -> x2, blocking collectives: 122 us -> 109 us  [swap(): return lax.all_to_all(values, axes, split_axis=0, concat_axis=0, tiled=True)]
    dynamic_update_slice x13 -> x0, local copies, waits for them, and re-layouts: 12.3 us -> none  [the longest x12 12.1 us: hop_gather(): lax.dynamic_update_slice_in_dim(gathered, hop[None], (at - s) % count, 0)]
  transfers between devices with their start and end apart: 19 -> 18, of which waited for: 11 -> 12; matrix products, arithmetic and copies ran while one was open for 10% -> 6% of each run, Pallas kernels for 7% -> 6%
where the time goes in v6:
time: 638 us; the launch traced here: 627 us
  waiting for transfers between devices  312 us (49%)
  blocking collectives  109 us (17%)
  Pallas kernels  103 us (16%)
  local copies, waits for them, and re-layouts  36.3 us (6%)
  starting transfers between devices  35.4 us (6%)
  between operations  15.3 us (2%)
  other arithmetic  14.8 us (2%)
    all_to_all x2, blocking collectives, swap(): return lax.all_to_all(values, axes, split_axis=0, concat_axis=0, tiled=True)  109 us
    all_to_all x6, waiting for transfers between devices, swap(): return lax.all_to_all(values, axes, split_axis=0, concat_axis=0, tiled=True)  106 us
    pallas_call x7, Pallas kernels, call_kernel(): pl.pallas_call(kernel, grid=grid, in_specs=[smem if b is None else pl.Blo...  71.8 us
    ppermute x8, waiting for transfers between devices, hop_gather(): hops.append(lax.ppermute(values, axes, [(i, i ^ s) for i in range(count)]))  56.5 us
    psum x1, waiting for transfers between devices, moved_plan(): grad_normed = lax.psum(normed_part, tensor_axes)  54.1 us
    all_gather x1, waiting for transfers between devices, moved_plan(): rows_all = lax.all_gather(rows_cut, tensor_axes)  53.2 us
    all_gather x1, waiting for transfers between devices, moved_plan(): output = lax.all_gather(output_cut, tensor_axes)  42.3 us
    all_to_all x6, starting transfers between devices, swap(): return lax.all_to_all(values, axes, split_axis=0, concat_axis=0, tiled=True)  24.4 us
  transfers between devices with their start and end apart: 18, of which 12 were waited for; matrix products, arithmetic and copies ran while one was open for 6% of the time, Pallas kernels for 6%

profile of v6, /device:TPU:0, one launch (start us, length us, event | category | flops | bytes accessed | tf_op | source)
XLA Modules:
  0.0 626.5 jit_solution(11684903248601519911)
XLA Ops:
  15.5 4.3 all-to-all-start
  29.7 4.5 collective-permute-done.1
  37.8 58.7 %all_to_all.40 = bf16[16,192,768]{2,1,0:T(8,128)(2,1)} all-to-all(bf16[16,192,768]{2,1,0:T(8,128)(2,1)} %param.31), channel_id=1, replica_groups=mesh['dp'=4,'expert'=2,'outer'=2,'inner'=2] {'dp','inner'}, dimensions={0} | all-to-all | bytes 9437184 | tf_op jit(solution)/shard_map/all_to_all | solution.py:351
  96.5 4.7 all-to-all-start.2
  104.5 6.6 %shard_map.289 = (bf16[2,197,384]{2,1,0:T(8,128)(2,1)}, bf16[4,197,576]{2,1,0:T(8,128)(2,1)}) custom-call(bf16[4,197,768]{2,1,0:T(8,128)(2,1)} %copy.225.images_ref, bf16[768,821]{1,0:T(8,128)(2,1)} %bitcast.49, f32[5,768]{1,0:T(8,128)} %convert_bitcast_fusion.vector_ref, f32[2,192]{1,0:T(2,128)} %convert_element_type.30.bias_ref), custom_call_target="tpu_custom_call" | custom-call | flops 935614464 | bytes 2488320 | tf_op jit(solution)/shard_map/pallas_call | solution.py:607
  119.4 32.6 %collective-permute-done.4 = bf16[768,192]{1,0:T(8,128)(2,1)S(1)} collective-permute-done((bf16[768,192]{1,0:T(8,128)(2,1)S(1)}, bf16[768,192]{1,0:T(8,128)(2,1)S(1)}, u32[]{:S(2)}, u32[]{:S(2)}) %collective-permute-start.4) | collective-permute-done | bytes 294944 | tf_op jit(solution)/shard_map/ppermute | solution.py:358
  151.9 16.6 %collective-permute-done.5 = bf16[768,192]{1,0:T(8,128)(2,1)} collective-permute-done((bf16[768,192]{1,0:T(8,128)(2,1)S(1)}, bf16[768,192]{1,0:T(8,128)(2,1)}, u32[]{:S(2)}, u32[]{:S(2)}) %collective-permute-start.5) | collective-permute-done | bytes 294944 | tf_op jit(solution)/shard_map/ppermute | solution.py:358
  171.3 15.6 %shard_map.290 = (f32[4,197,768]{2,1,0:T(8,128)}, f32[4,197,32]{2,1,0:T(8,128)}, bf16[8,272,768]{2,1,0:T(8,128)(2,1)}) custom-call(bf16[4,197,768]{2,1,0:T(8,128)(2,1)} %copy.225.images_ref, bf16[4,197,768]{2,1,0:T(8,128)(2,1)} %copy.226.cot_ref, bf16[4,2,197,384]{3,2,1,0:T(8,128)(2,1)} %bitcast.68, bf16[768,768]{1,0:T(8,128)(2,1)} %pad_maximum_fusion.1.out_ref, ...), custom_call_target="tpu_custom_call" | custom-call | flops 3408396288 | bytes 6099776 | tf_op jit(solution)/shard_map/pallas_call | solution.py:607
  193.2 36.6 %all-to-all-done.3.rows_ref.gate_ref.cot_ref = bf16[8,272,768]{2,1,0:T(8,128)(2,1)S(1)} async-done(((bf16[8,272,768]{2,1,0:T(8,128)(2,1)}), bf16[8,272,768]{2,1,0:T(8,128)(2,1)S(1)}, u32[]{:S(2)}, u32[]{:S(2)}) %all-to-all-start.3) | async-done | bytes 3342368 | tf_op jit(solution)/shard_map/all_to_all | solution.py:351
  231.6 19.0 %shard_map.291 = (bf16[8,4,192,128]{3,2,1,0:T(8,128)(2,1)}, bf16[8,4,208,128]{3,2,1,0:T(8,128)(2,1)}, bf16[2,2,512,768]{3,2,1,0:T(8,128)(2,1)}, bf16[2,2,512,768...) custom-call(bf16[8,272,768]{2,1,0:T(8,128)(2,1)} %copy-done, ...), custom_call_target="tpu_custom_call" | custom-call | flops 9663676416 | bytes 28311552 | tf_op jit(solution)/shard_map/pallas_call | solution.py:477
  250.5 50.1 %all_to_all.41.parts_ref = bf16[32,208,128]{2,1,0:T(8,128)(2,1)} all-to-all(bf16[32,208,128]{2,1,0:T(8,128)(2,1)} %bitcast.56), channel_id=1, replica_groups=mesh['dp'=4,'expert'=2,'outer'=2,'inner'=2] {'dp','expert','outer','inner'}, dimensions={0} | all-to-all | bytes 3407872 | tf_op jit(solution)/shard_map/all_to_all | solution.py:351
  300.6 6.2 shard_map.292
  311.2 53.2 %all-gather.9.cloned.1.call-done = bf16[8,197,384]{2,1,0:T(8,128)(2,1)} async-done(((bf16[2,197,384]{2,1,0:T(8,128)(2,1)}), bf16[8,197,384]{2,1,0:T(8,128)(2,1)}) %all-gather.9.cloned.1.call-update) | async-done | bytes 1210384 | tf_op jit(solution)/shard_map/all_gather | solution.py:1148
  367.1 21.8 %shard_map.295 = (f32[4,197,768]{2,1,0:T(8,128)}, bf16[4,197,768]{2,1,0:T(8,128)(2,1)}, bf16[768,800]{1,0:T(8,128)(2,1)}, f32[8,768]{1,0:T(8,128)}) custom-call(s32[1]{0:T(128)S(6)} %copy.258.held_ref, bf16[4,197,768]{2,1,0:T(8,128)(2,1)} %copy.225.images_ref, bf16[4,197,768]{2,1,0:T(8,128)(2,1)} %copy.226.cot_ref, ...), custom_call_target="tpu_custom_call" | custom-call | flops 3623236608 | bytes 8652100 | tf_op jit(solution)/shard_map/pallas_call | solution.py:607
  390.5 54.1 %all-reduce.2.cloned.1.call-done.normed_ref = bf16[4,197,768]{2,1,0:T(8,128)(2,1)} async-done(((bf16[4,197,768]{2,1,0:T(8,128)(2,1)}), bf16[4,197,768]{2,1,0:T(8,128)(2,1)}) %all-reduce.2.cloned.1.call-update) | async-done | bytes 1210384 | tf_op jit(solution)/shard_map/psum | solution.py:1168
  444.6 5.4 shard_map.296
  456.8 12.7 %shard_map.293 = bf16[4,2,784,768]{3,2,1,0:T(8,128)(2,1)} custom-call(bf16[8,272,768]{2,1,0:T(8,128)(2,1)} %copy-done, bf16[2,2,512,768]{3,2,1,0:T(8,128)(2,1)} %get-tuple-element.71.grad_pre_ref, bf16[2,768,512]{2,1,0:T(8,128)(2,1)} %get-tuple-element.72.grad_turned_ref, bf16[2,2,512,768]{3,2,1,0:T(8,128)(2,1)} %get-tuple-element.73.hidden_ref, ...), custom_call_target="tpu_custom_call" | custom-call | flops 4831838208 | bytes 15728640 | tf_op jit(solution)/shard_map/pallas_call | solution.py:555
  469.5 4.7 all-to-all-done.6
  474.2 5.0 all-to-all-start.7
  482.1 5.2 shard_map.294
  489.7 4.1 copy.243
  493.7 42.3 %all-gather.11.cloned.1.call-done = bf16[8,197,384]{2,1,0:T(8,128)(2,1)} async-done(((bf16[2,197,384]{2,1,0:T(8,128)(2,1)}), bf16[8,197,384]{2,1,0:T(8,128)(2,1)}) %all-gather.11.cloned.1.call-update) | async-done | bytes 1210384 | tf_op jit(solution)/shard_map/all_gather | solution.py:1174
  547.8 58.1 %all-to-all-done.7.parts_ref = bf16[8,784,768]{2,1,0:T(8,128)(2,1)} async-done(((bf16[8,784,768]{2,1,0:T(8,128)(2,1)}), bf16[8,784,768]{2,1,0:T(8,128)(2,1)}, u32[]{:S(2)}, u32[]{:S(2)}) %all-to-all-start.7) | async-done | bytes 9633824 | tf_op jit(solution)/shard_map/all_to_all | solution.py:351
  608.5 11.0 %shard_map.297 = (f32[16,192,768]{2,1,0:T(8,128)}, f32[16,192,768]{2,1,0:T(8,128)}) custom-call(bf16[8,784,768]{2,1,0:T(8,128)(2,1)} %all-to-all-done.7.parts_ref), custom_call_target="tpu_custom_call" | custom-call | bytes 9633792 | tf_op jit(solution)/shard_map/pallas_call | solution.py:607
  (129 shorter events, 78.1 us)
Async XLA Ops:
  15.5 6.8 %copy-start.7 = (bf16[192,192]{1,0:T(8,128)(2,1)S(1)}, bf16[192,192]{1,0:T(8,128)(2,1)}, u32[]{:S(2)}) copy-start(bf16[192,192]{1,0:T(8,128)(2,1)} %param.26) | copy-start | bytes 221188
  15.5 22.3 %all-to-all-start = ((bf16[4,192,821]{2,1,0:T(8,128)(2,1)}), bf16[4,192,821]{2,1,0:T(8,128)(2,1)S(1)}, u32[]{:S(2)}, u32[]{:S(2)}) async-start(bf16[4,192,821]{2,1,0:T(8,128)(2,1)} %broadcast_in_dim.18), calls=%async_computation | async-start | bytes 2752512 | tf_op jit(solution)/shard_map/all_to_all | solution.py:351
  19.8 6.8 %collective-permute-start.3 = (bf16[16,768]{1,0:T(8,128)(2,1)S(1)}, bf16[16,768]{1,0:T(8,128)(2,1)S(1)}, u32[]{:S(2)}, u32[]{:S(2)}) collective-permute-start(bf16[16,768]{1,0:T(8,128)(2,1)S(1)} %copy-done.10), channel_id=1, source_target_pairs={{0,1},{1,0},{2,3},{3,2},{4,5},{5,4},{6,7},{7,6},{8,9},{9,8},{10,11... | collective-permute-start | bytes 73736 | tf_op jit(solution)/shard_map/ppermute | solution.py:358
  22.2 7.5 %collective-permute-start = (bf16[192,192]{1,0:T(8,128)(2,1)S(1)}, bf16[192,192]{1,0:T(8,128)(2,1)S(1)}, u32[]{:S(2)}, u32[]{:S(2)}) collective-permute-start(bf16[192,192]{1,0:T(8,128)(2,1)S(1)} %copy-done.7), channel_id=1, source_target_pairs={{0,3},{1,2},{2,1},{3,0},{4,7},{5,6},{6,5},{7,4},{8,11},{9,10},{10,... | collective-permute-start | bytes 221192 | tf_op jit(solution)/shard_map/ppermute | solution.py:358
  24.7 9.5 %collective-permute-start.1 = (bf16[192,192]{1,0:T(8,128)(2,1)S(1)}, bf16[192,192]{1,0:T(8,128)(2,1)S(1)}, u32[]{:S(2)}, u32[]{:S(2)}) collective-permute-start(bf16[192,192]{1,0:T(8,128)(2,1)S(1)} %copy-done.7), channel_id=1, source_target_pairs={{0,2},{1,3},{2,0},{3,1},{4,6},{5,7},{6,4},{7,5},{8,10},{9,11},{10,... | collective-permute-start | bytes 221192 | tf_op jit(solution)/shard_map/ppermute | solution.py:358
  24.8 9.4 %collective-permute-start.2 = (bf16[192,192]{1,0:T(8,128)(2,1)S(1)}, bf16[192,192]{1,0:T(8,128)(2,1)S(1)}, u32[]{:S(2)}, u32[]{:S(2)}) collective-permute-start(bf16[192,192]{1,0:T(8,128)(2,1)S(1)} %copy-done.7), channel_id=1, source_target_pairs={{0,1},{1,0},{2,3},{3,2},{4,5},{5,4},{6,7},{7,6},{8,9},{9,8},{10,11... | collective-permute-start | bytes 221192 | tf_op jit(solution)/shard_map/ppermute | solution.py:358
  37.8 65.4 %copy-start.1 = (bf16[4,192,821]{2,1,0:T(8,128)(2,1)}, bf16[4,192,821]{2,1,0:T(8,128)(2,1)S(1)}, u32[]{:S(2)}) copy-start(bf16[4,192,821]{2,1,0:T(8,128)(2,1)S(1)} %all-to-all-done) | copy-start | bytes 3783172
  96.5 90.4 %all-to-all-start.2 = ((bf16[16,192,768]{2,1,0:T(8,128)(2,1)}), bf16[16,192,768]{2,1,0:T(8,128)(2,1)}, u32[]{:S(2)}, u32[]{:S(2)}) async-start(bf16[16,192,768]{2,1,0:T(8,128)(2,1)} %bitcast.53), calls=%async_computation.2 | async-start | bytes 9437184 | tf_op jit(solution)/shard_map/all_to_all | solution.py:351
  101.2 70.1 %all-gather.7.cloned.1.call-start = ((), (), s32[]{:S(2)}) async-start(), calls=%async_computation.9 | async-start | bytes 1536000 | tf_op jit(solution)/shard_map/all_gather | solution.py:1109
  104.5 6.6 %copy-start.9 = (s32[4,197,2]{1,2,0:T(2,128)S(1)}, s32[4,197,2]{1,2,0:T(2,128)}, u32[]{:S(2)}) copy-start(s32[4,197,2]{1,2,0:T(2,128)} %param.20) | copy-start | bytes 18916
  111.4 6.6 %copy-start.2 = (s32[4,197,2]{2,1,0:T(8,128)}, s32[4,197,2]{2,1,0:T(8,128)S(1)}, u32[]{:S(2)}) copy-start(s32[4,197,2]{2,1,0:T(8,128)S(1)} %copy.227.routes_ref) | copy-start | bytes 18916
  113.7 38.2 %collective-permute-start.4 = (bf16[768,192]{1,0:T(8,128)(2,1)S(1)}, bf16[768,192]{1,0:T(8,128)(2,1)S(1)}, u32[]{:S(2)}, u32[]{:S(2)}) collective-permute-start(bf16[768,192]{1,0:T(8,128)(2,1)S(1)} %pad_maximum_fusion.2), channel_id=1, source_target_pairs={{0,24},{8,16},{16,8},{24,0},{1,25},{9,17},{17,9},{25,1},{2,26},{10... | collective-permute-start | bytes 884744 | tf_op jit(solution)/shard_map/ppermute | solution.py:358
  115.4 53.1 %collective-permute-start.5 = (bf16[768,192]{1,0:T(8,128)(2,1)S(1)}, bf16[768,192]{1,0:T(8,128)(2,1)}, u32[]{:S(2)}, u32[]{:S(2)}) collective-permute-start(bf16[768,192]{1,0:T(8,128)(2,1)S(1)} %pad_maximum_fusion.2), channel_id=1, source_target_pairs={{0,16},{8,24},{16,0},{24,8},{1,17},{9,25},{17,1},{25,9},{2,18},{10... | collective-permute-start | bytes 884744 | tf_op jit(solution)/shard_map/ppermute | solution.py:358
  115.7 52.8 %collective-permute-start.6 = (bf16[768,192]{1,0:T(8,128)(2,1)S(1)}, bf16[768,192]{1,0:T(8,128)(2,1)}, u32[]{:S(2)}, u32[]{:S(2)}) collective-permute-start(bf16[768,192]{1,0:T(8,128)(2,1)S(1)} %pad_maximum_fusion.2), channel_id=1, source_target_pairs={{0,8},{8,0},{16,24},{24,16},{1,9},{9,1},{17,25},{25,17},{2,10},{10... | collective-permute-start | bytes 884744 | tf_op jit(solution)/shard_map/ppermute | solution.py:358
  186.9 42.9 %all-to-all-start.3 = ((bf16[8,272,768]{2,1,0:T(8,128)(2,1)}), bf16[8,272,768]{2,1,0:T(8,128)(2,1)S(1)}, u32[]{:S(2)}, u32[]{:S(2)}) async-start(bf16[8,272,768]{2,1,0:T(8,128)(2,1)} %get-tuple-element.61), calls=%async_computation.3 | async-start | bytes 6684672 | tf_op jit(solution)/shard_map/all_to_all | solution.py:351
  306.8 60.2 %all-to-all-start.5 = ((bf16[32,192,128]{2,1,0:T(8,128)(2,1)}), bf16[32,192,128]{2,1,0:T(8,128)(2,1)S(1)}, u32[]{:S(2)}, u32[]{:S(2)}) async-start(bf16[32,192,128]{2,1,0:T(8,128)(2,1)} %bitcast.57), calls=%async_computation.5 | async-start | bytes 3145728 | tf_op jit(solution)/shard_map/all_to_all | solution.py:351
  309.5 54.8 %all-gather.9.cloned.1.call-start = ((), (), s32[]{:S(2)}) async-start(), calls=%async_computation.10 | async-start | bytes 1536000 | tf_op jit(solution)/shard_map/all_gather | solution.py:1148
  310.3 134.3 %all-reduce.2.cloned.1.call-start = ((), (), s32[]{:S(2)}) async-start(), calls=%async_computation.8 | async-start | bytes 2457600 | tf_op jit(solution)/shard_map/psum | solution.py:1168
  367.1 21.8 %copy-start.3 = (bf16[32,192,128]{2,1,0:T(8,128)(2,1)}, bf16[32,192,128]{2,1,0:T(8,128)(2,1)S(1)}, u32[]{:S(2)}) copy-start(bf16[32,192,128]{2,1,0:T(8,128)(2,1)S(1)} %all-to-all-done.5.parts_ref) | copy-start | bytes 4718596
  444.6 6.5 %copy-start.4 = (bf16[768,800]{1,0:T(8,128)(2,1)S(1)}, bf16[768,800]{1,0:T(8,128)(2,1)}, u32[]{:S(2)}) copy-start(bf16[768,800]{1,0:T(8,128)(2,1)} %get-tuple-element.85) | copy-start | bytes 3686404
  452.4 21.8 %all-to-all-start.6 = ((bf16[8,96,814]{2,1,0:T(8,128)(2,1)}), bf16[8,96,814]{2,1,0:T(8,128)(2,1)S(1)}, u32[]{:S(2)}, u32[]{:S(2)}) async-start(bf16[8,96,814]{2,1,0:T(8,128)(2,1)} %bitcast.20), calls=%async_computation.6 | async-start | bytes 2752512 | tf_op jit(solution)/shard_map/all_to_all | solution.py:351
  474.2 131.7 %all-to-all-start.7 = ((bf16[8,784,768]{2,1,0:T(8,128)(2,1)}), bf16[8,784,768]{2,1,0:T(8,128)(2,1)}, u32[]{:S(2)}, u32[]{:S(2)}) async-start(bf16[8,784,768]{2,1,0:T(8,128)(2,1)} %bitcast.46), calls=%async_computation.7 | async-start | bytes 19267584 | tf_op jit(solution)/shard_map/all_to_all | solution.py:351
  479.3 56.7 %all-gather.11.cloned.1.call-start = ((), (), s32[]{:S(2)}) async-start(), calls=%async_computation.11 | async-start | bytes 1536000 | tf_op jit(solution)/shard_map/all_gather | solution.py:1174
  488.2 53.6 %collective-permute-start.7 = (f32[96,814]{1,0:T(8,128)}, f32[96,814]{1,0:T(8,128)}, u32[]{:S(2)}, u32[]{:S(2)}) collective-permute-start(f32[96,814]{1,0:T(8,128)} %convert_reduce_fusion), channel_id=1, source_target_pairs={{0,4},{4,0},{1,5},{5,1},{2,6},{6,2},{3,7},{7,3},{8,12},{12,8},{9,1... | collective-permute-start | bytes 937736 | tf_op jit(solution)/shard_map/ppermute | solution.py:358
  (7 other events, 21.8 us)
Sparse Core Ops, SparseCore 0:
  111.3 50.0 all-gather.6
  312.5 51.8 all-gather.8
  389.0 55.5 all-reduce.1
  487.4 48.5 all-gather.10

commit v7 on v6

--- a/solution.py
+++ b/solution.py
@@ -1082,18 +1082,11 @@
     packed = swap(jnp.broadcast_to(packed[None], (data, *packed.shape)), DP).reshape(width, -1)
     out_rows = jnp.concatenate(hop_gather(w_out, tensor_axes), axis=0)
     in_bias_all = jnp.stack(hop_gather(in_bias, INNER))
-    packed, out_rows, in_bias_all, w_in = lax.optimization_barrier(
-        (packed, out_rows, in_bias_all, w_in)
-    )
+    packed, out_rows, in_bias_all = lax.optimization_barrier((packed, out_rows, in_bias_all))
     vectors = packed[:, router_at + EXPERTS + experts_here :].T.astype(f32)
     out_whole = jnp.concatenate(hop_gather(out_rows, DP), axis=1)
     in_bias_mine = lax.dynamic_slice_in_dim(in_bias_all, owner_at * mine, mine, 1)
     in_bias_mine = in_bias_mine.transpose(1, 0, 2).astype(f32)
-
-    chunk_shape = (owners, mine, shard_width, ff_here)
-    in_raw, w_back = lax.optimization_barrier((swap(w_in, (DP, INNER)), w_back))
-    in_raw = in_raw.reshape(chunk_shape)
-    back_raw = swap(w_back.transpose(0, 2, 1), (DP, INNER)).reshape(chunk_shape)
 
     home, within = routes // experts_here, routes % experts_here
     owner, nth = within // mine, within % mine
@@ -1106,8 +1099,14 @@
     plane_target = plane_target.transpose(0, 2, 1)
 
     attended, proj = run_attend(images, packed, vectors, qv_bias.astype(f32))
+
+    attended, w_in = lax.optimization_barrier((attended, w_in))
     attended_all = lax.all_gather(attended, tensor_axes)
-    attended_all, in_raw = lax.optimization_barrier((attended_all, in_raw))
+    in_raw = swap(w_in, (DP, INNER))
+    attended_all, in_raw, w_back = lax.optimization_barrier((attended_all, in_raw, w_back))
+    back_raw = swap(w_back.transpose(0, 2, 1), (DP, INNER))
+    chunk_shape = (owners, mine, shard_width, ff_here)
+    in_raw, back_raw = in_raw.reshape(chunk_shape), back_raw.reshape(chunk_shape)
     mixed, probs, sent = run_route(
         images,
         cotangent,
@@ -1166,6 +1165,7 @@
         router_at,
     )
     grad_normed = lax.psum(normed_part, tensor_axes)
+    grad_normed, returned = lax.optimization_barrier((grad_normed, returned))
     grad_images, first_sums = run_last(images, grad_normed, grad_mixed, vectors)
     mixed_cut = lax.dynamic_slice_in_dim(mixed, tensor_at * slice_width, slice_width, 2)
     output_cut = run_take_rows(
@@ -1180,6 +1180,7 @@
     vector_grads = jnp.concatenate([first_sums[:2], sums[2:5], pair_sums], axis=0)
     high, low = high_low(vector_grads)
     small = jnp.concatenate([matrix, high.T, low.T], axis=1)
+    small, weight_parts = lax.optimization_barrier((small, weight_parts))
     small = swap(small.reshape(groups, shard_width // sources, -1), (DP, EXPERT))
     small = jnp.sum(small.astype(f32), axis=0)
     small = jnp.concatenate(hop_gather(small, EXPERT), axis=0)

time: 638 us -> 621 us (0.973)
  blocking collectives: 109 us -> 46.7 us
  waiting for transfers between devices: 312 us -> 360 us
  starting transfers between devices: 35.4 us -> 41.9 us
    all_to_all x2 -> x1, blocking collectives: 109 us -> 46.7 us  [swap(): return lax.all_to_all(values, axes, split_axis=0, concat_axis=0, tiled=True)]
    all_gather x1, waiting for transfers between devices: 0.01 us -> 51.8 us  [moved_plan(): attended_all = lax.all_gather(attended, tensor_axes)]
    all_gather x1, waiting for transfers between devices: 42.3 us -> 0.01 us  [moved_plan(): output = lax.all_gather(output_cut, tensor_axes)]
    psum x1, waiting for transfers between devices: 54.1 us -> 92.3 us  [moved_plan(): grad_normed = lax.psum(normed_part, tensor_axes)]
    ppermute x8, waiting for transfers between devices: 56.5 us -> 73.8 us  [hop_gather(): hops.append(lax.ppermute(values, axes, [(i, i ^ s) for i in range(count)]))]
    all_gather x1, waiting for transfers between devices: 53.2 us -> 40.7 us  [moved_plan(): rows_all = lax.all_gather(rows_cut, tensor_axes)]
    all_to_all x6 -> x7, starting transfers between devices: 24.4 us -> 30.5 us  [swap(): return lax.all_to_all(values, axes, split_axis=0, concat_axis=0, tiled=True)]
    all_to_all x6 -> x7, waiting for transfers between devices: 106 us -> 100 us  [swap(): return lax.all_to_all(values, axes, split_axis=0, concat_axis=0, tiled=True)]
  transfers between devices with their start and end apart: 18 -> 19, of which waited for: 12 -> 13; matrix products, arithmetic and copies ran while one was open for 6% -> 5% of each run, Pallas kernels for 6% -> 12%
where the time goes in v7:
time: 621 us; the launch traced here: 616 us
  waiting for transfers between devices  360 us (58%)
  Pallas kernels  103 us (17%)
  blocking collectives  46.7 us (8%)
  starting transfers between devices  41.9 us (7%)
  local copies, waits for them, and re-layouts  34.2 us (6%)
  between operations  15.2 us (2%)
  other arithmetic  14.4 us (2%)
    all_to_all x7, waiting for transfers between devices, swap(): return lax.all_to_all(values, axes, split_axis=0, concat_axis=0, tiled=True)  100 us
    psum x1, waiting for transfers between devices, moved_plan(): grad_normed = lax.psum(normed_part, tensor_axes)  92.3 us
    ppermute x8, waiting for transfers between devices, hop_gather(): hops.append(lax.ppermute(values, axes, [(i, i ^ s) for i in range(count)]))  73.8 us
    pallas_call x7, Pallas kernels, call_kernel(): pl.pallas_call(kernel, grid=grid, in_specs=[smem if b is None else pl.Blo...  71.3 us
    all_gather x1, waiting for transfers between devices, moved_plan(): attended_all = lax.all_gather(attended, tensor_axes)  51.8 us
    all_to_all x1, blocking collectives, swap(): return lax.all_to_all(values, axes, split_axis=0, concat_axis=0, tiled=True)  46.7 us
    all_gather x1, waiting for transfers between devices, moved_plan(): rows_all = lax.all_gather(rows_cut, tensor_axes)  40.7 us
    all_to_all x7, starting transfers between devices, swap(): return lax.all_to_all(values, axes, split_axis=0, concat_axis=0, tiled=True)  30.5 us
  transfers between devices with their start and end apart: 19, of which 13 were waited for; matrix products, arithmetic and copies ran while one was open for 5% of the time, Pallas kernels for 12%

profile of v7, /device:TPU:0, one launch (start us, length us, event | category | flops | bytes accessed | tf_op | source)
XLA Modules:
  0.0 615.6 jit_solution(9449217658399016451)
XLA Ops:
  29.7 4.5 collective-permute-done.1
  39.2 6.6 %shard_map.289 = (bf16[2,197,384]{2,1,0:T(8,128)(2,1)}, bf16[4,197,576]{2,1,0:T(8,128)(2,1)}) custom-call(bf16[4,197,768]{2,1,0:T(8,128)(2,1)} %copy.232.images_ref, bf16[768,821]{1,0:T(8,128)(2,1)} %bitcast.49, f32[5,768]{1,0:T(8,128)} %convert_bitcast_fusion.vector_ref, f32[2,192]{1,0:T(2,128)} %convert_element_type.30.bias_ref), custom_call_target="tpu_custom_call" | custom-call | flops 935614464 | bytes 2488320 | tf_op jit(solution)/shard_map/pallas_call | solution.py:607
  45.8 4.6 all-to-all-start.1
  51.2 51.8 %all-gather.7.cloned.1.call-done = bf16[8,197,384]{2,1,0:T(8,128)(2,1)} async-done(((bf16[2,197,384]{2,1,0:T(8,128)(2,1)}), bf16[8,197,384]{2,1,0:T(8,128)(2,1)}) %all-gather.7.cloned.1.call-update) | async-done | bytes 1210384 | tf_op jit(solution)/shard_map/all_gather | solution.py:1104
  103.0 21.4 %all-to-all-done.1 = bf16[16,192,768]{2,1,0:T(8,128)(2,1)} async-done(((bf16[16,192,768]{2,1,0:T(8,128)(2,1)}), bf16[16,192,768]{2,1,0:T(8,128)(2,1)}, u32[]{:S(2)}, u32[]{:S(2)}) %all-to-all-start.1) | async-done | bytes 4718624 | tf_op jit(solution)/shard_map/all_to_all | solution.py:351
  124.4 5.3 all-to-all-start.2
  138.0 53.4 %collective-permute-done.4 = bf16[768,192]{1,0:T(8,128)(2,1)S(1)} collective-permute-done((bf16[768,192]{1,0:T(8,128)(2,1)S(1)}, bf16[768,192]{1,0:T(8,128)(2,1)S(1)}, u32[]{:S(2)}, u32[]{:S(2)}) %collective-permute-start.4) | collective-permute-done | bytes 294944 | tf_op jit(solution)/shard_map/ppermute | solution.py:358
  191.3 9.0 %collective-permute-done.5 = bf16[768,192]{1,0:T(8,128)(2,1)} collective-permute-done((bf16[768,192]{1,0:T(8,128)(2,1)S(1)}, bf16[768,192]{1,0:T(8,128)(2,1)}, u32[]{:S(2)}, u32[]{:S(2)}) %collective-permute-start.5) | collective-permute-done | bytes 294944 | tf_op jit(solution)/shard_map/ppermute | solution.py:358
  203.2 15.6 %shard_map.290 = (f32[4,197,768]{2,1,0:T(8,128)}, f32[4,197,32]{2,1,0:T(8,128)}, bf16[8,272,768]{2,1,0:T(8,128)(2,1)}) custom-call(bf16[4,197,768]{2,1,0:T(8,128)(2,1)} %copy.232.images_ref, bf16[4,197,768]{2,1,0:T(8,128)(2,1)} %copy.233.cot_ref, bf16[4,2,197,384]{3,2,1,0:T(8,128)(2,1)} %bitcast.66, bf16[768,768]{1,0:T(8,128)(2,1)} %pad_maximum_fusion.1.out_ref, ...), custom_call_target="tpu_custom_call" | custom-call | flops 3408396288 | bytes 6099776 | tf_op jit(solution)/shard_map/pallas_call | solution.py:607
  225.1 36.6 %all-to-all-done.3.rows_ref.gate_ref.cot_ref = bf16[8,272,768]{2,1,0:T(8,128)(2,1)S(1)} async-done(((bf16[8,272,768]{2,1,0:T(8,128)(2,1)}), bf16[8,272,768]{2,1,0:T(8,128)(2,1)S(1)}, u32[]{:S(2)}, u32[]{:S(2)}) %all-to-all-start.3) | async-done | bytes 3342368 | tf_op jit(solution)/shard_map/all_to_all | solution.py:351
  263.4 18.9 %shard_map.291 = (bf16[8,4,192,128]{3,2,1,0:T(8,128)(2,1)}, bf16[8,4,208,128]{3,2,1,0:T(8,128)(2,1)}, bf16[2,2,512,768]{3,2,1,0:T(8,128)(2,1)}, bf16[2,2,512,768...) custom-call(bf16[8,272,768]{2,1,0:T(8,128)(2,1)} %copy-done, ...), custom_call_target="tpu_custom_call" | custom-call | flops 9663676416 | bytes 28311552 | tf_op jit(solution)/shard_map/pallas_call | solution.py:477
  282.3 46.7 %all_to_all.40.parts_ref = bf16[32,208,128]{2,1,0:T(8,128)(2,1)} all-to-all(bf16[32,208,128]{2,1,0:T(8,128)(2,1)} %bitcast.55), channel_id=1, replica_groups=mesh['dp'=4,'expert'=2,'outer'=2,'inner'=2] {'dp','expert','outer','inner'}, dimensions={0} | all-to-all | bytes 3407872 | tf_op jit(solution)/shard_map/all_to_all | solution.py:351
  329.0 6.2 %shard_map.292 = (bf16[2,197,384]{2,1,0:T(8,128)(2,1)}, f32[4,197,2]{2,1,0:T(8,128)}) custom-call(bf16[32,208,128]{2,1,0:T(8,128)(2,1)} %all_to_all.40.parts_ref, s32[4,197,2]{2,1,0:T(8,128)} %get-tuple-element.194.target_ref), custom_call_target="tpu_custom_call" | custom-call | flops 619708416 | bytes 1710240 | tf_op jit(solution)/shard_map/pallas_call | solution.py:607
  339.5 12.7 %shard_map.294 = bf16[4,2,784,768]{3,2,1,0:T(8,128)(2,1)} custom-call(bf16[8,272,768]{2,1,0:T(8,128)(2,1)} %copy-done, bf16[2,2,512,768]{3,2,1,0:T(8,128)(2,1)} %get-tuple-element.81.grad_pre_ref, bf16[2,768,512]{2,1,0:T(8,128)(2,1)} %get-tuple-element.82.grad_turned_ref, bf16[2,2,512,768]{3,2,1,0:T(8,128)(2,1)} %get-tuple-element.83.hidden_ref, ...), custom_call_target="tpu_custom_call" | custom-call | flops 4831838208 | bytes 15728640 | tf_op jit(solution)/shard_map/pallas_call | solution.py:555
  352.2 40.7 %all-gather.9.cloned.1.call-done = bf16[8,197,384]{2,1,0:T(8,128)(2,1)} async-done(((bf16[2,197,384]{2,1,0:T(8,128)(2,1)}), bf16[8,197,384]{2,1,0:T(8,128)(2,1)}) %all-gather.9.cloned.1.call-update) | async-done | bytes 1210384 | tf_op jit(solution)/shard_map/all_gather | solution.py:1147
  396.8 5.1 all-to-all-start.6
  402.8 21.3 %shard_map.293 = (f32[4,197,768]{2,1,0:T(8,128)}, bf16[4,197,768]{2,1,0:T(8,128)(2,1)}, bf16[768,800]{1,0:T(8,128)(2,1)}, f32[8,768]{1,0:T(8,128)}) custom-call(s32[1]{0:T(128)S(6)} %copy.258.held_ref, bf16[4,197,768]{2,1,0:T(8,128)(2,1)} %copy.232.images_ref, bf16[4,197,768]{2,1,0:T(8,128)(2,1)} %copy.233.cot_ref, ...), custom_call_target="tpu_custom_call" | custom-call | flops 3623236608 | bytes 8652100 | tf_op jit(solution)/shard_map/pallas_call | solution.py:607
  426.6 92.3 %all-reduce.2.cloned.1.call-done.normed_ref = bf16[4,197,768]{2,1,0:T(8,128)(2,1)} async-done(((bf16[4,197,768]{2,1,0:T(8,128)(2,1)}), bf16[4,197,768]{2,1,0:T(8,128)(2,1)}) %all-reduce.2.cloned.1.call-update) | async-done | bytes 1210384 | tf_op jit(solution)/shard_map/psum | solution.py:1167
  518.9 5.2 shard_map.295
  524.3 5.4 shard_map.296
  532.1 36.1 %all-to-all-done.6.parts_ref = bf16[8,784,768]{2,1,0:T(8,128)(2,1)} async-done(((bf16[8,784,768]{2,1,0:T(8,128)(2,1)}), bf16[8,784,768]{2,1,0:T(8,128)(2,1)}, u32[]{:S(2)}, u32[]{:S(2)}) %all-to-all-start.6) | async-done | bytes 9633824 | tf_op jit(solution)/shard_map/all_to_all | solution.py:351
  568.2 4.5 all-to-all-start.7
  580.8 11.0 %shard_map.297 = (f32[16,192,768]{2,1,0:T(8,128)}, f32[16,192,768]{2,1,0:T(8,128)}) custom-call(bf16[8,784,768]{2,1,0:T(8,128)(2,1)} %all-to-all-done.6.parts_ref), custom_call_target="tpu_custom_call" | custom-call | bytes 9633792 | tf_op jit(solution)/shard_map/pallas_call | solution.py:607
  598.1 5.9 collective-permute-done.7
  (134 shorter events, 79.6 us)
Async XLA Ops:
  15.5 6.8 %copy-start.8 = (bf16[192,192]{1,0:T(8,128)(2,1)S(1)}, bf16[192,192]{1,0:T(8,128)(2,1)}, u32[]{:S(2)}) copy-start(bf16[192,192]{1,0:T(8,128)(2,1)} %param.26) | copy-start | bytes 221188
  15.5 11.2 %copy-start.6 = (bf16[4,197,768]{2,0,1:T(4,128)(2,1)S(1)}, bf16[4,197,768]{2,0,1:T(4,128)(2,1)}, u32[]{:S(2)}) copy-start(bf16[4,197,768]{2,0,1:T(4,128)(2,1)} %param.18) | copy-start | bytes 3631108
  15.5 22.3 %all-to-all-start = ((bf16[4,192,821]{2,1,0:T(8,128)(2,1)}), bf16[4,192,821]{2,1,0:T(8,128)(2,1)S(1)}, u32[]{:S(2)}, u32[]{:S(2)}) async-start(bf16[4,192,821]{2,1,0:T(8,128)(2,1)} %broadcast_in_dim.18), calls=%async_computation | async-start | bytes 2752512 | tf_op jit(solution)/shard_map/all_to_all | solution.py:351
  19.8 8.0 %copy-start.14 = (bf16[2,192]{1,0:T(2,128)(2,1)S(1)}, bf16[2,192]{1,0:T(2,128)(2,1)}, u32[]{:S(2)}) copy-start(bf16[2,192]{1,0:T(2,128)(2,1)} %param.25) | copy-start | bytes 2308
  19.8 8.6 %collective-permute-start.3 = (bf16[16,768]{1,0:T(8,128)(2,1)S(1)}, bf16[16,768]{1,0:T(8,128)(2,1)S(1)}, u32[]{:S(2)}, u32[]{:S(2)}) collective-permute-start(bf16[16,768]{1,0:T(8,128)(2,1)S(1)} %copy-done.11), channel_id=1, source_target_pairs={{0,1},{1,0},{2,3},{3,2},{4,5},{5,4},{6,7},{7,6},{8,9},{9,8},{10,11... | collective-permute-start | bytes 73736 | tf_op jit(solution)/shard_map/ppermute | solution.py:358
  22.3 7.4 %collective-permute-start = (bf16[192,192]{1,0:T(8,128)(2,1)S(1)}, bf16[192,192]{1,0:T(8,128)(2,1)S(1)}, u32[]{:S(2)}, u32[]{:S(2)}) collective-permute-start(bf16[192,192]{1,0:T(8,128)(2,1)S(1)} %copy-done.8), channel_id=1, source_target_pairs={{0,3},{1,2},{2,1},{3,0},{4,7},{5,6},{6,5},{7,4},{8,11},{9,10},{10,... | collective-permute-start | bytes 221192 | tf_op jit(solution)/shard_map/ppermute | solution.py:358
  24.8 9.5 %collective-permute-start.1 = (bf16[192,192]{1,0:T(8,128)(2,1)S(1)}, bf16[192,192]{1,0:T(8,128)(2,1)S(1)}, u32[]{:S(2)}, u32[]{:S(2)}) collective-permute-start(bf16[192,192]{1,0:T(8,128)(2,1)S(1)} %copy-done.8), channel_id=1, source_target_pairs={{0,2},{1,3},{2,0},{3,1},{4,6},{5,7},{6,4},{7,5},{8,10},{9,11},{10,... | collective-permute-start | bytes 221192 | tf_op jit(solution)/shard_map/ppermute | solution.py:358
  24.9 9.4 %collective-permute-start.2 = (bf16[192,192]{1,0:T(8,128)(2,1)S(1)}, bf16[192,192]{1,0:T(8,128)(2,1)S(1)}, u32[]{:S(2)}, u32[]{:S(2)}) collective-permute-start(bf16[192,192]{1,0:T(8,128)(2,1)S(1)} %copy-done.8), channel_id=1, source_target_pairs={{0,1},{1,0},{2,3},{3,2},{4,5},{5,4},{6,7},{7,6},{8,9},{9,8},{10,11... | collective-permute-start | bytes 221192 | tf_op jit(solution)/shard_map/ppermute | solution.py:358
  45.8 78.6 %all-to-all-start.1 = ((bf16[16,192,768]{2,1,0:T(8,128)(2,1)}), bf16[16,192,768]{2,1,0:T(8,128)(2,1)}, u32[]{:S(2)}, u32[]{:S(2)}) async-start(bf16[16,192,768]{2,1,0:T(8,128)(2,1)} %param.31), calls=%async_computation.1 | async-start | bytes 9437184 | tf_op jit(solution)/shard_map/all_to_all | solution.py:351
  50.4 52.6 %all-gather.7.cloned.1.call-start = ((), (), s32[]{:S(2)}) async-start(), calls=%async_computation.9 | async-start | bytes 1536000 | tf_op jit(solution)/shard_map/all_gather | solution.py:1104
  124.4 94.4 %all-to-all-start.2 = ((bf16[16,192,768]{2,1,0:T(8,128)(2,1)}), bf16[16,192,768]{2,1,0:T(8,128)(2,1)}, u32[]{:S(2)}, u32[]{:S(2)}) async-start(bf16[16,192,768]{2,1,0:T(8,128)(2,1)} %bitcast.53), calls=%async_computation.2 | async-start | bytes 9437184 | tf_op jit(solution)/shard_map/all_to_all | solution.py:351
  132.2 59.1 %collective-permute-start.4 = (bf16[768,192]{1,0:T(8,128)(2,1)S(1)}, bf16[768,192]{1,0:T(8,128)(2,1)S(1)}, u32[]{:S(2)}, u32[]{:S(2)}) collective-permute-start(bf16[768,192]{1,0:T(8,128)(2,1)S(1)} %pad_maximum_fusion.2), channel_id=1, source_target_pairs={{0,24},{8,16},{16,8},{24,0},{1,25},{9,17},{17,9},{25,1},{2,26},{10... | collective-permute-start | bytes 884744 | tf_op jit(solution)/shard_map/ppermute | solution.py:358
  134.0 66.3 %collective-permute-start.5 = (bf16[768,192]{1,0:T(8,128)(2,1)S(1)}, bf16[768,192]{1,0:T(8,128)(2,1)}, u32[]{:S(2)}, u32[]{:S(2)}) collective-permute-start(bf16[768,192]{1,0:T(8,128)(2,1)S(1)} %pad_maximum_fusion.2), channel_id=1, source_target_pairs={{0,16},{8,24},{16,0},{24,8},{1,17},{9,25},{17,1},{25,9},{2,18},{10... | collective-permute-start | bytes 884744 | tf_op jit(solution)/shard_map/ppermute | solution.py:358
  134.3 66.0 %collective-permute-start.6 = (bf16[768,192]{1,0:T(8,128)(2,1)S(1)}, bf16[768,192]{1,0:T(8,128)(2,1)}, u32[]{:S(2)}, u32[]{:S(2)}) collective-permute-start(bf16[768,192]{1,0:T(8,128)(2,1)S(1)} %pad_maximum_fusion.2), channel_id=1, source_target_pairs={{0,8},{8,0},{16,24},{24,16},{1,9},{9,1},{17,25},{25,17},{2,10},{10... | collective-permute-start | bytes 884744 | tf_op jit(solution)/shard_map/ppermute | solution.py:358
  218.8 42.9 %all-to-all-start.3 = ((bf16[8,272,768]{2,1,0:T(8,128)(2,1)}), bf16[8,272,768]{2,1,0:T(8,128)(2,1)S(1)}, u32[]{:S(2)}, u32[]{:S(2)}) async-start(bf16[8,272,768]{2,1,0:T(8,128)(2,1)} %get-tuple-element.67), calls=%async_computation.3 | async-start | bytes 6684672 | tf_op jit(solution)/shard_map/all_to_all | solution.py:351
  335.3 60.4 %all-to-all-start.5 = ((bf16[32,192,128]{2,1,0:T(8,128)(2,1)}), bf16[32,192,128]{2,1,0:T(8,128)(2,1)S(1)}, u32[]{:S(2)}, u32[]{:S(2)}) async-start(bf16[32,192,128]{2,1,0:T(8,128)(2,1)} %bitcast.16), calls=%async_computation.5 | async-start | bytes 3145728 | tf_op jit(solution)/shard_map/all_to_all | solution.py:351
  338.1 54.8 %all-gather.9.cloned.1.call-start = ((), (), s32[]{:S(2)}) async-start(), calls=%async_computation.10 | async-start | bytes 1536000 | tf_op jit(solution)/shard_map/all_gather | solution.py:1147
  396.8 171.4 %all-to-all-start.6 = ((bf16[8,784,768]{2,1,0:T(8,128)(2,1)}), bf16[8,784,768]{2,1,0:T(8,128)(2,1)}, u32[]{:S(2)}, u32[]{:S(2)}) async-start(bf16[8,784,768]{2,1,0:T(8,128)(2,1)} %bitcast.46), calls=%async_computation.6 | async-start | bytes 19267584 | tf_op jit(solution)/shard_map/all_to_all | solution.py:351
  401.9 117.0 %all-reduce.2.cloned.1.call-start = ((), (), s32[]{:S(2)}) async-start(), calls=%async_computation.8 | async-start | bytes 2457600 | tf_op jit(solution)/shard_map/psum | solution.py:1167
  424.1 151.0 %all-gather.11.cloned.1.call-start = ((), (), s32[]{:S(2)}) async-start(), calls=%async_computation.11 | async-start | bytes 1536000 | tf_op jit(solution)/shard_map/all_gather | solution.py:1174
  426.6 97.5 %copy-start.13 = (f32[8,768]{1,0:T(8,128)S(1)}, f32[8,768]{1,0:T(8,128)}, u32[]{:S(2)}) copy-start(f32[8,768]{1,0:T(8,128)} %get-tuple-element.93) | copy-start | bytes 73732
  532.1 40.6 %copy-start.3 = (f32[4,197,768]{2,1,0:T(8,128)S(1)}, f32[4,197,768]{2,1,0:T(8,128)}, u32[]{:S(2)}) copy-start(f32[4,197,768]{2,1,0:T(8,128)} %get-tuple-element.175) | copy-start | bytes 7262212
  568.2 23.7 %all-to-all-start.7 = ((bf16[8,96,814]{2,1,0:T(8,128)(2,1)}), bf16[8,96,814]{2,1,0:T(8,128)(2,1)}, u32[]{:S(2)}, u32[]{:S(2)}) async-start(bf16[8,96,814]{2,1,0:T(8,128)(2,1)} %bitcast.21), calls=%async_computation.7 | async-start | bytes 2752512 | tf_op jit(solution)/shard_map/all_to_all | solution.py:351
  593.4 10.5 %collective-permute-start.7 = (f32[96,814]{1,0:T(8,128)S(1)}, f32[96,814]{1,0:T(8,128)S(1)}, u32[]{:S(2)}, u32[]{:S(2)}) collective-permute-start(f32[96,814]{1,0:T(8,128)S(1)} %convert_reduce_fusion), channel_id=1, source_target_pairs={{0,4},{4,0},{1,5},{5,1},{2,6},{6,2},{3,7},{7,3},{8,12},{12,8},{9,1... | collective-permute-start | bytes 937736 | tf_op jit(solution)/shard_map/ppermute | solution.py:358
  (10 other events, 36.6 us)
Sparse Core Ops, SparseCore 0:
  52.8 50.1 all-gather.6
  341.1 51.8 all-gather.8
  424.2 94.6 all-reduce.1
  524.3 42.8 all-gather.10

commit v8 on v6

--- a/solution.py
+++ b/solution.py
@@ -13,7 +13,7 @@
 EXPERTS = 32
 TOPK = 2
 CAP = 64
-FF_PAIR = 2
+FF_PAIR = 1
 PAIR = 2
 EXTRA = 16
 VMEM_LIMIT = 56 * 1024 * 1024
@@ -365,6 +365,11 @@
     return gathered
 
 
+def cross(values, s):
+    count = lax.axis_size((DP, INNER))
+    return lax.ppermute(values, (DP, INNER), [(i, i ^ s) for i in range(count)]) if s else values
+
+
 def high_low(values):
     high = lax.reduce_precision(values, 8, 7)
     return high.astype(jnp.bfloat16), (values - high).astype(jnp.bfloat16)
@@ -376,27 +381,18 @@
     )
 
 
-def expert_kernel(
-    inner,
-    rows_ref,
-    gate_ref,
-    cot_ref,
-    in_ref,
-    back_ref,
-    in_bias_ref,
-    back_bias_ref,
-    returned_ref,
-    grads_ref,
-    hidden_ref,
-    grad_pre_ref,
-    grad_turned_ref,
-    grad_in_bias_ref,
-    grad_back_bias_ref,
-):
+def expert_kernel(inner, owners, at_ref, rows_ref, gate_ref, cot_ref, in_bias_ref, back_bias_ref, *refs):
+    in_refs, back_refs, refs = refs[:owners], refs[owners : 2 * owners], refs[2 * owners :]
+    returned_ref, grads_ref, hidden_ref, grad_pre_ref, grad_turned_ref = refs[:5]
+    grad_in_bias_ref, grad_back_bias_ref, weight_ref = refs[5:]
     f32, bf16 = jnp.float32, jnp.bfloat16
     groups, cap, width = rows_ref.shape
-    chunks = in_ref.shape[0]
-    data = chunks // inner
+    depth = in_refs[0].shape[1]
+    for s in range(owners):
+        source = at_ref[0] ^ s
+        place = pl.ds(pl.multiple_of((source // inner) * depth, depth), depth)
+        weight_ref[0, source % inner, place] = in_refs[s][0]
+        weight_ref[1, source % inner, place] = back_refs[s][0]
     tensor, slice_width = returned_ref.shape[1:3]
     mine = back_bias_ref.shape[1]
     total = groups * cap
@@ -420,8 +416,7 @@
     part = jnp.broadcast_to(bias, (width, total))
     back = jnp.zeros((width, total), f32)
     for t in range(inner):
-        w_in = jnp.concatenate([in_ref[d * inner + t, 0] for d in range(data)], axis=0)
-        w_back = jnp.concatenate([back_ref[d * inner + t, 0] for d in range(data)], axis=0)
+        w_in, w_back = weight_ref[0, t], weight_ref[1, t]
         pre = jnp.dot(rows, w_in, preferred_element_type=f32) + in_bias_ref[0, t : t + 1, :]
         square = pre * pre
         bent = jnp.tanh(GELU_SCALE * pre * (1.0 + GELU_CUBE * square))
@@ -458,10 +453,11 @@
                     grads_ref[g, z, slice_width:, lanes] = tail[:, mine_lanes]
 
 
-def run_experts(arrived, in_raw, back_raw, in_bias, back_bias, inner, tensor):
+def run_experts(owner_at, arrived, in_pieces, back_pieces, in_bias, back_bias, inner, tensor):
     f32, bf16 = jnp.float32, jnp.bfloat16
     groups, _, width = arrived.shape
-    chunks, mine, depth, ff = in_raw.shape
+    owners = len(in_pieces)
+    mine, depth, ff = in_pieces[0].shape
     total = groups * CAP
     slice_width = width // tensor
     gate_at = 2 * mine * CAP // EXTRA
@@ -475,58 +471,55 @@
         ((mine, 1, width), f32, lambda j: (j, 0, 0), 1),
     ]
     return pl.pallas_call(
-        functools.partial(expert_kernel, inner),
+        functools.partial(expert_kernel, inner, owners),
         grid=(mine,),
         in_specs=[
+            pl.BlockSpec(memory_space=pltpu.SMEM),
             pl.BlockSpec((groups, CAP, width), lambda j: (0, j, 0)),
             pl.BlockSpec((groups, EXTRA, mine * CAP), lambda j: (0, gate_at, 0)),
             pl.BlockSpec((groups, CAP, width), lambda j: (0, mine + j, 0)),
-            pl.BlockSpec((chunks, 1, depth, ff), lambda j: (0, j, 0, 0)),
-            pl.BlockSpec((chunks, 1, depth, ff), lambda j: (0, j, 0, 0)),
             pl.BlockSpec((1, inner, ff), lambda j: (j, 0, 0)),
             pl.BlockSpec((width, mine), lambda j: (0, 0)),
-        ],
+        ]
+        + [pl.BlockSpec((1, depth, ff), lambda j: (j, 0, 0))] * (2 * owners),
         out_specs=[
             pl.BlockSpec(shape if lead is None else (lead, *shape[1:]), index)
             for shape, _, index, lead in outs
         ],
         out_shape=[jax.ShapeDtypeStruct(shape, dtype) for shape, dtype, _, _ in outs],
+        scratch_shapes=[pltpu.VMEM((2, inner, width, ff), bf16)],
         compiler_params=pltpu.CompilerParams(vmem_limit_bytes=VMEM_LIMIT),
         cost_estimate=pl.CostEstimate(
             flops=8 * mine * total * width * inner * ff,
-            bytes_accessed=4 * chunks * mine * depth * ff + 12 * mine * total * inner * ff,
+            bytes_accessed=4 * owners * mine * depth * ff + 12 * mine * total * inner * ff,
             transcendentals=mine * total * inner * ff,
         ),
-    )(arrived, arrived, arrived, in_raw, back_raw, in_bias, back_bias)
+    )(owner_at.reshape(1), arrived, arrived, arrived, in_bias, back_bias, *in_pieces, *back_pieces)
 
 
 def weight_kernel(
+    inner,
+    at_ref,
     rows_ref,
     grad_pre_ref,
     grad_turned_ref,
     hidden_ref,
     in_bias_ref,
     back_bias_ref,
-    out_ref,
+    *refs,
 ):
     f32, bf16 = jnp.float32, jnp.bfloat16
+    out_refs, sums_ref, tail_ref = refs[:-2], refs[-2], refs[-1]
     groups, cap, width = rows_ref.shape
-    data, ff = out_ref.shape[0], out_ref.shape[-1]
-    depth = width // data
     mine = back_bias_ref.shape[0]
-    at = pl.program_id(1)
+    ff = sums_ref.shape[-1]
+    depth = width * inner // len(out_refs)
+    data = width // depth
+    part, at = pl.program_id(0), pl.program_id(1)
     rows = rows_ref[...].reshape(groups * cap, width)
-    grad_in = turned_dot(rows, grad_pre_ref[0, 0], 0, 0).astype(bf16)
+    sums_ref[0] = turned_dot(rows, grad_pre_ref[0, 0], 0, 0).astype(bf16)
     grad_back = jnp.dot(grad_turned_ref[0], hidden_ref[0, 0], preferred_element_type=f32)
-    grad_back = grad_back.astype(bf16)
-    for j in range(mine):
-
-        @pl.when(at == j)
-        def _():
-            for d in range(data):
-                lines = slice(d * depth, (d + 1) * depth)
-                out_ref[d, 0, j * depth : (j + 1) * depth] = grad_in[lines]
-                out_ref[d, 0, (mine + j) * depth : (mine + j + 1) * depth] = grad_back[lines]
+    sums_ref[1] = grad_back.astype(bf16)
 
     @pl.when(at == mine - 1)
     def _():
@@ -543,19 +536,37 @@
                 gap = jnp.zeros((1, ff // 2 - depth), f32)
                 lines.append(jnp.concatenate([high, gap, values - high, gap], axis=1))
             lines.append(jnp.zeros((EXTRA - len(lines), ff), f32))
-            out_ref[d, 0, 2 * mine * depth :] = jnp.concatenate(lines, axis=0).astype(bf16)
-
-
-def weight_grads(arrived, grad_pre, grad_turned, hidden, grad_in_bias, grad_back_bias, data):
+            tail_ref[d] = jnp.concatenate(lines, axis=0).astype(bf16)
+
+    for s, out_ref in enumerate(out_refs):
+        owner = at_ref[0] ^ s
+        d = owner // inner
+        place = pl.ds(pl.multiple_of(d * depth, depth), depth)
+
+        @pl.when(owner % inner == part)
+        def _():
+            for k in range(2):
+                line = pl.multiple_of((k * mine + at) * depth, depth)
+                out_ref[pl.ds(line, depth)] = sums_ref[k, place]
+
+            @pl.when(at == mine - 1)
+            def _():
+                out_ref[2 * mine * depth :] = tail_ref[d]
+
+
+def weight_grads(
+    owner_at, arrived, grad_pre, grad_turned, hidden, grad_in_bias, grad_back_bias, owners
+):
     mine, inner, total, ff = hidden.shape
     groups, _, width = arrived.shape
-    depth = width // data
+    depth = width * inner // owners
     kept = pl.BlockSpec((1, 1, total, ff), lambda t, j: (j, t, 0, 0))
-    out = (data, inner, 2 * mine * depth + EXTRA, ff)
+    out = (2 * mine * depth + EXTRA, ff)
     return pl.pallas_call(
-        weight_kernel,
+        functools.partial(weight_kernel, inner),
         grid=(inner, mine),
         in_specs=[
+            pl.BlockSpec(memory_space=pltpu.SMEM),
             pl.BlockSpec((groups, CAP, width), lambda t, j: (0, j, 0)),
             kept,
             pl.BlockSpec((1, width, total), lambda t, j: (j, 0, 0)),
@@ -563,28 +574,55 @@
             pl.BlockSpec((mine, 1, 1, ff), lambda t, j: (0, t, 0, 0)),
             pl.BlockSpec((mine, 1, width), lambda t, j: (0, 0, 0)),
         ],
-        out_specs=pl.BlockSpec((data, 1, *out[2:]), lambda t, j: (0, t, 0, 0)),
-        out_shape=jax.ShapeDtypeStruct(out, jnp.bfloat16),
+        out_specs=[pl.BlockSpec(out, lambda t, j: (0, 0))] * owners,
+        out_shape=[jax.ShapeDtypeStruct(out, jnp.bfloat16)] * owners,
+        scratch_shapes=[
+            pltpu.VMEM((2, width, ff), jnp.bfloat16),
+            pltpu.VMEM((width // depth, EXTRA, ff), jnp.bfloat16),
+        ],
         compiler_params=pltpu.CompilerParams(vmem_limit_bytes=VMEM_LIMIT),
         cost_estimate=pl.CostEstimate(
             flops=4 * mine * total * width * inner * ff,
             bytes_accessed=4 * mine * inner * (total + width) * ff,
             transcendentals=0,
         ),
-    )(arrived, grad_pre, grad_turned, hidden, grad_in_bias[:, :, None], grad_back_bias)
-
-
-def widen_kernel(parts_ref, in_ref, back_ref):
+    )(
+        owner_at.reshape(1),
+        arrived,
+        grad_pre,
+        grad_turned,
+        hidden,
+        grad_in_bias[:, :, None],
+        grad_back_bias,
+    )
+
+
+def widen_kernel(at_ref, *refs):
+    part_refs, (in_ref, back_ref) = refs[:-2], refs[-2:]
     mine, depth, ff = in_ref.shape
     rows = mine * depth
-    in_ref[...] = parts_ref[0, :rows].astype(jnp.float32).reshape(mine, depth, ff)
-    back_ref[...] = parts_ref[0, rows : 2 * rows].astype(jnp.float32).reshape(mine, depth, ff)
-
-
-def run_widen(parts, mine, depth):
-    owners, _, ff = parts.shape
-    out = ((owners * mine, depth, ff), jnp.float32, (mine, depth, ff), lambda p: (p, 0, 0))
-    return call_kernel(widen_kernel, (owners,), [by_step(parts, 1)], [out, out])
+    for s, part_ref in enumerate(part_refs):
+
+        @pl.when(pl.program_id(0) == s)
+        def _():
+            in_ref[...] = part_ref[:rows].astype(jnp.float32).reshape(mine, depth, ff)
+            back_ref[...] = part_ref[rows : 2 * rows].astype(jnp.float32).reshape(mine, depth, ff)
+
+
+def run_widen(owner_at, parts, mine, depth):
+    owners, ff = len(parts), parts[0].shape[1]
+    out = pl.BlockSpec((mine, depth, ff), lambda p, at: (at[0] ^ p, 0, 0))
+    return pl.pallas_call(
+        widen_kernel,
+        grid_spec=pltpu.PrefetchScalarGridSpec(
+            num_scalar_prefetch=1,
+            grid=(owners,),
+            in_specs=[pl.BlockSpec((2 * mine * depth, ff), lambda p, at: (0, 0))] * owners,
+            out_specs=[out, out],
+        ),
+        out_shape=[jax.ShapeDtypeStruct((owners * mine, depth, ff), jnp.float32)] * 2,
+        compiler_params=pltpu.CompilerParams(vmem_limit_bytes=VMEM_LIMIT),
+    )(owner_at.reshape(1), *parts)
 
 
 def norm_rows(values):
@@ -1082,18 +1120,20 @@
     packed = swap(jnp.broadcast_to(packed[None], (data, *packed.shape)), DP).reshape(width, -1)
     out_rows = jnp.concatenate(hop_gather(w_out, tensor_axes), axis=0)
     in_bias_all = jnp.stack(hop_gather(in_bias, INNER))
-    packed, out_rows, in_bias_all, w_in = lax.optimization_barrier(
-        (packed, out_rows, in_bias_all, w_in)
+
+    def piece(shard, s):
+        return cross(lax.dynamic_slice_in_dim(shard, (owner_at ^ s) * mine, mine, 0), s)
+
+    in_pieces = [piece(w_in, s) for s in range(owners)]
+    back_pieces = [piece(w_back.transpose(0, 2, 1), s) for s in range(owners)]
+    far = owners // 2
+    packed, out_rows, in_bias_all, in_pieces[far] = lax.optimization_barrier(
+        (packed, out_rows, in_bias_all, in_pieces[far])
     )
     vectors = packed[:, router_at + EXPERTS + experts_here :].T.astype(f32)
     out_whole = jnp.concatenate(hop_gather(out_rows, DP), axis=1)
     in_bias_mine = lax.dynamic_slice_in_dim(in_bias_all, owner_at * mine, mine, 1)
     in_bias_mine = in_bias_mine.transpose(1, 0, 2).astype(f32)
-
-    chunk_shape = (owners, mine, shard_width, ff_here)
-    in_raw, w_back = lax.optimization_barrier((swap(w_in, (DP, INNER)), w_back))
-    in_raw = in_raw.reshape(chunk_shape)
-    back_raw = swap(w_back.transpose(0, 2, 1), (DP, INNER)).reshape(chunk_shape)
 
     home, within = routes // experts_here, routes % experts_here
     owner, nth = within // mine, within % mine
@@ -1106,8 +1146,12 @@
     plane_target = plane_target.transpose(0, 2, 1)
 
     attended, proj = run_attend(images, packed, vectors, qv_bias.astype(f32))
+
+    attended, out_whole = lax.optimization_barrier((attended, out_whole))
     attended_all = lax.all_gather(attended, tensor_axes)
-    attended_all, in_raw = lax.optimization_barrier((attended_all, in_raw))
+    attended_all, in_pieces[far + 1 :], back_pieces[: far + 1] = lax.optimization_barrier(
+        (attended_all, in_pieces[far + 1 :], back_pieces[: far + 1])
+    )
     mixed, probs, sent = run_route(
         images,
         cotangent,
@@ -1120,7 +1164,7 @@
         groups,
         slots // inner,
     )
-    sent, back_raw = lax.optimization_barrier((sent, back_raw))
+    sent, back_pieces = lax.optimization_barrier((sent, back_pieces))
     arrived = swap(sent, (DP, EXPERT))
     back_bias_mine = lax.dynamic_slice_in_dim(packed, router_at + EXPERTS + owner_at * mine, mine, 1)
     back_bias_mine = jnp.where(lax.axis_index(OUTER) == 0, back_bias_mine.astype(f32), 0.0)
@@ -1133,23 +1177,32 @@
         grad_in_bias_mine,
         grad_back_bias_mine,
     ) = run_experts(
-        arrived, in_raw, back_raw, in_bias_mine, back_bias_mine, inner, tensor
+        owner_at, arrived, in_pieces, back_pieces, in_bias_mine, back_bias_mine, inner, tensor
     )
 
     def bring(parts):
         return swap(parts.reshape(groups * tensor, *parts.shape[2:]), everywhere)
 
     grad_parts = bring(grads_out)
-    weight_out = weight_grads(
-        arrived, grad_pre_low, grad_turned, hidden_low, grad_in_bias_mine, grad_back_bias_mine, data
+    weight_parts = weight_grads(
+        owner_at,
+        arrived,
+        grad_pre_low,
+        grad_turned,
+        hidden_low,
+        grad_in_bias_mine,
+        grad_back_bias_mine,
+        owners,
+    )
+    weight_parts = [cross(part, s) for s, part in enumerate(weight_parts)]
+    grad_parts, weight_parts[: far + 1] = lax.optimization_barrier(
+        (grad_parts, weight_parts[: far + 1])
     )
     rows_cut, grad_gates = run_take_grads(grad_parts, target, slice_width, outer, inner, slots)
     rows_cut, returned_out = lax.optimization_barrier((rows_cut, returned_out))
     rows_all = lax.all_gather(rows_cut, tensor_axes)
     returned = bring(returned_out)
-    rows_all, returned = lax.optimization_barrier((rows_all, returned))
-    returned, weight_out = lax.optimization_barrier((returned, weight_out))
-    weight_parts = swap(weight_out.reshape(owners, *weight_out.shape[2:]), (DP, INNER))
+    rows_all, returned, weight_parts = lax.optimization_barrier((rows_all, returned, weight_parts))
     grad_mixed, normed_part, matrix, sums = run_pull(
         images_held,
         images,
@@ -1166,6 +1219,9 @@
         router_at,
     )
     grad_normed = lax.psum(normed_part, tensor_axes)
+    grad_normed, returned, weight_parts = lax.optimization_barrier(
+        (grad_normed, returned, weight_parts)
+    )
     grad_images, first_sums = run_last(images, grad_normed, grad_mixed, vectors)
     mixed_cut = lax.dynamic_slice_in_dim(mixed, tensor_at * slice_width, slice_width, 2)
     output_cut = run_take_rows(
@@ -1188,13 +1244,18 @@
     grad_w_router = small[:, router_at : router_at + EXPERTS]
     vector_grads = small[:, router_at + EXPERTS :].T
     vector_grads = vector_grads[:7] + vector_grads[7:]
-    grad_w_in, grad_w_back = run_widen(weight_parts, mine, shard_width)
+    grad_w_in, grad_w_back = run_widen(owner_at, weight_parts, mine, shard_width)
     grad_w_back = grad_w_back.transpose(0, 2, 1)
-    lines = weight_parts[:, 2 * mine * shard_width :].astype(f32)
-    grad_in_bias = lines[:, : 2 * mine].reshape(owners, mine, 2, ff_here)
-    grad_in_bias = jnp.sum(grad_in_bias, axis=2).reshape(experts_here, ff_here)
-    lines = lines[:, 2 * mine : 3 * mine].reshape(experts_here, 2, ff_here // 2)
-    grad_back_shard = jnp.sum(lines[:, :, :shard_width], axis=1)
+    grad_in_bias = jnp.zeros((experts_here, ff_here), f32)
+    grad_back_shard = jnp.zeros((experts_here, shard_width), f32)
+    for s, part in enumerate(weight_parts):
+        start = (owner_at ^ s) * mine
+        lines = part[2 * mine * shard_width :].astype(f32)
+        line = jnp.sum(lines[: 2 * mine].reshape(mine, 2, ff_here), axis=1)
+        grad_in_bias = lax.dynamic_update_slice_in_dim(grad_in_bias, line, start, 0)
+        line = lines[2 * mine : 3 * mine]
+        line = line[:, :shard_width] + line[:, ff_here // 2 : ff_here // 2 + shard_width]
+        grad_back_shard = lax.dynamic_update_slice_in_dim(grad_back_shard, line, start, 0)
     return (
         output,
         grad_images,

time: 638 us -> 621 us (0.973)
  blocking collectives: 109 us -> 0 us
  waiting for transfers between devices: 312 us -> 391 us
  Pallas kernels: 103 us -> 116 us
    ppermute x0 -> x9, waiting for transfers between devices: none -> 205 us  [cross(): lax.ppermute(values, (DP, INNER), [(i, i ^ s) for i in range(count)])]
    all_to_all x2 -> x0, blocking collectives: 109 us -> none  [swap(): return lax.all_to_all(values, axes, split_axis=0, concat_axis=0, tiled=True)]
    all_gather x1, waiting for transfers between devices: 53.2 us -> 0.01 us  [moved_plan(): rows_all = lax.all_gather(rows_cut, tensor_axes)]
    all_gather x1, waiting for transfers between devices: 42.3 us -> 4.41 us  [moved_plan(): output = lax.all_gather(output_cut, tensor_axes)]
    ppermute x8 -> x7, waiting for transfers between devices: 56.5 us -> 24.9 us  [hop_gather(): hops.append(lax.ppermute(values, axes, [(i, i ^ s) for i in range(count)]))]
    pallas_call x2 -> x3, Pallas kernels: 31.7 us -> 46.2 us  [the longest x1 23.1 us: run_experts(): pl.pallas_call(functools.partial(expert_kernel, inner, owners), grid=(min...]
    dynamic_slice x0 -> x2, local copies, waits for them, and re-layouts: none -> 9.4 us  [piece(): lax.dynamic_slice_in_dim(shard, (owner_at ^ s) * mine, mine, 0)]
    ppermute x0 -> x9, starting transfers between devices: none -> 9.21 us  [cross(): lax.ppermute(values, (DP, INNER), [(i, i ^ s) for i in range(count)])]
  transfers between devices with their start and end apart: 18 -> 25, of which waited for: 12 -> 18; matrix products, arithmetic and copies ran while one was open for 6% -> 5% of each run, Pallas kernels for 6% -> 8%
where the time goes in v8:
time: 621 us; the launch traced here: 614 us
  waiting for transfers between devices  391 us (63%)
  Pallas kernels  116 us (19%)
  starting transfers between devices  41.7 us (7%)
  local copies, waits for them, and re-layouts  37.7 us (6%)
  between operations  15.4 us (2%)
  other arithmetic  11.9 us (2%)
    ppermute x9, waiting for transfers between devices, cross(): lax.ppermute(values, (DP, INNER), [(i, i ^ s) for i in range(count)])  205 us
    all_to_all x5, waiting for transfers between devices, swap(): return lax.all_to_all(values, axes, split_axis=0, concat_axis=0, tiled=True)  103 us
    pallas_call x6, Pallas kernels, call_kernel(): pl.pallas_call(kernel, grid=grid, in_specs=[smem if b is None else pl.Blo...  69.9 us
    psum x1, waiting for transfers between devices, moved_plan(): grad_normed = lax.psum(normed_part, tensor_axes)  54.6 us
    ppermute x7, waiting for transfers between devices, hop_gather(): hops.append(lax.ppermute(values, axes, [(i, i ^ s) for i in range(count)]))  24.9 us
    all_to_all x5, starting transfers between devices, swap(): return lax.all_to_all(values, axes, split_axis=0, concat_axis=0, tiled=True)  24.4 us
    pallas_call x1, Pallas kernels, run_experts(): pl.pallas_call(functools.partial(expert_kernel, inner, owners), grid=(min...  23.1 us
    unnamed x64, local copies, waits for them, and re-layouts  16.7 us
  transfers between devices with their start and end apart: 25, of which 18 were waited for; matrix products, arithmetic and copies ran while one was open for 5% of the time, Pallas kernels for 8%

profile of v8, /device:TPU:0, one launch (start us, length us, event | category | flops | bytes accessed | tf_op | source)
XLA Modules:
  0.0 614.1 jit_solution(3422676560239887466)
XLA Ops:
  7.3 4.8 constant_dynamic-slice_fusion.1
  28.2 5.0 collective-permute-done.1
  33.3 22.6 %all-to-all-done = bf16[4,192,821]{2,1,0:T(8,128)(2,1)S(1)} async-done(((bf16[4,192,821]{2,1,0:T(8,128)(2,1)}), bf16[4,192,821]{2,1,0:T(8,128)(2,1)S(1)}, u32[]{:S(2)}, u32[]{:S(2)}) %all-to-all-start) | async-done | bytes 1261088 | tf_op jit(solution)/shard_map/all_to_all | solution.py:351
  59.2 6.6 %shard_map.289 = (bf16[2,197,384]{2,1,0:T(8,128)(2,1)}, bf16[4,197,576]{2,1,0:T(8,128)(2,1)}) custom-call(bf16[4,197,768]{2,1,0:T(8,128)(2,1)} %copy.193.images_ref, bf16[768,821]{1,0:T(8,128)(2,1)} %bitcast.46, f32[5,768]{1,0:T(8,128)} %convert_bitcast_fusion.vector_ref, f32[2,192]{1,0:T(2,128)} %convert_element_type.39.bias_ref), custom_call_target="tpu_custom_call" | custom-call | flops 935614464 | bytes 2488320 | tf_op jit(solution)/shard_map/pallas_call | solution.py:645
  67.1 8.8 %collective-permute-done.5 = bf16[768,192]{1,0:T(8,128)(2,1)} collective-permute-done((bf16[768,192]{1,0:T(8,128)(2,1)S(1)}, bf16[768,192]{1,0:T(8,128)(2,1)}, u32[]{:S(2)}, u32[]{:S(2)}) %collective-permute-start.5) | collective-permute-done | bytes 294944 | tf_op jit(solution)/shard_map/ppermute | solution.py:358
  90.6 16.7 %collective-permute-done.7.refs_3_ = bf16[4,192,768]{2,1,0:T(8,128)(2,1)} collective-permute-done((bf16[4,192,768]{2,1,0:T(8,128)(2,1)S(1)}, bf16[4,192,768]{2,1,0:T(8,128)(2,1)}, u32[]{:S(2)}, u32[]{:S(2)}) %collective-permute-start.7) | collective-permute-done | bytes 1179680 | tf_op jit(solution)/shard_map/ppermute | solution.py:370
  107.3 25.3 %collective-permute-done.9.refs_6_ = bf16[4,192,768]{2,1,0:T(8,128)(2,1)} collective-permute-done((bf16[4,192,768]{2,1,0:T(8,128)(2,1)}, bf16[4,192,768]{2,1,0:T(8,128)(2,1)}, u32[]{:S(2)}, u32[]{:S(2)}) %collective-permute-start.9) | collective-permute-done | bytes 1179680 | tf_op jit(solution)/shard_map/ppermute | solution.py:370
  132.5 22.5 %shard_map.290 = (f32[4,197,768]{2,1,0:T(8,128)}, f32[4,197,32]{2,1,0:T(8,128)}, bf16[8,528,768]{2,1,0:T(8,128)(2,1)}) custom-call(bf16[4,197,768]{2,1,0:T(8,128)(2,1)} %copy.193.images_ref, bf16[4,197,768]{2,1,0:T(8,128)(2,1)} %copy.194.cot_ref, bf16[4,2,197,384]{3,2,1,0:T(8,128)(2,1)} %bitcast.58, bf16[768,768]{1,0:T(8,128)(2,1)} %pad_maximum_fusion.1.out_ref, ...), custom_call_target="tpu_custom_call" | custom-call | flops 5887229952 | bytes 6099776 | tf_op jit(solution)/shard_map/pallas_call | solution.py:645
  157.8 5.3 all-to-all-start.1
  167.0 68.9 %all-to-all-done.1.rows_ref.gate_ref.cot_ref = bf16[8,528,768]{2,1,0:T(8,128)(2,1)} async-done(((bf16[8,528,768]{2,1,0:T(8,128)(2,1)}), bf16[8,528,768]{2,1,0:T(8,128)(2,1)}, u32[]{:S(2)}, u32[]{:S(2)}) %all-to-all-start.1) | async-done | bytes 6488096 | tf_op jit(solution)/shard_map/all_to_all | solution.py:351
  236.0 23.1 %shard_map.291 = (bf16[8,4,192,256]{3,2,1,0:T(8,128)(2,1)}, bf16[8,4,208,256]{3,2,1,0:T(8,128)(2,1)}, bf16[4,1,512,768]{3,2,1,0:T(8,128)(2,1)}, bf16[4,1,512,768...) custom-call(s32[1]{0:T(128)} %bitcast.11.at_ref, ...), custom_call_target="tpu_custom_call" | custom-call | flops 9663676416 | bytes 28311552 | tf_op jit(solution)/shard_map/pallas_call | solution.py:473
  259.1 4.9 all-to-all-start.2
  263.9 12.4 %shard_map.292 = (bf16[1552,768]{1,0:T(8,128)(2,1)}, bf16[1552,768]{1,0:T(8,128)(2,1)}, bf16[1552,768]{1,0:T(8,128)(2,1)}, bf16[1552,768]{1,0:T(8,128)(2,1)}) custom-call(s32[1]{0:T(128)} %bitcast.11.at_ref, bf16[8,528,768]{2,1,0:T(8,128)(2,1)} %all-to-all-done.1.rows_ref.gate_ref.cot_ref, bf16[4,1,512,768]{3,2,1,0:T(8,128)(2,1)} %get-tuple-element.96.grad_pre_ref, ...), custom_call_target="tpu_custom_call" | custom-call | flops 4831838208 | bytes 15728640 | tf_op jit(solution)/shard_map/pallas_call | solution.py:565
  282.6 72.1 %collective-permute-done.13.refs_2_ = bf16[1552,768]{1,0:T(8,128)(2,1)} collective-permute-done((bf16[1552,768]{1,0:T(8,128)(2,1)}, bf16[1552,768]{1,0:T(8,128)(2,1)}, u32[]{:S(2)}, u32[]{:S(2)}) %collective-permute-start.13) | collective-permute-done | bytes 2383904 | tf_op jit(solution)/shard_map/ppermute | solution.py:370
  356.5 6.9 %shard_map.293 = (bf16[2,197,384]{2,1,0:T(8,128)(2,1)}, f32[4,197,2]{2,1,0:T(8,128)}) custom-call(bf16[32,208,256]{2,1,0:T(8,128)(2,1)} %copy-done, s32[4,197,2]{2,1,0:T(8,128)} %get-tuple-element.229.target_ref), custom_call_target="tpu_custom_call" | custom-call | flops 619708416 | bytes 3414176 | tf_op jit(solution)/shard_map/pallas_call | solution.py:645
  363.3 6.9 %all-to-all-start.3 = ((bf16[32,192,256]{2,1,0:T(8,128)(2,1)}), bf16[32,192,256]{2,1,0:T(8,128)(2,1)S(1)}, u32[]{:S(2)}, u32[]{:S(2)}) async-start(bf16[32,192,256]{2,1,0:T(8,128)(2,1)} %bitcast.51), calls=%async_computation.3 | async-start | bytes 6291456 | tf_op jit(solution)/shard_map/all_to_all | solution.py:351
  372.6 84.0 %collective-permute-done.14.refs_3_ = bf16[1552,768]{1,0:T(8,128)(2,1)} collective-permute-done((bf16[1552,768]{1,0:T(8,128)(2,1)}, bf16[1552,768]{1,0:T(8,128)(2,1)}, u32[]{:S(2)}, u32[]{:S(2)}) %collective-permute-start.14) | collective-permute-done | bytes 2383904 | tf_op jit(solution)/shard_map/ppermute | solution.py:370
  460.5 22.3 %shard_map.294 = (f32[4,197,768]{2,1,0:T(8,128)}, bf16[4,197,768]{2,1,0:T(8,128)(2,1)}, bf16[768,800]{1,0:T(8,128)(2,1)}, f32[8,768]{1,0:T(8,128)}) custom-call(s32[1]{0:T(128)S(6)} %copy.246.held_ref, bf16[4,197,768]{2,1,0:T(8,128)(2,1)} %copy.193.images_ref, bf16[4,197,768]{2,1,0:T(8,128)(2,1)} %copy.194.cot_ref, ...), custom_call_target="tpu_custom_call" | custom-call | flops 3623236608 | bytes 8652100 | tf_op jit(solution)/shard_map/pallas_call | solution.py:645
  485.5 54.6 %all-reduce.2.cloned.1.call-done.normed_ref = bf16[4,197,768]{2,1,0:T(8,128)(2,1)} async-done(((bf16[4,197,768]{2,1,0:T(8,128)(2,1)}), bf16[4,197,768]{2,1,0:T(8,128)(2,1)}) %all-reduce.2.cloned.1.call-update) | async-done | bytes 1210384 | tf_op jit(solution)/shard_map/psum | solution.py:1221
  540.8 10.6 %shard_map.297 = (f32[16,192,768]{2,1,0:T(8,128)}, f32[16,192,768]{2,1,0:T(8,128)}) custom-call(s32[1]{0:T(128)} %bitcast.11.at_ref, bf16[1552,768]{1,0:T(8,128)(2,1)} %get-tuple-element.129.refs_0_, bf16[1552,768]{1,0:T(8,128)(2,1)} %copy-done.4, bf16[1552,768]{1,0:T(8,128)(2,1)} %collective-permute-done.13.refs_2_, ...), custom_call_target="tpu_custom_call" | custom-call | tf_op jit(solution)/shard_map/pallas_call | solution.py:615
  552.2 5.4 shard_map.296
  563.8 6.1 %shard_map.295 = bf16[2,197,384]{2,1,0:T(8,128)(2,1)} custom-call(s32[1]{0:T(128)S(6)} %copy.246.held_ref, bf16[32,192,256]{2,1,0:T(8,128)(2,1)} %copy-done.1, s32[4,197,2]{2,1,0:T(8,128)} %get-tuple-element.229.target_ref, f32[4,197,32]{2,1,0:T(8,128)} %get-tuple-element.82.probs_ref, s32[4,197,2]{2,1,0:T(8,128)} %copy-done.3, ...), custom_call_target="tpu_custom_call" | custom-call | flops 1239416832 | bytes 3864388 | tf_op jit(solution)/shard_map/pallas_call | solution.py:645
  574.5 7.3 %all-to-all-done.4 = bf16[8,96,814]{2,1,0:T(8,128)(2,1)S(1)} async-done(((bf16[8,96,814]{2,1,0:T(8,128)(2,1)}), bf16[8,96,814]{2,1,0:T(8,128)(2,1)S(1)}, u32[]{:S(2)}, u32[]{:S(2)}) %all-to-all-start.4) | async-done | bytes 1250336 | tf_op jit(solution)/shard_map/all_to_all | solution.py:351
  583.6 8.6 %collective-permute-done.15 = f32[96,814]{1,0:T(8,128)S(1)} collective-permute-done((f32[96,814]{1,0:T(8,128)S(1)}, f32[96,814]{1,0:T(8,128)S(1)}, u32[]{:S(2)}, u32[]{:S(2)}) %collective-permute-start.15) | collective-permute-done | bytes 312608 | tf_op jit(solution)/shard_map/ppermute | solution.py:358
  (181 shorter events, 86.9 us)
Async XLA Ops:
  12.1 43.9 %collective-permute-start.3 = (bf16[4,192,768]{2,1,0:T(8,128)(2,1)}, bf16[4,192,768]{2,1,0:T(8,128)(2,1)}, u32[]{:S(2)}, u32[]{:S(2)}) collective-permute-start(bf16[4,192,768]{2,1,0:T(8,128)(2,1)} %get-tuple-element.217), channel_id=1, source_target_pairs={{0,16},{8,24},{16,0},{24,8},{1,17},{9,25},{17,1},{25,9},{2,18},{10... | collective-permute-start | bytes 3538952 | tf_op jit(solution)/shard_map/ppermute | solution.py:370
  16.9 39.1 %all-to-all-start = ((bf16[4,192,821]{2,1,0:T(8,128)(2,1)}), bf16[4,192,821]{2,1,0:T(8,128)(2,1)S(1)}, u32[]{:S(2)}, u32[]{:S(2)}) async-start(bf16[4,192,821]{2,1,0:T(8,128)(2,1)} %broadcast_in_dim.24), calls=%async_computation | async-start | bytes 2752512 | tf_op jit(solution)/shard_map/all_to_all | solution.py:351
  20.6 111.9 %all-gather.7.cloned.1.call-start = ((), (), s32[]{:S(2)}) async-start(), calls=%async_computation.6 | async-start | bytes 1536000 | tf_op jit(solution)/shard_map/all_gather | solution.py:1151
  20.6 7.6 %collective-permute-start = (bf16[192,192]{1,0:T(8,128)(2,1)S(1)}, bf16[192,192]{1,0:T(8,128)(2,1)S(1)}, u32[]{:S(2)}, u32[]{:S(2)}) collective-permute-start(bf16[192,192]{1,0:T(8,128)(2,1)S(1)} %copy-done.10), channel_id=1, source_target_pairs={{0,3},{1,2},{2,1},{3,0},{4,7},{5,6},{6,5},{7,4},{8,11},{9,10},{10,... | collective-permute-start | bytes 221192 | tf_op jit(solution)/shard_map/ppermute | solution.py:358
  24.3 8.9 %collective-permute-start.1 = (bf16[192,192]{1,0:T(8,128)(2,1)S(1)}, bf16[192,192]{1,0:T(8,128)(2,1)S(1)}, u32[]{:S(2)}, u32[]{:S(2)}) collective-permute-start(bf16[192,192]{1,0:T(8,128)(2,1)S(1)} %copy-done.10), channel_id=1, source_target_pairs={{0,2},{1,3},{2,0},{3,1},{4,6},{5,7},{6,4},{7,5},{8,10},{9,11},{10,... | collective-permute-start | bytes 221192 | tf_op jit(solution)/shard_map/ppermute | solution.py:358
  24.3 8.9 %collective-permute-start.2 = (bf16[192,192]{1,0:T(8,128)(2,1)S(1)}, bf16[192,192]{1,0:T(8,128)(2,1)S(1)}, u32[]{:S(2)}, u32[]{:S(2)}) collective-permute-start(bf16[192,192]{1,0:T(8,128)(2,1)S(1)} %copy-done.10), channel_id=1, source_target_pairs={{0,1},{1,0},{2,3},{3,2},{4,5},{5,4},{6,7},{7,6},{8,9},{9,8},{10,11... | collective-permute-start | bytes 221192 | tf_op jit(solution)/shard_map/ppermute | solution.py:358
  55.9 11.1 %collective-permute-start.4 = (bf16[768,192]{1,0:T(8,128)(2,1)S(1)}, bf16[768,192]{1,0:T(8,128)(2,1)S(1)}, u32[]{:S(2)}, u32[]{:S(2)}) collective-permute-start(bf16[768,192]{1,0:T(8,128)(2,1)S(1)} %pad_maximum_fusion.2), channel_id=1, source_target_pairs={{0,24},{8,16},{16,8},{24,0},{1,25},{9,17},{17,9},{25,1},{2,26},{10... | collective-permute-start | bytes 884744 | tf_op jit(solution)/shard_map/ppermute | solution.py:358
  56.2 19.6 %collective-permute-start.5 = (bf16[768,192]{1,0:T(8,128)(2,1)S(1)}, bf16[768,192]{1,0:T(8,128)(2,1)}, u32[]{:S(2)}, u32[]{:S(2)}) collective-permute-start(bf16[768,192]{1,0:T(8,128)(2,1)S(1)} %pad_maximum_fusion.2), channel_id=1, source_target_pairs={{0,16},{8,24},{16,0},{24,8},{1,17},{9,25},{17,1},{25,9},{2,18},{10... | collective-permute-start | bytes 884744 | tf_op jit(solution)/shard_map/ppermute | solution.py:358
  57.7 18.1 %collective-permute-start.6 = (bf16[768,192]{1,0:T(8,128)(2,1)S(1)}, bf16[768,192]{1,0:T(8,128)(2,1)}, u32[]{:S(2)}, u32[]{:S(2)}) collective-permute-start(bf16[768,192]{1,0:T(8,128)(2,1)S(1)} %pad_maximum_fusion.2), channel_id=1, source_target_pairs={{0,8},{8,0},{16,24},{24,16},{1,9},{9,1},{17,25},{25,17},{2,10},{10... | collective-permute-start | bytes 884744 | tf_op jit(solution)/shard_map/ppermute | solution.py:358
  78.8 28.4 %collective-permute-start.7 = (bf16[4,192,768]{2,1,0:T(8,128)(2,1)S(1)}, bf16[4,192,768]{2,1,0:T(8,128)(2,1)}, u32[]{:S(2)}, u32[]{:S(2)}) collective-permute-start(bf16[4,192,768]{2,1,0:T(8,128)(2,1)S(1)} %copy-done.9), channel_id=1, source_target_pairs={{0,24},{8,16},{16,8},{24,0},{1,25},{9,17},{17,9},{25,1},{2,26},{10... | collective-permute-start | bytes 3538952 | tf_op jit(solution)/shard_map/ppermute | solution.py:370
  83.8 23.4 %collective-permute-start.8 = (bf16[4,192,768]{2,1,0:T(8,128)(2,1)}, bf16[4,192,768]{2,1,0:T(8,128)(2,1)}, u32[]{:S(2)}, u32[]{:S(2)}) collective-permute-start(bf16[4,192,768]{2,1,0:T(8,128)(2,1)} %get-tuple-element.220), channel_id=1, source_target_pairs={{0,8},{8,0},{16,24},{24,16},{1,9},{9,1},{17,25},{25,17},{2,10},{10... | collective-permute-start | bytes 3538952 | tf_op jit(solution)/shard_map/ppermute | solution.py:370
  83.8 48.7 %collective-permute-start.9 = (bf16[4,192,768]{2,1,0:T(8,128)(2,1)}, bf16[4,192,768]{2,1,0:T(8,128)(2,1)}, u32[]{:S(2)}, u32[]{:S(2)}) collective-permute-start(bf16[4,192,768]{2,1,0:T(8,128)(2,1)} %get-tuple-element.222), channel_id=1, source_target_pairs={{0,16},{8,24},{16,0},{24,8},{1,17},{9,25},{17,1},{25,9},{2,18},{10... | collective-permute-start | bytes 3538952 | tf_op jit(solution)/shard_map/ppermute | solution.py:370
  85.7 72.1 %collective-permute-start.10 = (bf16[4,192,768]{2,1,0:T(8,128)(2,1)}, bf16[4,192,768]{2,1,0:T(8,128)(2,1)}, u32[]{:S(2)}, u32[]{:S(2)}) collective-permute-start(bf16[4,192,768]{2,1,0:T(8,128)(2,1)} %get-tuple-element.219), channel_id=1, source_target_pairs={{0,24},{8,16},{16,8},{24,0},{1,25},{9,17},{17,9},{25,1},{2,26},{10... | collective-permute-start | bytes 3538952 | tf_op jit(solution)/shard_map/ppermute | solution.py:370
  157.8 78.2 %all-to-all-start.1 = ((bf16[8,528,768]{2,1,0:T(8,128)(2,1)}), bf16[8,528,768]{2,1,0:T(8,128)(2,1)}, u32[]{:S(2)}, u32[]{:S(2)}) async-start(bf16[8,528,768]{2,1,0:T(8,128)(2,1)} %get-tuple-element.87), calls=%async_computation.1 | async-start | bytes 12976128 | tf_op jit(solution)/shard_map/all_to_all | solution.py:351
  259.1 95.6 %all-to-all-start.2 = ((bf16[32,208,256]{2,1,0:T(8,128)(2,1)}), bf16[32,208,256]{2,1,0:T(8,128)(2,1)S(1)}, u32[]{:S(2)}, u32[]{:S(2)}) async-start(bf16[32,208,256]{2,1,0:T(8,128)(2,1)} %bitcast.50), calls=%async_computation.2 | async-start | bytes 6815744 | tf_op jit(solution)/shard_map/all_to_all | solution.py:351
  276.4 4.8 collective-permute-start.12
  276.6 78.1 %collective-permute-start.13 = (bf16[1552,768]{1,0:T(8,128)(2,1)}, bf16[1552,768]{1,0:T(8,128)(2,1)}, u32[]{:S(2)}, u32[]{:S(2)}) collective-permute-start(bf16[1552,768]{1,0:T(8,128)(2,1)} %get-tuple-element.103), channel_id=1, source_target_pairs={{0,16},{8,24},{16,0},{24,8},{1,17},{9,25},{17,1},{25,9},{2,18},{10... | collective-permute-start | bytes 7151624 | tf_op jit(solution)/shard_map/ppermute | solution.py:370
  363.3 97.2 %all-to-all-start.3 = ((bf16[32,192,256]{2,1,0:T(8,128)(2,1)}), bf16[32,192,256]{2,1,0:T(8,128)(2,1)S(1)}, u32[]{:S(2)}, u32[]{:S(2)}) async-start(bf16[32,192,256]{2,1,0:T(8,128)(2,1)} %bitcast.51), calls=%async_computation.3 | async-start | bytes 6291456 | tf_op jit(solution)/shard_map/all_to_all | solution.py:351
  370.3 86.3 %all-gather.9.cloned.1.call-start = ((), (), s32[]{:S(2)}) async-start(), calls=%async_computation.7 | async-start | bytes 1536000 | tf_op jit(solution)/shard_map/all_gather | solution.py:1203
  370.3 86.3 %collective-permute-start.14 = (bf16[1552,768]{1,0:T(8,128)(2,1)}, bf16[1552,768]{1,0:T(8,128)(2,1)}, u32[]{:S(2)}, u32[]{:S(2)}) collective-permute-start(bf16[1552,768]{1,0:T(8,128)(2,1)} %get-tuple-element.113), channel_id=1, source_target_pairs={{0,24},{8,16},{16,8},{24,0},{1,25},{9,17},{17,9},{25,1},{2,26},{10... | collective-permute-start | bytes 7151624 | tf_op jit(solution)/shard_map/ppermute | solution.py:370
  371.9 168.2 %all-reduce.2.cloned.1.call-start = ((), (), s32[]{:S(2)}) async-start(), calls=%async_computation.5 | async-start | bytes 2457600 | tf_op jit(solution)/shard_map/psum | solution.py:1221
  560.1 21.7 %all-to-all-start.4 = ((bf16[8,96,814]{2,1,0:T(8,128)(2,1)}), bf16[8,96,814]{2,1,0:T(8,128)(2,1)S(1)}, u32[]{:S(2)}, u32[]{:S(2)}) async-start(bf16[8,96,814]{2,1,0:T(8,128)(2,1)} %bitcast.21), calls=%async_computation.4 | async-start | bytes 2752512 | tf_op jit(solution)/shard_map/all_to_all | solution.py:351
  563.8 37.8 %all-gather.11.cloned.1.call-start = ((), (), s32[]{:S(2)}) async-start(), calls=%async_computation.8 | async-start | bytes 1536000 | tf_op jit(solution)/shard_map/all_gather | solution.py:1230
  582.1 10.2 %collective-permute-start.15 = (f32[96,814]{1,0:T(8,128)S(1)}, f32[96,814]{1,0:T(8,128)S(1)}, u32[]{:S(2)}, u32[]{:S(2)}) collective-permute-start(f32[96,814]{1,0:T(8,128)S(1)} %convert_reduce_fusion), channel_id=1, source_target_pairs={{0,4},{4,0},{1,5},{5,1},{2,6},{6,2},{3,7},{7,3},{8,12},{12,8},{9,1... | collective-permute-start | bytes 937736 | tf_op jit(solution)/shard_map/ppermute | solution.py:358
  (28 other events, 250.6 us)
Sparse Core Ops, SparseCore 0:
  78.9 31.8 all-gather.6
  372.7 65.0 all-gather.8
  483.0 57.0 all-reduce.1
  570.1 31.3 all-gather.10

commit v9 on v8

--- a/solution.py
+++ b/solution.py
@@ -13,7 +13,7 @@
 EXPERTS = 32
 TOPK = 2
 CAP = 64
-FF_PAIR = 1
+FF_PAIR = 2
 PAIR = 2
 EXTRA = 16
 VMEM_LIMIT = 56 * 1024 * 1024
@@ -382,17 +382,17 @@
 
 
 def expert_kernel(inner, owners, at_ref, rows_ref, gate_ref, cot_ref, in_bias_ref, back_bias_ref, *refs):
-    in_refs, back_refs, refs = refs[:owners], refs[owners : 2 * owners], refs[2 * owners :]
+    piece_refs, refs = refs[:owners], refs[owners:]
     returned_ref, grads_ref, hidden_ref, grad_pre_ref, grad_turned_ref = refs[:5]
     grad_in_bias_ref, grad_back_bias_ref, weight_ref = refs[5:]
     f32, bf16 = jnp.float32, jnp.bfloat16
     groups, cap, width = rows_ref.shape
-    depth = in_refs[0].shape[1]
+    depth = piece_refs[0].shape[2]
     for s in range(owners):
         source = at_ref[0] ^ s
         place = pl.ds(pl.multiple_of((source // inner) * depth, depth), depth)
-        weight_ref[0, source % inner, place] = in_refs[s][0]
-        weight_ref[1, source % inner, place] = back_refs[s][0]
+        for k in range(2):
+            weight_ref[k, source % inner, place] = piece_refs[s][k, 0]
     tensor, slice_width = returned_ref.shape[1:3]
     mine = back_bias_ref.shape[1]
     total = groups * cap
@@ -453,11 +453,11 @@
                     grads_ref[g, z, slice_width:, lanes] = tail[:, mine_lanes]
 
 
-def run_experts(owner_at, arrived, in_pieces, back_pieces, in_bias, back_bias, inner, tensor):
+def run_experts(owner_at, arrived, pieces, in_bias, back_bias, inner, tensor):
     f32, bf16 = jnp.float32, jnp.bfloat16
     groups, _, width = arrived.shape
-    owners = len(in_pieces)
-    mine, depth, ff = in_pieces[0].shape
+    owners = len(pieces)
+    _, mine, depth, ff = pieces[0].shape
     total = groups * CAP
     slice_width = width // tensor
     gate_at = 2 * mine * CAP // EXTRA
@@ -481,7 +481,7 @@
             pl.BlockSpec((1, inner, ff), lambda j: (j, 0, 0)),
             pl.BlockSpec((width, mine), lambda j: (0, 0)),
         ]
-        + [pl.BlockSpec((1, depth, ff), lambda j: (j, 0, 0))] * (2 * owners),
+        + [pl.BlockSpec((2, 1, depth, ff), lambda j: (0, j, 0, 0))] * owners,
         out_specs=[
             pl.BlockSpec(shape if lead is None else (lead, *shape[1:]), index)
             for shape, _, index, lead in outs
@@ -494,7 +494,7 @@
             bytes_accessed=4 * owners * mine * depth * ff + 12 * mine * total * inner * ff,
             transcendentals=mine * total * inner * ff,
         ),
-    )(owner_at.reshape(1), arrived, arrived, arrived, in_bias, back_bias, *in_pieces, *back_pieces)
+    )(owner_at.reshape(1), arrived, arrived, arrived, in_bias, back_bias, *pieces)
 
 
 def weight_kernel(
@@ -1121,15 +1121,13 @@
     out_rows = jnp.concatenate(hop_gather(w_out, tensor_axes), axis=0)
     in_bias_all = jnp.stack(hop_gather(in_bias, INNER))
 
-    def piece(shard, s):
-        return cross(lax.dynamic_slice_in_dim(shard, (owner_at ^ s) * mine, mine, 0), s)
-
-    in_pieces = [piece(w_in, s) for s in range(owners)]
-    back_pieces = [piece(w_back.transpose(0, 2, 1), s) for s in range(owners)]
-    far = owners // 2
-    packed, out_rows, in_bias_all, in_pieces[far] = lax.optimization_barrier(
-        (packed, out_rows, in_bias_all, in_pieces[far])
-    )
+    shards = (w_in, w_back.transpose(0, 2, 1))
+    pieces = []
+    for s in range(owners):
+        start = (owner_at ^ s) * mine
+        piece = [lax.dynamic_slice_in_dim(shard, start, mine, 0) for shard in shards]
+        pieces.append(cross(jnp.stack(piece), s))
+    packed, out_rows, in_bias_all = lax.optimization_barrier((packed, out_rows, in_bias_all))
     vectors = packed[:, router_at + EXPERTS + experts_here :].T.astype(f32)
     out_whole = jnp.concatenate(hop_gather(out_rows, DP), axis=1)
     in_bias_mine = lax.dynamic_slice_in_dim(in_bias_all, owner_at * mine, mine, 1)
@@ -1149,9 +1147,7 @@
 
     attended, out_whole = lax.optimization_barrier((attended, out_whole))
     attended_all = lax.all_gather(attended, tensor_axes)
-    attended_all, in_pieces[far + 1 :], back_pieces[: far + 1] = lax.optimization_barrier(
-        (attended_all, in_pieces[far + 1 :], back_pieces[: far + 1])
-    )
+    attended_all, pieces[::inner] = lax.optimization_barrier((attended_all, pieces[::inner]))
     mixed, probs, sent = run_route(
         images,
         cotangent,
@@ -1164,7 +1160,7 @@
         groups,
         slots // inner,
     )
-    sent, back_pieces = lax.optimization_barrier((sent, back_pieces))
+    sent, pieces = lax.optimization_barrier((sent, pieces))
     arrived = swap(sent, (DP, EXPERT))
     back_bias_mine = lax.dynamic_slice_in_dim(packed, router_at + EXPERTS + owner_at * mine, mine, 1)
     back_bias_mine = jnp.where(lax.axis_index(OUTER) == 0, back_bias_mine.astype(f32), 0.0)
@@ -1177,7 +1173,7 @@
         grad_in_bias_mine,
         grad_back_bias_mine,
     ) = run_experts(
-        owner_at, arrived, in_pieces, back_pieces, in_bias_mine, back_bias_mine, inner, tensor
+        owner_at, arrived, pieces, in_bias_mine, back_bias_mine, inner, tensor
     )
 
     def bring(parts):
@@ -1195,14 +1191,17 @@
         owners,
     )
     weight_parts = [cross(part, s) for s, part in enumerate(weight_parts)]
-    grad_parts, weight_parts[: far + 1] = lax.optimization_barrier(
-        (grad_parts, weight_parts[: far + 1])
+    far = owners // 2
+    grad_parts, weight_parts[: far + 1 : inner] = lax.optimization_barrier(
+        (grad_parts, weight_parts[: far + 1 : inner])
     )
     rows_cut, grad_gates = run_take_grads(grad_parts, target, slice_width, outer, inner, slots)
     rows_cut, returned_out = lax.optimization_barrier((rows_cut, returned_out))
     rows_all = lax.all_gather(rows_cut, tensor_axes)
     returned = bring(returned_out)
-    rows_all, returned, weight_parts = lax.optimization_barrier((rows_all, returned, weight_parts))
+    rows_all, returned, weight_parts[:far], weight_parts[far::inner] = lax.optimization_barrier(
+        (rows_all, returned, weight_parts[:far], weight_parts[far::inner])
+    )
     grad_mixed, normed_part, matrix, sums = run_pull(
         images_held,
         images,
@@ -1219,10 +1218,10 @@
         router_at,
     )
     grad_normed = lax.psum(normed_part, tensor_axes)
-    grad_normed, returned, weight_parts = lax.optimization_barrier(
-        (grad_normed, returned, weight_parts)
-    )
     grad_images, first_sums = run_last(images, grad_normed, grad_mixed, vectors)
+    first_sums, returned, weight_parts = lax.optimization_barrier(
+        (first_sums, returned, weight_parts)
+    )
     mixed_cut = lax.dynamic_slice_in_dim(mixed, tensor_at * slice_width, slice_width, 2)
     output_cut = run_take_rows(
         images_held, returned, target, probs, routes, mixed_cut, outer, inner, slots

time: 621 us -> 647 us (1.042)
  other arithmetic: 11.9 us -> 29.8 us
  Pallas kernels: 116 us -> 104 us
  starting transfers between devices: 41.7 us -> 49.6 us
  local copies, waits for them, and re-layouts: 37.7 us -> 44.7 us
    all_to_all x5, waiting for transfers between devices: 103 us -> 53.6 us  [swap(): return lax.all_to_all(values, axes, split_axis=0, concat_axis=0, tiled=True)]
    psum x1, waiting for transfers between devices: 54.6 us -> 88.3 us  [moved_plan(): grad_normed = lax.psum(normed_part, tensor_axes)]
    all_gather x1, waiting for transfers between devices: 0.01 us -> 28.7 us  [moved_plan(): attended_all = lax.all_gather(attended, tensor_axes)]
    ppermute x9 -> x14, waiting for transfers between devices: 205 us -> 185 us  [cross(): lax.ppermute(values, (DP, INNER), [(i, i ^ s) for i in range(count)])]
    ppermute x7 -> x8, waiting for transfers between devices: 24.9 us -> 37.7 us  [hop_gather(): hops.append(lax.ppermute(values, axes, [(i, i ^ s) for i in range(count)]))]
    another operation x0 -> x10, other arithmetic: none -> 11.7 us  [the longest x8 10.2 us: moved_plan(): pieces.append(cross(jnp.stack(piece), s))]
    dynamic_slice x2 -> x0, local copies, waits for them, and re-layouts: 9.4 us -> none  [piece(): lax.dynamic_slice_in_dim(shard, (owner_at ^ s) * mine, mine, 0)]
    pallas_call x6, Pallas kernels: 69.9 us -> 61.1 us  [call_kernel(): pl.pallas_call(kernel, grid=grid, in_specs=[smem if b is None else pl.Blo...]
  transfers between devices with their start and end apart: 25 -> 31, of which waited for: 18 -> 15; matrix products, arithmetic and copies ran while one was open for 5% -> 10% of each run, Pallas kernels for 8% -> 6%
where the time goes in v9:
time: 647 us; the launch traced here: 638 us
  waiting for transfers between devices  394 us (61%)
  Pallas kernels  104 us (16%)
  starting transfers between devices  49.6 us (8%)
  local copies, waits for them, and re-layouts  44.7 us (7%)
  other arithmetic  29.8 us (5%)
  between operations  15.3 us (2%)
    ppermute x14, waiting for transfers between devices, cross(): lax.ppermute(values, (DP, INNER), [(i, i ^ s) for i in range(count)])  185 us
    psum x1, waiting for transfers between devices, moved_plan(): grad_normed = lax.psum(normed_part, tensor_axes)  88.3 us
    pallas_call x6, Pallas kernels, call_kernel(): pl.pallas_call(kernel, grid=grid, in_specs=[smem if b is None else pl.Blo...  61.1 us
    all_to_all x5, waiting for transfers between devices, swap(): return lax.all_to_all(values, axes, split_axis=0, concat_axis=0, tiled=True)  53.6 us
    ppermute x8, waiting for transfers between devices, hop_gather(): hops.append(lax.ppermute(values, axes, [(i, i ^ s) for i in range(count)]))  37.7 us
    all_gather x1, waiting for transfers between devices, moved_plan(): attended_all = lax.all_gather(attended, tensor_axes)  28.7 us
    all_to_all x5, starting transfers between devices, swap(): return lax.all_to_all(values, axes, split_axis=0, concat_axis=0, tiled=True)  22.2 us
    pallas_call x1, Pallas kernels, run_experts(): pl.pallas_call(functools.partial(expert_kernel, inner, owners), grid=(min...  19.5 us
  transfers between devices with their start and end apart: 31, of which 15 were waited for; matrix products, arithmetic and copies ran while one was open for 10% of the time, Pallas kernels for 6%

profile of v9, /device:TPU:0, one launch (start us, length us, event | category | flops | bytes accessed | tf_op | source)
XLA Modules:
  0.0 637.5 jit_solution(14228720320194606186)
XLA Ops:
  7.2 5.1 collective-permute-start
  49.7 6.6 %shard_map.289 = (bf16[2,197,384]{2,1,0:T(8,128)(2,1)}, bf16[4,197,576]{2,1,0:T(8,128)(2,1)}) custom-call(bf16[4,197,768]{2,1,0:T(8,128)(2,1)} %copy.235.images_ref, bf16[768,821]{1,0:T(8,128)(2,1)} %bitcast.93, f32[5,768]{1,0:T(8,128)} %convert_bitcast_fusion.vector_ref, f32[2,192]{1,0:T(2,128)} %convert_element_type.51.bias_ref), custom_call_target="tpu_custom_call" | custom-call | flops 935614464 | bytes 2488320 | tf_op jit(solution)/shard_map/pallas_call | solution.py:645
  56.3 22.0 %collective-permute-done.4 = bf16[768,192]{1,0:T(8,128)(2,1)} collective-permute-done((bf16[768,192]{1,0:T(8,128)(2,1)S(1)}, bf16[768,192]{1,0:T(8,128)(2,1)}, u32[]{:S(2)}, u32[]{:S(2)}) %collective-permute-start.4) | collective-permute-done | bytes 294944 | tf_op jit(solution)/shard_map/ppermute | solution.py:358
  80.2 7.2 %collective-permute-done.5 = bf16[768,192]{1,0:T(8,128)(2,1)} collective-permute-done((bf16[768,192]{1,0:T(8,128)(2,1)S(1)}, bf16[768,192]{1,0:T(8,128)(2,1)}, u32[]{:S(2)}, u32[]{:S(2)}) %collective-permute-start.5) | collective-permute-done | bytes 294944 | tf_op jit(solution)/shard_map/ppermute | solution.py:358
  112.0 28.7 %all-gather.7.cloned.1.call-done = bf16[8,197,384]{2,1,0:T(8,128)(2,1)} async-done(((bf16[2,197,384]{2,1,0:T(8,128)(2,1)}), bf16[8,197,384]{2,1,0:T(8,128)(2,1)}) %all-gather.7.cloned.1.call-update) | async-done | bytes 1210384 | tf_op jit(solution)/shard_map/all_gather | solution.py:1149
  140.7 15.8 %shard_map.290 = (f32[4,197,768]{2,1,0:T(8,128)}, f32[4,197,32]{2,1,0:T(8,128)}, bf16[8,272,768]{2,1,0:T(8,128)(2,1)}) custom-call(bf16[4,197,768]{2,1,0:T(8,128)(2,1)} %copy.235.images_ref, bf16[4,197,768]{2,1,0:T(8,128)(2,1)} %copy.233.cot_ref, bf16[4,2,197,384]{3,2,1,0:T(8,128)(2,1)} %bitcast.109, bf16[768,768]{1,0:T(8,128)(2,1)} %pad_maximum_fusion.1.out_ref, ...), custom_call_target="tpu_custom_call" | custom-call | flops 3408396288 | bytes 6099776 | tf_op jit(solution)/shard_map/pallas_call | solution.py:645
  159.8 28.4 %collective-permute-done.12.refs_5_ = bf16[2,2,192,768]{3,2,1,0:T(8,128)(2,1)} collective-permute-done((bf16[2,2,192,768]{3,2,1,0:T(8,128)(2,1)}, bf16[2,2,192,768]{3,2,1,0:T(8,128)(2,1)}, u32[]{:S(2)}, u32[]{:S(2)}) %collective-permute-start.12) | collective-permute-done | bytes 1179680 | tf_op jit(solution)/shard_map/ppermute | solution.py:370
  188.2 21.9 %collective-permute-done.13.refs_7_ = bf16[2,2,192,768]{3,2,1,0:T(8,128)(2,1)} collective-permute-done((bf16[2,2,192,768]{3,2,1,0:T(8,128)(2,1)}, bf16[2,2,192,768]{3,2,1,0:T(8,128)(2,1)}, u32[]{:S(2)}, u32[]{:S(2)}) %collective-permute-start.13) | collective-permute-done | bytes 1179680 | tf_op jit(solution)/shard_map/ppermute | solution.py:370
  217.1 36.4 %all-to-all-done.1.rows_ref.gate_ref.cot_ref = bf16[8,272,768]{2,1,0:T(8,128)(2,1)S(1)} async-done(((bf16[8,272,768]{2,1,0:T(8,128)(2,1)}), bf16[8,272,768]{2,1,0:T(8,128)(2,1)S(1)}, u32[]{:S(2)}, u32[]{:S(2)}) %all-to-all-start.1) | async-done | bytes 3342368 | tf_op jit(solution)/shard_map/all_to_all | solution.py:351
  255.2 19.5 %shard_map.291 = (bf16[8,4,192,128]{3,2,1,0:T(8,128)(2,1)}, bf16[8,4,208,128]{3,2,1,0:T(8,128)(2,1)}, bf16[2,2,512,768]{3,2,1,0:T(8,128)(2,1)}, bf16[2,2,512,768...) custom-call(s32[1]{0:T(128)} %bitcast.22.at_ref, ...), custom_call_target="tpu_custom_call" | custom-call | flops 9663676416 | bytes 28311552 | tf_op jit(solution)/shard_map/pallas_call | solution.py:473
  274.7 4.3 all-to-all-start.2
  279.7 12.8 %shard_map.292 = (bf16[784,768]{1,0:T(8,128)(2,1)}, bf16[784,768]{1,0:T(8,128)(2,1)}, bf16[784,768]{1,0:T(8,128)(2,1)}, bf16[784,768]{1,0:T(8,128)(2,1)}, bf16[7...) custom-call(s32[1]{0:T(128)} %bitcast.22.at_ref, ...), custom_call_target="tpu_custom_call" | custom-call | flops 4831838208 | bytes 15728640 | tf_op jit(solution)/shard_map/pallas_call | solution.py:565
  295.5 32.8 %collective-permute-done.15.refs_4_ = bf16[784,768]{1,0:T(8,128)(2,1)} collective-permute-done((bf16[784,768]{1,0:T(8,128)(2,1)}, bf16[784,768]{1,0:T(8,128)(2,1)}, u32[]{:S(2)}, u32[]{:S(2)}) %collective-permute-start.15) | collective-permute-done | bytes 1204256 | tf_op jit(solution)/shard_map/ppermute | solution.py:370
  329.6 6.3 shard_map.293
  335.8 6.9 %all-to-all-start.3 = ((bf16[32,192,128]{2,1,0:T(8,128)(2,1)}), bf16[32,192,128]{2,1,0:T(8,128)(2,1)S(1)}, u32[]{:S(2)}, u32[]{:S(2)}) async-start(bf16[32,192,128]{2,1,0:T(8,128)(2,1)} %bitcast.38), calls=%async_computation.3 | async-start | bytes 3145728 | tf_op jit(solution)/shard_map/all_to_all | solution.py:351
  348.1 68.8 %collective-permute-done.16.refs_1_ = bf16[784,768]{1,0:T(8,128)(2,1)} collective-permute-done((bf16[784,768]{1,0:T(8,128)(2,1)}, bf16[784,768]{1,0:T(8,128)(2,1)}, u32[]{:S(2)}, u32[]{:S(2)}) %collective-permute-start.16) | collective-permute-done | bytes 1204256 | tf_op jit(solution)/shard_map/ppermute | solution.py:370
  417.0 24.9 %collective-permute-done.17.refs_3_ = bf16[784,768]{1,0:T(8,128)(2,1)} collective-permute-done((bf16[784,768]{1,0:T(8,128)(2,1)}, bf16[784,768]{1,0:T(8,128)(2,1)}, u32[]{:S(2)}, u32[]{:S(2)}) %collective-permute-start.17) | collective-permute-done | bytes 1204256 | tf_op jit(solution)/shard_map/ppermute | solution.py:370
  441.8 21.8 %shard_map.294 = (f32[4,197,768]{2,1,0:T(8,128)}, bf16[4,197,768]{2,1,0:T(8,128)(2,1)}, bf16[768,800]{1,0:T(8,128)(2,1)}, f32[8,768]{1,0:T(8,128)}) custom-call(s32[1]{0:T(128)S(6)} %copy.313.held_ref, bf16[4,197,768]{2,1,0:T(8,128)(2,1)} %copy.235.images_ref, bf16[4,197,768]{2,1,0:T(8,128)(2,1)} %copy.233.cot_ref, ...), custom_call_target="tpu_custom_call" | custom-call | flops 3623236608 | bytes 8652100 | tf_op jit(solution)/shard_map/pallas_call | solution.py:645
  469.2 88.3 %all-reduce.2.cloned.1.call-done.normed_ref = bf16[4,197,768]{2,1,0:T(8,128)(2,1)} async-done(((bf16[4,197,768]{2,1,0:T(8,128)(2,1)}), bf16[4,197,768]{2,1,0:T(8,128)(2,1)}) %all-reduce.2.cloned.1.call-update) | async-done | bytes 1210384 | tf_op jit(solution)/shard_map/psum | solution.py:1220
  557.5 5.3 shard_map.295
  565.2 10.7 %shard_map.297 = (f32[16,192,768]{2,1,0:T(8,128)}, f32[16,192,768]{2,1,0:T(8,128)}) custom-call(s32[1]{0:T(128)} %bitcast.22.at_ref, bf16[784,768]{1,0:T(8,128)(2,1)} %get-tuple-element.151.refs_0_, bf16[784,768]{1,0:T(8,128)(2,1)} %collective-permute-done.16.refs_1_, bf16[784,768]{1,0:T(8,128)(2,1)} %copy-done.10, ...), custom_call_target="tpu_custom_call" | custom-call | tf_op jit(solution)/shard_map/pallas_call | solution.py:615
  576.7 5.3 shard_map.296
  592.6 17.2 %all-to-all-done.4 = bf16[8,96,814]{2,1,0:T(8,128)(2,1)S(1)} async-done(((bf16[8,96,814]{2,1,0:T(8,128)(2,1)}), bf16[8,96,814]{2,1,0:T(8,128)(2,1)S(1)}, u32[]{:S(2)}, u32[]{:S(2)}) %all-to-all-start.4) | async-done | bytes 1250336 | tf_op jit(solution)/shard_map/all_to_all | solution.py:351
  611.5 8.6 %collective-permute-done.21 = f32[96,814]{1,0:T(8,128)S(1)} collective-permute-done((f32[96,814]{1,0:T(8,128)S(1)}, f32[96,814]{1,0:T(8,128)S(1)}, u32[]{:S(2)}, u32[]{:S(2)}) %collective-permute-start.21) | collective-permute-done | bytes 312608 | tf_op jit(solution)/shard_map/ppermute | solution.py:358
  (217 shorter events, 116.7 us)
Async XLA Ops:
  7.2 37.7 %collective-permute-start = (bf16[192,192]{1,0:T(8,128)(2,1)}, bf16[192,192]{1,0:T(8,128)(2,1)S(1)}, u32[]{:S(2)}, u32[]{:S(2)}) collective-permute-start(bf16[192,192]{1,0:T(8,128)(2,1)} %param.26), channel_id=1, source_target_pairs={{0,3},{1,2},{2,1},{3,0},{4,7},{5,6},{6,5},{7,4},{8,11},{9,10},{10,... | collective-permute-start | bytes 221192 | tf_op jit(solution)/shard_map/ppermute | solution.py:358
  24.8 115.9 %all-gather.7.cloned.1.call-start = ((), (), s32[]{:S(2)}) async-start(), calls=%async_computation.6 | async-start | bytes 1536000 | tf_op jit(solution)/shard_map/all_gather | solution.py:1149
  34.8 66.5 %collective-permute-start.7 = (bf16[2,2,192,768]{3,2,1,0:T(8,128)(2,1)}, bf16[2,2,192,768]{3,2,1,0:T(8,128)(2,1)}, u32[]{:S(2)}, u32[]{:S(2)}) collective-permute-start(bf16[2,2,192,768]{3,2,1,0:T(8,128)(2,1)} %pad_maximum_fusion.3), channel_id=1, source_target_pairs={{0,8},{1,9},{8,0},{9,1},{16,24},{17,25},{24,16},{25,17},{2,10},{3,... | collective-permute-start | bytes 3538952 | tf_op jit(solution)/shard_map/ppermute | solution.py:370
  41.5 62.5 %collective-permute-start.8 = (bf16[2,2,192,768]{3,2,1,0:T(8,128)(2,1)}, bf16[2,2,192,768]{3,2,1,0:T(8,128)(2,1)}, u32[]{:S(2)}, u32[]{:S(2)}) collective-permute-start(bf16[2,2,192,768]{3,2,1,0:T(8,128)(2,1)} %pad_maximum_fusion.4), channel_id=1, source_target_pairs={{0,16},{1,17},{8,24},{9,25},{16,0},{17,1},{24,8},{25,9},{2,18},{3,... | collective-permute-start | bytes 3538952 | tf_op jit(solution)/shard_map/ppermute | solution.py:370
  45.0 33.3 %collective-permute-start.4 = (bf16[768,192]{1,0:T(8,128)(2,1)S(1)}, bf16[768,192]{1,0:T(8,128)(2,1)}, u32[]{:S(2)}, u32[]{:S(2)}) collective-permute-start(bf16[768,192]{1,0:T(8,128)(2,1)S(1)} %pad_maximum_fusion.10), channel_id=1, source_target_pairs={{0,24},{8,16},{16,8},{24,0},{1,25},{9,17},{17,9},{25,1},{2,26},{10... | collective-permute-start | bytes 884744 | tf_op jit(solution)/shard_map/ppermute | solution.py:358
  45.2 42.2 %collective-permute-start.5 = (bf16[768,192]{1,0:T(8,128)(2,1)S(1)}, bf16[768,192]{1,0:T(8,128)(2,1)}, u32[]{:S(2)}, u32[]{:S(2)}) collective-permute-start(bf16[768,192]{1,0:T(8,128)(2,1)S(1)} %pad_maximum_fusion.10), channel_id=1, source_target_pairs={{0,16},{8,24},{16,0},{24,8},{1,17},{9,25},{17,1},{25,9},{2,18},{10... | collective-permute-start | bytes 884744 | tf_op jit(solution)/shard_map/ppermute | solution.py:358
  46.9 41.1 %collective-permute-start.6 = (bf16[768,192]{1,0:T(8,128)(2,1)S(1)}, bf16[768,192]{1,0:T(8,128)(2,1)}, u32[]{:S(2)}, u32[]{:S(2)}) collective-permute-start(bf16[768,192]{1,0:T(8,128)(2,1)S(1)} %pad_maximum_fusion.10), channel_id=1, source_target_pairs={{0,8},{8,0},{16,24},{24,16},{1,9},{9,1},{17,25},{25,17},{2,10},{10... | collective-permute-start | bytes 884744 | tf_op jit(solution)/shard_map/ppermute | solution.py:358
  78.3 33.7 %collective-permute-start.9 = (bf16[2,2,192,768]{3,2,1,0:T(8,128)(2,1)}, bf16[2,2,192,768]{3,2,1,0:T(8,128)(2,1)}, u32[]{:S(2)}, u32[]{:S(2)}) collective-permute-start(bf16[2,2,192,768]{3,2,1,0:T(8,128)(2,1)} %pad_maximum_fusion.5), channel_id=1, source_target_pairs={{0,24},{1,25},{8,16},{9,17},{16,8},{17,9},{24,0},{25,1},{2,26},{3,... | collective-permute-start | bytes 3538952 | tf_op jit(solution)/shard_map/ppermute | solution.py:370
  87.4 69.1 %collective-permute-start.10 = (bf16[2,2,192,768]{3,2,1,0:T(8,128)(2,1)}, bf16[2,2,192,768]{3,2,1,0:T(8,128)(2,1)}, u32[]{:S(2)}, u32[]{:S(2)}) collective-permute-start(bf16[2,2,192,768]{3,2,1,0:T(8,128)(2,1)} %pad_maximum_fusion.6), channel_id=1, source_target_pairs={{0,1},{1,0},{8,9},{9,8},{16,17},{17,16},{24,25},{25,24},{2,3},{3,2... | collective-permute-start | bytes 3538952 | tf_op jit(solution)/shard_map/ppermute | solution.py:370
  92.2 67.6 %collective-permute-start.11 = (bf16[2,2,192,768]{3,2,1,0:T(8,128)(2,1)}, bf16[2,2,192,768]{3,2,1,0:T(8,128)(2,1)}, u32[]{:S(2)}, u32[]{:S(2)}) collective-permute-start(bf16[2,2,192,768]{3,2,1,0:T(8,128)(2,1)} %pad_maximum_fusion.7), channel_id=1, source_target_pairs={{0,9},{1,8},{8,1},{9,0},{16,25},{17,24},{24,17},{25,16},{2,11},{3,... | collective-permute-start | bytes 3538952 | tf_op jit(solution)/shard_map/ppermute | solution.py:370
  101.3 86.8 %collective-permute-start.12 = (bf16[2,2,192,768]{3,2,1,0:T(8,128)(2,1)}, bf16[2,2,192,768]{3,2,1,0:T(8,128)(2,1)}, u32[]{:S(2)}, u32[]{:S(2)}) collective-permute-start(bf16[2,2,192,768]{3,2,1,0:T(8,128)(2,1)} %pad_maximum_fusion.8), channel_id=1, source_target_pairs={{0,17},{1,16},{8,25},{9,24},{16,1},{17,0},{24,9},{25,8},{2,19},{3,... | collective-permute-start | bytes 3538952 | tf_op jit(solution)/shard_map/ppermute | solution.py:370
  104.0 106.1 %collective-permute-start.13 = (bf16[2,2,192,768]{3,2,1,0:T(8,128)(2,1)}, bf16[2,2,192,768]{3,2,1,0:T(8,128)(2,1)}, u32[]{:S(2)}, u32[]{:S(2)}) collective-permute-start(bf16[2,2,192,768]{3,2,1,0:T(8,128)(2,1)} %pad_maximum_fusion.9), channel_id=1, source_target_pairs={{0,25},{1,24},{8,17},{9,16},{16,9},{17,8},{24,1},{25,0},{2,27},{3,... | collective-permute-start | bytes 3538952 | tf_op jit(solution)/shard_map/ppermute | solution.py:370
  210.0 43.4 %all-to-all-start.1 = ((bf16[8,272,768]{2,1,0:T(8,128)(2,1)}), bf16[8,272,768]{2,1,0:T(8,128)(2,1)S(1)}, u32[]{:S(2)}, u32[]{:S(2)}) async-start(bf16[8,272,768]{2,1,0:T(8,128)(2,1)} %get-tuple-element.101), calls=%async_computation.1 | async-start | bytes 6684672 | tf_op jit(solution)/shard_map/all_to_all | solution.py:351
  274.7 53.6 %all-to-all-start.2 = ((bf16[32,208,128]{2,1,0:T(8,128)(2,1)}), bf16[32,208,128]{2,1,0:T(8,128)(2,1)S(1)}, u32[]{:S(2)}, u32[]{:S(2)}) async-start(bf16[32,208,128]{2,1,0:T(8,128)(2,1)} %bitcast.98), calls=%async_computation.2 | async-start | bytes 3407872 | tf_op jit(solution)/shard_map/all_to_all | solution.py:351
  292.7 35.7 %collective-permute-start.15 = (bf16[784,768]{1,0:T(8,128)(2,1)}, bf16[784,768]{1,0:T(8,128)(2,1)}, u32[]{:S(2)}, u32[]{:S(2)}) collective-permute-start(bf16[784,768]{1,0:T(8,128)(2,1)} %get-tuple-element.119), channel_id=1, source_target_pairs={{0,16},{1,17},{8,24},{9,25},{16,0},{17,1},{24,8},{25,9},{2,18},{3,... | collective-permute-start | bytes 3612680 | tf_op jit(solution)/shard_map/ppermute | solution.py:370
  335.8 106.0 %all-to-all-start.3 = ((bf16[32,192,128]{2,1,0:T(8,128)(2,1)}), bf16[32,192,128]{2,1,0:T(8,128)(2,1)S(1)}, u32[]{:S(2)}, u32[]{:S(2)}) async-start(bf16[32,192,128]{2,1,0:T(8,128)(2,1)} %bitcast.38), calls=%async_computation.3 | async-start | bytes 3145728 | tf_op jit(solution)/shard_map/all_to_all | solution.py:351
  342.7 99.1 %all-gather.9.cloned.1.call-start = ((), (), s32[]{:S(2)}) async-start(), calls=%async_computation.7 | async-start | bytes 1536000 | tf_op jit(solution)/shard_map/all_gather | solution.py:1200
  343.4 214.1 %all-reduce.2.cloned.1.call-start = ((), (), s32[]{:S(2)}) async-start(), calls=%async_computation.5 | async-start | bytes 2457600 | tf_op jit(solution)/shard_map/psum | solution.py:1220
  343.9 73.1 %collective-permute-start.16 = (bf16[784,768]{1,0:T(8,128)(2,1)}, bf16[784,768]{1,0:T(8,128)(2,1)}, u32[]{:S(2)}, u32[]{:S(2)}) collective-permute-start(bf16[784,768]{1,0:T(8,128)(2,1)} %get-tuple-element.127), channel_id=1, source_target_pairs={{0,1},{1,0},{8,9},{9,8},{16,17},{17,16},{24,25},{25,24},{2,3},{3,2... | collective-permute-start | bytes 3612680 | tf_op jit(solution)/shard_map/ppermute | solution.py:370
  345.7 96.1 %collective-permute-start.17 = (bf16[784,768]{1,0:T(8,128)(2,1)}, bf16[784,768]{1,0:T(8,128)(2,1)}, u32[]{:S(2)}, u32[]{:S(2)}) collective-permute-start(bf16[784,768]{1,0:T(8,128)(2,1)} %get-tuple-element.129), channel_id=1, source_target_pairs={{0,9},{1,8},{8,1},{9,0},{16,25},{17,24},{24,17},{25,16},{2,11},{3,... | collective-permute-start | bytes 3612680 | tf_op jit(solution)/shard_map/ppermute | solution.py:370
  345.7 96.1 %collective-permute-start.18 = (bf16[784,768]{1,0:T(8,128)(2,1)}, bf16[784,768]{1,0:T(8,128)(2,1)}, u32[]{:S(2)}, u32[]{:S(2)}) collective-permute-start(bf16[784,768]{1,0:T(8,128)(2,1)} %get-tuple-element.131), channel_id=1, source_target_pairs={{0,24},{1,25},{8,16},{9,17},{16,8},{17,9},{24,0},{25,1},{2,26},{3,... | collective-permute-start | bytes 3612680 | tf_op jit(solution)/shard_map/ppermute | solution.py:370
  463.7 161.3 %all-gather.11.cloned.1.call-start = ((), (), s32[]{:S(2)}) async-start(), calls=%async_computation.8 | async-start | bytes 1536000 | tf_op jit(solution)/shard_map/all_gather | solution.py:1229
  464.0 98.9 %collective-permute-start.19 = (bf16[784,768]{1,0:T(8,128)(2,1)}, bf16[784,768]{1,0:T(8,128)(2,1)S(1)}, u32[]{:S(2)}, u32[]{:S(2)}) collective-permute-start(bf16[784,768]{1,0:T(8,128)(2,1)} %get-tuple-element.143), channel_id=1, source_target_pairs={{0,17},{1,16},{8,25},{9,24},{16,1},{17,0},{24,9},{25,8},{2,19},{3,... | collective-permute-start | bytes 3612680 | tf_op jit(solution)/shard_map/ppermute | solution.py:370
  465.5 97.3 %collective-permute-start.20 = (bf16[784,768]{1,0:T(8,128)(2,1)}, bf16[784,768]{1,0:T(8,128)(2,1)}, u32[]{:S(2)}, u32[]{:S(2)}) collective-permute-start(bf16[784,768]{1,0:T(8,128)(2,1)} %get-tuple-element.145), channel_id=1, source_target_pairs={{0,25},{1,24},{8,17},{9,16},{16,9},{17,8},{24,1},{25,0},{2,27},{3,... | collective-permute-start | bytes 3612680 | tf_op jit(solution)/shard_map/ppermute | solution.py:370
  (28 other events, 508.3 us)
Sparse Core Ops, SparseCore 0:
  91.1 49.5 all-gather.6
  345.7 52.0 all-gather.8
  463.9 93.6 all-reduce.1
  582.2 32.6 all-gather.10

commit v10 on v8

--- a/solution.py
+++ b/solution.py
@@ -1147,11 +1147,8 @@
 
     attended, proj = run_attend(images, packed, vectors, qv_bias.astype(f32))
 
-    attended, out_whole = lax.optimization_barrier((attended, out_whole))
     attended_all = lax.all_gather(attended, tensor_axes)
-    attended_all, in_pieces[far + 1 :], back_pieces[: far + 1] = lax.optimization_barrier(
-        (attended_all, in_pieces[far + 1 :], back_pieces[: far + 1])
-    )
+    attended_all, in_pieces = lax.optimization_barrier((attended_all, in_pieces))
     mixed, probs, sent = run_route(
         images,
         cotangent,
@@ -1194,7 +1191,8 @@
         grad_back_bias_mine,
         owners,
     )
-    weight_parts = [cross(part, s) for s, part in enumerate(weight_parts)]
+    weight_parts = list(weight_parts)
+    weight_parts[: far + 1] = [cross(part, s) for s, part in enumerate(weight_parts[: far + 1])]
     grad_parts, weight_parts[: far + 1] = lax.optimization_barrier(
         (grad_parts, weight_parts[: far + 1])
     )
@@ -1202,7 +1200,9 @@
     rows_cut, returned_out = lax.optimization_barrier((rows_cut, returned_out))
     rows_all = lax.all_gather(rows_cut, tensor_axes)
     returned = bring(returned_out)
-    rows_all, returned, weight_parts = lax.optimization_barrier((rows_all, returned, weight_parts))
+    rows_all, returned, weight_parts[far + 1 :] = lax.optimization_barrier(
+        (rows_all, returned, weight_parts[far + 1 :])
+    )
     grad_mixed, normed_part, matrix, sums = run_pull(
         images_held,
         images,
@@ -1219,10 +1219,10 @@
         router_at,
     )
     grad_normed = lax.psum(normed_part, tensor_axes)
-    grad_normed, returned, weight_parts = lax.optimization_barrier(
-        (grad_normed, returned, weight_parts)
-    )
+    last_parts = [cross(part, far + 1 + s) for s, part in enumerate(weight_parts[far + 1 :])]
+    grad_normed, weight_parts[far + 1 :] = lax.optimization_barrier((grad_normed, last_parts))
     grad_images, first_sums = run_last(images, grad_normed, grad_mixed, vectors)
+    first_sums, returned = lax.optimization_barrier((first_sums, returned))
     mixed_cut = lax.dynamic_slice_in_dim(mixed, tensor_at * slice_width, slice_width, 2)
     output_cut = run_take_rows(
         images_held, returned, target, probs, routes, mixed_cut, outer, inner, slots
@@ -1237,6 +1237,7 @@
     high, low = high_low(vector_grads)
     small = jnp.concatenate([matrix, high.T, low.T], axis=1)
     small = swap(small.reshape(groups, shard_width // sources, -1), (DP, EXPERT))
+    small, weight_parts = lax.optimization_barrier((small, weight_parts))
     small = jnp.sum(small.astype(f32), axis=0)
     small = jnp.concatenate(hop_gather(small, EXPERT), axis=0)
     grad_w_qkv = small[:, : 3 * local_width].reshape(shard_width, 3, local_width).transpose(1, 0, 2)

time: 621 us -> 619 us (level)
    ppermute x9, waiting for transfers between devices: 205 us -> 94.6 us  [cross(): lax.ppermute(values, (DP, INNER), [(i, i ^ s) for i in range(count)])]
    all_gather x1, waiting for transfers between devices: 0.01 us -> 66.7 us  [moved_plan(): rows_all = lax.all_gather(rows_cut, tensor_axes)]
    ppermute x7, waiting for transfers between devices: 24.9 us -> 48.8 us  [hop_gather(): hops.append(lax.ppermute(values, axes, [(i, i ^ s) for i in range(count)]))]
    all_to_all x5, waiting for transfers between devices: 103 us -> 121 us  [swap(): return lax.all_to_all(values, axes, split_axis=0, concat_axis=0, tiled=True)]
    unnamed x64 -> x56, local copies, waits for them, and re-layouts: 16.7 us -> 16.6 us
  transfers between devices with their start and end apart: 25 -> 25, of which waited for: 18 -> 14; matrix products, arithmetic and copies ran while one was open for 5% -> 5% of each run, Pallas kernels for 8% -> 12%
where the time goes in v10:
time: 619 us; the launch traced here: 613 us
  waiting for transfers between devices  388 us (63%)
  Pallas kernels  115 us (19%)
  starting transfers between devices  42.8 us (7%)
  local copies, waits for them, and re-layouts  39 us (6%)
  between operations  15.4 us (2%)
  other arithmetic  11.7 us (2%)
    all_to_all x5, waiting for transfers between devices, swap(): return lax.all_to_all(values, axes, split_axis=0, concat_axis=0, tiled=True)  121 us
    ppermute x9, waiting for transfers between devices, cross(): lax.ppermute(values, (DP, INNER), [(i, i ^ s) for i in range(count)])  94.6 us
    pallas_call x6, Pallas kernels, call_kernel(): pl.pallas_call(kernel, grid=grid, in_specs=[smem if b is None else pl.Blo...  68.9 us
    all_gather x1, waiting for transfers between devices, moved_plan(): rows_all = lax.all_gather(rows_cut, tensor_axes)  66.7 us
    psum x1, waiting for transfers between devices, moved_plan(): grad_normed = lax.psum(normed_part, tensor_axes)  56.4 us
    ppermute x7, waiting for transfers between devices, hop_gather(): hops.append(lax.ppermute(values, axes, [(i, i ^ s) for i in range(count)]))  48.8 us
    all_to_all x5, starting transfers between devices, swap(): return lax.all_to_all(values, axes, split_axis=0, concat_axis=0, tiled=True)  24.5 us
    pallas_call x1, Pallas kernels, run_experts(): pl.pallas_call(functools.partial(expert_kernel, inner, owners), grid=(min...  23.1 us
  transfers between devices with their start and end apart: 25, of which 14 were waited for; matrix products, arithmetic and copies ran while one was open for 5% of the time, Pallas kernels for 12%

profile of v10, /device:TPU:0, one launch (start us, length us, event | category | flops | bytes accessed | tf_op | source)
XLA Modules:
  0.0 612.5 jit_solution(2946332666227238507)
XLA Ops:
  28.2 4.9 collective-permute-done.1
  33.2 22.7 %all-to-all-done = bf16[4,192,821]{2,1,0:T(8,128)(2,1)S(1)} async-done(((bf16[4,192,821]{2,1,0:T(8,128)(2,1)}), bf16[4,192,821]{2,1,0:T(8,128)(2,1)S(1)}, u32[]{:S(2)}, u32[]{:S(2)}) %all-to-all-start) | async-done | bytes 1261088 | tf_op jit(solution)/shard_map/all_to_all | solution.py:351
  57.3 6.6 %shard_map.289 = (bf16[2,197,384]{2,1,0:T(8,128)(2,1)}, bf16[4,197,576]{2,1,0:T(8,128)(2,1)}) custom-call(bf16[4,197,768]{2,1,0:T(8,128)(2,1)} %copy.196.images_ref, bf16[768,821]{1,0:T(8,128)(2,1)} %bitcast.46, f32[5,768]{1,0:T(8,128)} %convert_bitcast_fusion.vector_ref, f32[2,192]{1,0:T(2,128)} %convert_element_type.39.bias_ref), custom_call_target="tpu_custom_call" | custom-call | flops 935614464 | bytes 2488320 | tf_op jit(solution)/shard_map/pallas_call | solution.py:645
  74.5 26.4 %collective-permute-done.6 = bf16[768,192]{1,0:T(8,128)(2,1)S(1)} collective-permute-done((bf16[768,192]{1,0:T(8,128)(2,1)S(1)}, bf16[768,192]{1,0:T(8,128)(2,1)S(1)}, u32[]{:S(2)}, u32[]{:S(2)}) %collective-permute-start.6) | collective-permute-done | bytes 294944 | tf_op jit(solution)/shard_map/ppermute | solution.py:358
  102.2 7.8 %collective-permute-done.7 = bf16[768,192]{1,0:T(8,128)(2,1)S(1)} collective-permute-done((bf16[768,192]{1,0:T(8,128)(2,1)S(1)}, bf16[768,192]{1,0:T(8,128)(2,1)S(1)}, u32[]{:S(2)}, u32[]{:S(2)}) %collective-permute-start.7) | collective-permute-done | bytes 294944 | tf_op jit(solution)/shard_map/ppermute | solution.py:358
  117.5 22.5 %shard_map.290 = (f32[4,197,768]{2,1,0:T(8,128)}, f32[4,197,32]{2,1,0:T(8,128)}, bf16[8,528,768]{2,1,0:T(8,128)(2,1)}) custom-call(bf16[4,197,768]{2,1,0:T(8,128)(2,1)} %copy.196.images_ref, bf16[4,197,768]{2,1,0:T(8,128)(2,1)} %copy.194.cot_ref, bf16[4,2,197,384]{3,2,1,0:T(8,128)(2,1)} %bitcast.58, bf16[768,768]{1,0:T(8,128)(2,1)} %pad_maximum_fusion.1.out_ref, ...), custom_call_target="tpu_custom_call" | custom-call | flops 5887229952 | bytes 6099776 | tf_op jit(solution)/shard_map/pallas_call | solution.py:645
  140.0 19.7 %collective-permute-done.11.refs_7_ = bf16[4,192,768]{2,1,0:T(8,128)(2,1)} collective-permute-done((bf16[4,192,768]{2,1,0:T(8,128)(2,1)}, bf16[4,192,768]{2,1,0:T(8,128)(2,1)}, u32[]{:S(2)}, u32[]{:S(2)}) %collective-permute-start.11) | collective-permute-done | bytes 1179680 | tf_op jit(solution)/shard_map/ppermute | solution.py:370
  159.6 5.2 all-to-all-start.1
  167.2 70.4 %all-to-all-done.1.rows_ref.gate_ref.cot_ref = bf16[8,528,768]{2,1,0:T(8,128)(2,1)} async-done(((bf16[8,528,768]{2,1,0:T(8,128)(2,1)}), bf16[8,528,768]{2,1,0:T(8,128)(2,1)}, u32[]{:S(2)}, u32[]{:S(2)}) %all-to-all-start.1) | async-done | bytes 6488096 | tf_op jit(solution)/shard_map/all_to_all | solution.py:351
  237.7 23.1 %shard_map.291 = (bf16[8,4,192,256]{3,2,1,0:T(8,128)(2,1)}, bf16[8,4,208,256]{3,2,1,0:T(8,128)(2,1)}, bf16[4,1,512,768]{3,2,1,0:T(8,128)(2,1)}, bf16[4,1,512,768...) custom-call(s32[1]{0:T(128)} %bitcast.8.at_ref, ...), custom_call_target="tpu_custom_call" | custom-call | flops 9663676416 | bytes 28311552 | tf_op jit(solution)/shard_map/pallas_call | solution.py:473
  260.7 5.1 all-to-all-start.2
  265.8 12.5 %shard_map.292 = (bf16[1552,768]{1,0:T(8,128)(2,1)}, bf16[1552,768]{1,0:T(8,128)(2,1)}, bf16[1552,768]{1,0:T(8,128)(2,1)}, bf16[1552,768]{1,0:T(8,128)(2,1)}) custom-call(s32[1]{0:T(128)} %bitcast.8.at_ref, bf16[8,528,768]{2,1,0:T(8,128)(2,1)} %all-to-all-done.1.rows_ref.gate_ref.cot_ref, bf16[4,1,512,768]{3,2,1,0:T(8,128)(2,1)} %get-tuple-element.92.grad_pre_ref, ...), custom_call_target="tpu_custom_call" | custom-call | flops 4831838208 | bytes 15728640 | tf_op jit(solution)/shard_map/pallas_call | solution.py:565
  284.5 72.1 %collective-permute-done.13.refs_2_ = bf16[1552,768]{1,0:T(8,128)(2,1)} collective-permute-done((bf16[1552,768]{1,0:T(8,128)(2,1)}, bf16[1552,768]{1,0:T(8,128)(2,1)}, u32[]{:S(2)}, u32[]{:S(2)}) %collective-permute-start.13) | collective-permute-done | bytes 2383904 | tf_op jit(solution)/shard_map/ppermute | solution.py:370
  358.3 6.9 %shard_map.293 = (bf16[2,197,384]{2,1,0:T(8,128)(2,1)}, f32[4,197,2]{2,1,0:T(8,128)}) custom-call(bf16[32,208,256]{2,1,0:T(8,128)(2,1)} %copy-done, s32[4,197,2]{2,1,0:T(8,128)} %get-tuple-element.225.target_ref), custom_call_target="tpu_custom_call" | custom-call | flops 619708416 | bytes 3414176 | tf_op jit(solution)/shard_map/pallas_call | solution.py:645
  365.2 6.9 %all-to-all-start.3 = ((bf16[32,192,256]{2,1,0:T(8,128)(2,1)}), bf16[32,192,256]{2,1,0:T(8,128)(2,1)S(1)}, u32[]{:S(2)}, u32[]{:S(2)}) async-start(bf16[32,192,256]{2,1,0:T(8,128)(2,1)} %bitcast.51), calls=%async_computation.3 | async-start | bytes 6291456 | tf_op jit(solution)/shard_map/all_to_all | solution.py:351
  372.9 66.7 %all-gather.9.cloned.1.call-done = bf16[8,197,384]{2,1,0:T(8,128)(2,1)} async-done(((bf16[2,197,384]{2,1,0:T(8,128)(2,1)}), bf16[8,197,384]{2,1,0:T(8,128)(2,1)}) %all-gather.9.cloned.1.call-update) | async-done | bytes 1210384 | tf_op jit(solution)/shard_map/all_gather | solution.py:1201
  439.6 22.7 %all-to-all-done.3.parts_ref = bf16[32,192,256]{2,1,0:T(8,128)(2,1)S(1)} async-done(((bf16[32,192,256]{2,1,0:T(8,128)(2,1)}), bf16[32,192,256]{2,1,0:T(8,128)(2,1)S(1)}, u32[]{:S(2)}, u32[]{:S(2)}) %all-to-all-start.3) | async-done | bytes 3145760 | tf_op jit(solution)/shard_map/all_to_all | solution.py:351
  463.3 21.5 %shard_map.294 = (f32[4,197,768]{2,1,0:T(8,128)}, bf16[4,197,768]{2,1,0:T(8,128)(2,1)}, bf16[768,800]{1,0:T(8,128)(2,1)}, f32[8,768]{1,0:T(8,128)}) custom-call(s32[1]{0:T(128)S(6)} %copy.246.held_ref, bf16[4,197,768]{2,1,0:T(8,128)(2,1)} %copy.196.images_ref, bf16[4,197,768]{2,1,0:T(8,128)(2,1)} %copy.194.cot_ref, ...), custom_call_target="tpu_custom_call" | custom-call | flops 3623236608 | bytes 8652100 | tf_op jit(solution)/shard_map/pallas_call | solution.py:645
  486.3 56.4 %all-reduce.2.cloned.1.call-done.normed_ref = bf16[4,197,768]{2,1,0:T(8,128)(2,1)} async-done(((bf16[4,197,768]{2,1,0:T(8,128)(2,1)}), bf16[4,197,768]{2,1,0:T(8,128)(2,1)}) %all-reduce.2.cloned.1.call-update) | async-done | bytes 1210384 | tf_op jit(solution)/shard_map/psum | solution.py:1221
  542.8 5.4 shard_map.295
  556.8 6.1 shard_map.296
  566.9 5.4 all-to-all-done.4
  573.8 10.7 %shard_map.297 = (f32[16,192,768]{2,1,0:T(8,128)}, f32[16,192,768]{2,1,0:T(8,128)}) custom-call(s32[1]{0:T(128)} %bitcast.8.at_ref, bf16[1552,768]{1,0:T(8,128)(2,1)} %get-tuple-element.125.refs_0_, bf16[1552,768]{1,0:T(8,128)(2,1)} %copy-done.4, bf16[1552,768]{1,0:T(8,128)(2,1)} %collective-permute-done.13.refs_2_, ...), custom_call_target="tpu_custom_call" | custom-call | tf_op jit(solution)/shard_map/pallas_call | solution.py:615
  586.7 8.4 %collective-permute-done.15 = f32[96,814]{1,0:T(8,128)S(1)} collective-permute-done((f32[96,814]{1,0:T(8,128)S(1)}, f32[96,814]{1,0:T(8,128)S(1)}, u32[]{:S(2)}, u32[]{:S(2)}) %collective-permute-start.15) | collective-permute-done | bytes 312608 | tf_op jit(solution)/shard_map/ppermute | solution.py:358
  (173 shorter events, 81.3 us)
Async XLA Ops:
  12.0 43.9 %collective-permute-start.3 = (bf16[4,192,768]{2,1,0:T(8,128)(2,1)}, bf16[4,192,768]{2,1,0:T(8,128)(2,1)}, u32[]{:S(2)}, u32[]{:S(2)}) collective-permute-start(bf16[4,192,768]{2,1,0:T(8,128)(2,1)} %get-tuple-element.217), channel_id=1, source_target_pairs={{0,16},{8,24},{16,0},{24,8},{1,17},{9,25},{17,1},{25,9},{2,18},{10... | collective-permute-start | bytes 3538952 | tf_op jit(solution)/shard_map/ppermute | solution.py:370
  16.8 39.1 %all-to-all-start = ((bf16[4,192,821]{2,1,0:T(8,128)(2,1)}), bf16[4,192,821]{2,1,0:T(8,128)(2,1)S(1)}, u32[]{:S(2)}, u32[]{:S(2)}) async-start(bf16[4,192,821]{2,1,0:T(8,128)(2,1)} %broadcast_in_dim.24), calls=%async_computation | async-start | bytes 2752512 | tf_op jit(solution)/shard_map/all_to_all | solution.py:351
  20.5 96.9 %all-gather.7.cloned.1.call-start = ((), (), s32[]{:S(2)}) async-start(), calls=%async_computation.6 | async-start | bytes 1536000 | tf_op jit(solution)/shard_map/all_gather | solution.py:1150
  20.6 7.6 %collective-permute-start = (bf16[192,192]{1,0:T(8,128)(2,1)S(1)}, bf16[192,192]{1,0:T(8,128)(2,1)S(1)}, u32[]{:S(2)}, u32[]{:S(2)}) collective-permute-start(bf16[192,192]{1,0:T(8,128)(2,1)S(1)} %copy-done.8), channel_id=1, source_target_pairs={{0,3},{1,2},{2,1},{3,0},{4,7},{5,6},{6,5},{7,4},{8,11},{9,10},{10,... | collective-permute-start | bytes 221192 | tf_op jit(solution)/shard_map/ppermute | solution.py:358
  24.3 8.8 %collective-permute-start.1 = (bf16[192,192]{1,0:T(8,128)(2,1)S(1)}, bf16[192,192]{1,0:T(8,128)(2,1)S(1)}, u32[]{:S(2)}, u32[]{:S(2)}) collective-permute-start(bf16[192,192]{1,0:T(8,128)(2,1)S(1)} %copy-done.8), channel_id=1, source_target_pairs={{0,2},{1,3},{2,0},{3,1},{4,6},{5,7},{6,4},{7,5},{8,10},{9,11},{10,... | collective-permute-start | bytes 221192 | tf_op jit(solution)/shard_map/ppermute | solution.py:358
  24.3 8.8 %collective-permute-start.2 = (bf16[192,192]{1,0:T(8,128)(2,1)S(1)}, bf16[192,192]{1,0:T(8,128)(2,1)S(1)}, u32[]{:S(2)}, u32[]{:S(2)}) collective-permute-start(bf16[192,192]{1,0:T(8,128)(2,1)S(1)} %copy-done.8), channel_id=1, source_target_pairs={{0,1},{1,0},{2,3},{3,2},{4,5},{5,4},{6,7},{7,6},{8,9},{9,8},{10,11... | collective-permute-start | bytes 221192 | tf_op jit(solution)/shard_map/ppermute | solution.py:358
  64.0 53.5 %collective-permute-start.4 = (bf16[4,192,768]{2,1,0:T(8,128)(2,1)}, bf16[4,192,768]{2,1,0:T(8,128)(2,1)}, u32[]{:S(2)}, u32[]{:S(2)}) collective-permute-start(bf16[4,192,768]{2,1,0:T(8,128)(2,1)} %get-tuple-element.218), channel_id=1, source_target_pairs={{0,8},{8,0},{16,24},{24,16},{1,9},{9,1},{17,25},{25,17},{2,10},{10... | collective-permute-start | bytes 3538952 | tf_op jit(solution)/shard_map/ppermute | solution.py:370
  64.1 53.4 %collective-permute-start.5 = (bf16[4,192,768]{2,1,0:T(8,128)(2,1)}, bf16[4,192,768]{2,1,0:T(8,128)(2,1)}, u32[]{:S(2)}, u32[]{:S(2)}) collective-permute-start(bf16[4,192,768]{2,1,0:T(8,128)(2,1)} %get-tuple-element.215), channel_id=1, source_target_pairs={{0,24},{8,16},{16,8},{24,0},{1,25},{9,17},{17,9},{25,1},{2,26},{10... | collective-permute-start | bytes 3538952 | tf_op jit(solution)/shard_map/ppermute | solution.py:370
  67.2 33.7 %collective-permute-start.6 = (bf16[768,192]{1,0:T(8,128)(2,1)S(1)}, bf16[768,192]{1,0:T(8,128)(2,1)S(1)}, u32[]{:S(2)}, u32[]{:S(2)}) collective-permute-start(bf16[768,192]{1,0:T(8,128)(2,1)S(1)} %pad_maximum_fusion.2), channel_id=1, source_target_pairs={{0,24},{8,16},{16,8},{24,0},{1,25},{9,17},{17,9},{25,1},{2,26},{10... | collective-permute-start | bytes 884744 | tf_op jit(solution)/shard_map/ppermute | solution.py:358
  67.3 42.7 %collective-permute-start.7 = (bf16[768,192]{1,0:T(8,128)(2,1)S(1)}, bf16[768,192]{1,0:T(8,128)(2,1)S(1)}, u32[]{:S(2)}, u32[]{:S(2)}) collective-permute-start(bf16[768,192]{1,0:T(8,128)(2,1)S(1)} %pad_maximum_fusion.2), channel_id=1, source_target_pairs={{0,16},{8,24},{16,0},{24,8},{1,17},{9,25},{17,1},{25,9},{2,18},{10... | collective-permute-start | bytes 884744 | tf_op jit(solution)/shard_map/ppermute | solution.py:358
  69.0 41.4 %collective-permute-start.8 = (bf16[768,192]{1,0:T(8,128)(2,1)S(1)}, bf16[768,192]{1,0:T(8,128)(2,1)}, u32[]{:S(2)}, u32[]{:S(2)}) collective-permute-start(bf16[768,192]{1,0:T(8,128)(2,1)S(1)} %pad_maximum_fusion.2), channel_id=1, source_target_pairs={{0,8},{8,0},{16,24},{24,16},{1,9},{9,1},{17,25},{25,17},{2,10},{10... | collective-permute-start | bytes 884744 | tf_op jit(solution)/shard_map/ppermute | solution.py:358
  100.9 39.1 %collective-permute-start.10 = (bf16[4,192,768]{2,1,0:T(8,128)(2,1)}, bf16[4,192,768]{2,1,0:T(8,128)(2,1)}, u32[]{:S(2)}, u32[]{:S(2)}) collective-permute-start(bf16[4,192,768]{2,1,0:T(8,128)(2,1)} %get-tuple-element.214), channel_id=1, source_target_pairs={{0,16},{8,24},{16,0},{24,8},{1,17},{9,25},{17,1},{25,9},{2,18},{10... | collective-permute-start | bytes 3538952 | tf_op jit(solution)/shard_map/ppermute | solution.py:370
  110.0 49.6 %collective-permute-start.11 = (bf16[4,192,768]{2,1,0:T(8,128)(2,1)}, bf16[4,192,768]{2,1,0:T(8,128)(2,1)}, u32[]{:S(2)}, u32[]{:S(2)}) collective-permute-start(bf16[4,192,768]{2,1,0:T(8,128)(2,1)} %get-tuple-element.211), channel_id=1, source_target_pairs={{0,24},{8,16},{16,8},{24,0},{1,25},{9,17},{17,9},{25,1},{2,26},{10... | collective-permute-start | bytes 3538952 | tf_op jit(solution)/shard_map/ppermute | solution.py:370
  110.4 49.3 %collective-permute-start.9 = (bf16[4,192,768]{2,1,0:T(8,128)(2,1)}, bf16[4,192,768]{2,1,0:T(8,128)(2,1)}, u32[]{:S(2)}, u32[]{:S(2)}) collective-permute-start(bf16[4,192,768]{2,1,0:T(8,128)(2,1)} %get-tuple-element.212), channel_id=1, source_target_pairs={{0,8},{8,0},{16,24},{24,16},{1,9},{9,1},{17,25},{25,17},{2,10},{10... | collective-permute-start | bytes 3538952 | tf_op jit(solution)/shard_map/ppermute | solution.py:370
  159.6 78.0 %all-to-all-start.1 = ((bf16[8,528,768]{2,1,0:T(8,128)(2,1)}), bf16[8,528,768]{2,1,0:T(8,128)(2,1)}, u32[]{:S(2)}, u32[]{:S(2)}) async-start(bf16[8,528,768]{2,1,0:T(8,128)(2,1)} %get-tuple-element.81), calls=%async_computation.1 | async-start | bytes 12976128 | tf_op jit(solution)/shard_map/all_to_all | solution.py:351
  260.7 95.8 %all-to-all-start.2 = ((bf16[32,208,256]{2,1,0:T(8,128)(2,1)}), bf16[32,208,256]{2,1,0:T(8,128)(2,1)S(1)}, u32[]{:S(2)}, u32[]{:S(2)}) async-start(bf16[32,208,256]{2,1,0:T(8,128)(2,1)} %bitcast.50), calls=%async_computation.2 | async-start | bytes 6815744 | tf_op jit(solution)/shard_map/all_to_all | solution.py:351
  278.5 78.0 %collective-permute-start.13 = (bf16[1552,768]{1,0:T(8,128)(2,1)}, bf16[1552,768]{1,0:T(8,128)(2,1)}, u32[]{:S(2)}, u32[]{:S(2)}) collective-permute-start(bf16[1552,768]{1,0:T(8,128)(2,1)} %get-tuple-element.99), channel_id=1, source_target_pairs={{0,16},{8,24},{16,0},{24,8},{1,17},{9,25},{17,1},{25,9},{2,18},{10... | collective-permute-start | bytes 7151624 | tf_op jit(solution)/shard_map/ppermute | solution.py:370
  365.2 97.1 %all-to-all-start.3 = ((bf16[32,192,256]{2,1,0:T(8,128)(2,1)}), bf16[32,192,256]{2,1,0:T(8,128)(2,1)S(1)}, u32[]{:S(2)}, u32[]{:S(2)}) async-start(bf16[32,192,256]{2,1,0:T(8,128)(2,1)} %bitcast.51), calls=%async_computation.3 | async-start | bytes 6291456 | tf_op jit(solution)/shard_map/all_to_all | solution.py:351
  372.1 67.5 %all-gather.9.cloned.1.call-start = ((), (), s32[]{:S(2)}) async-start(), calls=%async_computation.7 | async-start | bytes 1536000 | tf_op jit(solution)/shard_map/all_gather | solution.py:1201
  372.9 169.9 %all-reduce.2.cloned.1.call-start = ((), (), s32[]{:S(2)}) async-start(), calls=%async_computation.5 | async-start | bytes 2457600 | tf_op jit(solution)/shard_map/psum | solution.py:1221
  462.3 80.4 %collective-permute-start.14 = (bf16[1552,768]{1,0:T(8,128)(2,1)}, bf16[1552,768]{1,0:T(8,128)(2,1)}, u32[]{:S(2)}, u32[]{:S(2)}) collective-permute-start(bf16[1552,768]{1,0:T(8,128)(2,1)} %get-tuple-element.110), channel_id=1, source_target_pairs={{0,24},{8,16},{16,8},{24,0},{1,25},{9,17},{17,9},{25,1},{2,26},{10... | collective-permute-start | bytes 7151624 | tf_op jit(solution)/shard_map/ppermute | solution.py:370
  550.6 21.7 %all-to-all-start.4 = ((bf16[8,96,814]{2,1,0:T(8,128)(2,1)}), bf16[8,96,814]{2,1,0:T(8,128)(2,1)S(1)}, u32[]{:S(2)}, u32[]{:S(2)}) async-start(bf16[8,96,814]{2,1,0:T(8,128)(2,1)} %bitcast.21), calls=%async_computation.4 | async-start | bytes 2752512 | tf_op jit(solution)/shard_map/all_to_all | solution.py:351
  554.2 45.8 %all-gather.11.cloned.1.call-start = ((), (), s32[]{:S(2)}) async-start(), calls=%async_computation.8 | async-start | bytes 1536000 | tf_op jit(solution)/shard_map/all_gather | solution.py:1230
  585.0 10.1 %collective-permute-start.15 = (f32[96,814]{1,0:T(8,128)S(1)}, f32[96,814]{1,0:T(8,128)S(1)}, u32[]{:S(2)}, u32[]{:S(2)}) collective-permute-start(f32[96,814]{1,0:T(8,128)S(1)} %convert_reduce_fusion), channel_id=1, source_target_pairs={{0,4},{4,0},{1,5},{5,1},{2,6},{6,2},{3,7},{7,3},{8,12},{12,8},{9,1... | collective-permute-start | bytes 937736 | tf_op jit(solution)/shard_map/ppermute | solution.py:358
  (24 other events, 211.7 us)
Sparse Core Ops, SparseCore 0:
  64.1 32.7 all-gather.6
  375.1 64.4 all-gather.8
  484.9 57.8 all-reduce.1
  563.0 31.3 all-gather.10

commit v11 on v10

--- a/solution.py
+++ b/solution.py
@@ -609,15 +609,15 @@
             back_ref[...] = part_ref[rows : 2 * rows].astype(jnp.float32).reshape(mine, depth, ff)
 
 
-def run_widen(owner_at, parts, mine, depth):
-    owners, ff = len(parts), parts[0].shape[1]
+def run_widen(owner_at, parts, owners, mine, depth):
+    count, ff = len(parts), parts[0].shape[1]
     out = pl.BlockSpec((mine, depth, ff), lambda p, at: (at[0] ^ p, 0, 0))
     return pl.pallas_call(
         widen_kernel,
         grid_spec=pltpu.PrefetchScalarGridSpec(
             num_scalar_prefetch=1,
-            grid=(owners,),
-            in_specs=[pl.BlockSpec((2 * mine * depth, ff), lambda p, at: (0, 0))] * owners,
+            grid=(count,),
+            in_specs=[pl.BlockSpec((2 * mine * depth, ff), lambda p, at: (0, 0))] * count,
             out_specs=[out, out],
         ),
         out_shape=[jax.ShapeDtypeStruct((owners * mine, depth, ff), jnp.float32)] * 2,
@@ -1200,8 +1200,9 @@
     rows_cut, returned_out = lax.optimization_barrier((rows_cut, returned_out))
     rows_all = lax.all_gather(rows_cut, tensor_axes)
     returned = bring(returned_out)
-    rows_all, returned, weight_parts[far + 1 :] = lax.optimization_barrier(
-        (rows_all, returned, weight_parts[far + 1 :])
+    wide = run_widen(owner_at, weight_parts[: far + 1], owners, mine, shard_width)
+    rows_all, wide, weight_parts[far + 1 :] = lax.optimization_barrier(
+        (rows_all, wide, weight_parts[far + 1 :])
     )
     grad_mixed, normed_part, matrix, sums = run_pull(
         images_held,
@@ -1221,12 +1222,13 @@
     grad_normed = lax.psum(normed_part, tensor_axes)
     last_parts = [cross(part, far + 1 + s) for s, part in enumerate(weight_parts[far + 1 :])]
     grad_normed, weight_parts[far + 1 :] = lax.optimization_barrier((grad_normed, last_parts))
-    grad_images, first_sums = run_last(images, grad_normed, grad_mixed, vectors)
-    first_sums, returned = lax.optimization_barrier((first_sums, returned))
+    normed_part, returned = lax.optimization_barrier((normed_part, returned))
     mixed_cut = lax.dynamic_slice_in_dim(mixed, tensor_at * slice_width, slice_width, 2)
     output_cut = run_take_rows(
         images_held, returned, target, probs, routes, mixed_cut, outer, inner, slots
     )
+    grad_normed, output_cut = lax.optimization_barrier((grad_normed, output_cut))
+    grad_images, first_sums = run_last(images, grad_normed, grad_mixed, vectors)
     output = lax.all_gather(output_cut, tensor_axes)
     output = output.reshape(tensor, image_count // PAIR, seq_len, PAIR, slice_width)
     output = output.transpose(1, 3, 2, 0, 4).reshape(images.shape)
@@ -1237,7 +1239,7 @@
     high, low = high_low(vector_grads)
     small = jnp.concatenate([matrix, high.T, low.T], axis=1)
     small = swap(small.reshape(groups, shard_width // sources, -1), (DP, EXPERT))
-    small, weight_parts = lax.optimization_barrier((small, weight_parts))
+    small, weight_parts[far + 1 :] = lax.optimization_barrier((small, weight_parts[far + 1 :]))
     small = jnp.sum(small.astype(f32), axis=0)
     small = jnp.concatenate(hop_gather(small, EXPERT), axis=0)
     grad_w_qkv = small[:, : 3 * local_width].reshape(shard_width, 3, local_width).transpose(1, 0, 2)
@@ -1245,7 +1247,13 @@
     grad_w_router = small[:, router_at : router_at + EXPERTS]
     vector_grads = small[:, router_at + EXPERTS :].T
     vector_grads = vector_grads[:7] + vector_grads[7:]
-    grad_w_in, grad_w_back = run_widen(owner_at, weight_parts, mine, shard_width)
+    grad_w_in, grad_w_back = wide
+    for s in range(far + 1, owners):
+        two = weight_parts[s][: 2 * mine * shard_width].astype(f32)
+        two = two.reshape(2, mine, shard_width, ff_here)
+        start = (owner_at ^ s) * mine
+        grad_w_in = lax.dynamic_update_slice_in_dim(grad_w_in, two[0], start, 0)
+        grad_w_back = lax.dynamic_update_slice_in_dim(grad_w_back, two[1], start, 0)
     grad_w_back = grad_w_back.transpose(0, 2, 1)
     grad_in_bias = jnp.zeros((experts_here, ff_here), f32)
     grad_back_shard = jnp.zeros((experts_here, shard_width), f32)

time: 619 us -> 589 us (0.952)
  waiting for transfers between devices: 388 us -> 349 us
    psum x1, waiting for transfers between devices: 56.4 us -> 20.2 us  [moved_plan(): grad_normed = lax.psum(normed_part, tensor_axes)]
    ppermute x9, waiting for transfers between devices: 94.6 us -> 121 us  [cross(): lax.ppermute(values, (DP, INNER), [(i, i ^ s) for i in range(count)])]
    all_to_all x5, waiting for transfers between devices: 121 us -> 106 us  [swap(): return lax.all_to_all(values, axes, split_axis=0, concat_axis=0, tiled=True)]
    all_gather x1, waiting for transfers between devices: 66.7 us -> 58 us  [moved_plan(): rows_all = lax.all_gather(rows_cut, tensor_axes)]
    unnamed x56 -> x58, local copies, waits for them, and re-layouts: 16.6 us -> 16.7 us
  transfers between devices with their start and end apart: 25 -> 25, of which waited for: 14 -> 14; matrix products, arithmetic and copies ran while one was open for 5% -> 7% of each run, Pallas kernels for 12% -> 12%
where the time goes in v11:
time: 589 us; the launch traced here: 582 us
  waiting for transfers between devices  349 us (59%)
  Pallas kernels  113 us (19%)
  local copies, waits for them, and re-layouts  43.8 us (7%)
  starting transfers between devices  43.7 us (7%)
  other arithmetic  16.7 us (3%)
  between operations  15.4 us (3%)
    ppermute x9, waiting for transfers between devices, cross(): lax.ppermute(values, (DP, INNER), [(i, i ^ s) for i in range(count)])  121 us
    all_to_all x5, waiting for transfers between devices, swap(): return lax.all_to_all(values, axes, split_axis=0, concat_axis=0, tiled=True)  106 us
    pallas_call x6, Pallas kernels, call_kernel(): pl.pallas_call(kernel, grid=grid, in_specs=[smem if b is None else pl.Blo...  68.6 us
    all_gather x1, waiting for transfers between devices, moved_plan(): rows_all = lax.all_gather(rows_cut, tensor_axes)  58 us
    ppermute x7, waiting for transfers between devices, hop_gather(): hops.append(lax.ppermute(values, axes, [(i, i ^ s) for i in range(count)]))  43.7 us
    all_to_all x5, starting transfers between devices, swap(): return lax.all_to_all(values, axes, split_axis=0, concat_axis=0, tiled=True)  24.5 us
    pallas_call x1, Pallas kernels, run_experts(): pl.pallas_call(functools.partial(expert_kernel, inner, owners), grid=(min...  23.1 us
    psum x1, waiting for transfers between devices, moved_plan(): grad_normed = lax.psum(normed_part, tensor_axes)  20.2 us
  transfers between devices with their start and end apart: 25, of which 14 were waited for; matrix products, arithmetic and copies ran while one was open for 7% of the time, Pallas kernels for 12%

profile of v11, /device:TPU:0, one launch (start us, length us, event | category | flops | bytes accessed | tf_op | source)
XLA Modules:
  0.0 582.0 jit_solution(4548871122035034686)
XLA Ops:
  7.3 4.7 constant_dynamic-slice_fusion.1
  28.2 4.9 collective-permute-done.1
  33.2 22.7 %all-to-all-done = bf16[4,192,821]{2,1,0:T(8,128)(2,1)S(1)} async-done(((bf16[4,192,821]{2,1,0:T(8,128)(2,1)}), bf16[4,192,821]{2,1,0:T(8,128)(2,1)S(1)}, u32[]{:S(2)}, u32[]{:S(2)}) %all-to-all-start) | async-done | bytes 1261088 | tf_op jit(solution)/shard_map/all_to_all | solution.py:351
  57.3 6.6 %shard_map.289 = (bf16[2,197,384]{2,1,0:T(8,128)(2,1)}, bf16[4,197,576]{2,1,0:T(8,128)(2,1)}) custom-call(bf16[4,197,768]{2,1,0:T(8,128)(2,1)} %copy.193.images_ref, bf16[768,821]{1,0:T(8,128)(2,1)} %bitcast.50, f32[5,768]{1,0:T(8,128)} %convert_bitcast_fusion.vector_ref, f32[2,192]{1,0:T(2,128)} %convert_element_type.42.bias_ref), custom_call_target="tpu_custom_call" | custom-call | flops 935614464 | bytes 2488320 | tf_op jit(solution)/shard_map/pallas_call | solution.py:645
  74.5 26.3 %collective-permute-done.6 = bf16[768,192]{1,0:T(8,128)(2,1)S(1)} collective-permute-done((bf16[768,192]{1,0:T(8,128)(2,1)S(1)}, bf16[768,192]{1,0:T(8,128)(2,1)S(1)}, u32[]{:S(2)}, u32[]{:S(2)}) %collective-permute-start.6) | collective-permute-done | bytes 294944 | tf_op jit(solution)/shard_map/ppermute | solution.py:358
  102.2 7.8 %collective-permute-done.7 = bf16[768,192]{1,0:T(8,128)(2,1)S(1)} collective-permute-done((bf16[768,192]{1,0:T(8,128)(2,1)S(1)}, bf16[768,192]{1,0:T(8,128)(2,1)S(1)}, u32[]{:S(2)}, u32[]{:S(2)}) %collective-permute-start.7) | collective-permute-done | bytes 294944 | tf_op jit(solution)/shard_map/ppermute | solution.py:358
  117.5 22.5 %shard_map.290 = (f32[4,197,768]{2,1,0:T(8,128)}, f32[4,197,32]{2,1,0:T(8,128)}, bf16[8,528,768]{2,1,0:T(8,128)(2,1)}) custom-call(bf16[4,197,768]{2,1,0:T(8,128)(2,1)} %copy.193.images_ref, bf16[4,197,768]{2,1,0:T(8,128)(2,1)} %copy.194.cot_ref, bf16[4,2,197,384]{3,2,1,0:T(8,128)(2,1)} %bitcast.62, bf16[768,768]{1,0:T(8,128)(2,1)} %pad_maximum_fusion.1.out_ref, ...), custom_call_target="tpu_custom_call" | custom-call | flops 5887229952 | bytes 6099776 | tf_op jit(solution)/shard_map/pallas_call | solution.py:645
  140.0 19.6 %collective-permute-done.11.refs_7_ = bf16[4,192,768]{2,1,0:T(8,128)(2,1)} collective-permute-done((bf16[4,192,768]{2,1,0:T(8,128)(2,1)}, bf16[4,192,768]{2,1,0:T(8,128)(2,1)}, u32[]{:S(2)}, u32[]{:S(2)}) %collective-permute-start.11) | collective-permute-done | bytes 1179680 | tf_op jit(solution)/shard_map/ppermute | solution.py:370
  159.6 5.2 all-to-all-start.1
  167.2 70.4 %all-to-all-done.1.rows_ref.gate_ref.cot_ref = bf16[8,528,768]{2,1,0:T(8,128)(2,1)} async-done(((bf16[8,528,768]{2,1,0:T(8,128)(2,1)}), bf16[8,528,768]{2,1,0:T(8,128)(2,1)}, u32[]{:S(2)}, u32[]{:S(2)}) %all-to-all-start.1) | async-done | bytes 6488096 | tf_op jit(solution)/shard_map/all_to_all | solution.py:351
  237.6 23.1 %shard_map.291 = (bf16[8,4,192,256]{3,2,1,0:T(8,128)(2,1)}, bf16[8,4,208,256]{3,2,1,0:T(8,128)(2,1)}, bf16[4,1,512,768]{3,2,1,0:T(8,128)(2,1)}, bf16[4,1,512,768...) custom-call(s32[1]{0:T(128)} %bitcast.8.at_ref, ...), custom_call_target="tpu_custom_call" | custom-call | flops 9663676416 | bytes 28311552 | tf_op jit(solution)/shard_map/pallas_call | solution.py:473
  260.7 5.1 all-to-all-start.2
  265.8 12.4 %shard_map.292 = (bf16[1552,768]{1,0:T(8,128)(2,1)}, bf16[1552,768]{1,0:T(8,128)(2,1)}, bf16[1552,768]{1,0:T(8,128)(2,1)}, bf16[1552,768]{1,0:T(8,128)(2,1)}) custom-call(s32[1]{0:T(128)} %bitcast.8.at_ref, bf16[8,528,768]{2,1,0:T(8,128)(2,1)} %all-to-all-done.1.rows_ref.gate_ref.cot_ref, bf16[4,1,512,768]{3,2,1,0:T(8,128)(2,1)} %get-tuple-element.91.grad_pre_ref, ...), custom_call_target="tpu_custom_call" | custom-call | flops 4831838208 | bytes 15728640 | tf_op jit(solution)/shard_map/pallas_call | solution.py:565
  284.5 72.1 %collective-permute-done.13.refs_2_ = bf16[1552,768]{1,0:T(8,128)(2,1)} collective-permute-done((bf16[1552,768]{1,0:T(8,128)(2,1)}, bf16[1552,768]{1,0:T(8,128)(2,1)}, u32[]{:S(2)}, u32[]{:S(2)}) %collective-permute-start.13) | collective-permute-done | bytes 2383904 | tf_op jit(solution)/shard_map/ppermute | solution.py:370
  358.3 6.9 %shard_map.293 = (bf16[2,197,384]{2,1,0:T(8,128)(2,1)}, f32[4,197,2]{2,1,0:T(8,128)}) custom-call(bf16[32,208,256]{2,1,0:T(8,128)(2,1)} %copy-done, s32[4,197,2]{2,1,0:T(8,128)} %get-tuple-element.225.target_ref), custom_call_target="tpu_custom_call" | custom-call | flops 619708416 | bytes 3414176 | tf_op jit(solution)/shard_map/pallas_call | solution.py:645
  365.2 6.9 %all-to-all-start.3 = ((bf16[32,192,256]{2,1,0:T(8,128)(2,1)}), bf16[32,192,256]{2,1,0:T(8,128)(2,1)S(1)}, u32[]{:S(2)}, u32[]{:S(2)}) async-start(bf16[32,192,256]{2,1,0:T(8,128)(2,1)} %bitcast.55), calls=%async_computation.3 | async-start | bytes 6291456 | tf_op jit(solution)/shard_map/all_to_all | solution.py:351
  372.9 8.7 %shard_map.294 = (f32[16,192,768]{2,1,0:T(8,128)}, f32[16,192,768]{2,1,0:T(8,128)}) custom-call(s32[1]{0:T(128)} %bitcast.8.at_ref, bf16[1552,768]{1,0:T(8,128)(2,1)} %get-tuple-element.104.refs_0_, bf16[1552,768]{1,0:T(8,128)(2,1)} %copy-done.4, bf16[1552,768]{1,0:T(8,128)(2,1)} %collective-permute-done.13.refs_2_), custom_call_target="tpu_custom_call" | custom-call | tf_op jit(solution)/shard_map/pallas_call | solution.py:615
  381.6 58.0 %all-gather.9.cloned.1.call-done = bf16[8,197,384]{2,1,0:T(8,128)(2,1)} async-done(((bf16[2,197,384]{2,1,0:T(8,128)(2,1)}), bf16[8,197,384]{2,1,0:T(8,128)(2,1)}) %all-gather.9.cloned.1.call-update) | async-done | bytes 1210384 | tf_op jit(solution)/shard_map/all_gather | solution.py:1201
  441.2 21.3 %shard_map.295 = (f32[4,197,768]{2,1,0:T(8,128)}, bf16[4,197,768]{2,1,0:T(8,128)(2,1)}, bf16[768,800]{1,0:T(8,128)(2,1)}, f32[8,768]{1,0:T(8,128)}) custom-call(s32[1]{0:T(128)S(6)} %copy.250.held_ref, bf16[4,197,768]{2,1,0:T(8,128)(2,1)} %copy.193.images_ref, bf16[4,197,768]{2,1,0:T(8,128)(2,1)} %copy.194.cot_ref, ...), custom_call_target="tpu_custom_call" | custom-call | flops 3623236608 | bytes 8652100 | tf_op jit(solution)/shard_map/pallas_call | solution.py:645
  466.9 5.9 %shard_map.296 = bf16[2,197,384]{2,1,0:T(8,128)(2,1)} custom-call(s32[1]{0:T(128)S(6)} %copy.250.held_ref, bf16[32,192,256]{2,1,0:T(8,128)(2,1)} %copy-done.1, s32[4,197,2]{2,1,0:T(8,128)} %get-tuple-element.225.target_ref, f32[4,197,32]{2,1,0:T(8,128)} %get-tuple-element.78.probs_ref, s32[4,197,2]{2,1,0:T(8,128)} %copy-done.3, ...), custom_call_target="tpu_custom_call" | custom-call | flops 1239416832 | bytes 3864388 | tf_op jit(solution)/shard_map/pallas_call | solution.py:645
  472.8 26.6 %collective-permute-done.14 = bf16[1552,768]{1,0:T(8,128)(2,1)} collective-permute-done((bf16[1552,768]{1,0:T(8,128)(2,1)}, bf16[1552,768]{1,0:T(8,128)(2,1)}, u32[]{:S(2)}, u32[]{:S(2)}) %collective-permute-start.14) | collective-permute-done | bytes 2383904 | tf_op jit(solution)/shard_map/ppermute | solution.py:370
  499.4 20.2 %all-reduce.2.cloned.1.call-done.normed_ref = bf16[4,197,768]{2,1,0:T(8,128)(2,1)} async-done(((bf16[4,197,768]{2,1,0:T(8,128)(2,1)}), bf16[4,197,768]{2,1,0:T(8,128)(2,1)}) %all-reduce.2.cloned.1.call-update) | async-done | bytes 1210384 | tf_op jit(solution)/shard_map/psum | solution.py:1222
  519.6 5.4 shard_map.297
  536.5 12.6 %all-to-all-done.4 = bf16[8,96,814]{2,1,0:T(8,128)(2,1)S(1)} async-done(((bf16[8,96,814]{2,1,0:T(8,128)(2,1)}), bf16[8,96,814]{2,1,0:T(8,128)(2,1)S(1)}, u32[]{:S(2)}, u32[]{:S(2)}) %all-to-all-start.4) | async-done | bytes 1250336 | tf_op jit(solution)/shard_map/all_to_all | solution.py:351
  (179 shorter events, 90.7 us)
Async XLA Ops:
  12.0 43.9 %collective-permute-start.3 = (bf16[4,192,768]{2,1,0:T(8,128)(2,1)}, bf16[4,192,768]{2,1,0:T(8,128)(2,1)}, u32[]{:S(2)}, u32[]{:S(2)}) collective-permute-start(bf16[4,192,768]{2,1,0:T(8,128)(2,1)} %get-tuple-element.217), channel_id=1, source_target_pairs={{0,16},{8,24},{16,0},{24,8},{1,17},{9,25},{17,1},{25,9},{2,18},{10... | collective-permute-start | bytes 3538952 | tf_op jit(solution)/shard_map/ppermute | solution.py:370
  16.9 39.0 %all-to-all-start = ((bf16[4,192,821]{2,1,0:T(8,128)(2,1)}), bf16[4,192,821]{2,1,0:T(8,128)(2,1)S(1)}, u32[]{:S(2)}, u32[]{:S(2)}) async-start(bf16[4,192,821]{2,1,0:T(8,128)(2,1)} %broadcast_in_dim.24), calls=%async_computation | async-start | bytes 2752512 | tf_op jit(solution)/shard_map/all_to_all | solution.py:351
  20.5 96.9 %all-gather.7.cloned.1.call-start = ((), (), s32[]{:S(2)}) async-start(), calls=%async_computation.6 | async-start | bytes 1536000 | tf_op jit(solution)/shard_map/all_gather | solution.py:1150
  20.6 7.6 %collective-permute-start = (bf16[192,192]{1,0:T(8,128)(2,1)S(1)}, bf16[192,192]{1,0:T(8,128)(2,1)S(1)}, u32[]{:S(2)}, u32[]{:S(2)}) collective-permute-start(bf16[192,192]{1,0:T(8,128)(2,1)S(1)} %copy-done.8), channel_id=1, source_target_pairs={{0,3},{1,2},{2,1},{3,0},{4,7},{5,6},{6,5},{7,4},{8,11},{9,10},{10,... | collective-permute-start | bytes 221192 | tf_op jit(solution)/shard_map/ppermute | solution.py:358
  24.3 8.8 %collective-permute-start.1 = (bf16[192,192]{1,0:T(8,128)(2,1)S(1)}, bf16[192,192]{1,0:T(8,128)(2,1)S(1)}, u32[]{:S(2)}, u32[]{:S(2)}) collective-permute-start(bf16[192,192]{1,0:T(8,128)(2,1)S(1)} %copy-done.8), channel_id=1, source_target_pairs={{0,2},{1,3},{2,0},{3,1},{4,6},{5,7},{6,4},{7,5},{8,10},{9,11},{10,... | collective-permute-start | bytes 221192 | tf_op jit(solution)/shard_map/ppermute | solution.py:358
  24.3 8.8 %collective-permute-start.2 = (bf16[192,192]{1,0:T(8,128)(2,1)S(1)}, bf16[192,192]{1,0:T(8,128)(2,1)S(1)}, u32[]{:S(2)}, u32[]{:S(2)}) collective-permute-start(bf16[192,192]{1,0:T(8,128)(2,1)S(1)} %copy-done.8), channel_id=1, source_target_pairs={{0,1},{1,0},{2,3},{3,2},{4,5},{5,4},{6,7},{7,6},{8,9},{9,8},{10,11... | collective-permute-start | bytes 221192 | tf_op jit(solution)/shard_map/ppermute | solution.py:358
  64.0 53.5 %collective-permute-start.4 = (bf16[4,192,768]{2,1,0:T(8,128)(2,1)}, bf16[4,192,768]{2,1,0:T(8,128)(2,1)}, u32[]{:S(2)}, u32[]{:S(2)}) collective-permute-start(bf16[4,192,768]{2,1,0:T(8,128)(2,1)} %get-tuple-element.218), channel_id=1, source_target_pairs={{0,8},{8,0},{16,24},{24,16},{1,9},{9,1},{17,25},{25,17},{2,10},{10... | collective-permute-start | bytes 3538952 | tf_op jit(solution)/shard_map/ppermute | solution.py:370
  64.1 53.4 %collective-permute-start.5 = (bf16[4,192,768]{2,1,0:T(8,128)(2,1)}, bf16[4,192,768]{2,1,0:T(8,128)(2,1)}, u32[]{:S(2)}, u32[]{:S(2)}) collective-permute-start(bf16[4,192,768]{2,1,0:T(8,128)(2,1)} %get-tuple-element.215), channel_id=1, source_target_pairs={{0,24},{8,16},{16,8},{24,0},{1,25},{9,17},{17,9},{25,1},{2,26},{10... | collective-permute-start | bytes 3538952 | tf_op jit(solution)/shard_map/ppermute | solution.py:370
  67.2 33.7 %collective-permute-start.6 = (bf16[768,192]{1,0:T(8,128)(2,1)S(1)}, bf16[768,192]{1,0:T(8,128)(2,1)S(1)}, u32[]{:S(2)}, u32[]{:S(2)}) collective-permute-start(bf16[768,192]{1,0:T(8,128)(2,1)S(1)} %pad_maximum_fusion.2), channel_id=1, source_target_pairs={{0,24},{8,16},{16,8},{24,0},{1,25},{9,17},{17,9},{25,1},{2,26},{10... | collective-permute-start | bytes 884744 | tf_op jit(solution)/shard_map/ppermute | solution.py:358
  67.3 42.7 %collective-permute-start.7 = (bf16[768,192]{1,0:T(8,128)(2,1)S(1)}, bf16[768,192]{1,0:T(8,128)(2,1)S(1)}, u32[]{:S(2)}, u32[]{:S(2)}) collective-permute-start(bf16[768,192]{1,0:T(8,128)(2,1)S(1)} %pad_maximum_fusion.2), channel_id=1, source_target_pairs={{0,16},{8,24},{16,0},{24,8},{1,17},{9,25},{17,1},{25,9},{2,18},{10... | collective-permute-start | bytes 884744 | tf_op jit(solution)/shard_map/ppermute | solution.py:358
  69.0 41.4 %collective-permute-start.8 = (bf16[768,192]{1,0:T(8,128)(2,1)S(1)}, bf16[768,192]{1,0:T(8,128)(2,1)}, u32[]{:S(2)}, u32[]{:S(2)}) collective-permute-start(bf16[768,192]{1,0:T(8,128)(2,1)S(1)} %pad_maximum_fusion.2), channel_id=1, source_target_pairs={{0,8},{8,0},{16,24},{24,16},{1,9},{9,1},{17,25},{25,17},{2,10},{10... | collective-permute-start | bytes 884744 | tf_op jit(solution)/shard_map/ppermute | solution.py:358
  100.9 39.1 %collective-permute-start.10 = (bf16[4,192,768]{2,1,0:T(8,128)(2,1)}, bf16[4,192,768]{2,1,0:T(8,128)(2,1)}, u32[]{:S(2)}, u32[]{:S(2)}) collective-permute-start(bf16[4,192,768]{2,1,0:T(8,128)(2,1)} %get-tuple-element.214), channel_id=1, source_target_pairs={{0,16},{8,24},{16,0},{24,8},{1,17},{9,25},{17,1},{25,9},{2,18},{10... | collective-permute-start | bytes 3538952 | tf_op jit(solution)/shard_map/ppermute | solution.py:370
  110.0 49.6 %collective-permute-start.11 = (bf16[4,192,768]{2,1,0:T(8,128)(2,1)}, bf16[4,192,768]{2,1,0:T(8,128)(2,1)}, u32[]{:S(2)}, u32[]{:S(2)}) collective-permute-start(bf16[4,192,768]{2,1,0:T(8,128)(2,1)} %get-tuple-element.211), channel_id=1, source_target_pairs={{0,24},{8,16},{16,8},{24,0},{1,25},{9,17},{17,9},{25,1},{2,26},{10... | collective-permute-start | bytes 3538952 | tf_op jit(solution)/shard_map/ppermute | solution.py:370
  110.4 49.3 %collective-permute-start.9 = (bf16[4,192,768]{2,1,0:T(8,128)(2,1)}, bf16[4,192,768]{2,1,0:T(8,128)(2,1)}, u32[]{:S(2)}, u32[]{:S(2)}) collective-permute-start(bf16[4,192,768]{2,1,0:T(8,128)(2,1)} %get-tuple-element.212), channel_id=1, source_target_pairs={{0,8},{8,0},{16,24},{24,16},{1,9},{9,1},{17,25},{25,17},{2,10},{10... | collective-permute-start | bytes 3538952 | tf_op jit(solution)/shard_map/ppermute | solution.py:370
  159.6 78.0 %all-to-all-start.1 = ((bf16[8,528,768]{2,1,0:T(8,128)(2,1)}), bf16[8,528,768]{2,1,0:T(8,128)(2,1)}, u32[]{:S(2)}, u32[]{:S(2)}) async-start(bf16[8,528,768]{2,1,0:T(8,128)(2,1)} %get-tuple-element.80), calls=%async_computation.1 | async-start | bytes 12976128 | tf_op jit(solution)/shard_map/all_to_all | solution.py:351
  260.7 95.8 %all-to-all-start.2 = ((bf16[32,208,256]{2,1,0:T(8,128)(2,1)}), bf16[32,208,256]{2,1,0:T(8,128)(2,1)S(1)}, u32[]{:S(2)}, u32[]{:S(2)}) async-start(bf16[32,208,256]{2,1,0:T(8,128)(2,1)} %bitcast.54), calls=%async_computation.2 | async-start | bytes 6815744 | tf_op jit(solution)/shard_map/all_to_all | solution.py:351
  278.5 78.1 %collective-permute-start.13 = (bf16[1552,768]{1,0:T(8,128)(2,1)}, bf16[1552,768]{1,0:T(8,128)(2,1)}, u32[]{:S(2)}, u32[]{:S(2)}) collective-permute-start(bf16[1552,768]{1,0:T(8,128)(2,1)} %get-tuple-element.98), channel_id=1, source_target_pairs={{0,16},{8,24},{16,0},{24,8},{1,17},{9,25},{17,1},{25,9},{2,18},{10... | collective-permute-start | bytes 7151624 | tf_op jit(solution)/shard_map/ppermute | solution.py:370
  365.2 97.3 %all-to-all-start.3 = ((bf16[32,192,256]{2,1,0:T(8,128)(2,1)}), bf16[32,192,256]{2,1,0:T(8,128)(2,1)S(1)}, u32[]{:S(2)}, u32[]{:S(2)}) async-start(bf16[32,192,256]{2,1,0:T(8,128)(2,1)} %bitcast.55), calls=%async_computation.3 | async-start | bytes 6291456 | tf_op jit(solution)/shard_map/all_to_all | solution.py:351
  372.1 67.5 %all-gather.9.cloned.1.call-start = ((), (), s32[]{:S(2)}) async-start(), calls=%async_computation.7 | async-start | bytes 1536000 | tf_op jit(solution)/shard_map/all_gather | solution.py:1201
  372.8 146.7 %all-reduce.2.cloned.1.call-start = ((), (), s32[]{:S(2)}) async-start(), calls=%async_computation.5 | async-start | bytes 2457600 | tf_op jit(solution)/shard_map/psum | solution.py:1222
  439.6 59.8 %collective-permute-start.14 = (bf16[1552,768]{1,0:T(8,128)(2,1)}, bf16[1552,768]{1,0:T(8,128)(2,1)}, u32[]{:S(2)}, u32[]{:S(2)}) collective-permute-start(bf16[1552,768]{1,0:T(8,128)(2,1)} %get-tuple-element.113), channel_id=1, source_target_pairs={{0,24},{8,16},{16,8},{24,0},{1,25},{9,17},{17,9},{25,1},{2,26},{10... | collective-permute-start | bytes 7151624 | tf_op jit(solution)/shard_map/ppermute | solution.py:370
  527.4 21.7 %all-to-all-start.4 = ((bf16[8,96,814]{2,1,0:T(8,128)(2,1)}), bf16[8,96,814]{2,1,0:T(8,128)(2,1)S(1)}, u32[]{:S(2)}, u32[]{:S(2)}) async-start(bf16[8,96,814]{2,1,0:T(8,128)(2,1)} %bitcast.21), calls=%async_computation.4 | async-start | bytes 2752512 | tf_op jit(solution)/shard_map/all_to_all | solution.py:351
  531.1 38.4 %all-gather.11.cloned.1.call-start = ((), (), s32[]{:S(2)}) async-start(), calls=%async_computation.8 | async-start | bytes 1536000 | tf_op jit(solution)/shard_map/all_gather | solution.py:1232
  554.4 10.2 %collective-permute-start.15 = (f32[96,814]{1,0:T(8,128)S(1)}, f32[96,814]{1,0:T(8,128)S(1)}, u32[]{:S(2)}, u32[]{:S(2)}) collective-permute-start(f32[96,814]{1,0:T(8,128)S(1)} %convert_reduce_fusion), channel_id=1, source_target_pairs={{0,4},{4,0},{1,5},{5,1},{2,6},{6,2},{3,7},{7,3},{8,12},{12,8},{9,1... | collective-permute-start | bytes 937736 | tf_op jit(solution)/shard_map/ppermute | solution.py:358
  (25 other events, 199.8 us)
Sparse Core Ops, SparseCore 0:
  64.1 32.7 all-gather.6
  374.5 65.0 all-gather.8
  462.7 56.8 all-reduce.1
  536.7 31.4 all-gather.10

commit v12 on v11

--- a/solution.py
+++ b/solution.py
@@ -1127,8 +1127,8 @@
     in_pieces = [piece(w_in, s) for s in range(owners)]
     back_pieces = [piece(w_back.transpose(0, 2, 1), s) for s in range(owners)]
     far = owners // 2
-    packed, out_rows, in_bias_all, in_pieces[far] = lax.optimization_barrier(
-        (packed, out_rows, in_bias_all, in_pieces[far])
+    packed, out_rows, in_bias_all, in_pieces[far:] = lax.optimization_barrier(
+        (packed, out_rows, in_bias_all, in_pieces[far:])
     )
     vectors = packed[:, router_at + EXPERTS + experts_here :].T.astype(f32)
     out_whole = jnp.concatenate(hop_gather(out_rows, DP), axis=1)
@@ -1192,10 +1192,8 @@
         owners,
     )
     weight_parts = list(weight_parts)
+    grad_parts, weight_parts[far:] = lax.optimization_barrier((grad_parts, weight_parts[far:]))
     weight_parts[: far + 1] = [cross(part, s) for s, part in enumerate(weight_parts[: far + 1])]
-    grad_parts, weight_parts[: far + 1] = lax.optimization_barrier(
-        (grad_parts, weight_parts[: far + 1])
-    )
     rows_cut, grad_gates = run_take_grads(grad_parts, target, slice_width, outer, inner, slots)
     rows_cut, returned_out = lax.optimization_barrier((rows_cut, returned_out))
     rows_all = lax.all_gather(rows_cut, tensor_axes)
@@ -1221,13 +1219,22 @@
     )
     grad_normed = lax.psum(normed_part, tensor_axes)
     last_parts = [cross(part, far + 1 + s) for s, part in enumerate(weight_parts[far + 1 :])]
-    grad_normed, weight_parts[far + 1 :] = lax.optimization_barrier((grad_normed, last_parts))
+    weight_parts[far + 1 :] = last_parts
+    grad_w_in, grad_w_back = wide
+    for s in range(far + 1, owners):
+        two = weight_parts[s][: 2 * mine * shard_width].astype(f32)
+        two = two.reshape(2, mine, shard_width, ff_here)
+        start = (owner_at ^ s) * mine
+        grad_w_in = lax.dynamic_update_slice_in_dim(grad_w_in, two[0], start, 0)
+        grad_w_back = lax.dynamic_update_slice_in_dim(grad_w_back, two[1], start, 0)
     normed_part, returned = lax.optimization_barrier((normed_part, returned))
     mixed_cut = lax.dynamic_slice_in_dim(mixed, tensor_at * slice_width, slice_width, 2)
     output_cut = run_take_rows(
         images_held, returned, target, probs, routes, mixed_cut, outer, inner, slots
     )
-    grad_normed, output_cut = lax.optimization_barrier((grad_normed, output_cut))
+    grad_normed, output_cut, grad_w_in, grad_w_back = lax.optimization_barrier(
+        (grad_normed, output_cut, grad_w_in, grad_w_back)
+    )
     grad_images, first_sums = run_last(images, grad_normed, grad_mixed, vectors)
     output = lax.all_gather(output_cut, tensor_axes)
     output = output.reshape(tensor, image_count // PAIR, seq_len, PAIR, slice_width)
@@ -1239,7 +1246,6 @@
     high, low = high_low(vector_grads)
     small = jnp.concatenate([matrix, high.T, low.T], axis=1)
     small = swap(small.reshape(groups, shard_width // sources, -1), (DP, EXPERT))
-    small, weight_parts[far + 1 :] = lax.optimization_barrier((small, weight_parts[far + 1 :]))
     small = jnp.sum(small.astype(f32), axis=0)
     small = jnp.concatenate(hop_gather(small, EXPERT), axis=0)
     grad_w_qkv = small[:, : 3 * local_width].reshape(shard_width, 3, local_width).transpose(1, 0, 2)
@@ -1247,13 +1253,6 @@
     grad_w_router = small[:, router_at : router_at + EXPERTS]
     vector_grads = small[:, router_at + EXPERTS :].T
     vector_grads = vector_grads[:7] + vector_grads[7:]
-    grad_w_in, grad_w_back = wide
-    for s in range(far + 1, owners):
-        two = weight_parts[s][: 2 * mine * shard_width].astype(f32)
-        two = two.reshape(2, mine, shard_width, ff_here)
-        start = (owner_at ^ s) * mine
-        grad_w_in = lax.dynamic_update_slice_in_dim(grad_w_in, two[0], start, 0)
-        grad_w_back = lax.dynamic_update_slice_in_dim(grad_w_back, two[1], start, 0)
     grad_w_back = grad_w_back.transpose(0, 2, 1)
     grad_in_bias = jnp.zeros((experts_here, ff_here), f32)
     grad_back_shard = jnp.zeros((experts_here, shard_width), f32)

time: 589 us -> 610 us (1.036)
  waiting for transfers between devices: 349 us -> 379 us
    all_to_all x5, waiting for transfers between devices: 106 us -> 199 us  [swap(): return lax.all_to_all(values, axes, split_axis=0, concat_axis=0, tiled=True)]
    all_gather x1, waiting for transfers between devices: 58 us -> 0.01 us  [moved_plan(): rows_all = lax.all_gather(rows_cut, tensor_axes)]
    ppermute x9, waiting for transfers between devices: 121 us -> 111 us  [cross(): lax.ppermute(values, (DP, INNER), [(i, i ^ s) for i in range(count)])]
    unnamed x58 -> x54, local copies, waits for them, and re-layouts: 16.7 us -> 15.2 us
  transfers between devices with their start and end apart: 25 -> 25, of which waited for: 14 -> 15; matrix products, arithmetic and copies ran while one was open for 7% -> 7% of each run, Pallas kernels for 12% -> 12%
where the time goes in v12:
time: 610 us; the launch traced here: 603 us
  waiting for transfers between devices  379 us (62%)
  Pallas kernels  113 us (19%)
  local copies, waits for them, and re-layouts  40.3 us (7%)
  starting transfers between devices  39.2 us (6%)
  other arithmetic  15.3 us (3%)
  between operations  15.3 us (3%)
    all_to_all x5, waiting for transfers between devices, swap(): return lax.all_to_all(values, axes, split_axis=0, concat_axis=0, tiled=True)  199 us
    ppermute x9, waiting for transfers between devices, cross(): lax.ppermute(values, (DP, INNER), [(i, i ^ s) for i in range(count)])  111 us
    pallas_call x6, Pallas kernels, call_kernel(): pl.pallas_call(kernel, grid=grid, in_specs=[smem if b is None else pl.Blo...  68.7 us
    ppermute x7, waiting for transfers between devices, hop_gather(): hops.append(lax.ppermute(values, axes, [(i, i ^ s) for i in range(count)]))  44.2 us
    psum x1, waiting for transfers between devices, moved_plan(): grad_normed = lax.psum(normed_part, tensor_axes)  24.2 us
    pallas_call x1, Pallas kernels, run_experts(): pl.pallas_call(functools.partial(expert_kernel, inner, owners), grid=(min...  23.1 us
    all_to_all x5, starting transfers between devices, swap(): return lax.all_to_all(values, axes, split_axis=0, concat_axis=0, tiled=True)  21.4 us
    unnamed x54, local copies, waits for them, and re-layouts  15.2 us
  transfers between devices with their start and end apart: 25, of which 15 were waited for; matrix products, arithmetic and copies ran while one was open for 7% of the time, Pallas kernels for 12%

profile of v12, /device:TPU:0, one launch (start us, length us, event | category | flops | bytes accessed | tf_op | source)
XLA Modules:
  0.0 602.6 jit_solution(14945086785357800622)
XLA Ops:
  7.3 4.7 constant_dynamic-slice_fusion.1
  26.5 4.8 collective-permute-done.1
  32.1 49.0 %all-to-all-done = bf16[4,192,821]{2,1,0:T(8,128)(2,1)S(1)} async-done(((bf16[4,192,821]{2,1,0:T(8,128)(2,1)}), bf16[4,192,821]{2,1,0:T(8,128)(2,1)S(1)}, u32[]{:S(2)}, u32[]{:S(2)}) %all-to-all-start) | async-done | bytes 1261088 | tf_op jit(solution)/shard_map/all_to_all | solution.py:351
  82.5 6.6 %shard_map.289 = (bf16[2,197,384]{2,1,0:T(8,128)(2,1)}, bf16[4,197,576]{2,1,0:T(8,128)(2,1)}) custom-call(bf16[4,197,768]{2,1,0:T(8,128)(2,1)} %copy.193.images_ref, bf16[768,821]{1,0:T(8,128)(2,1)} %bitcast.50, f32[5,768]{1,0:T(8,128)} %convert_bitcast_fusion.vector_ref, f32[2,192]{1,0:T(2,128)} %convert_element_type.42.bias_ref), custom_call_target="tpu_custom_call" | custom-call | flops 935614464 | bytes 2488320 | tf_op jit(solution)/shard_map/pallas_call | solution.py:645
  89.3 4.6 dynamic-slice_bitcast_fusion
  100.7 31.1 %collective-permute-done.7 = bf16[768,192]{1,0:T(8,128)(2,1)} collective-permute-done((bf16[768,192]{1,0:T(8,128)(2,1)S(1)}, bf16[768,192]{1,0:T(8,128)(2,1)}, u32[]{:S(2)}, u32[]{:S(2)}) %collective-permute-start.7) | collective-permute-done | bytes 294944 | tf_op jit(solution)/shard_map/ppermute | solution.py:358
  142.5 22.5 %shard_map.290 = (f32[4,197,768]{2,1,0:T(8,128)}, f32[4,197,32]{2,1,0:T(8,128)}, bf16[8,528,768]{2,1,0:T(8,128)(2,1)}) custom-call(bf16[4,197,768]{2,1,0:T(8,128)(2,1)} %copy.193.images_ref, bf16[4,197,768]{2,1,0:T(8,128)(2,1)} %copy.194.cot_ref, bf16[4,2,197,384]{3,2,1,0:T(8,128)(2,1)} %bitcast.62, bf16[768,768]{1,0:T(8,128)(2,1)} %pad_maximum_fusion.1.out_ref, ...), custom_call_target="tpu_custom_call" | custom-call | flops 5887229952 | bytes 6099776 | tf_op jit(solution)/shard_map/pallas_call | solution.py:645
  165.3 5.2 all-to-all-start.1
  172.9 70.4 %all-to-all-done.1.rows_ref.gate_ref.cot_ref = bf16[8,528,768]{2,1,0:T(8,128)(2,1)} async-done(((bf16[8,528,768]{2,1,0:T(8,128)(2,1)}), bf16[8,528,768]{2,1,0:T(8,128)(2,1)}, u32[]{:S(2)}, u32[]{:S(2)}) %all-to-all-start.1) | async-done | bytes 6488096 | tf_op jit(solution)/shard_map/all_to_all | solution.py:351
  243.3 23.1 %shard_map.291 = (bf16[8,4,192,256]{3,2,1,0:T(8,128)(2,1)}, bf16[8,4,208,256]{3,2,1,0:T(8,128)(2,1)}, bf16[4,1,512,768]{3,2,1,0:T(8,128)(2,1)}, bf16[4,1,512,768...) custom-call(s32[1]{0:T(128)} %bitcast.8.at_ref, ...), custom_call_target="tpu_custom_call" | custom-call | flops 9663676416 | bytes 28311552 | tf_op jit(solution)/shard_map/pallas_call | solution.py:473
  266.4 5.1 all-to-all-start.2
  271.5 12.4 %shard_map.292 = (bf16[1552,768]{1,0:T(8,128)(2,1)}, bf16[1552,768]{1,0:T(8,128)(2,1)}, bf16[1552,768]{1,0:T(8,128)(2,1)}, bf16[1552,768]{1,0:T(8,128)(2,1)}) custom-call(s32[1]{0:T(128)} %bitcast.8.at_ref, bf16[8,528,768]{2,1,0:T(8,128)(2,1)} %all-to-all-done.1.rows_ref.gate_ref.cot_ref, bf16[4,1,512,768]{3,2,1,0:T(8,128)(2,1)} %get-tuple-element.90.grad_pre_ref, ...), custom_call_target="tpu_custom_call" | custom-call | flops 4831838208 | bytes 15728640 | tf_op jit(solution)/shard_map/pallas_call | solution.py:565
  283.9 63.6 %all-to-all-done.2.parts_ref = bf16[32,208,256]{2,1,0:T(8,128)(2,1)S(1)} async-done(((bf16[32,208,256]{2,1,0:T(8,128)(2,1)}), bf16[32,208,256]{2,1,0:T(8,128)(2,1)S(1)}, u32[]{:S(2)}, u32[]{:S(2)}) %all-to-all-start.2) | async-done | bytes 3407904 | tf_op jit(solution)/shard_map/all_to_all | solution.py:351
  349.3 6.9 %shard_map.293 = (bf16[2,197,384]{2,1,0:T(8,128)(2,1)}, f32[4,197,2]{2,1,0:T(8,128)}) custom-call(bf16[32,208,256]{2,1,0:T(8,128)(2,1)} %copy-done, s32[4,197,2]{2,1,0:T(8,128)} %get-tuple-element.221.target_ref), custom_call_target="tpu_custom_call" | custom-call | flops 619708416 | bytes 3414176 | tf_op jit(solution)/shard_map/pallas_call | solution.py:645
  365.2 81.8 %collective-permute-done.13.refs_2_ = bf16[1552,768]{1,0:T(8,128)(2,1)} collective-permute-done((bf16[1552,768]{1,0:T(8,128)(2,1)}, bf16[1552,768]{1,0:T(8,128)(2,1)}, u32[]{:S(2)}, u32[]{:S(2)}) %collective-permute-start.13) | collective-permute-done | bytes 2383904 | tf_op jit(solution)/shard_map/ppermute | solution.py:370
  446.9 8.7 %shard_map.294 = (f32[16,192,768]{2,1,0:T(8,128)}, f32[16,192,768]{2,1,0:T(8,128)}) custom-call(s32[1]{0:T(128)} %bitcast.8.at_ref, bf16[1552,768]{1,0:T(8,128)(2,1)} %get-tuple-element.102.refs_0_, bf16[1552,768]{1,0:T(8,128)(2,1)} %collective-permute-done.12.refs_1_, bf16[1552,768]{1,0:T(8,128)(2,1)} %collective-permute-done.13.refs_2_), custom_call_target="tpu_custom_call" | custom-call | tf_op jit(solution)/shard_map/pallas_call | solution.py:615
  460.4 21.3 %shard_map.295 = (f32[4,197,768]{2,1,0:T(8,128)}, bf16[4,197,768]{2,1,0:T(8,128)(2,1)}, bf16[768,800]{1,0:T(8,128)(2,1)}, f32[8,768]{1,0:T(8,128)}) custom-call(s32[1]{0:T(128)S(6)} %copy.250.held_ref, bf16[4,197,768]{2,1,0:T(8,128)(2,1)} %copy.193.images_ref, bf16[4,197,768]{2,1,0:T(8,128)(2,1)} %copy.194.cot_ref, ...), custom_call_target="tpu_custom_call" | custom-call | flops 3623236608 | bytes 8652100 | tf_op jit(solution)/shard_map/pallas_call | solution.py:645
  483.3 26.5 %collective-permute-done.14 = bf16[1552,768]{1,0:T(8,128)(2,1)} collective-permute-done((bf16[1552,768]{1,0:T(8,128)(2,1)}, bf16[1552,768]{1,0:T(8,128)(2,1)}, u32[]{:S(2)}, u32[]{:S(2)}) %collective-permute-start.14) | collective-permute-done | bytes 2383904 | tf_op jit(solution)/shard_map/ppermute | solution.py:370
  514.7 5.9 shard_map.296
  520.6 24.2 %all-reduce.2.cloned.1.call-done.normed_ref = bf16[4,197,768]{2,1,0:T(8,128)(2,1)} async-done(((bf16[4,197,768]{2,1,0:T(8,128)(2,1)}), bf16[4,197,768]{2,1,0:T(8,128)(2,1)}) %all-reduce.2.cloned.1.call-update) | async-done | bytes 1210384 | tf_op jit(solution)/shard_map/psum | solution.py:1220
  544.8 5.6 shard_map.297
  558.2 16.3 %all-to-all-done.4 = bf16[8,96,814]{2,1,0:T(8,128)(2,1)S(1)} async-done(((bf16[8,96,814]{2,1,0:T(8,128)(2,1)}), bf16[8,96,814]{2,1,0:T(8,128)(2,1)S(1)}, u32[]{:S(2)}, u32[]{:S(2)}) %all-to-all-start.4) | async-done | bytes 1250336 | tf_op jit(solution)/shard_map/all_to_all | solution.py:351
  576.2 4.1 copy.204
  580.3 4.5 collective-permute-done.15
  (176 shorter events, 78.5 us)
Async XLA Ops:
  12.0 69.1 %collective-permute-start.4 = (bf16[4,192,768]{2,1,0:T(8,128)(2,1)}, bf16[4,192,768]{2,1,0:T(8,128)(2,1)}, u32[]{:S(2)}, u32[]{:S(2)}) collective-permute-start(bf16[4,192,768]{2,1,0:T(8,128)(2,1)} %get-tuple-element.212), channel_id=1, source_target_pairs={{0,24},{8,16},{16,8},{24,0},{1,25},{9,17},{17,9},{25,1},{2,26},{10... | collective-permute-start | bytes 3538952 | tf_op jit(solution)/shard_map/ppermute | solution.py:370
  14.3 66.8 %collective-permute-start.3 = (bf16[4,192,768]{2,1,0:T(8,128)(2,1)}, bf16[4,192,768]{2,1,0:T(8,128)(2,1)}, u32[]{:S(2)}, u32[]{:S(2)}) collective-permute-start(bf16[4,192,768]{2,1,0:T(8,128)(2,1)} %get-tuple-element.213), channel_id=1, source_target_pairs={{0,16},{8,24},{16,0},{24,8},{1,17},{9,25},{17,1},{25,9},{2,18},{10... | collective-permute-start | bytes 3538952 | tf_op jit(solution)/shard_map/ppermute | solution.py:370
  16.8 64.3 %all-to-all-start = ((bf16[4,192,821]{2,1,0:T(8,128)(2,1)}), bf16[4,192,821]{2,1,0:T(8,128)(2,1)S(1)}, u32[]{:S(2)}, u32[]{:S(2)}) async-start(bf16[4,192,821]{2,1,0:T(8,128)(2,1)} %broadcast_in_dim.24), calls=%async_computation | async-start | bytes 2752512 | tf_op jit(solution)/shard_map/all_to_all | solution.py:351
  20.4 122.1 %all-gather.7.cloned.1.call-start = ((), (), s32[]{:S(2)}) async-start(), calls=%async_computation.6 | async-start | bytes 1536000 | tf_op jit(solution)/shard_map/all_gather | solution.py:1150
  20.4 10.9 %collective-permute-start.1 = (bf16[192,192]{1,0:T(8,128)(2,1)S(1)}, bf16[192,192]{1,0:T(8,128)(2,1)S(1)}, u32[]{:S(2)}, u32[]{:S(2)}) collective-permute-start(bf16[192,192]{1,0:T(8,128)(2,1)S(1)} %copy-done.7), channel_id=1, source_target_pairs={{0,2},{1,3},{2,0},{3,1},{4,6},{5,7},{6,4},{7,5},{8,10},{9,11},{10,... | collective-permute-start | bytes 221192 | tf_op jit(solution)/shard_map/ppermute | solution.py:358
  23.1 8.2 %collective-permute-start = (bf16[192,192]{1,0:T(8,128)(2,1)S(1)}, bf16[192,192]{1,0:T(8,128)(2,1)S(1)}, u32[]{:S(2)}, u32[]{:S(2)}) collective-permute-start(bf16[192,192]{1,0:T(8,128)(2,1)S(1)} %copy-done.7), channel_id=1, source_target_pairs={{0,3},{1,2},{2,1},{3,0},{4,7},{5,6},{6,5},{7,4},{8,11},{9,10},{10,... | collective-permute-start | bytes 221192 | tf_op jit(solution)/shard_map/ppermute | solution.py:358
  24.4 7.6 %collective-permute-start.2 = (bf16[192,192]{1,0:T(8,128)(2,1)S(1)}, bf16[192,192]{1,0:T(8,128)(2,1)S(1)}, u32[]{:S(2)}, u32[]{:S(2)}) collective-permute-start(bf16[192,192]{1,0:T(8,128)(2,1)S(1)} %copy-done.7), channel_id=1, source_target_pairs={{0,1},{1,0},{2,3},{3,2},{4,5},{5,4},{6,7},{7,6},{8,9},{9,8},{10,11... | collective-permute-start | bytes 221192 | tf_op jit(solution)/shard_map/ppermute | solution.py:358
  89.2 53.3 %collective-permute-start.5 = (bf16[4,192,768]{2,1,0:T(8,128)(2,1)}, bf16[4,192,768]{2,1,0:T(8,128)(2,1)}, u32[]{:S(2)}, u32[]{:S(2)}) collective-permute-start(bf16[4,192,768]{2,1,0:T(8,128)(2,1)} %get-tuple-element.211), channel_id=1, source_target_pairs={{0,8},{8,0},{16,24},{24,16},{1,9},{9,1},{17,25},{25,17},{2,10},{10... | collective-permute-start | bytes 3538952 | tf_op jit(solution)/shard_map/ppermute | solution.py:370
  93.9 71.1 %collective-permute-start.11 = (bf16[4,192,768]{2,1,0:T(8,128)(2,1)}, bf16[4,192,768]{2,1,0:T(8,128)(2,1)}, u32[]{:S(2)}, u32[]{:S(2)}) collective-permute-start(bf16[4,192,768]{2,1,0:T(8,128)(2,1)} %get-tuple-element.207), channel_id=1, source_target_pairs={{0,24},{8,16},{16,8},{24,0},{1,25},{9,17},{17,9},{25,1},{2,26},{10... | collective-permute-start | bytes 3538952 | tf_op jit(solution)/shard_map/ppermute | solution.py:370
  97.0 34.9 %collective-permute-start.7 = (bf16[768,192]{1,0:T(8,128)(2,1)S(1)}, bf16[768,192]{1,0:T(8,128)(2,1)}, u32[]{:S(2)}, u32[]{:S(2)}) collective-permute-start(bf16[768,192]{1,0:T(8,128)(2,1)S(1)} %pad_maximum_fusion.2), channel_id=1, source_target_pairs={{0,16},{8,24},{16,0},{24,8},{1,17},{9,25},{17,1},{25,9},{2,18},{10... | collective-permute-start | bytes 884744 | tf_op jit(solution)/shard_map/ppermute | solution.py:358
  98.0 41.7 %collective-permute-start.6 = (bf16[768,192]{1,0:T(8,128)(2,1)S(1)}, bf16[768,192]{1,0:T(8,128)(2,1)}, u32[]{:S(2)}, u32[]{:S(2)}) collective-permute-start(bf16[768,192]{1,0:T(8,128)(2,1)S(1)} %pad_maximum_fusion.2), channel_id=1, source_target_pairs={{0,24},{8,16},{16,8},{24,0},{1,25},{9,17},{17,9},{25,1},{2,26},{10... | collective-permute-start | bytes 884744 | tf_op jit(solution)/shard_map/ppermute | solution.py:358
  100.3 64.7 %collective-permute-start.9 = (bf16[4,192,768]{2,1,0:T(8,128)(2,1)}, bf16[4,192,768]{2,1,0:T(8,128)(2,1)}, u32[]{:S(2)}, u32[]{:S(2)}) collective-permute-start(bf16[4,192,768]{2,1,0:T(8,128)(2,1)} %get-tuple-element.208), channel_id=1, source_target_pairs={{0,8},{8,0},{16,24},{24,16},{1,9},{9,1},{17,25},{25,17},{2,10},{10... | collective-permute-start | bytes 3538952 | tf_op jit(solution)/shard_map/ppermute | solution.py:370
  131.9 33.4 %collective-permute-start.10 = (bf16[4,192,768]{2,1,0:T(8,128)(2,1)}, bf16[4,192,768]{2,1,0:T(8,128)(2,1)}, u32[]{:S(2)}, u32[]{:S(2)}) collective-permute-start(bf16[4,192,768]{2,1,0:T(8,128)(2,1)} %get-tuple-element.210), channel_id=1, source_target_pairs={{0,16},{8,24},{16,0},{24,8},{1,17},{9,25},{17,1},{25,9},{2,18},{10... | collective-permute-start | bytes 3538952 | tf_op jit(solution)/shard_map/ppermute | solution.py:370
  165.3 78.0 %all-to-all-start.1 = ((bf16[8,528,768]{2,1,0:T(8,128)(2,1)}), bf16[8,528,768]{2,1,0:T(8,128)(2,1)}, u32[]{:S(2)}, u32[]{:S(2)}) async-start(bf16[8,528,768]{2,1,0:T(8,128)(2,1)} %get-tuple-element.79), calls=%async_computation.1 | async-start | bytes 12976128 | tf_op jit(solution)/shard_map/all_to_all | solution.py:351
  266.4 81.2 %all-to-all-start.2 = ((bf16[32,208,256]{2,1,0:T(8,128)(2,1)}), bf16[32,208,256]{2,1,0:T(8,128)(2,1)S(1)}, u32[]{:S(2)}, u32[]{:S(2)}) async-start(bf16[32,208,256]{2,1,0:T(8,128)(2,1)} %bitcast.54), calls=%async_computation.2 | async-start | bytes 6815744 | tf_op jit(solution)/shard_map/all_to_all | solution.py:351
  356.2 127.1 %all-to-all-start.3 = ((bf16[32,192,256]{2,1,0:T(8,128)(2,1)}), bf16[32,192,256]{2,1,0:T(8,128)(2,1)S(1)}, u32[]{:S(2)}, u32[]{:S(2)}) async-start(bf16[32,192,256]{2,1,0:T(8,128)(2,1)} %bitcast.55), calls=%async_computation.3 | async-start | bytes 6291456 | tf_op jit(solution)/shard_map/all_to_all | solution.py:351
  360.2 95.5 %all-gather.9.cloned.1.call-start = ((), (), s32[]{:S(2)}) async-start(), calls=%async_computation.7 | async-start | bytes 1536000 | tf_op jit(solution)/shard_map/all_gather | solution.py:1199
  360.2 5.0 collective-permute-start.12
  360.5 86.4 %collective-permute-start.13 = (bf16[1552,768]{1,0:T(8,128)(2,1)}, bf16[1552,768]{1,0:T(8,128)(2,1)}, u32[]{:S(2)}, u32[]{:S(2)}) collective-permute-start(bf16[1552,768]{1,0:T(8,128)(2,1)} %get-tuple-element.104), channel_id=1, source_target_pairs={{0,16},{8,24},{16,0},{24,8},{1,17},{9,25},{17,1},{25,9},{2,18},{10... | collective-permute-start | bytes 7151624 | tf_op jit(solution)/shard_map/ppermute | solution.py:370
  362.2 182.5 %all-reduce.2.cloned.1.call-start = ((), (), s32[]{:S(2)}) async-start(), calls=%async_computation.5 | async-start | bytes 2457600 | tf_op jit(solution)/shard_map/psum | solution.py:1220
  455.6 54.2 %collective-permute-start.14 = (bf16[1552,768]{1,0:T(8,128)(2,1)}, bf16[1552,768]{1,0:T(8,128)(2,1)}, u32[]{:S(2)}, u32[]{:S(2)}) collective-permute-start(bf16[1552,768]{1,0:T(8,128)(2,1)} %get-tuple-element.114), channel_id=1, source_target_pairs={{0,24},{8,16},{16,8},{24,0},{1,25},{9,17},{17,9},{25,1},{2,26},{10... | collective-permute-start | bytes 7151624 | tf_op jit(solution)/shard_map/ppermute | solution.py:370
  552.8 21.7 %all-to-all-start.4 = ((bf16[8,96,814]{2,1,0:T(8,128)(2,1)}), bf16[8,96,814]{2,1,0:T(8,128)(2,1)S(1)}, u32[]{:S(2)}, u32[]{:S(2)}) async-start(bf16[8,96,814]{2,1,0:T(8,128)(2,1)} %bitcast.23), calls=%async_computation.4 | async-start | bytes 2752512 | tf_op jit(solution)/shard_map/all_to_all | solution.py:351
  556.4 33.6 %all-gather.11.cloned.1.call-start = ((), (), s32[]{:S(2)}) async-start(), calls=%async_computation.8 | async-start | bytes 1536000 | tf_op jit(solution)/shard_map/all_gather | solution.py:1239
  574.7 10.2 %collective-permute-start.15 = (f32[96,814]{1,0:T(8,128)S(1)}, f32[96,814]{1,0:T(8,128)S(1)}, u32[]{:S(2)}, u32[]{:S(2)}) collective-permute-start(f32[96,814]{1,0:T(8,128)S(1)} %convert_reduce_fusion), channel_id=1, source_target_pairs={{0,4},{4,0},{1,5},{5,1},{2,6},{6,2},{3,7},{7,3},{8,12},{12,8},{9,1... | collective-permute-start | bytes 937736 | tf_op jit(solution)/shard_map/ppermute | solution.py:358
  (23 other events, 248.1 us)
Sparse Core Ops, SparseCore 0:
  89.3 33.3 all-gather.6
  363.1 64.4 all-gather.8
  483.4 61.2 all-reduce.1
  558.6 31.4 all-gather.10

commit v13 on v12

--- a/solution.py
+++ b/solution.py
@@ -1127,8 +1127,8 @@
     in_pieces = [piece(w_in, s) for s in range(owners)]
     back_pieces = [piece(w_back.transpose(0, 2, 1), s) for s in range(owners)]
     far = owners // 2
-    packed, out_rows, in_bias_all, in_pieces[far:] = lax.optimization_barrier(
-        (packed, out_rows, in_bias_all, in_pieces[far:])
+    packed, out_rows, in_bias_all, in_pieces[far] = lax.optimization_barrier(
+        (packed, out_rows, in_bias_all, in_pieces[far])
     )
     vectors = packed[:, router_at + EXPERTS + experts_here :].T.astype(f32)
     out_whole = jnp.concatenate(hop_gather(out_rows, DP), axis=1)
@@ -1198,7 +1198,7 @@
     rows_cut, returned_out = lax.optimization_barrier((rows_cut, returned_out))
     rows_all = lax.all_gather(rows_cut, tensor_axes)
     returned = bring(returned_out)
-    wide = run_widen(owner_at, weight_parts[: far + 1], owners, mine, shard_width)
+    wide = run_widen(owner_at, weight_parts[:far], owners, mine, shard_width)
     rows_all, wide, weight_parts[far + 1 :] = lax.optimization_barrier(
         (rows_all, wide, weight_parts[far + 1 :])
     )
@@ -1220,14 +1220,16 @@
     grad_normed = lax.psum(normed_part, tensor_axes)
     last_parts = [cross(part, far + 1 + s) for s, part in enumerate(weight_parts[far + 1 :])]
     weight_parts[far + 1 :] = last_parts
+    normed_part, returned, weight_parts[far] = lax.optimization_barrier(
+        (normed_part, returned, weight_parts[far])
+    )
     grad_w_in, grad_w_back = wide
-    for s in range(far + 1, owners):
+    for s in range(far, owners):
         two = weight_parts[s][: 2 * mine * shard_width].astype(f32)
         two = two.reshape(2, mine, shard_width, ff_here)
         start = (owner_at ^ s) * mine
         grad_w_in = lax.dynamic_update_slice_in_dim(grad_w_in, two[0], start, 0)
         grad_w_back = lax.dynamic_update_slice_in_dim(grad_w_back, two[1], start, 0)
-    normed_part, returned = lax.optimization_barrier((normed_part, returned))
     mixed_cut = lax.dynamic_slice_in_dim(mixed, tensor_at * slice_width, slice_width, 2)
     output_cut = run_take_rows(
         images_held, returned, target, probs, routes, mixed_cut, outer, inner, slots

time: 610 us -> 655 us (1.074)
  waiting for transfers between devices: 379 us -> 413 us
  local copies, waits for them, and re-layouts: 40.3 us -> 50 us
    all_gather x1, waiting for transfers between devices: 0.01 us -> 55.9 us  [moved_plan(): rows_all = lax.all_gather(rows_cut, tensor_axes)]
    all_to_all x5, waiting for transfers between devices: 199 us -> 174 us  [swap(): return lax.all_to_all(values, axes, split_axis=0, concat_axis=0, tiled=True)]
    psum x1, waiting for transfers between devices: 24.2 us -> 35.4 us  [moved_plan(): grad_normed = lax.psum(normed_part, tensor_axes)]
    ppermute x9, waiting for transfers between devices: 111 us -> 102 us  [cross(): lax.ppermute(values, (DP, INNER), [(i, i ^ s) for i in range(count)])]
    unnamed x54 -> x58, local copies, waits for them, and re-layouts: 15.2 us -> 16.9 us
  transfers between devices with their start and end apart: 25 -> 25, of which waited for: 15 -> 16; matrix products, arithmetic and copies ran while one was open for 7% -> 8% of each run, Pallas kernels for 12% -> 11%
where the time goes in v13:
time: 655 us; the launch traced here: 648 us
  waiting for transfers between devices  413 us (63%)
  Pallas kernels  111 us (17%)
  local copies, waits for them, and re-layouts  50 us (8%)
  starting transfers between devices  38.5 us (6%)
  other arithmetic  20.4 us (3%)
  between operations  15.3 us (2%)
    all_to_all x5, waiting for transfers between devices, swap(): return lax.all_to_all(values, axes, split_axis=0, concat_axis=0, tiled=True)  174 us
    ppermute x9, waiting for transfers between devices, cross(): lax.ppermute(values, (DP, INNER), [(i, i ^ s) for i in range(count)])  102 us
    pallas_call x6, Pallas kernels, call_kernel(): pl.pallas_call(kernel, grid=grid, in_specs=[smem if b is None else pl.Blo...  68.8 us
    all_gather x1, waiting for transfers between devices, moved_plan(): rows_all = lax.all_gather(rows_cut, tensor_axes)  55.9 us
    ppermute x7, waiting for transfers between devices, hop_gather(): hops.append(lax.ppermute(values, axes, [(i, i ^ s) for i in range(count)]))  44.3 us
    psum x1, waiting for transfers between devices, moved_plan(): grad_normed = lax.psum(normed_part, tensor_axes)  35.4 us
    pallas_call x1, Pallas kernels, run_experts(): pl.pallas_call(functools.partial(expert_kernel, inner, owners), grid=(min...  23.1 us
    all_to_all x5, starting transfers between devices, swap(): return lax.all_to_all(values, axes, split_axis=0, concat_axis=0, tiled=True)  21.4 us
  transfers between devices with their start and end apart: 25, of which 16 were waited for; matrix products, arithmetic and copies ran while one was open for 8% of the time, Pallas kernels for 11%

profile of v13, /device:TPU:0, one launch (start us, length us, event | category | flops | bytes accessed | tf_op | source)
XLA Modules:
  0.0 647.7 jit_solution(17865232691341201061)
XLA Ops:
  26.5 4.7 collective-permute-done.1
  32.1 23.7 %all-to-all-done = bf16[4,192,821]{2,1,0:T(8,128)(2,1)S(1)} async-done(((bf16[4,192,821]{2,1,0:T(8,128)(2,1)}), bf16[4,192,821]{2,1,0:T(8,128)(2,1)S(1)}, u32[]{:S(2)}, u32[]{:S(2)}) %all-to-all-start) | async-done | bytes 1261088 | tf_op jit(solution)/shard_map/all_to_all | solution.py:351
  57.3 6.6 %shard_map.289 = (bf16[2,197,384]{2,1,0:T(8,128)(2,1)}, bf16[4,197,576]{2,1,0:T(8,128)(2,1)}) custom-call(bf16[4,197,768]{2,1,0:T(8,128)(2,1)} %copy.193.images_ref, bf16[768,821]{1,0:T(8,128)(2,1)} %bitcast.54, f32[5,768]{1,0:T(8,128)} %convert_bitcast_fusion.vector_ref, f32[2,192]{1,0:T(2,128)} %convert_element_type.45.bias_ref), custom_call_target="tpu_custom_call" | custom-call | flops 935614464 | bytes 2488320 | tf_op jit(solution)/shard_map/pallas_call | solution.py:645
  74.8 26.4 %collective-permute-done.7 = bf16[768,192]{1,0:T(8,128)(2,1)S(1)} collective-permute-done((bf16[768,192]{1,0:T(8,128)(2,1)S(1)}, bf16[768,192]{1,0:T(8,128)(2,1)S(1)}, u32[]{:S(2)}, u32[]{:S(2)}) %collective-permute-start.7) | collective-permute-done | bytes 294944 | tf_op jit(solution)/shard_map/ppermute | solution.py:358
  101.2 7.9 %collective-permute-done.6 = bf16[768,192]{1,0:T(8,128)(2,1)} collective-permute-done((bf16[768,192]{1,0:T(8,128)(2,1)S(1)}, bf16[768,192]{1,0:T(8,128)(2,1)}, u32[]{:S(2)}, u32[]{:S(2)}) %collective-permute-start.6) | collective-permute-done | bytes 294944 | tf_op jit(solution)/shard_map/ppermute | solution.py:358
  116.6 22.5 %shard_map.290 = (f32[4,197,768]{2,1,0:T(8,128)}, f32[4,197,32]{2,1,0:T(8,128)}, bf16[8,528,768]{2,1,0:T(8,128)(2,1)}) custom-call(bf16[4,197,768]{2,1,0:T(8,128)(2,1)} %copy.193.images_ref, bf16[4,197,768]{2,1,0:T(8,128)(2,1)} %copy.194.cot_ref, bf16[4,2,197,384]{3,2,1,0:T(8,128)(2,1)} %bitcast.66, bf16[768,768]{1,0:T(8,128)(2,1)} %pad_maximum_fusion.1.out_ref, ...), custom_call_target="tpu_custom_call" | custom-call | flops 5887229952 | bytes 6099776 | tf_op jit(solution)/shard_map/pallas_call | solution.py:645
  139.1 20.9 %collective-permute-done.10.refs_6_ = bf16[4,192,768]{2,1,0:T(8,128)(2,1)} collective-permute-done((bf16[4,192,768]{2,1,0:T(8,128)(2,1)}, bf16[4,192,768]{2,1,0:T(8,128)(2,1)}, u32[]{:S(2)}, u32[]{:S(2)}) %collective-permute-start.10) | collective-permute-done | bytes 1179680 | tf_op jit(solution)/shard_map/ppermute | solution.py:370
  160.0 5.2 all-to-all-start.1
  167.6 70.4 %all-to-all-done.1.rows_ref.gate_ref.cot_ref = bf16[8,528,768]{2,1,0:T(8,128)(2,1)} async-done(((bf16[8,528,768]{2,1,0:T(8,128)(2,1)}), bf16[8,528,768]{2,1,0:T(8,128)(2,1)}, u32[]{:S(2)}, u32[]{:S(2)}) %all-to-all-start.1) | async-done | bytes 6488096 | tf_op jit(solution)/shard_map/all_to_all | solution.py:351
  238.0 23.1 %shard_map.291 = (bf16[8,4,192,256]{3,2,1,0:T(8,128)(2,1)}, bf16[8,4,208,256]{3,2,1,0:T(8,128)(2,1)}, bf16[4,1,512,768]{3,2,1,0:T(8,128)(2,1)}, bf16[4,1,512,768...) custom-call(s32[1]{0:T(128)} %bitcast.8.at_ref, ...), custom_call_target="tpu_custom_call" | custom-call | flops 9663676416 | bytes 28311552 | tf_op jit(solution)/shard_map/pallas_call | solution.py:473
  261.1 5.1 all-to-all-start.2
  266.2 12.5 %shard_map.292 = (bf16[1552,768]{1,0:T(8,128)(2,1)}, bf16[1552,768]{1,0:T(8,128)(2,1)}, bf16[1552,768]{1,0:T(8,128)(2,1)}, bf16[1552,768]{1,0:T(8,128)(2,1)}) custom-call(s32[1]{0:T(128)} %bitcast.8.at_ref, bf16[8,528,768]{2,1,0:T(8,128)(2,1)} %all-to-all-done.1.rows_ref.gate_ref.cot_ref, bf16[4,1,512,768]{3,2,1,0:T(8,128)(2,1)} %get-tuple-element.89.grad_pre_ref, ...), custom_call_target="tpu_custom_call" | custom-call | flops 4831838208 | bytes 15728640 | tf_op jit(solution)/shard_map/pallas_call | solution.py:565
  278.7 63.6 %all-to-all-done.2.parts_ref = bf16[32,208,256]{2,1,0:T(8,128)(2,1)S(1)} async-done(((bf16[32,208,256]{2,1,0:T(8,128)(2,1)}), bf16[32,208,256]{2,1,0:T(8,128)(2,1)S(1)}, u32[]{:S(2)}, u32[]{:S(2)}) %all-to-all-start.2) | async-done | bytes 3407904 | tf_op jit(solution)/shard_map/all_to_all | solution.py:351
  344.1 6.9 %shard_map.293 = (bf16[2,197,384]{2,1,0:T(8,128)(2,1)}, f32[4,197,2]{2,1,0:T(8,128)}) custom-call(bf16[32,208,256]{2,1,0:T(8,128)(2,1)} %copy-done, s32[4,197,2]{2,1,0:T(8,128)} %get-tuple-element.223.target_ref), custom_call_target="tpu_custom_call" | custom-call | flops 619708416 | bytes 3414176 | tf_op jit(solution)/shard_map/pallas_call | solution.py:645
  359.9 6.5 %shard_map.294 = (f32[16,192,768]{2,1,0:T(8,128)}, f32[16,192,768]{2,1,0:T(8,128)}) custom-call(s32[1]{0:T(128)} %bitcast.8.at_ref, bf16[1552,768]{1,0:T(8,128)(2,1)} %get-tuple-element.101.refs_0_, bf16[1552,768]{1,0:T(8,128)(2,1)} %collective-permute-done.12.refs_1_), custom_call_target="tpu_custom_call" | custom-call | tf_op jit(solution)/shard_map/pallas_call | solution.py:615
  366.5 55.9 %all-gather.9.cloned.1.call-done = bf16[8,197,384]{2,1,0:T(8,128)(2,1)} async-done(((bf16[2,197,384]{2,1,0:T(8,128)(2,1)}), bf16[8,197,384]{2,1,0:T(8,128)(2,1)}) %all-gather.9.cloned.1.call-update) | async-done | bytes 1210384 | tf_op jit(solution)/shard_map/all_gather | solution.py:1199
  428.8 21.3 %shard_map.295 = (f32[4,197,768]{2,1,0:T(8,128)}, bf16[4,197,768]{2,1,0:T(8,128)(2,1)}, bf16[768,800]{1,0:T(8,128)(2,1)}, f32[8,768]{1,0:T(8,128)}) custom-call(s32[1]{0:T(128)S(6)} %copy.254.held_ref, bf16[4,197,768]{2,1,0:T(8,128)(2,1)} %copy.193.images_ref, bf16[4,197,768]{2,1,0:T(8,128)(2,1)} %copy.194.cot_ref, ...), custom_call_target="tpu_custom_call" | custom-call | flops 3623236608 | bytes 8652100 | tf_op jit(solution)/shard_map/pallas_call | solution.py:645
  451.7 30.4 %collective-permute-done.14 = bf16[1552,768]{1,0:T(8,128)(2,1)} collective-permute-done((bf16[1552,768]{1,0:T(8,128)(2,1)}, bf16[1552,768]{1,0:T(8,128)(2,1)}, u32[]{:S(2)}, u32[]{:S(2)}) %collective-permute-start.14) | collective-permute-done | bytes 2383904 | tf_op jit(solution)/shard_map/ppermute | solution.py:370
  486.6 46.7 %collective-permute-done.13 = bf16[1552,768]{1,0:T(8,128)(2,1)} collective-permute-done((bf16[1552,768]{1,0:T(8,128)(2,1)}, bf16[1552,768]{1,0:T(8,128)(2,1)}, u32[]{:S(2)}, u32[]{:S(2)}) %collective-permute-start.13) | collective-permute-done | bytes 2383904 | tf_op jit(solution)/shard_map/ppermute | solution.py:370
  533.4 5.3 slice_convert_fusion.1
  538.7 5.9 shard_map.296
  554.6 35.4 %all-reduce.2.cloned.1.call-done.normed_ref = bf16[4,197,768]{2,1,0:T(8,128)(2,1)} async-done(((bf16[4,197,768]{2,1,0:T(8,128)(2,1)}), bf16[4,197,768]{2,1,0:T(8,128)(2,1)}) %all-reduce.2.cloned.1.call-update) | async-done | bytes 1210384 | tf_op jit(solution)/shard_map/psum | solution.py:1220
  589.9 5.6 shard_map.297
  603.4 16.3 %all-to-all-done.4 = bf16[8,96,814]{2,1,0:T(8,128)(2,1)S(1)} async-done(((bf16[8,96,814]{2,1,0:T(8,128)(2,1)}), bf16[8,96,814]{2,1,0:T(8,128)(2,1)S(1)}, u32[]{:S(2)}, u32[]{:S(2)}) %all-to-all-start.4) | async-done | bytes 1250336 | tf_op jit(solution)/shard_map/all_to_all | solution.py:351
  (184 shorter events, 103.6 us)
Async XLA Ops:
  12.0 43.9 %collective-permute-start.3 = (bf16[4,192,768]{2,1,0:T(8,128)(2,1)}, bf16[4,192,768]{2,1,0:T(8,128)(2,1)}, u32[]{:S(2)}, u32[]{:S(2)}) collective-permute-start(bf16[4,192,768]{2,1,0:T(8,128)(2,1)} %get-tuple-element.215), channel_id=1, source_target_pairs={{0,16},{8,24},{16,0},{24,8},{1,17},{9,25},{17,1},{25,9},{2,18},{10... | collective-permute-start | bytes 3538952 | tf_op jit(solution)/shard_map/ppermute | solution.py:370
  16.8 39.0 %all-to-all-start = ((bf16[4,192,821]{2,1,0:T(8,128)(2,1)}), bf16[4,192,821]{2,1,0:T(8,128)(2,1)S(1)}, u32[]{:S(2)}, u32[]{:S(2)}) async-start(bf16[4,192,821]{2,1,0:T(8,128)(2,1)} %broadcast_in_dim.24), calls=%async_computation | async-start | bytes 2752512 | tf_op jit(solution)/shard_map/all_to_all | solution.py:351
  20.3 96.3 %all-gather.7.cloned.1.call-start = ((), (), s32[]{:S(2)}) async-start(), calls=%async_computation.6 | async-start | bytes 1536000 | tf_op jit(solution)/shard_map/all_gather | solution.py:1150
  20.4 10.9 %collective-permute-start.1 = (bf16[192,192]{1,0:T(8,128)(2,1)S(1)}, bf16[192,192]{1,0:T(8,128)(2,1)S(1)}, u32[]{:S(2)}, u32[]{:S(2)}) collective-permute-start(bf16[192,192]{1,0:T(8,128)(2,1)S(1)} %copy-done.9), channel_id=1, source_target_pairs={{0,2},{1,3},{2,0},{3,1},{4,6},{5,7},{6,4},{7,5},{8,10},{9,11},{10,... | collective-permute-start | bytes 221192 | tf_op jit(solution)/shard_map/ppermute | solution.py:358
  23.1 8.2 %collective-permute-start = (bf16[192,192]{1,0:T(8,128)(2,1)S(1)}, bf16[192,192]{1,0:T(8,128)(2,1)S(1)}, u32[]{:S(2)}, u32[]{:S(2)}) collective-permute-start(bf16[192,192]{1,0:T(8,128)(2,1)S(1)} %copy-done.9), channel_id=1, source_target_pairs={{0,3},{1,2},{2,1},{3,0},{4,7},{5,6},{6,5},{7,4},{8,11},{9,10},{10,... | collective-permute-start | bytes 221192 | tf_op jit(solution)/shard_map/ppermute | solution.py:358
  24.4 7.6 %collective-permute-start.2 = (bf16[192,192]{1,0:T(8,128)(2,1)S(1)}, bf16[192,192]{1,0:T(8,128)(2,1)S(1)}, u32[]{:S(2)}, u32[]{:S(2)}) collective-permute-start(bf16[192,192]{1,0:T(8,128)(2,1)S(1)} %copy-done.9), channel_id=1, source_target_pairs={{0,1},{1,0},{2,3},{3,2},{4,5},{5,4},{6,7},{7,6},{8,9},{9,8},{10,11... | collective-permute-start | bytes 221192 | tf_op jit(solution)/shard_map/ppermute | solution.py:358
  63.9 52.7 %collective-permute-start.5 = (bf16[4,192,768]{2,1,0:T(8,128)(2,1)}, bf16[4,192,768]{2,1,0:T(8,128)(2,1)}, u32[]{:S(2)}, u32[]{:S(2)}) collective-permute-start(bf16[4,192,768]{2,1,0:T(8,128)(2,1)} %get-tuple-element.213), channel_id=1, source_target_pairs={{0,24},{8,16},{16,8},{24,0},{1,25},{9,17},{17,9},{25,1},{2,26},{10... | collective-permute-start | bytes 3538952 | tf_op jit(solution)/shard_map/ppermute | solution.py:370
  64.3 52.3 %collective-permute-start.4 = (bf16[4,192,768]{2,1,0:T(8,128)(2,1)}, bf16[4,192,768]{2,1,0:T(8,128)(2,1)}, u32[]{:S(2)}, u32[]{:S(2)}) collective-permute-start(bf16[4,192,768]{2,1,0:T(8,128)(2,1)} %get-tuple-element.216), channel_id=1, source_target_pairs={{0,8},{8,0},{16,24},{24,16},{1,9},{9,1},{17,25},{25,17},{2,10},{10... | collective-permute-start | bytes 3538952 | tf_op jit(solution)/shard_map/ppermute | solution.py:370
  67.1 7.3 %collective-permute-start.8 = (bf16[768,192]{1,0:T(8,128)(2,1)S(1)}, bf16[768,192]{1,0:T(8,128)(2,1)S(1)}, u32[]{:S(2)}, u32[]{:S(2)}) collective-permute-start(bf16[768,192]{1,0:T(8,128)(2,1)S(1)} %pad_maximum_fusion.2), channel_id=1, source_target_pairs={{0,8},{8,0},{16,24},{24,16},{1,9},{9,1},{17,25},{25,17},{2,10},{10... | collective-permute-start | bytes 884744 | tf_op jit(solution)/shard_map/ppermute | solution.py:358
  67.2 34.0 %collective-permute-start.7 = (bf16[768,192]{1,0:T(8,128)(2,1)S(1)}, bf16[768,192]{1,0:T(8,128)(2,1)S(1)}, u32[]{:S(2)}, u32[]{:S(2)}) collective-permute-start(bf16[768,192]{1,0:T(8,128)(2,1)S(1)} %pad_maximum_fusion.2), channel_id=1, source_target_pairs={{0,16},{8,24},{16,0},{24,8},{1,17},{9,25},{17,1},{25,9},{2,18},{10... | collective-permute-start | bytes 884744 | tf_op jit(solution)/shard_map/ppermute | solution.py:358
  67.7 41.5 %collective-permute-start.6 = (bf16[768,192]{1,0:T(8,128)(2,1)S(1)}, bf16[768,192]{1,0:T(8,128)(2,1)}, u32[]{:S(2)}, u32[]{:S(2)}) collective-permute-start(bf16[768,192]{1,0:T(8,128)(2,1)S(1)} %pad_maximum_fusion.2), channel_id=1, source_target_pairs={{0,24},{8,16},{16,8},{24,0},{1,25},{9,17},{17,9},{25,1},{2,26},{10... | collective-permute-start | bytes 884744 | tf_op jit(solution)/shard_map/ppermute | solution.py:358
  74.4 64.7 %collective-permute-start.11 = (bf16[4,192,768]{2,1,0:T(8,128)(2,1)}, bf16[4,192,768]{2,1,0:T(8,128)(2,1)}, u32[]{:S(2)}, u32[]{:S(2)}) collective-permute-start(bf16[4,192,768]{2,1,0:T(8,128)(2,1)} %get-tuple-element.209), channel_id=1, source_target_pairs={{0,24},{8,16},{16,8},{24,0},{1,25},{9,17},{17,9},{25,1},{2,26},{10... | collective-permute-start | bytes 3538952 | tf_op jit(solution)/shard_map/ppermute | solution.py:370
  101.2 37.9 %collective-permute-start.9 = (bf16[4,192,768]{2,1,0:T(8,128)(2,1)}, bf16[4,192,768]{2,1,0:T(8,128)(2,1)}, u32[]{:S(2)}, u32[]{:S(2)}) collective-permute-start(bf16[4,192,768]{2,1,0:T(8,128)(2,1)} %get-tuple-element.210), channel_id=1, source_target_pairs={{0,8},{8,0},{16,24},{24,16},{1,9},{9,1},{17,25},{25,17},{2,10},{10... | collective-permute-start | bytes 3538952 | tf_op jit(solution)/shard_map/ppermute | solution.py:370
  109.1 50.9 %collective-permute-start.10 = (bf16[4,192,768]{2,1,0:T(8,128)(2,1)}, bf16[4,192,768]{2,1,0:T(8,128)(2,1)}, u32[]{:S(2)}, u32[]{:S(2)}) collective-permute-start(bf16[4,192,768]{2,1,0:T(8,128)(2,1)} %get-tuple-element.212), channel_id=1, source_target_pairs={{0,16},{8,24},{16,0},{24,8},{1,17},{9,25},{17,1},{25,9},{2,18},{10... | collective-permute-start | bytes 3538952 | tf_op jit(solution)/shard_map/ppermute | solution.py:370
  160.0 78.0 %all-to-all-start.1 = ((bf16[8,528,768]{2,1,0:T(8,128)(2,1)}), bf16[8,528,768]{2,1,0:T(8,128)(2,1)}, u32[]{:S(2)}, u32[]{:S(2)}) async-start(bf16[8,528,768]{2,1,0:T(8,128)(2,1)} %get-tuple-element.78), calls=%async_computation.1 | async-start | bytes 12976128 | tf_op jit(solution)/shard_map/all_to_all | solution.py:351
  261.1 81.2 %all-to-all-start.2 = ((bf16[32,208,256]{2,1,0:T(8,128)(2,1)}), bf16[32,208,256]{2,1,0:T(8,128)(2,1)S(1)}, u32[]{:S(2)}, u32[]{:S(2)}) async-start(bf16[32,208,256]{2,1,0:T(8,128)(2,1)} %bitcast.58), calls=%async_computation.2 | async-start | bytes 6815744 | tf_op jit(solution)/shard_map/all_to_all | solution.py:351
  351.0 182.4 %all-to-all-start.3 = ((bf16[32,192,256]{2,1,0:T(8,128)(2,1)}), bf16[32,192,256]{2,1,0:T(8,128)(2,1)S(1)}, u32[]{:S(2)}, u32[]{:S(2)}) async-start(bf16[32,192,256]{2,1,0:T(8,128)(2,1)} %bitcast.59), calls=%async_computation.3 | async-start | bytes 6291456 | tf_op jit(solution)/shard_map/all_to_all | solution.py:351
  354.9 67.5 %all-gather.9.cloned.1.call-start = ((), (), s32[]{:S(2)}) async-start(), calls=%async_computation.7 | async-start | bytes 1536000 | tf_op jit(solution)/shard_map/all_gather | solution.py:1199
  355.6 234.3 %all-reduce.2.cloned.1.call-start = ((), (), s32[]{:S(2)}) async-start(), calls=%async_computation.5 | async-start | bytes 2457600 | tf_op jit(solution)/shard_map/psum | solution.py:1220
  422.4 59.8 %collective-permute-start.14 = (bf16[1552,768]{1,0:T(8,128)(2,1)}, bf16[1552,768]{1,0:T(8,128)(2,1)}, u32[]{:S(2)}, u32[]{:S(2)}) collective-permute-start(bf16[1552,768]{1,0:T(8,128)(2,1)} %get-tuple-element.114), channel_id=1, source_target_pairs={{0,24},{8,16},{16,8},{24,0},{1,25},{9,17},{17,9},{25,1},{2,26},{10... | collective-permute-start | bytes 7151624 | tf_op jit(solution)/shard_map/ppermute | solution.py:370
  426.5 106.9 %collective-permute-start.13 = (bf16[1552,768]{1,0:T(8,128)(2,1)}, bf16[1552,768]{1,0:T(8,128)(2,1)}, u32[]{:S(2)}, u32[]{:S(2)}) collective-permute-start(bf16[1552,768]{1,0:T(8,128)(2,1)} %get-tuple-element.110), channel_id=1, source_target_pairs={{0,16},{8,24},{16,0},{24,8},{1,17},{9,25},{17,1},{25,9},{2,18},{10... | collective-permute-start | bytes 7151624 | tf_op jit(solution)/shard_map/ppermute | solution.py:370
  597.9 21.7 %all-to-all-start.4 = ((bf16[8,96,814]{2,1,0:T(8,128)(2,1)}), bf16[8,96,814]{2,1,0:T(8,128)(2,1)S(1)}, u32[]{:S(2)}, u32[]{:S(2)}) async-start(bf16[8,96,814]{2,1,0:T(8,128)(2,1)} %bitcast.25), calls=%async_computation.4 | async-start | bytes 2752512 | tf_op jit(solution)/shard_map/all_to_all | solution.py:351
  601.6 33.6 %all-gather.11.cloned.1.call-start = ((), (), s32[]{:S(2)}) async-start(), calls=%async_computation.8 | async-start | bytes 1536000 | tf_op jit(solution)/shard_map/all_gather | solution.py:1241
  619.8 10.2 %collective-permute-start.15 = (f32[96,814]{1,0:T(8,128)S(1)}, f32[96,814]{1,0:T(8,128)S(1)}, u32[]{:S(2)}, u32[]{:S(2)}) collective-permute-start(f32[96,814]{1,0:T(8,128)S(1)} %convert_reduce_fusion), channel_id=1, source_target_pairs={{0,4},{4,0},{1,5},{5,1},{2,6},{6,2},{3,7},{7,3},{8,12},{12,8},{9,1... | collective-permute-start | bytes 937736 | tf_op jit(solution)/shard_map/ppermute | solution.py:358
  (25 other events, 200.1 us)
Sparse Core Ops, SparseCore 0:
  64.0 32.7 all-gather.6
  357.9 64.4 all-gather.8
  533.5 56.3 all-reduce.1
  603.7 31.4 all-gather.10
